TPU v7x, 512 devices: a whole 4x8x8 slice. The times are simulated.
512 devices in a mesh: enc: 64 (over x, y, core), tp: 8 (over z).
Axes of the slice: x: 4, y: 8, z: 8, core: 2. Of those that a mesh axis runs over, the one named last changes fastest.
Arguments:
- queries: bfloat16 [8192, 4096], P('enc', 'tp'), may hold values from -3 to 3
- out_grad: bfloat16 [8192, 4096], P('enc', 'tp'), may hold values from -8 to 8
- encodings: bfloat16 [64, 128, 896], P('enc', 'tp'), may hold values from -3 to 3
- kv_weight: bfloat16 [2, 896, 4096], P(None, None, 'tp'), may hold values from -0.1875 to 0.1875
- neighbour_ids: int32 [128, 2], P('enc'), may hold values from 0 to 63
- rot_offset: int32 [128, 2], P('enc'), may hold values from 0 to 255
Outputs:
- grad_query: bfloat16 [8192, 4096], P('enc', 'tp')
- grad_encodings: float32 [64, 128, 896], P('enc', 'tp')
Inputs may be any that keep to these rules, and one draw needn't show every extreme that they name: `neighbour_ids`: block index = owner index of enc times 1 plus the owner's own block.
All inputs are finite; a program needn't handle non-finite values.
Results may differ from a plain program's by a relative error of at most 0.011.
Values may be sent and summed in bfloat16 or wider, within the bound.
No kernel may reach another device: no remote copies, remote signals or barrier semaphores. Data moves between devices by JAX's collectives and lax.ppermute only.
A program may use at most 64 MiB of HBM per device.

v0:
```python
import math

import jax
import jax.numpy as jnp
from jax import lax
from jax.sharding import PartitionSpec as P

HEAD = 128
DE = 896
SPAN = 64
NEIGH = 2
NLEN = 128


def rotary_tables(positions, head_width):
    halfway = head_width // 2
    exponent = jnp.arange(halfway, dtype=jnp.float32) * (2.0 / head_width)
    frequency = jnp.exp(-math.log(10000.0) * exponent)
    angles = positions.astype(jnp.float32)[:, None] * frequency[None, :]
    return (jnp.cos(angles), jnp.sin(angles))


def rotate(vectors, cosine, sine_table):
    halfway = vectors.shape[-1] // 2
    former = vectors[..., :halfway]
    latter = vectors[..., halfway:]
    return jnp.concatenate(
        [former * cosine - latter * sine_table, former * sine_table + latter * cosine], axis=-1
    )


def rotate_back(vectors, cosine, sine_table):
    halfway = vectors.shape[-1] // 2
    former = vectors[..., :halfway]
    latter = vectors[..., halfway:]
    return jnp.concatenate(
        [former * cosine + latter * sine_table, latter * cosine - former * sine_table], axis=-1
    )


def local(queries, out_grad, encodings, kv_weight, neighbour_ids, rot_offset):
    enc_count = lax.axis_size("enc")
    owned_blocks = encodings.shape[0]
    slice_rows = encodings.shape[1]
    blocks_all = owned_blocks * enc_count
    span_count = neighbour_ids.shape[0]
    read_count = span_count * NEIGH
    width_here = kv_weight.shape[2]
    heads_here = width_here // HEAD
    halfway = HEAD // 2
    row_width = slice_rows * DE
    score_scale = 1.0 / math.sqrt(HEAD)
    flat_ids = neighbour_ids.reshape(read_count)
    selector = flat_ids[:, None] == jnp.arange(blocks_all, dtype=jnp.int32)[None, :]
    select_low = selector.astype(jnp.bfloat16)
    gathered = lax.all_gather(encodings, "enc", axis=0, tiled=True)
    picked = jnp.dot(
        select_low, gathered.reshape(blocks_all, row_width), preferred_element_type=jnp.float32
    )
    picked = picked.astype(jnp.bfloat16).reshape(read_count, slice_rows, DE)
    neighbours = lax.all_gather(picked, "tp", axis=1, tiled=True)
    rows_flat = neighbours.reshape(read_count * NLEN, DE)
    key_raw = jnp.dot(rows_flat, kv_weight[0], preferred_element_type=jnp.float32).reshape(
        read_count, NLEN, heads_here, HEAD
    )
    values_low = jnp.dot(rows_flat, kv_weight[1], preferred_element_type=jnp.float32).astype(
        jnp.bfloat16
    )
    values_low = values_low.reshape(span_count, NEIGH * NLEN, heads_here, HEAD)
    positions = rot_offset.reshape(read_count)[:, None] + jnp.arange(NLEN, dtype=jnp.int32)[None, :]
    key_cos, key_sin = rotary_tables(positions.reshape(read_count * NLEN), HEAD)
    key_cos = key_cos.reshape(read_count, NLEN, 1, halfway)
    key_sin = key_sin.reshape(read_count, NLEN, 1, halfway)
    keys_low = (
        rotate(key_raw, key_cos, key_sin)
        .astype(jnp.bfloat16)
        .reshape(span_count, NEIGH * NLEN, heads_here, HEAD)
    )
    query_cos, query_sin = rotary_tables(jnp.arange(SPAN, dtype=jnp.int32), HEAD)
    query_cos = query_cos.reshape(1, SPAN, 1, halfway)
    query_sin = query_sin.reshape(1, SPAN, 1, halfway)
    query_rows = queries.astype(jnp.float32).reshape(span_count, SPAN, heads_here, HEAD)
    query_low = rotate(query_rows, query_cos, query_sin).astype(jnp.bfloat16)
    scores = (
        jnp.einsum("cqhd,ckhd->chqk", query_low, keys_low, preferred_element_type=jnp.float32)
        * score_scale
    )
    exponentials = jnp.exp(scores)
    weights = exponentials / jnp.sum(exponentials, axis=-1, keepdims=True)
    weights_low = weights.astype(jnp.bfloat16)
    attended = jnp.einsum(
        "chqk,ckhd->cqhd", weights_low, values_low, preferred_element_type=jnp.float32
    )
    grads_low = out_grad.reshape(span_count, SPAN, heads_here, HEAD)
    row_dots = jnp.sum(grads_low.astype(jnp.float32) * attended, axis=-1)
    grad_values = jnp.einsum(
        "chqk,cqhd->ckhd", weights_low, grads_low, preferred_element_type=jnp.float32
    ).astype(jnp.bfloat16)
    grad_weights = jnp.einsum(
        "cqhd,ckhd->chqk", grads_low, values_low, preferred_element_type=jnp.float32
    )
    grad_scores = (
        weights * (grad_weights - jnp.transpose(row_dots, (0, 2, 1))[..., None]) * score_scale
    ).astype(jnp.bfloat16)
    grad_rot = jnp.einsum(
        "chqk,ckhd->cqhd", grad_scores, keys_low, preferred_element_type=jnp.float32
    )
    grad_query = (
        rotate_back(grad_rot, query_cos, query_sin)
        .astype(jnp.bfloat16)
        .reshape(span_count * SPAN, width_here)
    )
    grad_keys_rot = jnp.einsum(
        "chqk,cqhd->ckhd", grad_scores, query_low, preferred_element_type=jnp.float32
    )
    grad_keys_rot = grad_keys_rot.reshape(read_count, NLEN, heads_here, HEAD)
    grad_keys = (
        rotate_back(grad_keys_rot, key_cos, key_sin)
        .astype(jnp.bfloat16)
        .reshape(read_count * NLEN, width_here)
    )
    grad_values = grad_values.reshape(read_count * NLEN, width_here)
    partial_value = jnp.einsum(
        "rk,dk->rd", grad_keys, kv_weight[0], preferred_element_type=jnp.float32
    )
    partial_value = partial_value + jnp.einsum(
        "rk,dk->rd", grad_values, kv_weight[1], preferred_element_type=jnp.float32
    )
    partial_value = partial_value.reshape(read_count, NLEN, DE)
    summed_heads = lax.psum(partial_value, "tp")
    slice_sum = lax.dynamic_slice_in_dim(
        summed_heads, lax.axis_index("tp") * slice_rows, slice_rows, 1
    )
    slice_flat = slice_sum.reshape(read_count, row_width)
    select_wide = selector.astype(jnp.float32)
    owner_part = jnp.einsum("rb,rx->bx", select_wide, slice_flat, precision=lax.Precision.HIGHEST)
    owned_sum = lax.psum_scatter(owner_part, "enc", scatter_dimension=0, tiled=True)
    return (grad_query, owned_sum.reshape(owned_blocks, slice_rows, DE))


def solution(mesh):
    in_specs = (
        P("enc", "tp"),
        P("enc", "tp"),
        P("enc", "tp", None),
        P(None, None, "tp"),
        P("enc", None),
        P("enc", None),
    )
    out_specs = (P("enc", "tp"), P("enc", "tp", None))
    return jax.shard_map(local, mesh=mesh, in_specs=in_specs, out_specs=out_specs, check_vma=False)
```

profile of v0, /device:TPU:1, one launch (start us, length us, event | category | flops | bytes accessed | tf_op | source)
XLA Modules:
  0.0 445.7 jit_solution(12369861616704195191)
XLA Ops:
  7.2 0.7 all-gather.2.cloned.1.call-update
  8.0 1.3 slice_bitcast_fusion
  9.3 0.6 copy.29
  11.3 0.8 subtract_convert_fusion.3
  12.1 87.5 %all-gather.2.cloned.1.call-done = bf16[64,16,896]{2,1,0:T(8,128)(2,1)} async-done(((bf16[1,16,896]{2,1,0:T(8,128)(2,1)}), bf16[64,16,896]{2,1,0:T(8,128)(2,1)}) %all-gather.2.cloned.1.call-update) | async-done | bytes 1835024 | tf_op jit(solution)/shard_map/all_gather | solution.py:56
  99.6 1.9 copy.52
  101.9 23.1 %all_gather.7 = bf16[4,128,896]{2,1,0:T(8,128)(2,1)S(1)} all-gather(bf16[4,16,896]{2,1,0:T(8,128)(2,1)S(1)} %bitcast.89), channel_id=1, replica_groups=mesh['enc'=64,'tp'=8] {'tp'}, dimensions={1}, use_global_device_ids=true | all-gather | bytes 1032192 | tf_op jit(solution)/shard_map/all_gather | solution.py:61
  125.0 0.7 fusion.8
  127.7 2.8 convolution_convert_fusion.2
  130.5 1.2 reshape.176
  132.3 1.2 fusion
  135.2 1.1 copy.51
  136.7 0.7 copy-done.2
  137.4 1.2 add_convert_fusion
  139.0 0.7 fusion.12
  140.4 2.0 convolution_add_fusion
  142.7 84.0 %all-reduce.4.cloned.1.call-done = f32[4,128,896]{2,1,0:T(8,128)} async-done(((f32[4,128,896]{2,1,0:T(8,128)}), f32[4,128,896]{2,1,0:T(8,128)}) %all-reduce.4.cloned.1.call-update) | async-done | bytes 1835024 | tf_op jit(solution)/shard_map/psum | solution.py:130
  226.7 1.0 dynamic-slice_bitcast_fusion
  227.8 3.6 fusion.29
  231.4 1.4 dynamic-slice
  233.6 0.7 copy.81
  234.3 202.4 %all-reduce.6.cloned.1.call-done = f32[64,14336]{1,0:T(8,128)} async-done(((f32[64,14336]{1,0:T(8,128)}), f32[64,14336]{1,0:T(8,128)}) %all-reduce.6.cloned.1.call-update) | async-done | bytes 3670032
  436.7 1.8 dynamic-slice_reduce_fusion
  438.5 0.6 reshape.182
  (80 shorter events, 8.5 us)
Async XLA Ops:
  7.2 92.4 %all-gather.2.cloned.1.call-start = ((), (), s32[]{:S(2)}) async-start(), calls=%async_computation | async-start | bytes 1863680 | tf_op jit(solution)/shard_map/all_gather | solution.py:56
  7.9 2.0 copy-start.19
  7.9 2.1 copy-start.20
  7.9 2.2 copy-start.17
  7.9 2.2 copy-start.18
  7.9 218.8 %all-reduce.4.cloned.1.call-start = ((), (), s32[]{:S(2)}) async-start(), calls=%async_computation.1 | async-start | bytes 3670016 | tf_op jit(solution)/shard_map/psum | solution.py:130
  10.5 91.0 %copy-start.13 = (f32[64,64]{1,0:T(8,128)}, f32[64,64]{1,0:T(8,128)S(1)}, u32[]{:S(2)}) copy-start(f32[64,64]{1,0:T(8,128)S(1)} %get-tuple-element.16) | copy-start | bytes 49156
  10.5 91.0 %copy-start.15 = (f32[64,64]{1,0:T(8,128)}, f32[64,64]{1,0:T(8,128)S(1)}, u32[]{:S(2)}) copy-start(f32[64,64]{1,0:T(8,128)S(1)} %get-tuple-element.17) | copy-start | bytes 49156
  11.1 114.9 %copy-start.8 = (f32[4,128,64]{1,2,0:T(8,128)}, f32[4,128,64]{1,2,0:T(8,128)S(1)}, u32[]{:S(2)}) copy-start(f32[4,128,64]{1,2,0:T(8,128)S(1)} %get-tuple-element.15) | copy-start | bytes 393220
  125.0 0.9 copy-start.9
  126.1 1.5 copy-start
  126.9 4.8 %copy-start.3 = (bf16[2,256,4,64]{3,1,2,0:T(8,128)(2,1)}, bf16[2,256,4,64]{3,1,2,0:T(8,128)(2,1)S(1)}, u32[]{:S(2)}) copy-start(bf16[2,256,4,64]{3,1,2,0:T(8,128)(2,1)S(1)} %copy.33) | copy-start | bytes 786436
  127.6 4.1 copy-start.5
  127.6 4.0 copy-start.10
  127.7 4.0 copy-start.11
  132.3 1.8 copy-start.12
  136.4 1.0 copy-start.2
  137.4 1.6 copy-start.1
  139.0 1.0 copy-start.7
  142.4 294.3 %all-reduce.6.cloned.1.call-start = ((), (), s32[]{:S(2)}) async-start(), calls=%async_computation.2 | async-start | bytes 7340032
  231.3 1.5 copy-start.4
  231.3 1.5 copy-start.6
  231.3 1.9 copy-start.14
  231.3 1.9 copy-start.16
Sparse Core Ops, SparseCore 0:
  11.3 88.2 all-gather.1
  142.5 84.1 all-reduce.3
  231.5 205.2 all-reduce.5
where the time goes:
time: 448 us; the launch traced here: 446 us
  waiting for transfers between devices  375 us (84%)
  blocking collectives  23.1 us (5%)
  local copies, waits for them, and re-layouts  16.7 us (4%)
  between operations  14.2 us (3%)
  matrix products  13.5 us (3%)
    unnamed x4, waiting for transfers between devices  203 us
    all_gather x1, waiting for transfers between devices, local(): gathered = lax.all_gather(encodings, 'enc', axis=0, tiled=True)  87.5 us
    psum x1, waiting for transfers between devices, local(): summed_heads = lax.psum(partial_value, 'tp')  84 us
    all_gather x1, blocking collectives, local(): neighbours = lax.all_gather(picked, 'tp', axis=1, tiled=True)  23.1 us
    unnamed x51, local copies, waits for them, and re-layouts  9.64 us
  transfers between devices with their start and end apart: 3, of which 3 were waited for; matrix products, arithmetic and copies ran while one was open for 2% of the time, Pallas kernels for 0%

commit v1 on v0

v1 whole, which is shorter than its diff:
```python
import math

import jax
import jax.numpy as jnp
from jax import lax
from jax.experimental import pallas as pl
from jax.experimental.pallas import tpu as pltpu
from jax.sharding import Mesh, PartitionSpec as P

HEAD = 128
DE = 896
SPAN = 64
NEIGH = 2
NLEN = 128
NX, NY, NC, NZ = 4, 8, 2, 8
ROWS = NLEN // NZ
F32, BF16 = jnp.float32, jnp.bfloat16
VMEM = pl.BlockSpec(memory_space=pltpu.VMEM)
SMEM = pl.BlockSpec(memory_space=pltpu.SMEM)


def rotary_tables(positions):
    halfway = HEAD // 2
    exponent = jnp.arange(halfway, dtype=F32) * (2.0 / HEAD)
    frequency = jnp.exp(-math.log(10000.0) * exponent)
    angles = positions.astype(F32)[:, None] * frequency[None, :]
    cosine, sine = jnp.cos(angles), jnp.sin(angles)
    return jnp.concatenate([cosine, cosine], axis=-1), jnp.concatenate([-sine, sine], axis=-1)


def shifted(value, axis, size, shift):
    return lax.ppermute(value, axis, [(i, (i + shift) % size) for i in range(size)])


def swapped(value, axis, size):
    return lax.ppermute(value, axis, [(i, i ^ 1) for i in range(size)])


def dot(a, b, over=(1, 0)):
    return lax.dot_general(
        a, b, (((over[0],), (over[1],)), ((), ())), preferred_element_type=F32
    )


def near_id(near_ref, column, read, reads):
    distance = lax.rem(near_ref[NX * reads] - column + NX, NX)
    return near_ref[distance * reads + read]


def pick_kernel(near_ref, mine_ref, theirs_ref, out_ref):
    core, reads = near_ref[near_ref.shape[0] - 1], out_ref.shape[1]
    for column in range(NX):
        for read in range(reads):
            block = near_id(near_ref, column, read, reads)
            row, same = lax.rem(block // NC, NY), lax.rem(block, NC) == core

            @pl.when(same)
            def _():
                out_ref[column, read] = mine_ref[row]

            @pl.when(jnp.logical_not(same))
            def _():
                out_ref[column, read] = theirs_ref[row]


def spread_kernel(near_ref, from_ref, out_ref):
    reads = from_ref.shape[1]
    spans = reads // NEIGH
    for read in range(reads):
        block = from_ref[near_ref[read] // (NY * NC), read]
        for at in range(read // NEIGH, NZ, spans):
            out_ref[at, read % NEIGH] = block


def owner_kernel(near_ref, from_ref, mine_ref, theirs_ref, total):
    total[...] = jnp.zeros_like(total)
    reads = from_ref.shape[1]
    here, core = near_ref[NX * reads], near_ref[near_ref.shape[0] - 1]
    for column in range(NX):
        for read in range(reads):
            block = near_id(near_ref, column, read, reads)

            @pl.when(block // (NY * NC) == here)
            def _():
                side = jnp.where(lax.rem(block, NC) == core, 0, NY)
                at = side + lax.rem(block // NC, NY)
                total[at] = total[at] + from_ref[column, read].astype(F32)

    mine_ref[...] = total[:NY]
    theirs_ref[...] = total[NY:].astype(BF16)


def attention_kernel(
    tok, w_own, w_pair, q_own, q_pair, g_own, g_pair, kc, ks, qc, qs,
    part, dq_own, dq_pair, dk_all, dv_all, total,
):
    scale = 1.0 / math.sqrt(HEAD)
    rows = jnp.concatenate([tok[:, n].reshape(NLEN, DE) for n in range(NEIGH)], axis=0)
    key_cos, key_sin, query_cos, query_sin = kc[...], ks[...], qc[...], qs[...]
    half = HEAD // 2
    for turn, (w, q, g, dq) in enumerate(
        ((w_own, q_own, g_own, dq_own), (w_pair, q_pair, g_pair, dq_pair))
    ):
        key_raw = dot(rows, w[0])
        values = dot(rows, w[1]).astype(BF16)
        for head in range(w.shape[2] // HEAD):
            cols = slice(head * HEAD, (head + 1) * HEAD)
            raw = key_raw[:, cols]
            key = (raw * key_cos + pltpu.roll(raw, half, 1) * key_sin).astype(BF16)
            value = values[:, cols]
            wide = q[:, cols].astype(F32)
            query = (wide * query_cos + pltpu.roll(wide, half, 1) * query_sin).astype(BF16)
            grad = g[:, cols]
            exponentials = jnp.exp(dot(query, key, (1, 1)) * scale)
            weights = exponentials / jnp.sum(exponentials, axis=-1, keepdims=True)
            weights_low = weights.astype(BF16)
            grad_weights = dot(grad, value, (1, 1))
            delta = jnp.sum(weights_low.astype(F32) * grad_weights, axis=-1, keepdims=True)
            grad_scores = (weights * (grad_weights - delta) * scale).astype(BF16)
            dv_all[:, cols] = dot(weights_low, grad, (0, 0)).astype(BF16)
            grad_query = dot(grad_scores, key)
            dq[:, cols] = (
                grad_query * query_cos - pltpu.roll(grad_query, half, 1) * query_sin
            ).astype(BF16)
            grad_key = dot(grad_scores, query, (0, 0))
            dk_all[:, cols] = (
                grad_key * key_cos - pltpu.roll(grad_key, half, 1) * key_sin
            ).astype(BF16)
        product = dot(dk_all[...], w[0], (1, 1)) + dot(dv_all[...], w[1], (1, 1))
        if turn == 0:
            total[...] = product
        else:
            product = total[...] + product
            for n in range(NEIGH):
                piece = product[n * NLEN:(n + 1) * NLEN].astype(BF16)
                part[:, n] = piece.reshape(NZ, ROWS, DE)


def on_core(kernel, name, shapes, near, *operands, scratch=()):
    return pl.pallas_call(
        kernel,
        out_shape=shapes,
        in_specs=[SMEM] + [VMEM] * len(operands),
        out_specs=jax.tree.map(lambda _: VMEM, shapes),
        scratch_shapes=scratch,
        compiler_params=pltpu.CompilerParams(vmem_limit_bytes=16 << 20),
        name=name,
    )(near, *operands)


def attention(*operands):
    width = operands[1].shape[2]
    return pl.pallas_call(
        attention_kernel,
        out_shape=(
            jax.ShapeDtypeStruct((NZ, NEIGH, ROWS, DE), BF16),
            jax.ShapeDtypeStruct((SPAN, width), BF16),
            jax.ShapeDtypeStruct((SPAN, width), BF16),
        ),
        in_specs=[VMEM] * len(operands),
        out_specs=(VMEM, VMEM, VMEM),
        scratch_shapes=[
            pltpu.VMEM((NEIGH * NLEN, width), BF16),
            pltpu.VMEM((NEIGH * NLEN, width), BF16),
            pltpu.VMEM((NEIGH * NLEN, DE), F32),
        ],
        compiler_params=pltpu.CompilerParams(vmem_limit_bytes=40 << 20),
        cost_estimate=pl.CostEstimate(
            flops=2_100_000_000, bytes_accessed=6_000_000, transcendentals=131072
        ),
        name="attention",
    )(*operands)


def local(queries, out_grad, encodings, kv_weight, neighbour_ids, rot_offset):
    x_at, c_at, z_at = lax.axis_index("x"), lax.axis_index("c"), lax.axis_index("z")
    spans = neighbour_ids.shape[0]
    reads = spans * NEIGH
    span_at = z_at % 2
    ids = neighbour_ids.reshape(reads)

    weight_pair = swapped(kv_weight, "z", NZ)
    rows_q = queries.reshape(spans, SPAN, -1)
    rows_g = out_grad.reshape(spans, SPAN, -1)
    other = jnp.concatenate(
        [
            lax.dynamic_index_in_dim(rows_q, 1 - span_at, 0, keepdims=False),
            lax.dynamic_index_in_dim(rows_g, 1 - span_at, 0, keepdims=False),
        ],
        axis=0,
    )
    q_own = lax.dynamic_index_in_dim(rows_q, span_at, 0, keepdims=False)
    g_own = lax.dynamic_index_in_dim(rows_g, span_at, 0, keepdims=False)
    offsets = lax.dynamic_index_in_dim(rot_offset, span_at, 0, keepdims=False)
    positions = offsets[:, None] + jnp.arange(NLEN, dtype=jnp.int32)[None, :]
    key_cos, key_sin = rotary_tables(positions.reshape(NEIGH * NLEN))
    query_cos, query_sin = rotary_tables(jnp.arange(SPAN, dtype=jnp.int32))

    near = [ids] + [shifted(ids, "x", NX, s) for s in range(1, NX)]
    near = jnp.concatenate(near + [x_at.reshape(1), c_at.reshape(1)])
    copies = jnp.broadcast_to(encodings, (NY, ROWS, DE))
    over_y = lax.all_to_all(copies, "y", split_axis=0, concat_axis=0, tiled=True)
    other, over_y = lax.optimization_barrier((other, over_y))
    beside = swapped(over_y, "c", NC)
    block = (reads, ROWS, DE)
    asked = on_core(
        pick_kernel, "pick", jax.ShapeDtypeStruct((NX, *block), BF16), near, over_y, beside
    )
    from_pair = swapped(other, "z", NZ)
    q_pair, g_pair = from_pair[:SPAN], from_pair[SPAN:]
    found = lax.all_to_all(asked, "x", split_axis=0, concat_axis=0, tiled=True)

    to_z = on_core(
        spread_kernel, "spread", jax.ShapeDtypeStruct((NZ, NEIGH, ROWS, DE), BF16), near, found
    )
    tok = lax.all_to_all(to_z, "z", split_axis=0, concat_axis=0, tiled=True)
    part, dq_own, dq_pair = attention(
        tok, kv_weight, weight_pair, q_own, q_pair, g_own, g_pair,
        key_cos, key_sin, query_cos, query_sin,
    )

    from_heads = lax.all_to_all(part, "z", split_axis=0, concat_axis=0, tiled=True)
    from_heads = from_heads.reshape(NZ // spans, spans, NEIGH, ROWS, DE)
    read_sum = jnp.sum(from_heads.astype(F32), axis=0).astype(BF16).reshape(reads, ROWS, DE)

    read_copies = jnp.broadcast_to(read_sum, (NX, *block))
    read_x = lax.all_to_all(read_copies, "x", split_axis=0, concat_axis=0, tiled=True)
    owners = (NY, ROWS, DE)
    mine, theirs = on_core(
        owner_kernel, "owner_sums",
        (jax.ShapeDtypeStruct(owners, F32), jax.ShapeDtypeStruct(owners, BF16)),
        near, read_x, scratch=[pltpu.VMEM((NC * NY, ROWS, DE), F32)],
    )
    owner_part = (mine + swapped(theirs, "c", NC).astype(F32)).astype(BF16)
    owner_part, dq_pair = lax.optimization_barrier((owner_part, dq_pair))
    from_y = lax.all_to_all(owner_part, "y", split_axis=0, concat_axis=0, tiled=True)
    owned = jnp.sum(from_y.astype(F32), axis=0)

    dq_back = swapped(dq_pair, "z", NZ)
    first = jnp.where(span_at == 0, dq_own, dq_back)
    second = jnp.where(span_at == 0, dq_back, dq_own)
    grad_query = jnp.concatenate([first, second], axis=0)
    return (grad_query, owned.reshape(1, ROWS, DE))


def solution(mesh):
    fine = Mesh(mesh.devices.reshape(NX, NY, NC, NZ), ("x", "y", "c", "z"))
    enc = ("x", "y", "c")
    in_specs = (
        P(enc, "z"),
        P(enc, "z"),
        P(enc, "z", None),
        P(None, None, "z"),
        P(enc, None),
        P(enc, None),
    )
    out_specs = (P(enc, "z"), P(enc, "z", None))
    return jax.shard_map(local, mesh=fine, in_specs=in_specs, out_specs=out_specs, check_vma=False)
```

time: 448 us -> 135 us (0.30)
  waiting for transfers between devices: 375 us -> 31.4 us
  starting transfers between devices: 0.3 us -> 56.8 us
  matrix products: 13.5 us -> 0 us
  local copies, waits for them, and re-layouts: 16.7 us -> 3.35 us
  between operations: 14.2 us -> 0.89 us
  Pallas kernels: 0 us -> 11.1 us
  blocking collectives: 23.1 us -> 27.7 us
    unnamed x4 -> x0, waiting for transfers between devices: 203 us -> none
    all_gather x1 -> x0, waiting for transfers between devices: 87.5 us -> none  [local(): gathered = lax.all_gather(encodings, 'enc', axis=0, tiled=True)]
    psum x1 -> x0, waiting for transfers between devices: 84 us -> none  [local(): summed_heads = lax.psum(partial_value, 'tp')]
    ppermute x0 -> x8, starting transfers between devices: none -> 31.7 us  [the longest x5 23 us: swapped(): return lax.ppermute(value, axis, [(i, i ^ 1) for i in range(size)])]
    all_to_all x0 -> x2, blocking collectives: none -> 27.7 us  [the longest x1 18.7 us: local(): lax.all_to_all(part, 'z', split_axis=0, concat_axis=0, tiled=True)]
    all_to_all x0 -> x4, starting transfers between devices: none -> 25 us  [the longest x1 10 us: local(): tok = lax.all_to_all(to_z, 'z', split_axis=0, concat_axis=0, tiled=True)]
    all_gather x1 -> x0, blocking collectives: 23.1 us -> none  [local(): neighbours = lax.all_gather(picked, 'tp', axis=1, tiled=True)]
    all_to_all x0 -> x4, waiting for transfers between devices: none -> 19.6 us  [the longest x1 9.08 us: local(): lax.all_to_all(owner_part, 'y', split_axis=0, concat_axis=0, tiled=True)]
  transfers between devices with their start and end apart: 3 -> 12, of which waited for: 3 -> 7; matrix products, arithmetic and copies ran while one was open for 2% -> 3% of each run, Pallas kernels for 0% -> 2%
where the time goes in v1:
time: 135 us; the launch traced here: 134 us
  starting transfers between devices  56.8 us (42%)
  waiting for transfers between devices  31.4 us (23%)
  blocking collectives  27.7 us (21%)
  Pallas kernels  11.1 us (8%)
  local copies, waits for them, and re-layouts  3.35 us (2%)
  other arithmetic  3.17 us (2%)
    ppermute x5, starting transfers between devices, swapped(): return lax.ppermute(value, axis, [(i, i ^ 1) for i in range(size)])  23 us
    all_to_all x1, blocking collectives, local(): lax.all_to_all(part, 'z', split_axis=0, concat_axis=0, tiled=True)  18.7 us
    all_to_all x1, starting transfers between devices, local(): tok = lax.all_to_all(to_z, 'z', split_axis=0, concat_axis=0, tiled=True)  10 us
    all_to_all x1, waiting for transfers between devices, local(): lax.all_to_all(owner_part, 'y', split_axis=0, concat_axis=0, tiled=True)  9.08 us
    all_to_all x1, blocking collectives, local(): lax.all_to_all(read_copies, 'x', split_axis=0, concat_axis=0, tiled=True)  8.96 us
    ppermute x5, waiting for transfers between devices, swapped(): return lax.ppermute(value, axis, [(i, i ^ 1) for i in range(size)])  8.9 us
    ppermute x3, starting transfers between devices, shifted(): lax.ppermute(value, axis, [(i, (i + shift) % size) for i in range(size)])  8.77 us
    all_to_all x1, starting transfers between devices, local(): lax.all_to_all(copies, 'y', split_axis=0, concat_axis=0, tiled=True)  7.65 us
  transfers between devices with their start and end apart: 12, of which 7 were waited for; matrix products, arithmetic and copies ran while one was open for 3% of the time, Pallas kernels for 2%

profile of v1, /device:TPU:1, one launch (start us, length us, event | category | flops | bytes accessed | tf_op | source)
XLA Modules:
  0.0 134.4 jit_solution(9606840065705980577)
XLA Ops:
  0.6 1.5 %broadcast_in_dim.7 = bf16[8,16,896]{2,1,0:T(8,128)(2,1)} broadcast(bf16[16,896]{1,0:T(8,128)(2,1)} %bitcast.25), dimensions={1,2} | broadcast | bytes 258048 | tf_op jit(solution)/shard_map/broadcast_in_dim | solution.py:201
  2.1 7.7 %all-to-all-start = ((bf16[8,16,896]{2,1,0:T(8,128)(2,1)}), bf16[8,16,896]{2,1,0:T(8,128)(2,1)S(1)}, u32[]{:S(2)}, u32[]{:S(2)}) async-start(bf16[8,16,896]{2,1,0:T(8,128)(2,1)} %broadcast_in_dim.7), calls=%async_computation | async-start | bytes 458752 | tf_op jit(solution)/shard_map/all_to_all | solution.py:202
  9.8 4.0 %collective-permute-start.4 = (bf16[2,896,512]{2,1,0:T(8,128)(2,1)}, bf16[2,896,512]{2,1,0:T(8,128)(2,1)}, u32[]{:S(2)}, u32[]{:S(2)}) collective-permute-start(bf16[2,896,512]{2,1,0:T(8,128)(2,1)} %w_own.1), channel_id=1, source_target_pairs={{0,1},{1,0},{2,3},{3,2},{4,5},{5,4},{6,7},{7,6},{8,9},{9,8},{10,11... | collective-permute-start | bytes 5505032 | tf_op jit(solution)/shard_map/ppermute | solution.py:36
  14.8 4.0 %all-to-all-done.mine_ref = bf16[8,16,896]{2,1,0:T(8,128)(2,1)S(1)} async-done(((bf16[8,16,896]{2,1,0:T(8,128)(2,1)}), bf16[8,16,896]{2,1,0:T(8,128)(2,1)S(1)}, u32[]{:S(2)}, u32[]{:S(2)}) %all-to-all-start) | async-done | bytes 229408 | tf_op jit(solution)/shard_map/all_to_all | solution.py:202
  18.8 5.6 %collective-permute-start.3 = (bf16[8,16,896]{2,1,0:T(8,128)(2,1)S(1)}, bf16[8,16,896]{2,1,0:T(8,128)(2,1)S(1)}, u32[]{:S(2)}, u32[]{:S(2)}) collective-permute-start(bf16[8,16,896]{2,1,0:T(8,128)(2,1)S(1)} %all-to-all-done.mine_ref), channel_id=1, source_target_pairs={{0,8},{8,0},{1,9},{9,1},{2,10},{10,2},{3,11},{11,3},{4,12},{12,4},... | collective-permute-start | bytes 688136 | tf_op jit(solution)/shard_map/ppermute | solution.py:36
  25.1 3.8 %collective-permute-start.2 = (s32[4]{0:T(128)S(1)}, s32[4]{0:T(128)S(1)}, u32[]{:S(2)}, u32[]{:S(2)}) collective-permute-start(s32[4]{0:T(128)S(1)} %reshape.54), channel_id=1, source_target_pairs={{0,384},{128,0},{256,128},{384,256},{1,385},{129,1},{257,129},{385... | collective-permute-start | bytes 56 | tf_op jit(solution)/shard_map/ppermute | solution.py:32
  29.0 2.4 %collective-permute-start.1 = (s32[4]{0:T(128)S(1)}, s32[4]{0:T(128)S(1)}, u32[]{:S(2)}, u32[]{:S(2)}) collective-permute-start(s32[4]{0:T(128)S(1)} %reshape.54), channel_id=1, source_target_pairs={{0,256},{128,384},{256,0},{384,128},{1,257},{129,385},{257,1},{385... | collective-permute-start | bytes 56 | tf_op jit(solution)/shard_map/ppermute | solution.py:32
  31.4 2.5 %collective-permute-start = (s32[4]{0:T(128)S(1)}, s32[4]{0:T(128)S(1)}, u32[]{:S(2)}, u32[]{:S(2)}) collective-permute-start(s32[4]{0:T(128)S(1)} %reshape.54), channel_id=1, source_target_pairs={{0,128},{128,256},{256,384},{384,0},{1,129},{129,257},{257,385},{3... | collective-permute-start | bytes 56 | tf_op jit(solution)/shard_map/ppermute | solution.py:32
  34.7 2.1 %collective-permute-done = s32[4]{0:T(128)S(1)} collective-permute-done((s32[4]{0:T(128)S(1)}, s32[4]{0:T(128)S(1)}, u32[]{:S(2)}, u32[]{:S(2)}) %collective-permute-start) | collective-permute-done | bytes 48 | tf_op jit(solution)/shard_map/ppermute | solution.py:32
  37.0 1.7 %pick.1 = bf16[4,4,16,896]{3,2,1,0:T(8,128)(2,1)} custom-call(s32[18]{0:T(128)S(1)} %concatenate.21.near_ref, bf16[8,16,896]{2,1,0:T(8,128)(2,1)S(1)} %all-to-all-done.mine_ref, bf16[8,16,896]{2,1,0:T(8,128)(2,1)S(1)} %collective-permute-done.3.theirs_ref), custom_call_target="tpu_custom_call" | custom-call | tf_op jit(solution)/shard_map/pick/pallas_call | solution.py:140
  38.7 3.5 %all-to-all-start.1 = ((bf16[4,4,16,896]{3,2,1,0:T(8,128)(2,1)}), bf16[4,4,16,896]{3,2,1,0:T(8,128)(2,1)S(1)}, u32[]{:S(2)}, u32[]{:S(2)}) async-start(bf16[4,4,16,896]{3,2,1,0:T(8,128)(2,1)} %pick.1), calls=%async_computation.1 | async-start | bytes 917504 | tf_op jit(solution)/shard_map/all_to_all | solution.py:211
  42.4 6.5 %all-to-all-done.1.from_ref = bf16[4,4,16,896]{3,2,1,0:T(8,128)(2,1)S(1)} async-done(((bf16[4,4,16,896]{3,2,1,0:T(8,128)(2,1)}), bf16[4,4,16,896]{3,2,1,0:T(8,128)(2,1)S(1)}, u32[]{:S(2)}, u32[]{:S(2)}) %all-to-all-start.1) | async-done | bytes 458784 | tf_op jit(solution)/shard_map/all_to_all | solution.py:211
  48.9 1.4 %spread.1 = bf16[8,2,16,896]{3,2,1,0:T(8,128)(2,1)} custom-call(s32[18]{0:T(128)S(1)} %concatenate.21.near_ref, bf16[4,4,16,896]{3,2,1,0:T(8,128)(2,1)S(1)} %all-to-all-done.1.from_ref), custom_call_target="tpu_custom_call" | custom-call | tf_op jit(solution)/shard_map/spread/pallas_call | solution.py:140
  50.3 10.0 %all-to-all-start.2 = ((bf16[8,2,16,896]{3,2,1,0:T(8,128)(2,1)}), bf16[8,2,16,896]{3,2,1,0:T(8,128)(2,1)S(1)}, u32[]{:S(2)}, u32[]{:S(2)}) async-start(bf16[8,2,16,896]{3,2,1,0:T(8,128)(2,1)} %spread.1), calls=%async_computation.2 | async-start | bytes 917504 | tf_op jit(solution)/shard_map/all_to_all | solution.py:216
  60.9 3.4 %collective-permute-start.5 = (bf16[128,512]{1,0:T(8,128)(2,1)S(1)}, bf16[128,512]{1,0:T(8,128)(2,1)S(1)}, u32[]{:S(2)}, u32[]{:S(2)}) collective-permute-start(bf16[128,512]{1,0:T(8,128)(2,1)S(1)} %pad_maximum_fusion), channel_id=1, source_target_pairs={{0,1},{1,0},{2,3},{3,2},{4,5},{5,4},{6,7},{7,6},{8,9},{9,8},{10,11... | collective-permute-start | bytes 393224 | tf_op jit(solution)/shard_map/ppermute | solution.py:36
  64.5 7.8 %collective-permute-done.5 = bf16[128,512]{1,0:T(8,128)(2,1)S(1)} collective-permute-done((bf16[128,512]{1,0:T(8,128)(2,1)S(1)}, bf16[128,512]{1,0:T(8,128)(2,1)S(1)}, u32[]{:S(2)}, u32[]{:S(2)}) %collective-permute-start.5) | collective-permute-done | bytes 131104 | tf_op jit(solution)/shard_map/ppermute | solution.py:36
  72.4 7.0 %attention.1 = (bf16[8,2,16,896]{3,2,1,0:T(8,128)(2,1)S(1)}, bf16[64,512]{1,0:T(8,128)(2,1)S(1)}, bf16[64,512]{1,0:T(8,128)(2,1)S(1)}) custom-call(bf16[8,2,16,896]{3,2,1,0:T(8,128)(2,1)S(1)} %all-to-all-done.2.tok, bf16[2,896,512]{2,1,0:T(8,128)(2,1)S(1)} %copy-done.1, bf16[2,896,512]{2,1,0:T(8,128)(2,1)} %collective-permute-done.4.w_pair, ...), custom_call_target="tpu_custom_call" | custom-call | flops 2100000000 | bytes 6000000 | tf_op jit(solution)/shard_map/attention/pallas_call | solution.py:153
  79.3 18.7 %all_to_all.30 = bf16[8,2,16,896]{3,2,1,0:T(8,128)(2,1)S(1)} all-to-all(bf16[8,2,16,896]{3,2,1,0:T(8,128)(2,1)S(1)} %get-tuple-element.14), channel_id=1, replica_groups=mesh['x'=4,'y'=8,'c'=2,'z'=8] {'z'}, dimensions={0} | all-to-all | bytes 917504 | tf_op jit(solution)/shard_map/all_to_all | solution.py:222
  98.2 9.0 %all_to_all.31.from_ref = bf16[4,4,16,896]{3,2,1,0:T(8,128)(2,1)S(1)} all-to-all(bf16[4,4,16,896]{3,2,1,0:T(8,128)(2,1)S(1)} %broadcast_in_dim.8), channel_id=1, replica_groups=mesh['x'=4,'y'=8,'c'=2,'z'=8] {'x'}, dimensions={0} | all-to-all | bytes 917504 | tf_op jit(solution)/shard_map/all_to_all | solution.py:227
  108.2 7.9 %collective-permute-start.6 = (bf16[8,16,896]{2,1,0:T(8,128)(2,1)S(1)}, bf16[8,16,896]{2,1,0:T(8,128)(2,1)S(1)}, u32[]{:S(2)}, u32[]{:S(2)}) collective-permute-start(bf16[8,16,896]{2,1,0:T(8,128)(2,1)S(1)} %get-tuple-element.16), channel_id=1, source_target_pairs={{0,8},{8,0},{1,9},{9,1},{2,10},{10,2},{3,11},{11,3},{4,12},{12,4},... | collective-permute-start | bytes 688136 | tf_op jit(solution)/shard_map/ppermute | solution.py:36
  116.1 1.1 collective-permute-done.6
  117.9 2.2 %collective-permute-start.7 = (bf16[64,512]{1,0:T(8,128)(2,1)S(1)}, bf16[64,512]{1,0:T(8,128)(2,1)S(1)}, u32[]{:S(2)}, u32[]{:S(2)}) collective-permute-start(bf16[64,512]{1,0:T(8,128)(2,1)S(1)} %get-tuple-element.18), channel_id=1, source_target_pairs={{0,1},{1,0},{2,3},{3,2},{4,5},{5,4},{6,7},{7,6},{8,9},{9,8},{10,11... | collective-permute-start | bytes 196616 | tf_op jit(solution)/shard_map/ppermute | solution.py:36
  120.1 3.9 %all-to-all-start.5 = ((bf16[8,16,896]{2,1,0:T(8,128)(2,1)}), bf16[8,16,896]{2,1,0:T(8,128)(2,1)S(1)}, u32[]{:S(2)}, u32[]{:S(2)}) async-start(bf16[8,16,896]{2,1,0:T(8,128)(2,1)} %add_convert_fusion), calls=%async_computation.5 | async-start | bytes 458752 | tf_op jit(solution)/shard_map/all_to_all | solution.py:236
  124.6 9.1 %all-to-all-done.5 = bf16[8,16,896]{2,1,0:T(8,128)(2,1)S(1)} async-done(((bf16[8,16,896]{2,1,0:T(8,128)(2,1)}), bf16[8,16,896]{2,1,0:T(8,128)(2,1)S(1)}, u32[]{:S(2)}, u32[]{:S(2)}) %all-to-all-start.5) | async-done | bytes 229408 | tf_op jit(solution)/shard_map/all_to_all | solution.py:236
  (30 shorter events, 6.9 us)
Async XLA Ops:
  0.6 41.6 %copy-start = (s32[2,2]{1,0:T(2,128)S(1)}, s32[2,2]{1,0:T(2,128)}, u32[]{:S(2)}) copy-start(s32[2,2]{1,0:T(2,128)} %param.11) | copy-start | bytes 52
  2.1 16.7 %all-to-all-start = ((bf16[8,16,896]{2,1,0:T(8,128)(2,1)}), bf16[8,16,896]{2,1,0:T(8,128)(2,1)S(1)}, u32[]{:S(2)}, u32[]{:S(2)}) async-start(bf16[8,16,896]{2,1,0:T(8,128)(2,1)} %broadcast_in_dim.7), calls=%async_computation | async-start | bytes 458752 | tf_op jit(solution)/shard_map/all_to_all | solution.py:202
  9.8 62.6 %collective-permute-start.4 = (bf16[2,896,512]{2,1,0:T(8,128)(2,1)}, bf16[2,896,512]{2,1,0:T(8,128)(2,1)}, u32[]{:S(2)}, u32[]{:S(2)}) collective-permute-start(bf16[2,896,512]{2,1,0:T(8,128)(2,1)} %w_own.1), channel_id=1, source_target_pairs={{0,1},{1,0},{2,3},{3,2},{4,5},{5,4},{6,7},{7,6},{8,9},{9,8},{10,11... | collective-permute-start | bytes 5505032 | tf_op jit(solution)/shard_map/ppermute | solution.py:36
  18.8 18.2 %collective-permute-start.3 = (bf16[8,16,896]{2,1,0:T(8,128)(2,1)S(1)}, bf16[8,16,896]{2,1,0:T(8,128)(2,1)S(1)}, u32[]{:S(2)}, u32[]{:S(2)}) collective-permute-start(bf16[8,16,896]{2,1,0:T(8,128)(2,1)S(1)} %all-to-all-done.mine_ref), channel_id=1, source_target_pairs={{0,8},{8,0},{1,9},{9,1},{2,10},{10,2},{3,11},{11,3},{4,12},{12,4},... | collective-permute-start | bytes 688136 | tf_op jit(solution)/shard_map/ppermute | solution.py:36
  25.1 8.8 %collective-permute-start.2 = (s32[4]{0:T(128)S(1)}, s32[4]{0:T(128)S(1)}, u32[]{:S(2)}, u32[]{:S(2)}) collective-permute-start(s32[4]{0:T(128)S(1)} %reshape.54), channel_id=1, source_target_pairs={{0,384},{128,0},{256,128},{384,256},{1,385},{129,1},{257,129},{385... | collective-permute-start | bytes 56 | tf_op jit(solution)/shard_map/ppermute | solution.py:32
  29.0 5.8 %collective-permute-start.1 = (s32[4]{0:T(128)S(1)}, s32[4]{0:T(128)S(1)}, u32[]{:S(2)}, u32[]{:S(2)}) collective-permute-start(s32[4]{0:T(128)S(1)} %reshape.54), channel_id=1, source_target_pairs={{0,256},{128,384},{256,0},{384,128},{1,257},{129,385},{257,1},{385... | collective-permute-start | bytes 56 | tf_op jit(solution)/shard_map/ppermute | solution.py:32
  31.4 5.5 %collective-permute-start = (s32[4]{0:T(128)S(1)}, s32[4]{0:T(128)S(1)}, u32[]{:S(2)}, u32[]{:S(2)}) collective-permute-start(s32[4]{0:T(128)S(1)} %reshape.54), channel_id=1, source_target_pairs={{0,128},{128,256},{256,384},{384,0},{1,129},{129,257},{257,385},{3... | collective-permute-start | bytes 56 | tf_op jit(solution)/shard_map/ppermute | solution.py:32
  38.7 10.2 %all-to-all-start.1 = ((bf16[4,4,16,896]{3,2,1,0:T(8,128)(2,1)}), bf16[4,4,16,896]{3,2,1,0:T(8,128)(2,1)S(1)}, u32[]{:S(2)}, u32[]{:S(2)}) async-start(bf16[4,4,16,896]{3,2,1,0:T(8,128)(2,1)} %pick.1), calls=%async_computation.1 | async-start | bytes 917504 | tf_op jit(solution)/shard_map/all_to_all | solution.py:211
  42.2 30.2 %copy-start.1 = (bf16[2,896,512]{2,1,0:T(8,128)(2,1)S(1)}, bf16[2,896,512]{2,1,0:T(8,128)(2,1)}, u32[]{:S(2)}) copy-start(bf16[2,896,512]{2,1,0:T(8,128)(2,1)} %w_own.1) | copy-start | bytes 5505028
  50.3 22.1 %all-to-all-start.2 = ((bf16[8,2,16,896]{3,2,1,0:T(8,128)(2,1)}), bf16[8,2,16,896]{3,2,1,0:T(8,128)(2,1)S(1)}, u32[]{:S(2)}, u32[]{:S(2)}) async-start(bf16[8,2,16,896]{3,2,1,0:T(8,128)(2,1)} %spread.1), calls=%async_computation.2 | async-start | bytes 917504 | tf_op jit(solution)/shard_map/all_to_all | solution.py:216
  60.9 11.4 %collective-permute-start.5 = (bf16[128,512]{1,0:T(8,128)(2,1)S(1)}, bf16[128,512]{1,0:T(8,128)(2,1)S(1)}, u32[]{:S(2)}, u32[]{:S(2)}) collective-permute-start(bf16[128,512]{1,0:T(8,128)(2,1)S(1)} %pad_maximum_fusion), channel_id=1, source_target_pairs={{0,1},{1,0},{2,3},{3,2},{4,5},{5,4},{6,7},{7,6},{8,9},{9,8},{10,11... | collective-permute-start | bytes 393224 | tf_op jit(solution)/shard_map/ppermute | solution.py:36
  108.2 9.0 %collective-permute-start.6 = (bf16[8,16,896]{2,1,0:T(8,128)(2,1)S(1)}, bf16[8,16,896]{2,1,0:T(8,128)(2,1)S(1)}, u32[]{:S(2)}, u32[]{:S(2)}) collective-permute-start(bf16[8,16,896]{2,1,0:T(8,128)(2,1)S(1)} %get-tuple-element.16), channel_id=1, source_target_pairs={{0,8},{8,0},{1,9},{9,1},{2,10},{10,2},{3,11},{11,3},{4,12},{12,4},... | collective-permute-start | bytes 688136 | tf_op jit(solution)/shard_map/ppermute | solution.py:36
  117.9 6.1 %collective-permute-start.7 = (bf16[64,512]{1,0:T(8,128)(2,1)S(1)}, bf16[64,512]{1,0:T(8,128)(2,1)S(1)}, u32[]{:S(2)}, u32[]{:S(2)}) collective-permute-start(bf16[64,512]{1,0:T(8,128)(2,1)S(1)} %get-tuple-element.18), channel_id=1, source_target_pairs={{0,1},{1,0},{2,3},{3,2},{4,5},{5,4},{6,7},{7,6},{8,9},{9,8},{10,11... | collective-permute-start | bytes 196616 | tf_op jit(solution)/shard_map/ppermute | solution.py:36
  120.1 13.6 %all-to-all-start.5 = ((bf16[8,16,896]{2,1,0:T(8,128)(2,1)}), bf16[8,16,896]{2,1,0:T(8,128)(2,1)S(1)}, u32[]{:S(2)}, u32[]{:S(2)}) async-start(bf16[8,16,896]{2,1,0:T(8,128)(2,1)} %add_convert_fusion), calls=%async_computation.5 | async-start | bytes 458752 | tf_op jit(solution)/shard_map/all_to_all | solution.py:236

commit v2 on v1

--- a/solution.py
+++ b/solution.py
@@ -17,6 +17,7 @@
 F32, BF16 = jnp.float32, jnp.bfloat16
 VMEM = pl.BlockSpec(memory_space=pltpu.VMEM)
 SMEM = pl.BlockSpec(memory_space=pltpu.SMEM)
+ANY = pl.BlockSpec(memory_space=pl.ANY)
 
 
 def rotary_tables(positions):
@@ -28,12 +29,8 @@
     return jnp.concatenate([cosine, cosine], axis=-1), jnp.concatenate([-sine, sine], axis=-1)
 
 
-def shifted(value, axis, size, shift):
-    return lax.ppermute(value, axis, [(i, (i + shift) % size) for i in range(size)])
-
-
-def swapped(value, axis, size):
-    return lax.ppermute(value, axis, [(i, i ^ 1) for i in range(size)])
+def swapped(value, axis, size, bit=1):
+    return lax.ppermute(value, axis, [(i, i ^ bit) for i in range(size)])
 
 
 def dot(a, b, over=(1, 0)):
@@ -42,43 +39,55 @@
     )
 
 
-def near_id(near_ref, column, read, reads):
-    distance = lax.rem(near_ref[NX * reads] - column + NX, NX)
-    return near_ref[distance * reads + read]
-
-
-def pick_kernel(near_ref, mine_ref, theirs_ref, out_ref):
-    core, reads = near_ref[near_ref.shape[0] - 1], out_ref.shape[1]
+def near_id(near_ref, at_ref, column, read):
+    return near_ref[jnp.bitwise_xor(at_ref[0], column), read // NEIGH, read % NEIGH]
+
+
+def pick_kernel(near_ref, at_ref, mine_ref, theirs_ref, out_ref, sems):
+    core, reads = at_ref[1], out_ref.shape[1]
     for column in range(NX):
         for read in range(reads):
-            block = near_id(near_ref, column, read, reads)
+            block = near_id(near_ref, at_ref, column, read)
             row, same = lax.rem(block // NC, NY), lax.rem(block, NC) == core
+            sem = sems.at[column * reads + read]
 
             @pl.when(same)
             def _():
-                out_ref[column, read] = mine_ref[row]
+                pltpu.make_async_copy(mine_ref.at[row], out_ref.at[column, read], sem).start()
 
             @pl.when(jnp.logical_not(same))
             def _():
-                out_ref[column, read] = theirs_ref[row]
-
-
-def spread_kernel(near_ref, from_ref, out_ref):
+                pltpu.make_async_copy(theirs_ref.at[row], out_ref.at[column, read], sem).start()
+
+    for column in range(NX):
+        for read in range(reads):
+            sem = sems.at[column * reads + read]
+            pltpu.make_async_copy(mine_ref.at[0], out_ref.at[column, read], sem).wait()
+
+
+def spread_kernel(near_ref, at_ref, from_ref, out_ref, sems):
     reads = from_ref.shape[1]
     spans = reads // NEIGH
+    copies = []
     for read in range(reads):
-        block = from_ref[near_ref[read] // (NY * NC), read]
+        column = near_ref[0, read // NEIGH, read % NEIGH] // (NY * NC)
         for at in range(read // NEIGH, NZ, spans):
-            out_ref[at, read % NEIGH] = block
-
-
-def owner_kernel(near_ref, from_ref, mine_ref, theirs_ref, total):
+            copies.append(
+                pltpu.make_async_copy(
+                    from_ref.at[column, read], out_ref.at[at, read % NEIGH], sems.at[len(copies)]
+                )
+            )
+            copies[-1].start()
+    for copy in copies:
+        copy.wait()
+
+
+def owner_kernel(near_ref, at_ref, from_ref, mine_ref, theirs_ref, total):
     total[...] = jnp.zeros_like(total)
-    reads = from_ref.shape[1]
-    here, core = near_ref[NX * reads], near_ref[near_ref.shape[0] - 1]
+    here, core = at_ref[0], at_ref[1]
     for column in range(NX):
-        for read in range(reads):
-            block = near_id(near_ref, column, read, reads)
+        for read in range(from_ref.shape[1]):
+            block = near_id(near_ref, at_ref, column, read)
 
             @pl.when(block // (NY * NC) == here)
             def _():
@@ -91,9 +100,18 @@
 
 
 def attention_kernel(
-    tok, w_own, w_pair, q_own, q_pair, g_own, g_pair, kc, ks, qc, qs,
-    part, dq_own, dq_pair, dk_all, dv_all, total,
+    at_ref, tok, w_own, q_own, g_own, kc, ks, qc, qs, near_pair, far_pair,
+    part, dq_own, dq_pair, dk_all, dv_all, total, w_pair, q_pair, g_pair, sems,
 ):
+    core, depth = at_ref[1], w_own.shape[1]
+    fetches = [
+        pltpu.make_async_copy(near_pair.at[:depth], w_pair.at[core], sems.at[0]),
+        pltpu.make_async_copy(far_pair.at[:depth], w_pair.at[1 - core], sems.at[1]),
+        pltpu.make_async_copy(near_pair.at[depth:depth + SPAN], q_pair, sems.at[2]),
+        pltpu.make_async_copy(near_pair.at[depth + SPAN:], g_pair, sems.at[3]),
+    ]
+    for fetch in fetches:
+        fetch.start()
     scale = 1.0 / math.sqrt(HEAD)
     rows = jnp.concatenate([tok[:, n].reshape(NLEN, DE) for n in range(NEIGH)], axis=0)
     key_cos, key_sin, query_cos, query_sin = kc[...], ks[...], qc[...], qs[...]
@@ -101,6 +119,9 @@
     for turn, (w, q, g, dq) in enumerate(
         ((w_own, q_own, g_own, dq_own), (w_pair, q_pair, g_pair, dq_pair))
     ):
+        if turn == 1:
+            for fetch in fetches:
+                fetch.wait()
         key_raw = dot(rows, w[0])
         values = dot(rows, w[1]).astype(BF16)
         for head in range(w.shape[2] // HEAD):
@@ -136,20 +157,20 @@
                 part[:, n] = piece.reshape(NZ, ROWS, DE)
 
 
-def on_core(kernel, name, shapes, near, *operands, scratch=()):
+def on_core(kernel, name, shapes, scalars, *operands, scratch=(), space=VMEM):
     return pl.pallas_call(
         kernel,
         out_shape=shapes,
-        in_specs=[SMEM] + [VMEM] * len(operands),
-        out_specs=jax.tree.map(lambda _: VMEM, shapes),
+        in_specs=[SMEM] * len(scalars) + [space] * len(operands),
+        out_specs=jax.tree.map(lambda _: space, shapes),
         scratch_shapes=scratch,
         compiler_params=pltpu.CompilerParams(vmem_limit_bytes=16 << 20),
         name=name,
-    )(near, *operands)
-
-
-def attention(*operands):
-    width = operands[1].shape[2]
+    )(*scalars, *operands)
+
+
+def attention(at, *operands):
+    _, depth, width = operands[1].shape
     return pl.pallas_call(
         attention_kernel,
         out_shape=(
@@ -157,19 +178,23 @@
             jax.ShapeDtypeStruct((SPAN, width), BF16),
             jax.ShapeDtypeStruct((SPAN, width), BF16),
         ),
-        in_specs=[VMEM] * len(operands),
+        in_specs=[SMEM] + [VMEM] * (len(operands) - 2) + [ANY] * 2,
         out_specs=(VMEM, VMEM, VMEM),
         scratch_shapes=[
             pltpu.VMEM((NEIGH * NLEN, width), BF16),
             pltpu.VMEM((NEIGH * NLEN, width), BF16),
             pltpu.VMEM((NEIGH * NLEN, DE), F32),
+            pltpu.VMEM((2, depth, width), BF16),
+            pltpu.VMEM((SPAN, width), BF16),
+            pltpu.VMEM((SPAN, width), BF16),
+            pltpu.SemaphoreType.DMA((4,)),
         ],
         compiler_params=pltpu.CompilerParams(vmem_limit_bytes=40 << 20),
         cost_estimate=pl.CostEstimate(
             flops=2_100_000_000, bytes_accessed=6_000_000, transcendentals=131072
         ),
         name="attention",
-    )(*operands)
+    )(at, *operands)
 
 
 def local(queries, out_grad, encodings, kv_weight, neighbour_ids, rot_offset):
@@ -177,18 +202,18 @@
     spans = neighbour_ids.shape[0]
     reads = spans * NEIGH
     span_at = z_at % 2
-    ids = neighbour_ids.reshape(reads)
-
-    weight_pair = swapped(kv_weight, "z", NZ)
+
     rows_q = queries.reshape(spans, SPAN, -1)
     rows_g = out_grad.reshape(spans, SPAN, -1)
-    other = jnp.concatenate(
+    to_pair = jnp.concatenate(
         [
+            lax.dynamic_index_in_dim(kv_weight, c_at, 0, keepdims=False),
             lax.dynamic_index_in_dim(rows_q, 1 - span_at, 0, keepdims=False),
             lax.dynamic_index_in_dim(rows_g, 1 - span_at, 0, keepdims=False),
         ],
         axis=0,
     )
+    near_pair = swapped(to_pair, "z", NZ)
     q_own = lax.dynamic_index_in_dim(rows_q, span_at, 0, keepdims=False)
     g_own = lax.dynamic_index_in_dim(rows_g, span_at, 0, keepdims=False)
     offsets = lax.dynamic_index_in_dim(rot_offset, span_at, 0, keepdims=False)
@@ -196,30 +221,35 @@
     key_cos, key_sin = rotary_tables(positions.reshape(NEIGH * NLEN))
     query_cos, query_sin = rotary_tables(jnp.arange(SPAN, dtype=jnp.int32))
 
-    near = [ids] + [shifted(ids, "x", NX, s) for s in range(1, NX)]
-    near = jnp.concatenate(near + [x_at.reshape(1), c_at.reshape(1)])
+    at = jnp.stack([x_at, c_at])
+    near = jnp.stack([neighbour_ids, swapped(neighbour_ids, "x", NX)])
+    near = jnp.concatenate([near, swapped(near, "x", NX, 2)])
     copies = jnp.broadcast_to(encodings, (NY, ROWS, DE))
     over_y = lax.all_to_all(copies, "y", split_axis=0, concat_axis=0, tiled=True)
-    other, over_y = lax.optimization_barrier((other, over_y))
+    over_y, near = lax.optimization_barrier((over_y, near))
     beside = swapped(over_y, "c", NC)
     block = (reads, ROWS, DE)
     asked = on_core(
-        pick_kernel, "pick", jax.ShapeDtypeStruct((NX, *block), BF16), near, over_y, beside
-    )
-    from_pair = swapped(other, "z", NZ)
-    q_pair, g_pair = from_pair[:SPAN], from_pair[SPAN:]
+        pick_kernel, "pick", jax.ShapeDtypeStruct((NX, *block), BF16), (near, at),
+        over_y, beside, scratch=[pltpu.SemaphoreType.DMA((NX * reads,))], space=ANY,
+    )
     found = lax.all_to_all(asked, "x", split_axis=0, concat_axis=0, tiled=True)
 
     to_z = on_core(
-        spread_kernel, "spread", jax.ShapeDtypeStruct((NZ, NEIGH, ROWS, DE), BF16), near, found
-    )
+        spread_kernel, "spread", jax.ShapeDtypeStruct((NZ, NEIGH, ROWS, DE), BF16), (near, at),
+        found, scratch=[pltpu.SemaphoreType.DMA((NZ * NEIGH,))], space=ANY,
+    )
+    to_z, near_pair = lax.optimization_barrier((to_z, near_pair))
     tok = lax.all_to_all(to_z, "z", split_axis=0, concat_axis=0, tiled=True)
+    far_pair = swapped(near_pair, "c", NC)
     part, dq_own, dq_pair = attention(
-        tok, kv_weight, weight_pair, q_own, q_pair, g_own, g_pair,
-        key_cos, key_sin, query_cos, query_sin,
+        at, tok, kv_weight, q_own, g_own, key_cos, key_sin, query_cos, query_sin,
+        near_pair, far_pair,
     )
 
     from_heads = lax.all_to_all(part, "z", split_axis=0, concat_axis=0, tiled=True)
+    dq_back = swapped(dq_pair, "z", NZ)
+    from_heads, dq_back = lax.optimization_barrier((from_heads, dq_back))
     from_heads = from_heads.reshape(NZ // spans, spans, NEIGH, ROWS, DE)
     read_sum = jnp.sum(from_heads.astype(F32), axis=0).astype(BF16).reshape(reads, ROWS, DE)
 
@@ -229,14 +259,12 @@
     mine, theirs = on_core(
         owner_kernel, "owner_sums",
         (jax.ShapeDtypeStruct(owners, F32), jax.ShapeDtypeStruct(owners, BF16)),
-        near, read_x, scratch=[pltpu.VMEM((NC * NY, ROWS, DE), F32)],
+        (near, at), read_x, scratch=[pltpu.VMEM((NC * NY, ROWS, DE), F32)],
     )
     owner_part = (mine + swapped(theirs, "c", NC).astype(F32)).astype(BF16)
-    owner_part, dq_pair = lax.optimization_barrier((owner_part, dq_pair))
     from_y = lax.all_to_all(owner_part, "y", split_axis=0, concat_axis=0, tiled=True)
     owned = jnp.sum(from_y.astype(F32), axis=0)
 
-    dq_back = swapped(dq_pair, "z", NZ)
     first = jnp.where(span_at == 0, dq_own, dq_back)
     second = jnp.where(span_at == 0, dq_back, dq_own)
     grad_query = jnp.concatenate([first, second], axis=0)

time: 135 us -> 141 us (1.044)
  waiting for transfers between devices: 31.4 us -> 51.7 us
  blocking collectives: 27.7 us -> 10.6 us
    all_to_all x1 -> x0, blocking collectives: 18.7 us -> none  [local(): lax.all_to_all(part, 'z', split_axis=0, concat_axis=0, tiled=True)]
    all_to_all x1, waiting for transfers between devices: 0.01 us -> 15.8 us  [local(): tok = lax.all_to_all(to_z, 'z', split_axis=0, concat_axis=0, tiled=True)]
    ppermute x8 -> x7, starting transfers between devices: 31.7 us -> 27.5 us  [swapped(): return lax.ppermute(value, axis, [(i, i ^ bit) for i in range(size)])]
    all_to_all x1, waiting for transfers between devices: 4.01 us -> 0.01 us  [local(): lax.all_to_all(copies, 'y', split_axis=0, concat_axis=0, tiled=True)]
    all_to_all x0 -> x1, waiting for transfers between devices: none -> 3.87 us  [local(): lax.all_to_all(part, 'z', split_axis=0, concat_axis=0, tiled=True)]
    all_to_all x0 -> x1, starting transfers between devices: none -> 3.48 us  [local(): lax.all_to_all(part, 'z', split_axis=0, concat_axis=0, tiled=True)]
    all_to_all x1, starting transfers between devices: 3.87 us -> 6.93 us  [local(): lax.all_to_all(owner_part, 'y', split_axis=0, concat_axis=0, tiled=True)]
    ppermute x8 -> x7, waiting for transfers between devices: 11.8 us -> 14.4 us  [swapped(): return lax.ppermute(value, axis, [(i, i ^ bit) for i in range(size)])]
  transfers between devices with their start and end apart: 12 -> 12, of which waited for: 7 -> 9; matrix products, arithmetic and copies ran while one was open for 3% -> 2% of each run, Pallas kernels for 2% -> 2%
where the time goes in v2:
time: 141 us; the launch traced here: 140 us
  starting transfers between devices  58 us (41%)
  waiting for transfers between devices  51.7 us (37%)
  Pallas kernels  12.3 us (9%)
  blocking collectives  10.6 us (8%)
  other arithmetic  4.29 us (3%)
  local copies, waits for them, and re-layouts  2.16 us (2%)
    ppermute x7, starting transfers between devices, swapped(): return lax.ppermute(value, axis, [(i, i ^ bit) for i in range(size)])  27.5 us
    all_to_all x1, waiting for transfers between devices, local(): tok = lax.all_to_all(to_z, 'z', split_axis=0, concat_axis=0, tiled=True)  15.8 us
    ppermute x7, waiting for transfers between devices, swapped(): return lax.ppermute(value, axis, [(i, i ^ bit) for i in range(size)])  14.4 us
    all_to_all x1, blocking collectives, local(): lax.all_to_all(read_copies, 'x', split_axis=0, concat_axis=0, tiled=True)  10.6 us
    all_to_all x1, waiting for transfers between devices, local(): lax.all_to_all(owner_part, 'y', split_axis=0, concat_axis=0, tiled=True)  9.48 us
    all_to_all x1, starting transfers between devices, local(): tok = lax.all_to_all(to_z, 'z', split_axis=0, concat_axis=0, tiled=True)  9.14 us
    all_to_all x1, waiting for transfers between devices, local(): found = lax.all_to_all(asked, 'x', split_axis=0, concat_axis=0, tiled=True)  8.2 us
    pallas_call x1, Pallas kernels, attention(): pl.pallas_call(attention_kernel, out_shape=(jax.ShapeDtypeStruct((NZ, NEI...  8.19 us
  transfers between devices with their start and end apart: 12, of which 9 were waited for; matrix products, arithmetic and copies ran while one was open for 2% of the time, Pallas kernels for 2%

profile of v2, /device:TPU:1, one launch (start us, length us, event | category | flops | bytes accessed | tf_op | source)
XLA Modules:
  0.0 140.0 jit_solution(3965089281216958550)
XLA Ops:
  0.7 1.3 dynamic-slice_bitcast_fusion
  3.1 4.8 %collective-permute-start.3 = (bf16[1024,512]{1,0:T(8,128)(2,1)}, bf16[1024,512]{1,0:T(8,128)(2,1)}, u32[]{:S(2)}, u32[]{:S(2)}) collective-permute-start(bf16[1024,512]{1,0:T(8,128)(2,1)} %pad_maximum_fusion), channel_id=1, source_target_pairs={{0,1},{1,0},{2,3},{3,2},{4,5},{5,4},{6,7},{7,6},{8,9},{9,8},{10,11... | collective-permute-start | bytes 3145736 | tf_op jit(solution)/shard_map/ppermute | solution.py:33
  8.7 6.8 %all-to-all-start = ((bf16[8,16,896]{2,1,0:T(8,128)(2,1)}), bf16[8,16,896]{2,1,0:T(8,128)(2,1)S(1)}, u32[]{:S(2)}, u32[]{:S(2)}) async-start(bf16[8,16,896]{2,1,0:T(8,128)(2,1)} %broadcast_in_dim.7), calls=%async_computation | async-start | bytes 458752 | tf_op jit(solution)/shard_map/all_to_all | solution.py:228
  15.5 3.1 %collective-permute-start = (s32[2,2]{1,0:T(2,128)S(1)}, s32[2,2]{1,0:T(2,128)S(1)}, u32[]{:S(2)}, u32[]{:S(2)}) collective-permute-start(s32[2,2]{1,0:T(2,128)S(1)} %copy-done.5), channel_id=1, source_target_pairs={{0,128},{128,0},{256,384},{384,256},{1,129},{129,1},{257,385},{385... | collective-permute-start | bytes 56 | tf_op jit(solution)/shard_map/ppermute | solution.py:33
  18.6 1.6 %collective-permute-done = s32[2,2]{1,0:T(2,128)S(1)} collective-permute-done((s32[2,2]{1,0:T(2,128)S(1)}, s32[2,2]{1,0:T(2,128)S(1)}, u32[]{:S(2)}, u32[]{:S(2)}) %collective-permute-start) | collective-permute-done | bytes 48 | tf_op jit(solution)/shard_map/ppermute | solution.py:33
  20.2 4.6 %collective-permute-start.1 = (s32[2,2,2]{2,1,0:T(2,128)S(1)}, s32[2,2,2]{2,1,0:T(2,128)S(1)}, u32[]{:S(2)}, u32[]{:S(2)}) collective-permute-start(s32[2,2,2]{2,1,0:T(2,128)S(1)} %pad_add_fusion.1), channel_id=1, source_target_pairs={{0,256},{128,384},{256,0},{384,128},{1,257},{129,385},{257,1},{385... | collective-permute-start | bytes 104 | tf_op jit(solution)/shard_map/ppermute | solution.py:33
  24.9 1.5 %collective-permute-done.1 = s32[2,2,2]{2,1,0:T(2,128)S(1)} collective-permute-done((s32[2,2,2]{2,1,0:T(2,128)S(1)}, s32[2,2,2]{2,1,0:T(2,128)S(1)}, u32[]{:S(2)}, u32[]{:S(2)}) %collective-permute-start.1) | collective-permute-done | bytes 64 | tf_op jit(solution)/shard_map/ppermute | solution.py:33
  26.4 4.7 %collective-permute-start.2 = (bf16[8,16,896]{2,1,0:T(8,128)(2,1)S(1)}, bf16[8,16,896]{2,1,0:T(8,128)(2,1)S(1)}, u32[]{:S(2)}, u32[]{:S(2)}) collective-permute-start(bf16[8,16,896]{2,1,0:T(8,128)(2,1)S(1)} %all-to-all-done.mine_ref), channel_id=1, source_target_pairs={{0,8},{8,0},{1,9},{9,1},{2,10},{10,2},{3,11},{11,3},{4,12},{12,4},... | collective-permute-start | bytes 688136 | tf_op jit(solution)/shard_map/ppermute | solution.py:33
  32.2 1.5 %pick.1 = bf16[4,4,16,896]{3,2,1,0:T(8,128)(2,1)} custom-call(s32[4,2,2]{2,1,0:T(2,128)S(1)} %pad_add_fusion.near_ref, s32[2]{0:T(128)S(1)} %pad_add_fusion.2.at_ref, bf16[8,16,896]{2,1,0:T(8,128)(2,1)S(1)} %all-to-all-done.mine_ref, bf16[8,16,896]{2,1,0:T(8,128)(2,1)S(1)} %collective-permute-done.2.theirs_ref), custom_call_target="tpu_custom_call" | custom-call | tf_op jit(solution)/shard_map/pick/pallas_call | solution.py:161
  33.8 4.2 %all-to-all-start.1 = ((bf16[4,4,16,896]{3,2,1,0:T(8,128)(2,1)}), bf16[4,4,16,896]{3,2,1,0:T(8,128)(2,1)S(1)}, u32[]{:S(2)}, u32[]{:S(2)}) async-start(bf16[4,4,16,896]{3,2,1,0:T(8,128)(2,1)} %pick.1), calls=%async_computation.1 | async-start | bytes 917504 | tf_op jit(solution)/shard_map/all_to_all | solution.py:236
  37.9 8.2 %all-to-all-done.1.from_ref = bf16[4,4,16,896]{3,2,1,0:T(8,128)(2,1)S(1)} async-done(((bf16[4,4,16,896]{3,2,1,0:T(8,128)(2,1)}), bf16[4,4,16,896]{3,2,1,0:T(8,128)(2,1)S(1)}, u32[]{:S(2)}, u32[]{:S(2)}) %all-to-all-start.1) | async-done | bytes 458784 | tf_op jit(solution)/shard_map/all_to_all | solution.py:236
  46.1 1.5 %spread.1 = bf16[8,2,16,896]{3,2,1,0:T(8,128)(2,1)} custom-call(s32[4,2,2]{2,1,0:T(2,128)S(1)} %pad_add_fusion.near_ref, s32[2]{0:T(128)S(1)} %pad_add_fusion.2.at_ref, bf16[4,4,16,896]{3,2,1,0:T(8,128)(2,1)S(1)} %all-to-all-done.1.from_ref), custom_call_target="tpu_custom_call" | custom-call | tf_op jit(solution)/shard_map/spread/pallas_call | solution.py:161
  47.7 3.4 %collective-permute-start.4 = (bf16[1024,512]{1,0:T(8,128)(2,1)}, bf16[1024,512]{1,0:T(8,128)(2,1)}, u32[]{:S(2)}, u32[]{:S(2)}) collective-permute-start(bf16[1024,512]{1,0:T(8,128)(2,1)} %collective-permute-done.3.near_pair), channel_id=1, source_target_pairs={{0,8},{8,0},{1,9},{9,1},{2,10},{10,2},{3,11},{11,3},{4,12},{12,4},... | collective-permute-start | bytes 3145736 | tf_op jit(solution)/shard_map/ppermute | solution.py:33
  51.3 9.1 %all-to-all-start.2 = ((bf16[8,2,16,896]{3,2,1,0:T(8,128)(2,1)}), bf16[8,2,16,896]{3,2,1,0:T(8,128)(2,1)S(1)}, u32[]{:S(2)}, u32[]{:S(2)}) async-start(bf16[8,2,16,896]{3,2,1,0:T(8,128)(2,1)} %spread.1), calls=%async_computation.2 | async-start | bytes 917504 | tf_op jit(solution)/shard_map/all_to_all | solution.py:243
  61.3 15.8 %all-to-all-done.2.tok = bf16[8,2,16,896]{3,2,1,0:T(8,128)(2,1)S(1)} async-done(((bf16[8,2,16,896]{3,2,1,0:T(8,128)(2,1)}), bf16[8,2,16,896]{3,2,1,0:T(8,128)(2,1)S(1)}, u32[]{:S(2)}, u32[]{:S(2)}) %all-to-all-start.2) | async-done | bytes 458784 | tf_op jit(solution)/shard_map/all_to_all | solution.py:243
  77.1 8.2 %attention.1 = (bf16[8,2,16,896]{3,2,1,0:T(8,128)(2,1)}, bf16[64,512]{1,0:T(8,128)(2,1)S(1)}, bf16[64,512]{1,0:T(8,128)(2,1)S(1)}) custom-call(s32[2]{0:T(128)S(1)} %pad_add_fusion.2.at_ref, bf16[8,2,16,896]{3,2,1,0:T(8,128)(2,1)S(1)} %all-to-all-done.2.tok, bf16[2,896,512]{2,1,0:T(8,128)(2,1)S(1)} %copy-done.1, ...), custom_call_target="tpu_custom_call" | custom-call | flops 2100000000 | bytes 6000000 | tf_op jit(solution)/shard_map/attention/pallas_call | solution.py:174
  85.3 3.5 %all-to-all-start.3 = ((bf16[8,2,16,896]{3,2,1,0:T(8,128)(2,1)}), bf16[8,2,16,896]{3,2,1,0:T(8,128)(2,1)S(1)}, u32[]{:S(2)}, u32[]{:S(2)}) async-start(bf16[8,2,16,896]{3,2,1,0:T(8,128)(2,1)} %get-tuple-element.18), calls=%async_computation.3 | async-start | bytes 917504 | tf_op jit(solution)/shard_map/all_to_all | solution.py:250
  88.8 3.3 %collective-permute-start.5 = (bf16[64,512]{1,0:T(8,128)(2,1)S(1)}, bf16[64,512]{1,0:T(8,128)(2,1)S(1)}, u32[]{:S(2)}, u32[]{:S(2)}) collective-permute-start(bf16[64,512]{1,0:T(8,128)(2,1)S(1)} %get-tuple-element.19), channel_id=1, source_target_pairs={{0,1},{1,0},{2,3},{3,2},{4,5},{5,4},{6,7},{7,6},{8,9},{9,8},{10,11... | collective-permute-start | bytes 196616 | tf_op jit(solution)/shard_map/ppermute | solution.py:33
  92.1 9.3 %collective-permute-done.5 = bf16[64,512]{1,0:T(8,128)(2,1)S(1)} collective-permute-done((bf16[64,512]{1,0:T(8,128)(2,1)S(1)}, bf16[64,512]{1,0:T(8,128)(2,1)S(1)}, u32[]{:S(2)}, u32[]{:S(2)}) %collective-permute-start.5) | collective-permute-done | bytes 65568 | tf_op jit(solution)/shard_map/ppermute | solution.py:33
  101.3 3.9 %all-to-all-done.3 = bf16[8,2,16,896]{3,2,1,0:T(8,128)(2,1)S(1)} async-done(((bf16[8,2,16,896]{3,2,1,0:T(8,128)(2,1)}), bf16[8,2,16,896]{3,2,1,0:T(8,128)(2,1)S(1)}, u32[]{:S(2)}, u32[]{:S(2)}) %all-to-all-start.3) | async-done | bytes 458784 | tf_op jit(solution)/shard_map/all_to_all | solution.py:250
  105.3 10.6 %all_to_all.30.from_ref = bf16[4,4,16,896]{3,2,1,0:T(8,128)(2,1)S(1)} all-to-all(bf16[4,4,16,896]{3,2,1,0:T(8,128)(2,1)S(1)} %broadcast_in_dim.8), channel_id=1, replica_groups=mesh['x'=4,'y'=8,'c'=2,'z'=8] {'x'}, dimensions={0} | all-to-all | bytes 917504 | tf_op jit(solution)/shard_map/all_to_all | solution.py:257
  116.9 3.4 %collective-permute-start.6 = (bf16[8,16,896]{2,1,0:T(8,128)(2,1)S(1)}, bf16[8,16,896]{2,1,0:T(8,128)(2,1)S(1)}, u32[]{:S(2)}, u32[]{:S(2)}) collective-permute-start(bf16[8,16,896]{2,1,0:T(8,128)(2,1)S(1)} %get-tuple-element.23), channel_id=1, source_target_pairs={{0,8},{8,0},{1,9},{9,1},{2,10},{10,2},{3,11},{11,3},{4,12},{12,4},... | collective-permute-start | bytes 688136 | tf_op jit(solution)/shard_map/ppermute | solution.py:33
  122.2 6.9 %all-to-all-start.5 = ((bf16[8,16,896]{2,1,0:T(8,128)(2,1)}), bf16[8,16,896]{2,1,0:T(8,128)(2,1)S(1)}, u32[]{:S(2)}, u32[]{:S(2)}) async-start(bf16[8,16,896]{2,1,0:T(8,128)(2,1)} %add_convert_fusion), calls=%async_computation.5 | async-start | bytes 458752 | tf_op jit(solution)/shard_map/all_to_all | solution.py:265
  129.8 9.5 %all-to-all-done.5 = bf16[8,16,896]{2,1,0:T(8,128)(2,1)S(1)} async-done(((bf16[8,16,896]{2,1,0:T(8,128)(2,1)}), bf16[8,16,896]{2,1,0:T(8,128)(2,1)S(1)}, u32[]{:S(2)}, u32[]{:S(2)}) %all-to-all-start.5) | async-done | bytes 229408 | tf_op jit(solution)/shard_map/all_to_all | solution.py:265
  (38 shorter events, 8.3 us)
Async XLA Ops:
  0.6 59.8 %copy-start = (s32[2,2]{1,0:T(2,128)S(1)}, s32[2,2]{1,0:T(2,128)}, u32[]{:S(2)}) copy-start(s32[2,2]{1,0:T(2,128)} %param.11) | copy-start | bytes 52
  0.6 1.4 %copy-start.2 = (bf16[128,512]{1,0:T(8,128)(2,1)S(1)}, bf16[128,512]{1,0:T(8,128)(2,1)}, u32[]{:S(2)}) copy-start(bf16[128,512]{1,0:T(8,128)(2,1)} %param.7) | copy-start | bytes 393220
  0.7 1.4 %copy-start.3 = (bf16[128,512]{1,0:T(8,128)(2,1)S(1)}, bf16[128,512]{1,0:T(8,128)(2,1)}, u32[]{:S(2)}) copy-start(bf16[128,512]{1,0:T(8,128)(2,1)} %param.6) | copy-start | bytes 393220
  0.7 7.3 %copy-start.4 = (bf16[1,16,896]{2,1,0:T(8,128)(2,1)S(1)}, bf16[1,16,896]{2,1,0:T(8,128)(2,1)}, u32[]{:S(2)}) copy-start(bf16[1,16,896]{2,1,0:T(8,128)(2,1)} %param.8) | copy-start | bytes 86020
  2.0 13.5 %copy-start.5 = (s32[2,2]{1,0:T(2,128)S(1)}, s32[2,2]{1,0:T(2,128)}, u32[]{:S(2)}) copy-start(s32[2,2]{1,0:T(2,128)} %param.10) | copy-start | bytes 52
  3.1 44.5 %collective-permute-start.3 = (bf16[1024,512]{1,0:T(8,128)(2,1)}, bf16[1024,512]{1,0:T(8,128)(2,1)}, u32[]{:S(2)}, u32[]{:S(2)}) collective-permute-start(bf16[1024,512]{1,0:T(8,128)(2,1)} %pad_maximum_fusion), channel_id=1, source_target_pairs={{0,1},{1,0},{2,3},{3,2},{4,5},{5,4},{6,7},{7,6},{8,9},{9,8},{10,11... | collective-permute-start | bytes 3145736 | tf_op jit(solution)/shard_map/ppermute | solution.py:33
  8.7 17.7 %all-to-all-start = ((bf16[8,16,896]{2,1,0:T(8,128)(2,1)}), bf16[8,16,896]{2,1,0:T(8,128)(2,1)S(1)}, u32[]{:S(2)}, u32[]{:S(2)}) async-start(bf16[8,16,896]{2,1,0:T(8,128)(2,1)} %broadcast_in_dim.7), calls=%async_computation | async-start | bytes 458752 | tf_op jit(solution)/shard_map/all_to_all | solution.py:228
  15.5 4.7 %collective-permute-start = (s32[2,2]{1,0:T(2,128)S(1)}, s32[2,2]{1,0:T(2,128)S(1)}, u32[]{:S(2)}, u32[]{:S(2)}) collective-permute-start(s32[2,2]{1,0:T(2,128)S(1)} %copy-done.5), channel_id=1, source_target_pairs={{0,128},{128,0},{256,384},{384,256},{1,129},{129,1},{257,385},{385... | collective-permute-start | bytes 56 | tf_op jit(solution)/shard_map/ppermute | solution.py:33
  20.2 6.1 %collective-permute-start.1 = (s32[2,2,2]{2,1,0:T(2,128)S(1)}, s32[2,2,2]{2,1,0:T(2,128)S(1)}, u32[]{:S(2)}, u32[]{:S(2)}) collective-permute-start(s32[2,2,2]{2,1,0:T(2,128)S(1)} %pad_add_fusion.1), channel_id=1, source_target_pairs={{0,256},{128,384},{256,0},{384,128},{1,257},{129,385},{257,1},{385... | collective-permute-start | bytes 104 | tf_op jit(solution)/shard_map/ppermute | solution.py:33
  26.4 5.8 %collective-permute-start.2 = (bf16[8,16,896]{2,1,0:T(8,128)(2,1)S(1)}, bf16[8,16,896]{2,1,0:T(8,128)(2,1)S(1)}, u32[]{:S(2)}, u32[]{:S(2)}) collective-permute-start(bf16[8,16,896]{2,1,0:T(8,128)(2,1)S(1)} %all-to-all-done.mine_ref), channel_id=1, source_target_pairs={{0,8},{8,0},{1,9},{9,1},{2,10},{10,2},{3,11},{11,3},{4,12},{12,4},... | collective-permute-start | bytes 688136 | tf_op jit(solution)/shard_map/ppermute | solution.py:33
  33.8 43.3 %copy-start.1 = (bf16[2,896,512]{2,1,0:T(8,128)(2,1)S(1)}, bf16[2,896,512]{2,1,0:T(8,128)(2,1)}, u32[]{:S(2)}) copy-start(bf16[2,896,512]{2,1,0:T(8,128)(2,1)} %w_own.1) | copy-start | bytes 5505028
  33.8 12.4 %all-to-all-start.1 = ((bf16[4,4,16,896]{3,2,1,0:T(8,128)(2,1)}), bf16[4,4,16,896]{3,2,1,0:T(8,128)(2,1)S(1)}, u32[]{:S(2)}, u32[]{:S(2)}) async-start(bf16[4,4,16,896]{3,2,1,0:T(8,128)(2,1)} %pick.1), calls=%async_computation.1 | async-start | bytes 917504 | tf_op jit(solution)/shard_map/all_to_all | solution.py:236
  47.7 29.4 %collective-permute-start.4 = (bf16[1024,512]{1,0:T(8,128)(2,1)}, bf16[1024,512]{1,0:T(8,128)(2,1)}, u32[]{:S(2)}, u32[]{:S(2)}) collective-permute-start(bf16[1024,512]{1,0:T(8,128)(2,1)} %collective-permute-done.3.near_pair), channel_id=1, source_target_pairs={{0,8},{8,0},{1,9},{9,1},{2,10},{10,2},{3,11},{11,3},{4,12},{12,4},... | collective-permute-start | bytes 3145736 | tf_op jit(solution)/shard_map/ppermute | solution.py:33
  51.3 25.8 %all-to-all-start.2 = ((bf16[8,2,16,896]{3,2,1,0:T(8,128)(2,1)}), bf16[8,2,16,896]{3,2,1,0:T(8,128)(2,1)S(1)}, u32[]{:S(2)}, u32[]{:S(2)}) async-start(bf16[8,2,16,896]{3,2,1,0:T(8,128)(2,1)} %spread.1), calls=%async_computation.2 | async-start | bytes 917504 | tf_op jit(solution)/shard_map/all_to_all | solution.py:243
  85.3 19.9 %all-to-all-start.3 = ((bf16[8,2,16,896]{3,2,1,0:T(8,128)(2,1)}), bf16[8,2,16,896]{3,2,1,0:T(8,128)(2,1)S(1)}, u32[]{:S(2)}, u32[]{:S(2)}) async-start(bf16[8,2,16,896]{3,2,1,0:T(8,128)(2,1)} %get-tuple-element.18), calls=%async_computation.3 | async-start | bytes 917504 | tf_op jit(solution)/shard_map/all_to_all | solution.py:250
  88.8 12.5 %collective-permute-start.5 = (bf16[64,512]{1,0:T(8,128)(2,1)S(1)}, bf16[64,512]{1,0:T(8,128)(2,1)S(1)}, u32[]{:S(2)}, u32[]{:S(2)}) collective-permute-start(bf16[64,512]{1,0:T(8,128)(2,1)S(1)} %get-tuple-element.19), channel_id=1, source_target_pairs={{0,1},{1,0},{2,3},{3,2},{4,5},{5,4},{6,7},{7,6},{8,9},{9,8},{10,11... | collective-permute-start | bytes 196616 | tf_op jit(solution)/shard_map/ppermute | solution.py:33
  116.9 4.5 %collective-permute-start.6 = (bf16[8,16,896]{2,1,0:T(8,128)(2,1)S(1)}, bf16[8,16,896]{2,1,0:T(8,128)(2,1)S(1)}, u32[]{:S(2)}, u32[]{:S(2)}) collective-permute-start(bf16[8,16,896]{2,1,0:T(8,128)(2,1)S(1)} %get-tuple-element.23), channel_id=1, source_target_pairs={{0,8},{8,0},{1,9},{9,1},{2,10},{10,2},{3,11},{11,3},{4,12},{12,4},... | collective-permute-start | bytes 688136 | tf_op jit(solution)/shard_map/ppermute | solution.py:33
  122.2 17.1 %all-to-all-start.5 = ((bf16[8,16,896]{2,1,0:T(8,128)(2,1)}), bf16[8,16,896]{2,1,0:T(8,128)(2,1)S(1)}, u32[]{:S(2)}, u32[]{:S(2)}) async-start(bf16[8,16,896]{2,1,0:T(8,128)(2,1)} %add_convert_fusion), calls=%async_computation.5 | async-start | bytes 458752 | tf_op jit(solution)/shard_map/all_to_all | solution.py:265

commit v3 on v2

--- a/solution.py
+++ b/solution.py
@@ -29,8 +29,12 @@
     return jnp.concatenate([cosine, cosine], axis=-1), jnp.concatenate([-sine, sine], axis=-1)
 
 
-def swapped(value, axis, size, bit=1):
-    return lax.ppermute(value, axis, [(i, i ^ bit) for i in range(size)])
+def shifted(value, axis, size, shift):
+    return lax.ppermute(value, axis, [(i, (i + shift) % size) for i in range(size)])
+
+
+def swapped(value, axis, size):
+    return lax.ppermute(value, axis, [(i, i ^ 1) for i in range(size)])
 
 
 def dot(a, b, over=(1, 0)):
@@ -40,7 +44,7 @@
 
 
 def near_id(near_ref, at_ref, column, read):
-    return near_ref[jnp.bitwise_xor(at_ref[0], column), read // NEIGH, read % NEIGH]
+    return near_ref[lax.rem(at_ref[0] - column + NX, NX), read // NEIGH, read % NEIGH]
 
 
 def pick_kernel(near_ref, at_ref, mine_ref, theirs_ref, out_ref, sems):
@@ -65,21 +69,14 @@
             pltpu.make_async_copy(mine_ref.at[0], out_ref.at[column, read], sem).wait()
 
 
-def spread_kernel(near_ref, at_ref, from_ref, out_ref, sems):
+def spread_kernel(near_ref, at_ref, from_ref, out_ref):
     reads = from_ref.shape[1]
     spans = reads // NEIGH
-    copies = []
     for read in range(reads):
-        column = near_ref[0, read // NEIGH, read % NEIGH] // (NY * NC)
+        owner = near_ref[0, read // NEIGH, read % NEIGH]
+        block = from_ref[owner // (NY * NC), read]
         for at in range(read // NEIGH, NZ, spans):
-            copies.append(
-                pltpu.make_async_copy(
-                    from_ref.at[column, read], out_ref.at[at, read % NEIGH], sems.at[len(copies)]
-                )
-            )
-            copies[-1].start()
-    for copy in copies:
-        copy.wait()
+            out_ref[at, read % NEIGH] = block
 
 
 def owner_kernel(near_ref, at_ref, from_ref, mine_ref, theirs_ref, total):
@@ -100,32 +97,24 @@
 
 
 def attention_kernel(
-    at_ref, tok, w_own, q_own, g_own, kc, ks, qc, qs, near_pair, far_pair,
-    part, dq_own, dq_pair, dk_all, dv_all, total, w_pair, q_pair, g_pair, sems,
+    tok, w_own, q_own, g_own, q_pair, g_pair, kc, ks, qc, qs, w_far,
+    part, dq_own, dq_pair, dk_all, dv_all, w_pair, sem,
 ):
-    core, depth = at_ref[1], w_own.shape[1]
-    fetches = [
-        pltpu.make_async_copy(near_pair.at[:depth], w_pair.at[core], sems.at[0]),
-        pltpu.make_async_copy(far_pair.at[:depth], w_pair.at[1 - core], sems.at[1]),
-        pltpu.make_async_copy(near_pair.at[depth:depth + SPAN], q_pair, sems.at[2]),
-        pltpu.make_async_copy(near_pair.at[depth + SPAN:], g_pair, sems.at[3]),
-    ]
-    for fetch in fetches:
-        fetch.start()
+    fetch = pltpu.make_async_copy(w_far, w_pair, sem)
+    fetch.start()
     scale = 1.0 / math.sqrt(HEAD)
+    half = HEAD // 2
+    width = w_own.shape[2]
     rows = jnp.concatenate([tok[:, n].reshape(NLEN, DE) for n in range(NEIGH)], axis=0)
+    projected = [(dot(rows, w_own[0]), dot(rows, w_own[1]).astype(BF16))]
+    fetch.wait()
+    projected.append((dot(rows, w_pair[0]), dot(rows, w_pair[1]).astype(BF16)))
     key_cos, key_sin, query_cos, query_sin = kc[...], ks[...], qc[...], qs[...]
-    half = HEAD // 2
-    for turn, (w, q, g, dq) in enumerate(
-        ((w_own, q_own, g_own, dq_own), (w_pair, q_pair, g_pair, dq_pair))
-    ):
-        if turn == 1:
-            for fetch in fetches:
-                fetch.wait()
-        key_raw = dot(rows, w[0])
-        values = dot(rows, w[1]).astype(BF16)
-        for head in range(w.shape[2] // HEAD):
+    for turn, (q, g, dq) in enumerate(((q_own, g_own, dq_own), (q_pair, g_pair, dq_pair))):
+        key_raw, values = projected[turn]
+        for head in range(width // HEAD):
             cols = slice(head * HEAD, (head + 1) * HEAD)
+            place = slice(turn * width + head * HEAD, turn * width + (head + 1) * HEAD)
             raw = key_raw[:, cols]
             key = (raw * key_cos + pltpu.roll(raw, half, 1) * key_sin).astype(BF16)
             value = values[:, cols]
@@ -138,23 +127,21 @@
             grad_weights = dot(grad, value, (1, 1))
             delta = jnp.sum(weights_low.astype(F32) * grad_weights, axis=-1, keepdims=True)
             grad_scores = (weights * (grad_weights - delta) * scale).astype(BF16)
-            dv_all[:, cols] = dot(weights_low, grad, (0, 0)).astype(BF16)
+            dv_all[:, place] = dot(weights_low, grad, (0, 0)).astype(BF16)
             grad_query = dot(grad_scores, key)
             dq[:, cols] = (
                 grad_query * query_cos - pltpu.roll(grad_query, half, 1) * query_sin
             ).astype(BF16)
             grad_key = dot(grad_scores, query, (0, 0))
-            dk_all[:, cols] = (
+            dk_all[:, place] = (
                 grad_key * key_cos - pltpu.roll(grad_key, half, 1) * key_sin
             ).astype(BF16)
-        product = dot(dk_all[...], w[0], (1, 1)) + dot(dv_all[...], w[1], (1, 1))
-        if turn == 0:
-            total[...] = product
-        else:
-            product = total[...] + product
-            for n in range(NEIGH):
-                piece = product[n * NLEN:(n + 1) * NLEN].astype(BF16)
-                part[:, n] = piece.reshape(NZ, ROWS, DE)
+    product = dot(dk_all[:, :width], w_own[0], (1, 1)) + dot(dv_all[:, :width], w_own[1], (1, 1))
+    product = product + dot(dk_all[:, width:], w_pair[0], (1, 1))
+    product = product + dot(dv_all[:, width:], w_pair[1], (1, 1))
+    for n in range(NEIGH):
+        piece = product[n * NLEN:(n + 1) * NLEN].astype(BF16)
+        part[:, n] = piece.reshape(NZ, ROWS, DE)
 
 
 def on_core(kernel, name, shapes, scalars, *operands, scratch=(), space=VMEM):
@@ -169,7 +156,7 @@
     )(*scalars, *operands)
 
 
-def attention(at, *operands):
+def attention(*operands):
     _, depth, width = operands[1].shape
     return pl.pallas_call(
         attention_kernel,
@@ -178,23 +165,20 @@
             jax.ShapeDtypeStruct((SPAN, width), BF16),
             jax.ShapeDtypeStruct((SPAN, width), BF16),
         ),
-        in_specs=[SMEM] + [VMEM] * (len(operands) - 2) + [ANY] * 2,
+        in_specs=[VMEM] * (len(operands) - 1) + [ANY],
         out_specs=(VMEM, VMEM, VMEM),
         scratch_shapes=[
-            pltpu.VMEM((NEIGH * NLEN, width), BF16),
-            pltpu.VMEM((NEIGH * NLEN, width), BF16),
-            pltpu.VMEM((NEIGH * NLEN, DE), F32),
+            pltpu.VMEM((NEIGH * NLEN, 2 * width), BF16),
+            pltpu.VMEM((NEIGH * NLEN, 2 * width), BF16),
             pltpu.VMEM((2, depth, width), BF16),
-            pltpu.VMEM((SPAN, width), BF16),
-            pltpu.VMEM((SPAN, width), BF16),
-            pltpu.SemaphoreType.DMA((4,)),
+            pltpu.SemaphoreType.DMA,
         ],
         compiler_params=pltpu.CompilerParams(vmem_limit_bytes=40 << 20),
         cost_estimate=pl.CostEstimate(
             flops=2_100_000_000, bytes_accessed=6_000_000, transcendentals=131072
         ),
         name="attention",
-    )(at, *operands)
+    )(*operands)
 
 
 def local(queries, out_grad, encodings, kv_weight, neighbour_ids, rot_offset):
@@ -203,17 +187,16 @@
     reads = spans * NEIGH
     span_at = z_at % 2
 
+    w_far = swapped(kv_weight, "z", NZ)
     rows_q = queries.reshape(spans, SPAN, -1)
     rows_g = out_grad.reshape(spans, SPAN, -1)
-    to_pair = jnp.concatenate(
+    other = jnp.concatenate(
         [
-            lax.dynamic_index_in_dim(kv_weight, c_at, 0, keepdims=False),
             lax.dynamic_index_in_dim(rows_q, 1 - span_at, 0, keepdims=False),
             lax.dynamic_index_in_dim(rows_g, 1 - span_at, 0, keepdims=False),
         ],
         axis=0,
     )
-    near_pair = swapped(to_pair, "z", NZ)
     q_own = lax.dynamic_index_in_dim(rows_q, span_at, 0, keepdims=False)
     g_own = lax.dynamic_index_in_dim(rows_g, span_at, 0, keepdims=False)
     offsets = lax.dynamic_index_in_dim(rot_offset, span_at, 0, keepdims=False)
@@ -222,11 +205,11 @@
     query_cos, query_sin = rotary_tables(jnp.arange(SPAN, dtype=jnp.int32))
 
     at = jnp.stack([x_at, c_at])
-    near = jnp.stack([neighbour_ids, swapped(neighbour_ids, "x", NX)])
-    near = jnp.concatenate([near, swapped(near, "x", NX, 2)])
+    near = [neighbour_ids] + [shifted(neighbour_ids, "x", NX, s) for s in range(1, NX)]
+    near = jnp.stack(near)
     copies = jnp.broadcast_to(encodings, (NY, ROWS, DE))
     over_y = lax.all_to_all(copies, "y", split_axis=0, concat_axis=0, tiled=True)
-    over_y, near = lax.optimization_barrier((over_y, near))
+    over_y, near, other = lax.optimization_barrier((over_y, near, other))
     beside = swapped(over_y, "c", NC)
     block = (reads, ROWS, DE)
     asked = on_core(
@@ -237,19 +220,17 @@
 
     to_z = on_core(
         spread_kernel, "spread", jax.ShapeDtypeStruct((NZ, NEIGH, ROWS, DE), BF16), (near, at),
-        found, scratch=[pltpu.SemaphoreType.DMA((NZ * NEIGH,))], space=ANY,
-    )
-    to_z, near_pair = lax.optimization_barrier((to_z, near_pair))
+        found,
+    )
+    to_z, w_far = lax.optimization_barrier((to_z, w_far))
     tok = lax.all_to_all(to_z, "z", split_axis=0, concat_axis=0, tiled=True)
-    far_pair = swapped(near_pair, "c", NC)
+    from_pair = swapped(other, "z", NZ)
     part, dq_own, dq_pair = attention(
-        at, tok, kv_weight, q_own, g_own, key_cos, key_sin, query_cos, query_sin,
-        near_pair, far_pair,
+        tok, kv_weight, q_own, g_own, from_pair[:SPAN], from_pair[SPAN:],
+        key_cos, key_sin, query_cos, query_sin, w_far,
     )
 
     from_heads = lax.all_to_all(part, "z", split_axis=0, concat_axis=0, tiled=True)
-    dq_back = swapped(dq_pair, "z", NZ)
-    from_heads, dq_back = lax.optimization_barrier((from_heads, dq_back))
     from_heads = from_heads.reshape(NZ // spans, spans, NEIGH, ROWS, DE)
     read_sum = jnp.sum(from_heads.astype(F32), axis=0).astype(BF16).reshape(reads, ROWS, DE)
 
@@ -262,6 +243,8 @@
         (near, at), read_x, scratch=[pltpu.VMEM((NC * NY, ROWS, DE), F32)],
     )
     owner_part = (mine + swapped(theirs, "c", NC).astype(F32)).astype(BF16)
+    owner_part, dq_pair = lax.optimization_barrier((owner_part, dq_pair))
+    dq_back = swapped(dq_pair, "z", NZ)
     from_y = lax.all_to_all(owner_part, "y", split_axis=0, concat_axis=0, tiled=True)
     owned = jnp.sum(from_y.astype(F32), axis=0)
 

time: 141 us -> 136 us (0.965)
  waiting for transfers between devices: 51.7 us -> 31.7 us
  blocking collectives: 10.6 us -> 28.2 us
  Pallas kernels: 12.3 us -> 10.4 us
    all_to_all x0 -> x1, blocking collectives: none -> 19.3 us  [local(): lax.all_to_all(part, 'z', split_axis=0, concat_axis=0, tiled=True)]
    all_to_all x1, waiting for transfers between devices: 15.8 us -> 1.96 us  [local(): tok = lax.all_to_all(to_z, 'z', split_axis=0, concat_axis=0, tiled=True)]
    all_to_all x1 -> x0, waiting for transfers between devices: 3.87 us -> none  [local(): lax.all_to_all(part, 'z', split_axis=0, concat_axis=0, tiled=True)]
    ppermute x7 -> x8, starting transfers between devices: 27.5 us -> 31.1 us  [the longest x5 21.2 us: swapped(): return lax.ppermute(value, axis, [(i, i ^ 1) for i in range(size)])]
    all_to_all x1 -> x0, starting transfers between devices: 3.48 us -> none  [local(): lax.all_to_all(part, 'z', split_axis=0, concat_axis=0, tiled=True)]
    ppermute x7 -> x8, waiting for transfers between devices: 14.4 us -> 12.4 us  [the longest x5 10.8 us: swapped(): return lax.ppermute(value, axis, [(i, i ^ 1) for i in range(size)])]
    pallas_call x1, Pallas kernels: 8.19 us -> 6.4 us  [attention(): pl.pallas_call(attention_kernel, out_shape=(jax.ShapeDtypeStruct((NZ, NEI...]
    all_to_all x1, blocking collectives: 10.6 us -> 8.96 us  [local(): lax.all_to_all(read_copies, 'x', split_axis=0, concat_axis=0, tiled=True)]
  transfers between devices with their start and end apart: 12 -> 12, of which waited for: 9 -> 7; matrix products, arithmetic and copies ran while one was open for 2% -> 4% of each run, Pallas kernels for 2% -> 2%
where the time goes in v3:
time: 136 us; the launch traced here: 135 us
  starting transfers between devices  57.5 us (42%)
  waiting for transfers between devices  31.7 us (23%)
  blocking collectives  28.2 us (21%)
  Pallas kernels  10.4 us (8%)
  other arithmetic  3.94 us (3%)
  local copies, waits for them, and re-layouts  2.5 us (2%)
    ppermute x5, starting transfers between devices, swapped(): return lax.ppermute(value, axis, [(i, i ^ 1) for i in range(size)])  21.2 us
    all_to_all x1, blocking collectives, local(): lax.all_to_all(part, 'z', split_axis=0, concat_axis=0, tiled=True)  19.3 us
    ppermute x5, waiting for transfers between devices, swapped(): return lax.ppermute(value, axis, [(i, i ^ 1) for i in range(size)])  10.8 us
    ppermute x3, starting transfers between devices, shifted(): lax.ppermute(value, axis, [(i, (i + shift) % size) for i in range(size)])  9.93 us
    all_to_all x1, starting transfers between devices, local(): tok = lax.all_to_all(to_z, 'z', split_axis=0, concat_axis=0, tiled=True)  9.13 us
    all_to_all x1, waiting for transfers between devices, local(): lax.all_to_all(owner_part, 'y', split_axis=0, concat_axis=0, tiled=True)  9.08 us
    all_to_all x1, blocking collectives, local(): lax.all_to_all(read_copies, 'x', split_axis=0, concat_axis=0, tiled=True)  8.96 us
    all_to_all x1, waiting for transfers between devices, local(): found = lax.all_to_all(asked, 'x', split_axis=0, concat_axis=0, tiled=True)  8.24 us
  transfers between devices with their start and end apart: 12, of which 7 were waited for; matrix products, arithmetic and copies ran while one was open for 4% of the time, Pallas kernels for 2%

profile of v3, /device:TPU:1, one launch (start us, length us, event | category | flops | bytes accessed | tf_op | source)
XLA Modules:
  0.0 135.1 jit_solution(3554863487999300677)
XLA Ops:
  0.6 4.8 %collective-permute-start.4 = (bf16[2,896,512]{2,1,0:T(8,128)(2,1)}, bf16[2,896,512]{2,1,0:T(8,128)(2,1)}, u32[]{:S(2)}, u32[]{:S(2)}) collective-permute-start(bf16[2,896,512]{2,1,0:T(8,128)(2,1)} %w_own.1), channel_id=1, source_target_pairs={{0,1},{1,0},{2,3},{3,2},{4,5},{5,4},{6,7},{7,6},{8,9},{9,8},{10,11... | collective-permute-start | bytes 5505032 | tf_op jit(solution)/shard_map/ppermute | solution.py:37
  5.5 1.5 %broadcast_in_dim.7 = bf16[8,16,896]{2,1,0:T(8,128)(2,1)} broadcast(bf16[16,896]{1,0:T(8,128)(2,1)} %bitcast.29), dimensions={1,2} | broadcast | bytes 258048 | tf_op jit(solution)/shard_map/broadcast_in_dim | solution.py:210
  7.0 6.8 %all-to-all-start = ((bf16[8,16,896]{2,1,0:T(8,128)(2,1)}), bf16[8,16,896]{2,1,0:T(8,128)(2,1)S(1)}, u32[]{:S(2)}, u32[]{:S(2)}) async-start(bf16[8,16,896]{2,1,0:T(8,128)(2,1)} %broadcast_in_dim.7), calls=%async_computation | async-start | bytes 458752 | tf_op jit(solution)/shard_map/all_to_all | solution.py:211
  13.8 3.1 %collective-permute-start = (s32[2,2]{1,0:T(2,128)}, s32[2,2]{1,0:T(2,128)S(1)}, u32[]{:S(2)}, u32[]{:S(2)}) collective-permute-start(s32[2,2]{1,0:T(2,128)} %param.10), channel_id=1, source_target_pairs={{0,128},{128,256},{256,384},{384,0},{1,129},{129,257},{257,385},{3... | collective-permute-start | bytes 56 | tf_op jit(solution)/shard_map/ppermute | solution.py:33
  16.9 3.4 %collective-permute-start.2 = (s32[2,2]{1,0:T(2,128)}, s32[2,2]{1,0:T(2,128)S(1)}, u32[]{:S(2)}, u32[]{:S(2)}) collective-permute-start(s32[2,2]{1,0:T(2,128)} %param.10), channel_id=1, source_target_pairs={{0,384},{128,0},{256,128},{384,256},{1,385},{129,1},{257,129},{385... | collective-permute-start | bytes 56 | tf_op jit(solution)/shard_map/ppermute | solution.py:33
  20.3 3.4 %collective-permute-start.1 = (s32[2,2]{1,0:T(2,128)}, s32[2,2]{1,0:T(2,128)S(1)}, u32[]{:S(2)}, u32[]{:S(2)}) collective-permute-start(s32[2,2]{1,0:T(2,128)} %param.10), channel_id=1, source_target_pairs={{0,256},{128,384},{256,0},{384,128},{1,257},{129,385},{257,1},{385... | collective-permute-start | bytes 56 | tf_op jit(solution)/shard_map/ppermute | solution.py:33
  24.8 1.6 %collective-permute-done.1 = s32[2,2]{1,0:T(2,128)S(1)} collective-permute-done((s32[2,2]{1,0:T(2,128)}, s32[2,2]{1,0:T(2,128)S(1)}, u32[]{:S(2)}, u32[]{:S(2)}) %collective-permute-start.1) | collective-permute-done | bytes 48 | tf_op jit(solution)/shard_map/ppermute | solution.py:33
  27.0 4.8 %collective-permute-start.3 = (bf16[8,16,896]{2,1,0:T(8,128)(2,1)S(1)}, bf16[8,16,896]{2,1,0:T(8,128)(2,1)S(1)}, u32[]{:S(2)}, u32[]{:S(2)}) collective-permute-start(bf16[8,16,896]{2,1,0:T(8,128)(2,1)S(1)} %all-to-all-done.mine_ref), channel_id=1, source_target_pairs={{0,8},{8,0},{1,9},{9,1},{2,10},{10,2},{3,11},{11,3},{4,12},{12,4},... | collective-permute-start | bytes 688136 | tf_op jit(solution)/shard_map/ppermute | solution.py:37
  32.9 1.5 %pick.1 = bf16[4,4,16,896]{3,2,1,0:T(8,128)(2,1)} custom-call(s32[4,2,2]{2,1,0:T(2,128)S(1)} %pad_add_fusion.near_ref, s32[2]{0:T(128)S(1)} %pad_add_fusion.1.at_ref, bf16[8,16,896]{2,1,0:T(8,128)(2,1)S(1)} %all-to-all-done.mine_ref, bf16[8,16,896]{2,1,0:T(8,128)(2,1)S(1)} %collective-permute-done.3.theirs_ref), custom_call_target="tpu_custom_call" | custom-call | tf_op jit(solution)/shard_map/pick/pallas_call | solution.py:148
  34.5 3.5 %all-to-all-start.1 = ((bf16[4,4,16,896]{3,2,1,0:T(8,128)(2,1)}), bf16[4,4,16,896]{3,2,1,0:T(8,128)(2,1)S(1)}, u32[]{:S(2)}, u32[]{:S(2)}) async-start(bf16[4,4,16,896]{3,2,1,0:T(8,128)(2,1)} %pick.1), calls=%async_computation.1 | async-start | bytes 917504 | tf_op jit(solution)/shard_map/all_to_all | solution.py:219
  38.2 8.2 %all-to-all-done.1.from_ref = bf16[4,4,16,896]{3,2,1,0:T(8,128)(2,1)S(1)} async-done(((bf16[4,4,16,896]{3,2,1,0:T(8,128)(2,1)}), bf16[4,4,16,896]{3,2,1,0:T(8,128)(2,1)S(1)}, u32[]{:S(2)}, u32[]{:S(2)}) %all-to-all-start.1) | async-done | bytes 458784 | tf_op jit(solution)/shard_map/all_to_all | solution.py:219
  46.5 1.4 %spread.1 = bf16[8,2,16,896]{3,2,1,0:T(8,128)(2,1)} custom-call(s32[4,2,2]{2,1,0:T(2,128)S(1)} %pad_add_fusion.near_ref, s32[2]{0:T(128)S(1)} %pad_add_fusion.1.at_ref, bf16[4,4,16,896]{3,2,1,0:T(8,128)(2,1)S(1)} %all-to-all-done.1.from_ref), custom_call_target="tpu_custom_call" | custom-call | tf_op jit(solution)/shard_map/spread/pallas_call | solution.py:148
  47.9 9.1 %all-to-all-start.2 = ((bf16[8,2,16,896]{3,2,1,0:T(8,128)(2,1)}), bf16[8,2,16,896]{3,2,1,0:T(8,128)(2,1)S(1)}, u32[]{:S(2)}, u32[]{:S(2)}) async-start(bf16[8,2,16,896]{3,2,1,0:T(8,128)(2,1)} %spread.1), calls=%async_computation.2 | async-start | bytes 917504 | tf_op jit(solution)/shard_map/all_to_all | solution.py:226
  57.6 3.4 %collective-permute-start.5 = (bf16[128,512]{1,0:T(8,128)(2,1)S(1)}, bf16[128,512]{1,0:T(8,128)(2,1)S(1)}, u32[]{:S(2)}, u32[]{:S(2)}) collective-permute-start(bf16[128,512]{1,0:T(8,128)(2,1)S(1)} %pad_maximum_fusion), channel_id=1, source_target_pairs={{0,1},{1,0},{2,3},{3,2},{4,5},{5,4},{6,7},{7,6},{8,9},{9,8},{10,11... | collective-permute-start | bytes 393224 | tf_op jit(solution)/shard_map/ppermute | solution.py:37
  61.2 8.7 %collective-permute-done.5 = bf16[128,512]{1,0:T(8,128)(2,1)S(1)} collective-permute-done((bf16[128,512]{1,0:T(8,128)(2,1)S(1)}, bf16[128,512]{1,0:T(8,128)(2,1)S(1)}, u32[]{:S(2)}, u32[]{:S(2)}) %collective-permute-start.5) | collective-permute-done | bytes 131104 | tf_op jit(solution)/shard_map/ppermute | solution.py:37
  70.0 2.0 %all-to-all-done.2.tok = bf16[8,2,16,896]{3,2,1,0:T(8,128)(2,1)S(1)} async-done(((bf16[8,2,16,896]{3,2,1,0:T(8,128)(2,1)}), bf16[8,2,16,896]{3,2,1,0:T(8,128)(2,1)S(1)}, u32[]{:S(2)}, u32[]{:S(2)}) %all-to-all-start.2) | async-done | bytes 458784 | tf_op jit(solution)/shard_map/all_to_all | solution.py:226
  72.0 6.4 %attention.1 = (bf16[8,2,16,896]{3,2,1,0:T(8,128)(2,1)S(1)}, bf16[64,512]{1,0:T(8,128)(2,1)S(1)}, bf16[64,512]{1,0:T(8,128)(2,1)S(1)}) custom-call(bf16[8,2,16,896]{3,2,1,0:T(8,128)(2,1)S(1)} %all-to-all-done.2.tok, bf16[2,896,512]{2,1,0:T(8,128)(2,1)S(1)} %copy-done.1, bf16[64,512]{1,0:T(8,128)(2,1)S(1)} %get-tuple-element.41.q_own, ...), custom_call_target="tpu_custom_call" | custom-call | flops 2100000000 | bytes 6000000 | tf_op jit(solution)/shard_map/attention/pallas_call | solution.py:161
  78.4 19.3 %all_to_all.30 = bf16[8,2,16,896]{3,2,1,0:T(8,128)(2,1)S(1)} all-to-all(bf16[8,2,16,896]{3,2,1,0:T(8,128)(2,1)S(1)} %get-tuple-element.20), channel_id=1, replica_groups=mesh['x'=4,'y'=8,'c'=2,'z'=8] {'z'}, dimensions={0} | all-to-all | bytes 917504 | tf_op jit(solution)/shard_map/all_to_all | solution.py:233
  97.7 9.0 %all_to_all.31.from_ref = bf16[4,4,16,896]{3,2,1,0:T(8,128)(2,1)S(1)} all-to-all(bf16[4,4,16,896]{3,2,1,0:T(8,128)(2,1)S(1)} %broadcast_in_dim.8), channel_id=1, replica_groups=mesh['x'=4,'y'=8,'c'=2,'z'=8] {'x'}, dimensions={0} | all-to-all | bytes 917504 | tf_op jit(solution)/shard_map/all_to_all | solution.py:238
  107.8 5.9 %collective-permute-start.6 = (bf16[8,16,896]{2,1,0:T(8,128)(2,1)S(1)}, bf16[8,16,896]{2,1,0:T(8,128)(2,1)S(1)}, u32[]{:S(2)}, u32[]{:S(2)}) collective-permute-start(bf16[8,16,896]{2,1,0:T(8,128)(2,1)S(1)} %get-tuple-element.22), channel_id=1, source_target_pairs={{0,8},{8,0},{1,9},{9,1},{2,10},{10,2},{3,11},{11,3},{4,12},{12,4},... | collective-permute-start | bytes 688136 | tf_op jit(solution)/shard_map/ppermute | solution.py:37
  113.7 1.1 collective-permute-done.6
  115.5 2.2 %collective-permute-start.7 = (bf16[64,512]{1,0:T(8,128)(2,1)S(1)}, bf16[64,512]{1,0:T(8,128)(2,1)S(1)}, u32[]{:S(2)}, u32[]{:S(2)}) collective-permute-start(bf16[64,512]{1,0:T(8,128)(2,1)S(1)} %get-tuple-element.24), channel_id=1, source_target_pairs={{0,1},{1,0},{2,3},{3,2},{4,5},{5,4},{6,7},{7,6},{8,9},{9,8},{10,11... | collective-permute-start | bytes 196616 | tf_op jit(solution)/shard_map/ppermute | solution.py:37
  117.7 7.0 %all-to-all-start.5 = ((bf16[8,16,896]{2,1,0:T(8,128)(2,1)}), bf16[8,16,896]{2,1,0:T(8,128)(2,1)S(1)}, u32[]{:S(2)}, u32[]{:S(2)}) async-start(bf16[8,16,896]{2,1,0:T(8,128)(2,1)} %add_convert_fusion), calls=%async_computation.5 | async-start | bytes 458752 | tf_op jit(solution)/shard_map/all_to_all | solution.py:248
  125.4 9.1 %all-to-all-done.5 = bf16[8,16,896]{2,1,0:T(8,128)(2,1)S(1)} async-done(((bf16[8,16,896]{2,1,0:T(8,128)(2,1)}), bf16[8,16,896]{2,1,0:T(8,128)(2,1)S(1)}, u32[]{:S(2)}, u32[]{:S(2)}) %all-to-all-start.5) | async-done | bytes 229408 | tf_op jit(solution)/shard_map/all_to_all | solution.py:248
  (30 shorter events, 7.0 us)
Async XLA Ops:
  0.6 37.4 %copy-start = (s32[2,2]{1,0:T(2,128)S(1)}, s32[2,2]{1,0:T(2,128)}, u32[]{:S(2)}) copy-start(s32[2,2]{1,0:T(2,128)} %param.11) | copy-start | bytes 52
  0.6 47.2 %collective-permute-start.4 = (bf16[2,896,512]{2,1,0:T(8,128)(2,1)}, bf16[2,896,512]{2,1,0:T(8,128)(2,1)}, u32[]{:S(2)}, u32[]{:S(2)}) collective-permute-start(bf16[2,896,512]{2,1,0:T(8,128)(2,1)} %w_own.1), channel_id=1, source_target_pairs={{0,1},{1,0},{2,3},{3,2},{4,5},{5,4},{6,7},{7,6},{8,9},{9,8},{10,11... | collective-permute-start | bytes 5505032 | tf_op jit(solution)/shard_map/ppermute | solution.py:37
  7.0 20.0 %all-to-all-start = ((bf16[8,16,896]{2,1,0:T(8,128)(2,1)}), bf16[8,16,896]{2,1,0:T(8,128)(2,1)S(1)}, u32[]{:S(2)}, u32[]{:S(2)}) async-start(bf16[8,16,896]{2,1,0:T(8,128)(2,1)} %broadcast_in_dim.7), calls=%async_computation | async-start | bytes 458752 | tf_op jit(solution)/shard_map/all_to_all | solution.py:211
  13.8 11.0 %collective-permute-start = (s32[2,2]{1,0:T(2,128)}, s32[2,2]{1,0:T(2,128)S(1)}, u32[]{:S(2)}, u32[]{:S(2)}) collective-permute-start(s32[2,2]{1,0:T(2,128)} %param.10), channel_id=1, source_target_pairs={{0,128},{128,256},{256,384},{384,0},{1,129},{129,257},{257,385},{3... | collective-permute-start | bytes 56 | tf_op jit(solution)/shard_map/ppermute | solution.py:33
  16.9 7.9 %collective-permute-start.2 = (s32[2,2]{1,0:T(2,128)}, s32[2,2]{1,0:T(2,128)S(1)}, u32[]{:S(2)}, u32[]{:S(2)}) collective-permute-start(s32[2,2]{1,0:T(2,128)} %param.10), channel_id=1, source_target_pairs={{0,384},{128,0},{256,128},{384,256},{1,385},{129,1},{257,129},{385... | collective-permute-start | bytes 56 | tf_op jit(solution)/shard_map/ppermute | solution.py:33
  20.3 6.0 %collective-permute-start.1 = (s32[2,2]{1,0:T(2,128)}, s32[2,2]{1,0:T(2,128)S(1)}, u32[]{:S(2)}, u32[]{:S(2)}) collective-permute-start(s32[2,2]{1,0:T(2,128)} %param.10), channel_id=1, source_target_pairs={{0,256},{128,384},{256,0},{384,128},{1,257},{129,385},{257,1},{385... | collective-permute-start | bytes 56 | tf_op jit(solution)/shard_map/ppermute | solution.py:33
  27.0 5.9 %collective-permute-start.3 = (bf16[8,16,896]{2,1,0:T(8,128)(2,1)S(1)}, bf16[8,16,896]{2,1,0:T(8,128)(2,1)S(1)}, u32[]{:S(2)}, u32[]{:S(2)}) collective-permute-start(bf16[8,16,896]{2,1,0:T(8,128)(2,1)S(1)} %all-to-all-done.mine_ref), channel_id=1, source_target_pairs={{0,8},{8,0},{1,9},{9,1},{2,10},{10,2},{3,11},{11,3},{4,12},{12,4},... | collective-permute-start | bytes 688136 | tf_op jit(solution)/shard_map/ppermute | solution.py:37
  34.5 12.0 %all-to-all-start.1 = ((bf16[4,4,16,896]{3,2,1,0:T(8,128)(2,1)}), bf16[4,4,16,896]{3,2,1,0:T(8,128)(2,1)S(1)}, u32[]{:S(2)}, u32[]{:S(2)}) async-start(bf16[4,4,16,896]{3,2,1,0:T(8,128)(2,1)} %pick.1), calls=%async_computation.1 | async-start | bytes 917504 | tf_op jit(solution)/shard_map/all_to_all | solution.py:219
  38.0 34.0 %copy-start.1 = (bf16[2,896,512]{2,1,0:T(8,128)(2,1)S(1)}, bf16[2,896,512]{2,1,0:T(8,128)(2,1)}, u32[]{:S(2)}) copy-start(bf16[2,896,512]{2,1,0:T(8,128)(2,1)} %w_own.1) | copy-start | bytes 5505028
  47.9 24.1 %all-to-all-start.2 = ((bf16[8,2,16,896]{3,2,1,0:T(8,128)(2,1)}), bf16[8,2,16,896]{3,2,1,0:T(8,128)(2,1)S(1)}, u32[]{:S(2)}, u32[]{:S(2)}) async-start(bf16[8,2,16,896]{3,2,1,0:T(8,128)(2,1)} %spread.1), calls=%async_computation.2 | async-start | bytes 917504 | tf_op jit(solution)/shard_map/all_to_all | solution.py:226
  57.6 12.4 %collective-permute-start.5 = (bf16[128,512]{1,0:T(8,128)(2,1)S(1)}, bf16[128,512]{1,0:T(8,128)(2,1)S(1)}, u32[]{:S(2)}, u32[]{:S(2)}) collective-permute-start(bf16[128,512]{1,0:T(8,128)(2,1)S(1)} %pad_maximum_fusion), channel_id=1, source_target_pairs={{0,1},{1,0},{2,3},{3,2},{4,5},{5,4},{6,7},{7,6},{8,9},{9,8},{10,11... | collective-permute-start | bytes 393224 | tf_op jit(solution)/shard_map/ppermute | solution.py:37
  107.8 7.0 %collective-permute-start.6 = (bf16[8,16,896]{2,1,0:T(8,128)(2,1)S(1)}, bf16[8,16,896]{2,1,0:T(8,128)(2,1)S(1)}, u32[]{:S(2)}, u32[]{:S(2)}) collective-permute-start(bf16[8,16,896]{2,1,0:T(8,128)(2,1)S(1)} %get-tuple-element.22), channel_id=1, source_target_pairs={{0,8},{8,0},{1,9},{9,1},{2,10},{10,2},{3,11},{11,3},{4,12},{12,4},... | collective-permute-start | bytes 688136 | tf_op jit(solution)/shard_map/ppermute | solution.py:37
  115.5 9.2 %collective-permute-start.7 = (bf16[64,512]{1,0:T(8,128)(2,1)S(1)}, bf16[64,512]{1,0:T(8,128)(2,1)S(1)}, u32[]{:S(2)}, u32[]{:S(2)}) collective-permute-start(bf16[64,512]{1,0:T(8,128)(2,1)S(1)} %get-tuple-element.24), channel_id=1, source_target_pairs={{0,1},{1,0},{2,3},{3,2},{4,5},{5,4},{6,7},{7,6},{8,9},{9,8},{10,11... | collective-permute-start | bytes 196616 | tf_op jit(solution)/shard_map/ppermute | solution.py:37
  117.7 16.8 %all-to-all-start.5 = ((bf16[8,16,896]{2,1,0:T(8,128)(2,1)}), bf16[8,16,896]{2,1,0:T(8,128)(2,1)S(1)}, u32[]{:S(2)}, u32[]{:S(2)}) async-start(bf16[8,16,896]{2,1,0:T(8,128)(2,1)} %add_convert_fusion), calls=%async_computation.5 | async-start | bytes 458752 | tf_op jit(solution)/shard_map/all_to_all | solution.py:248

commit v4 on v3

--- a/solution.py
+++ b/solution.py
@@ -20,6 +20,25 @@
 ANY = pl.BlockSpec(memory_space=pl.ANY)
 
 
+def both_orders(major, count, minor, flip):
+    return [[i * major for i in range(count)], [(i ^ flip) * major + minor for i in range(count)]]
+
+
+FLIP_Y, FLIP_X, FLIP_Z = NY - 1, NX - 1, NZ - 2
+GROUPS = {
+    "y": (("y", "c"), both_orders(NC, NY, 1, FLIP_Y)),
+    "x": (("x", "c"), both_orders(NC, NX, 1, FLIP_X)),
+    "z": (("c", "z"), both_orders(1, NZ, NZ, FLIP_Z)),
+}
+
+
+def exchange(value, axis):
+    axes, groups = GROUPS[axis]
+    return lax.all_to_all(
+        value, axes, split_axis=0, concat_axis=0, axis_index_groups=groups, tiled=True
+    )
+
+
 def rotary_tables(positions):
     halfway = HEAD // 2
     exponent = jnp.arange(halfway, dtype=F32) * (2.0 / HEAD)
@@ -51,8 +70,9 @@
     core, reads = at_ref[1], out_ref.shape[1]
     for column in range(NX):
         for read in range(reads):
-            block = near_id(near_ref, at_ref, column, read)
-            row, same = lax.rem(block // NC, NY), lax.rem(block, NC) == core
+            block = near_id(near_ref, at_ref, column ^ (FLIP_X * core), read)
+            side = lax.rem(block, NC)
+            row, same = lax.rem(block // NC, NY) ^ (FLIP_Y * side), side == core
             sem = sems.at[column * reads + read]
 
             @pl.when(same)
@@ -74,7 +94,7 @@
     spans = reads // NEIGH
     for read in range(reads):
         owner = near_ref[0, read // NEIGH, read % NEIGH]
-        block = from_ref[owner // (NY * NC), read]
+        block = from_ref[(owner // (NY * NC)) ^ (FLIP_X * at_ref[1]), read]
         for at in range(read // NEIGH, NZ, spans):
             out_ref[at, read % NEIGH] = block
 
@@ -84,12 +104,13 @@
     here, core = at_ref[0], at_ref[1]
     for column in range(NX):
         for read in range(from_ref.shape[1]):
-            block = near_id(near_ref, at_ref, column, read)
+            block = near_id(near_ref, at_ref, column ^ (FLIP_X * core), read)
 
             @pl.when(block // (NY * NC) == here)
             def _():
-                side = jnp.where(lax.rem(block, NC) == core, 0, NY)
-                at = side + lax.rem(block // NC, NY)
+                side = lax.rem(block, NC)
+                row = lax.rem(block // NC, NY) ^ (FLIP_Y * side)
+                at = jnp.where(side == core, 0, NY) + row
                 total[at] = total[at] + from_ref[column, read].astype(F32)
 
     mine_ref[...] = total[:NY]
@@ -188,6 +209,28 @@
     span_at = z_at % 2
 
     w_far = swapped(kv_weight, "z", NZ)
+    offsets = lax.dynamic_index_in_dim(rot_offset, span_at, 0, keepdims=False)
+    slices = jnp.arange(NZ, dtype=jnp.int32) ^ (FLIP_Z * c_at)
+    tokens = (slices[:, None] * ROWS + jnp.arange(ROWS, dtype=jnp.int32)[None, :]).reshape(NLEN)
+    positions = offsets[:, None] + tokens[None, :]
+    key_cos, key_sin = rotary_tables(positions.reshape(NEIGH * NLEN))
+    query_cos, query_sin = rotary_tables(jnp.arange(SPAN, dtype=jnp.int32))
+
+    at = jnp.stack([x_at, c_at])
+    near = [neighbour_ids] + [shifted(neighbour_ids, "x", NX, s) for s in range(1, NX)]
+    near = jnp.stack(near)
+    copies = jnp.broadcast_to(encodings, (NY, ROWS, DE))
+    over_y = exchange(copies, "y")
+    over_y, near = lax.optimization_barrier((over_y, near))
+    beside = swapped(over_y, "c", NC)
+    block = (reads, ROWS, DE)
+    asked = on_core(
+        pick_kernel, "pick", jax.ShapeDtypeStruct((NX, *block), BF16), (near, at),
+        over_y, beside, scratch=[pltpu.SemaphoreType.DMA((NX * reads,))], space=ANY,
+    )
+    asked, queries, out_grad = lax.optimization_barrier((asked, queries, out_grad))
+    found = exchange(asked, "x")
+
     rows_q = queries.reshape(spans, SPAN, -1)
     rows_g = out_grad.reshape(spans, SPAN, -1)
     other = jnp.concatenate(
@@ -199,43 +242,25 @@
     )
     q_own = lax.dynamic_index_in_dim(rows_q, span_at, 0, keepdims=False)
     g_own = lax.dynamic_index_in_dim(rows_g, span_at, 0, keepdims=False)
-    offsets = lax.dynamic_index_in_dim(rot_offset, span_at, 0, keepdims=False)
-    positions = offsets[:, None] + jnp.arange(NLEN, dtype=jnp.int32)[None, :]
-    key_cos, key_sin = rotary_tables(positions.reshape(NEIGH * NLEN))
-    query_cos, query_sin = rotary_tables(jnp.arange(SPAN, dtype=jnp.int32))
-
-    at = jnp.stack([x_at, c_at])
-    near = [neighbour_ids] + [shifted(neighbour_ids, "x", NX, s) for s in range(1, NX)]
-    near = jnp.stack(near)
-    copies = jnp.broadcast_to(encodings, (NY, ROWS, DE))
-    over_y = lax.all_to_all(copies, "y", split_axis=0, concat_axis=0, tiled=True)
-    over_y, near, other = lax.optimization_barrier((over_y, near, other))
-    beside = swapped(over_y, "c", NC)
-    block = (reads, ROWS, DE)
-    asked = on_core(
-        pick_kernel, "pick", jax.ShapeDtypeStruct((NX, *block), BF16), (near, at),
-        over_y, beside, scratch=[pltpu.SemaphoreType.DMA((NX * reads,))], space=ANY,
-    )
-    found = lax.all_to_all(asked, "x", split_axis=0, concat_axis=0, tiled=True)
 
     to_z = on_core(
         spread_kernel, "spread", jax.ShapeDtypeStruct((NZ, NEIGH, ROWS, DE), BF16), (near, at),
         found,
     )
     to_z, w_far = lax.optimization_barrier((to_z, w_far))
-    tok = lax.all_to_all(to_z, "z", split_axis=0, concat_axis=0, tiled=True)
+    tok = exchange(to_z, "z")
     from_pair = swapped(other, "z", NZ)
     part, dq_own, dq_pair = attention(
         tok, kv_weight, q_own, g_own, from_pair[:SPAN], from_pair[SPAN:],
         key_cos, key_sin, query_cos, query_sin, w_far,
     )
 
-    from_heads = lax.all_to_all(part, "z", split_axis=0, concat_axis=0, tiled=True)
+    from_heads = exchange(part, "z")
     from_heads = from_heads.reshape(NZ // spans, spans, NEIGH, ROWS, DE)
     read_sum = jnp.sum(from_heads.astype(F32), axis=0).astype(BF16).reshape(reads, ROWS, DE)
 
     read_copies = jnp.broadcast_to(read_sum, (NX, *block))
-    read_x = lax.all_to_all(read_copies, "x", split_axis=0, concat_axis=0, tiled=True)
+    read_x = exchange(read_copies, "x")
     owners = (NY, ROWS, DE)
     mine, theirs = on_core(
         owner_kernel, "owner_sums",
@@ -245,7 +270,7 @@
     owner_part = (mine + swapped(theirs, "c", NC).astype(F32)).astype(BF16)
     owner_part, dq_pair = lax.optimization_barrier((owner_part, dq_pair))
     dq_back = swapped(dq_pair, "z", NZ)
-    from_y = lax.all_to_all(owner_part, "y", split_axis=0, concat_axis=0, tiled=True)
+    from_y = exchange(owner_part, "y")
     owned = jnp.sum(from_y.astype(F32), axis=0)
 
     first = jnp.where(span_at == 0, dq_own, dq_back)

time: 136 us -> 137 us (level)
  the two profiles are of different devices: /device:TPU:1 before, /device:TPU:2 now
where the time goes in v4:
time: 137 us; the launch traced here: 136 us
  starting transfers between devices  50.5 us (37%)
  waiting for transfers between devices  38.6 us (28%)
  blocking collectives  29.8 us (22%)
  Pallas kernels  10.4 us (8%)
  other arithmetic  4.02 us (3%)
  local copies, waits for them, and re-layouts  1.64 us (1%)
    all_to_all x2, blocking collectives, exchange(): lax.all_to_all(value, axes, split_axis=0, concat_axis=0, axis_index_group...  29.8 us
    all_to_all x4, waiting for transfers between devices, exchange(): lax.all_to_all(value, axes, split_axis=0, concat_axis=0, axis_index_group...  25 us
    all_to_all x4, starting transfers between devices, exchange(): lax.all_to_all(value, axes, split_axis=0, concat_axis=0, axis_index_group...  23.5 us
    ppermute x5, starting transfers between devices, swapped(): return lax.ppermute(value, axis, [(i, i ^ 1) for i in range(size)])  15.7 us
    ppermute x5, waiting for transfers between devices, swapped(): return lax.ppermute(value, axis, [(i, i ^ 1) for i in range(size)])  13.5 us
    ppermute x3, starting transfers between devices, shifted(): lax.ppermute(value, axis, [(i, (i + shift) % size) for i in range(size)])  11.4 us
    pallas_call x1, Pallas kernels, attention(): pl.pallas_call(attention_kernel, out_shape=(jax.ShapeDtypeStruct((NZ, NEI...  6.4 us
    pallas_call x3, Pallas kernels, on_core(): pl.pallas_call(kernel, out_shape=shapes, in_specs=[SMEM] * len(scalars) +...  4.01 us
  transfers between devices with their start and end apart: 12, of which 6 were waited for; matrix products, arithmetic and copies ran while one was open for 3% of the time, Pallas kernels for 2%

profile of v4, /device:TPU:2, one launch (start us, length us, event | category | flops | bytes accessed | tf_op | source)
XLA Modules:
  0.0 135.9 jit_solution(13720480921921218209)
XLA Ops:
  0.6 4.3 %collective-permute-start.4 = (bf16[2,896,512]{2,1,0:T(8,128)(2,1)}, bf16[2,896,512]{2,1,0:T(8,128)(2,1)}, u32[]{:S(2)}, u32[]{:S(2)}) collective-permute-start(bf16[2,896,512]{2,1,0:T(8,128)(2,1)} %w_own.1), channel_id=1, source_target_pairs={{0,1},{1,0},{2,3},{3,2},{4,5},{5,4},{6,7},{7,6},{8,9},{9,8},{10,11... | collective-permute-start | bytes 5505032 | tf_op jit(solution)/shard_map/ppermute | solution.py:56
  4.9 3.4 %collective-permute-start = (s32[2,2]{1,0:T(2,128)}, s32[2,2]{1,0:T(2,128)S(1)}, u32[]{:S(2)}, u32[]{:S(2)}) collective-permute-start(s32[2,2]{1,0:T(2,128)} %param.10), channel_id=1, source_target_pairs={{0,128},{128,256},{256,384},{384,0},{1,129},{129,257},{257,385},{3... | collective-permute-start | bytes 56 | tf_op jit(solution)/shard_map/ppermute | solution.py:52
  8.3 4.0 %collective-permute-start.2 = (s32[2,2]{1,0:T(2,128)}, s32[2,2]{1,0:T(2,128)S(1)}, u32[]{:S(2)}, u32[]{:S(2)}) collective-permute-start(s32[2,2]{1,0:T(2,128)} %param.10), channel_id=1, source_target_pairs={{0,384},{128,0},{256,128},{384,256},{1,385},{129,1},{257,129},{385... | collective-permute-start | bytes 56 | tf_op jit(solution)/shard_map/ppermute | solution.py:52
  12.3 4.0 %collective-permute-start.1 = (s32[2,2]{1,0:T(2,128)}, s32[2,2]{1,0:T(2,128)S(1)}, u32[]{:S(2)}, u32[]{:S(2)}) collective-permute-start(s32[2,2]{1,0:T(2,128)} %param.10), channel_id=1, source_target_pairs={{0,256},{128,384},{256,0},{384,128},{1,257},{129,385},{257,1},{385... | collective-permute-start | bytes 56 | tf_op jit(solution)/shard_map/ppermute | solution.py:52
  16.3 1.4 %broadcast_in_dim.7 = bf16[8,16,896]{2,1,0:T(8,128)(2,1)} broadcast(bf16[16,896]{1,0:T(8,128)(2,1)} %bitcast.29), dimensions={1,2} | broadcast | bytes 258048 | tf_op jit(solution)/shard_map/broadcast_in_dim | solution.py:222
  17.8 5.6 %all-to-all-start = ((bf16[8,16,896]{2,1,0:T(8,128)(2,1)}), bf16[8,16,896]{2,1,0:T(8,128)(2,1)S(1)}, u32[]{:S(2)}, u32[]{:S(2)}) async-start(bf16[8,16,896]{2,1,0:T(8,128)(2,1)} %broadcast_in_dim.7), calls=%async_computation | async-start | bytes 458752 | tf_op jit(solution)/shard_map/all_to_all | solution.py:37
  24.3 9.3 %all-to-all-done.mine_ref = bf16[8,16,896]{2,1,0:T(8,128)(2,1)S(1)} async-done(((bf16[8,16,896]{2,1,0:T(8,128)(2,1)}), bf16[8,16,896]{2,1,0:T(8,128)(2,1)S(1)}, u32[]{:S(2)}, u32[]{:S(2)}) %all-to-all-start) | async-done | bytes 229408 | tf_op jit(solution)/shard_map/all_to_all | solution.py:37
  33.5 1.9 %collective-permute-start.3 = (bf16[8,16,896]{2,1,0:T(8,128)(2,1)S(1)}, bf16[8,16,896]{2,1,0:T(8,128)(2,1)S(1)}, u32[]{:S(2)}, u32[]{:S(2)}) collective-permute-start(bf16[8,16,896]{2,1,0:T(8,128)(2,1)S(1)} %all-to-all-done.mine_ref), channel_id=1, source_target_pairs={{0,8},{8,0},{1,9},{9,1},{2,10},{10,2},{3,11},{11,3},{4,12},{12,4},... | collective-permute-start | bytes 688136 | tf_op jit(solution)/shard_map/ppermute | solution.py:56
  35.6 1.3 collective-permute-done.3.theirs_ref
  36.9 1.5 %pick.1 = bf16[4,4,16,896]{3,2,1,0:T(8,128)(2,1)} custom-call(s32[4,2,2]{2,1,0:T(2,128)S(1)} %pad_add_fusion.near_ref, s32[2]{0:T(128)S(1)} %pad_add_fusion.1.at_ref, bf16[8,16,896]{2,1,0:T(8,128)(2,1)S(1)} %all-to-all-done.mine_ref, bf16[8,16,896]{2,1,0:T(8,128)(2,1)S(1)} %collective-permute-done.3.theirs_ref), custom_call_target="tpu_custom_call" | custom-call | tf_op jit(solution)/shard_map/pick/pallas_call | solution.py:169
  38.5 5.0 %all-to-all-start.1 = ((bf16[4,4,16,896]{3,2,1,0:T(8,128)(2,1)}), bf16[4,4,16,896]{3,2,1,0:T(8,128)(2,1)S(1)}, u32[]{:S(2)}, u32[]{:S(2)}) async-start(bf16[4,4,16,896]{3,2,1,0:T(8,128)(2,1)} %pick.1), calls=%async_computation.1 | async-start | bytes 917504 | tf_op jit(solution)/shard_map/all_to_all | solution.py:37
  44.0 5.8 %all-to-all-done.1.from_ref = bf16[4,4,16,896]{3,2,1,0:T(8,128)(2,1)S(1)} async-done(((bf16[4,4,16,896]{3,2,1,0:T(8,128)(2,1)}), bf16[4,4,16,896]{3,2,1,0:T(8,128)(2,1)S(1)}, u32[]{:S(2)}, u32[]{:S(2)}) %all-to-all-start.1) | async-done | bytes 458784 | tf_op jit(solution)/shard_map/all_to_all | solution.py:37
  49.8 1.4 %spread.1 = bf16[8,2,16,896]{3,2,1,0:T(8,128)(2,1)} custom-call(s32[4,2,2]{2,1,0:T(2,128)S(1)} %pad_add_fusion.near_ref, s32[2]{0:T(128)S(1)} %pad_add_fusion.1.at_ref, bf16[4,4,16,896]{3,2,1,0:T(8,128)(2,1)S(1)} %all-to-all-done.1.from_ref), custom_call_target="tpu_custom_call" | custom-call | tf_op jit(solution)/shard_map/spread/pallas_call | solution.py:169
  51.3 9.4 %all-to-all-start.2 = ((bf16[8,2,16,896]{3,2,1,0:T(8,128)(2,1)}), bf16[8,2,16,896]{3,2,1,0:T(8,128)(2,1)S(1)}, u32[]{:S(2)}, u32[]{:S(2)}) async-start(bf16[8,2,16,896]{3,2,1,0:T(8,128)(2,1)} %spread.1), calls=%async_computation.2 | async-start | bytes 917504 | tf_op jit(solution)/shard_map/all_to_all | solution.py:37
  60.9 3.9 %collective-permute-start.5 = (bf16[128,512]{1,0:T(8,128)(2,1)S(1)}, bf16[128,512]{1,0:T(8,128)(2,1)S(1)}, u32[]{:S(2)}, u32[]{:S(2)}) collective-permute-start(bf16[128,512]{1,0:T(8,128)(2,1)S(1)} %pad_maximum_fusion), channel_id=1, source_target_pairs={{0,1},{1,0},{2,3},{3,2},{4,5},{5,4},{6,7},{7,6},{8,9},{9,8},{10,11... | collective-permute-start | bytes 393224 | tf_op jit(solution)/shard_map/ppermute | solution.py:56
  65.1 10.9 %collective-permute-done.5 = bf16[128,512]{1,0:T(8,128)(2,1)S(1)} collective-permute-done((bf16[128,512]{1,0:T(8,128)(2,1)S(1)}, bf16[128,512]{1,0:T(8,128)(2,1)S(1)}, u32[]{:S(2)}, u32[]{:S(2)}) %collective-permute-start.5) | collective-permute-done | bytes 131104 | tf_op jit(solution)/shard_map/ppermute | solution.py:56
  76.1 6.4 %attention.1 = (bf16[8,2,16,896]{3,2,1,0:T(8,128)(2,1)S(1)}, bf16[64,512]{1,0:T(8,128)(2,1)S(1)}, bf16[64,512]{1,0:T(8,128)(2,1)S(1)}) custom-call(bf16[8,2,16,896]{3,2,1,0:T(8,128)(2,1)S(1)} %all-to-all-done.2.tok, bf16[2,896,512]{2,1,0:T(8,128)(2,1)S(1)} %copy-done.1, bf16[64,512]{1,0:T(8,128)(2,1)S(1)} %get-tuple-element.44.q_own, ...), custom_call_target="tpu_custom_call" | custom-call | flops 2100000000 | bytes 6000000 | tf_op jit(solution)/shard_map/attention/pallas_call | solution.py:182
  82.5 17.4 %all_to_all.30 = bf16[8,2,16,896]{3,2,1,0:T(8,128)(2,1)S(1)} all-to-all(bf16[8,2,16,896]{3,2,1,0:T(8,128)(2,1)S(1)} %get-tuple-element.24), channel_id=1, replica_groups={{0,1,2,3,4,5,6,7},{14,15,12,13,10,11,8,9},{16,17,18,19,20,21,22,23},{30..., dimensions={0} | all-to-all | bytes 917504 | tf_op jit(solution)/shard_map/all_to_all | solution.py:37
  100.0 12.4 %all_to_all.31.from_ref = bf16[4,4,16,896]{3,2,1,0:T(8,128)(2,1)S(1)} all-to-all(bf16[4,4,16,896]{3,2,1,0:T(8,128)(2,1)S(1)} %broadcast_in_dim.8), channel_id=1, replica_groups={{0,128,256,384},{392,264,136,8},{1,129,257,385},{393,265,137,9},{2,130,..., dimensions={0} | all-to-all | bytes 917504 | tf_op jit(solution)/shard_map/all_to_all | solution.py:37
  113.5 2.0 %collective-permute-start.6 = (bf16[8,16,896]{2,1,0:T(8,128)(2,1)S(1)}, bf16[8,16,896]{2,1,0:T(8,128)(2,1)S(1)}, u32[]{:S(2)}, u32[]{:S(2)}) collective-permute-start(bf16[8,16,896]{2,1,0:T(8,128)(2,1)S(1)} %get-tuple-element.26), channel_id=1, source_target_pairs={{0,8},{8,0},{1,9},{9,1},{2,10},{10,2},{3,11},{11,3},{4,12},{12,4},... | collective-permute-start | bytes 688136 | tf_op jit(solution)/shard_map/ppermute | solution.py:56
  115.5 1.3 collective-permute-done.6
  117.6 3.5 %collective-permute-start.7 = (bf16[64,512]{1,0:T(8,128)(2,1)S(1)}, bf16[64,512]{1,0:T(8,128)(2,1)S(1)}, u32[]{:S(2)}, u32[]{:S(2)}) collective-permute-start(bf16[64,512]{1,0:T(8,128)(2,1)S(1)} %get-tuple-element.28), channel_id=1, source_target_pairs={{0,1},{1,0},{2,3},{3,2},{4,5},{5,4},{6,7},{7,6},{8,9},{9,8},{10,11... | collective-permute-start | bytes 196616 | tf_op jit(solution)/shard_map/ppermute | solution.py:56
  121.1 3.4 %all-to-all-start.5 = ((bf16[8,16,896]{2,1,0:T(8,128)(2,1)}), bf16[8,16,896]{2,1,0:T(8,128)(2,1)S(1)}, u32[]{:S(2)}, u32[]{:S(2)}) async-start(bf16[8,16,896]{2,1,0:T(8,128)(2,1)} %add_convert_fusion), calls=%async_computation.5 | async-start | bytes 458752 | tf_op jit(solution)/shard_map/all_to_all | solution.py:37
  125.3 10.0 %all-to-all-done.5 = bf16[8,16,896]{2,1,0:T(8,128)(2,1)S(1)} async-done(((bf16[8,16,896]{2,1,0:T(8,128)(2,1)}), bf16[8,16,896]{2,1,0:T(8,128)(2,1)S(1)}, u32[]{:S(2)}, u32[]{:S(2)}) %all-to-all-start.5) | async-done | bytes 229408 | tf_op jit(solution)/shard_map/all_to_all | solution.py:37
  (37 shorter events, 5.3 us)
Async XLA Ops:
  0.6 34.8 %copy-start = (s32[2,2]{1,0:T(2,128)S(1)}, s32[2,2]{1,0:T(2,128)}, u32[]{:S(2)}) copy-start(s32[2,2]{1,0:T(2,128)} %param.11) | copy-start | bytes 52
  0.6 50.6 %collective-permute-start.4 = (bf16[2,896,512]{2,1,0:T(8,128)(2,1)}, bf16[2,896,512]{2,1,0:T(8,128)(2,1)}, u32[]{:S(2)}, u32[]{:S(2)}) collective-permute-start(bf16[2,896,512]{2,1,0:T(8,128)(2,1)} %w_own.1), channel_id=1, source_target_pairs={{0,1},{1,0},{2,3},{3,2},{4,5},{5,4},{6,7},{7,6},{8,9},{9,8},{10,11... | collective-permute-start | bytes 5505032 | tf_op jit(solution)/shard_map/ppermute | solution.py:56
  4.9 18.6 %collective-permute-start = (s32[2,2]{1,0:T(2,128)}, s32[2,2]{1,0:T(2,128)S(1)}, u32[]{:S(2)}, u32[]{:S(2)}) collective-permute-start(s32[2,2]{1,0:T(2,128)} %param.10), channel_id=1, source_target_pairs={{0,128},{128,256},{256,384},{384,0},{1,129},{129,257},{257,385},{3... | collective-permute-start | bytes 56 | tf_op jit(solution)/shard_map/ppermute | solution.py:52
  8.3 15.2 %collective-permute-start.2 = (s32[2,2]{1,0:T(2,128)}, s32[2,2]{1,0:T(2,128)S(1)}, u32[]{:S(2)}, u32[]{:S(2)}) collective-permute-start(s32[2,2]{1,0:T(2,128)} %param.10), channel_id=1, source_target_pairs={{0,384},{128,0},{256,128},{384,256},{1,385},{129,1},{257,129},{385... | collective-permute-start | bytes 56 | tf_op jit(solution)/shard_map/ppermute | solution.py:52
  12.3 11.2 %collective-permute-start.1 = (s32[2,2]{1,0:T(2,128)}, s32[2,2]{1,0:T(2,128)S(1)}, u32[]{:S(2)}, u32[]{:S(2)}) collective-permute-start(s32[2,2]{1,0:T(2,128)} %param.10), channel_id=1, source_target_pairs={{0,256},{128,384},{256,0},{384,128},{1,257},{129,385},{257,1},{385... | collective-permute-start | bytes 56 | tf_op jit(solution)/shard_map/ppermute | solution.py:52
  17.8 15.8 %all-to-all-start = ((bf16[8,16,896]{2,1,0:T(8,128)(2,1)}), bf16[8,16,896]{2,1,0:T(8,128)(2,1)S(1)}, u32[]{:S(2)}, u32[]{:S(2)}) async-start(bf16[8,16,896]{2,1,0:T(8,128)(2,1)} %broadcast_in_dim.7), calls=%async_computation | async-start | bytes 458752 | tf_op jit(solution)/shard_map/all_to_all | solution.py:37
  33.5 3.4 %collective-permute-start.3 = (bf16[8,16,896]{2,1,0:T(8,128)(2,1)S(1)}, bf16[8,16,896]{2,1,0:T(8,128)(2,1)S(1)}, u32[]{:S(2)}, u32[]{:S(2)}) collective-permute-start(bf16[8,16,896]{2,1,0:T(8,128)(2,1)S(1)} %all-to-all-done.mine_ref), channel_id=1, source_target_pairs={{0,8},{8,0},{1,9},{9,1},{2,10},{10,2},{3,11},{11,3},{4,12},{12,4},... | collective-permute-start | bytes 688136 | tf_op jit(solution)/shard_map/ppermute | solution.py:56
  38.4 22.4 %copy-start.2 = (bf16[128,512]{1,0:T(8,128)(2,1)S(1)}, bf16[128,512]{1,0:T(8,128)(2,1)}, u32[]{:S(2)}) copy-start(bf16[128,512]{1,0:T(8,128)(2,1)} %param.7) | copy-start | bytes 393220
  38.5 22.4 %copy-start.3 = (bf16[128,512]{1,0:T(8,128)(2,1)S(1)}, bf16[128,512]{1,0:T(8,128)(2,1)}, u32[]{:S(2)}) copy-start(bf16[128,512]{1,0:T(8,128)(2,1)} %param.6) | copy-start | bytes 393220
  38.5 11.4 %all-to-all-start.1 = ((bf16[4,4,16,896]{3,2,1,0:T(8,128)(2,1)}), bf16[4,4,16,896]{3,2,1,0:T(8,128)(2,1)S(1)}, u32[]{:S(2)}, u32[]{:S(2)}) async-start(bf16[4,4,16,896]{3,2,1,0:T(8,128)(2,1)} %pick.1), calls=%async_computation.1 | async-start | bytes 917504 | tf_op jit(solution)/shard_map/all_to_all | solution.py:37
  44.0 32.1 %copy-start.1 = (bf16[2,896,512]{2,1,0:T(8,128)(2,1)S(1)}, bf16[2,896,512]{2,1,0:T(8,128)(2,1)}, u32[]{:S(2)}) copy-start(bf16[2,896,512]{2,1,0:T(8,128)(2,1)} %w_own.1) | copy-start | bytes 5505028
  51.3 24.8 %all-to-all-start.2 = ((bf16[8,2,16,896]{3,2,1,0:T(8,128)(2,1)}), bf16[8,2,16,896]{3,2,1,0:T(8,128)(2,1)S(1)}, u32[]{:S(2)}, u32[]{:S(2)}) async-start(bf16[8,2,16,896]{3,2,1,0:T(8,128)(2,1)} %spread.1), calls=%async_computation.2 | async-start | bytes 917504 | tf_op jit(solution)/shard_map/all_to_all | solution.py:37
  60.9 15.1 %collective-permute-start.5 = (bf16[128,512]{1,0:T(8,128)(2,1)S(1)}, bf16[128,512]{1,0:T(8,128)(2,1)S(1)}, u32[]{:S(2)}, u32[]{:S(2)}) collective-permute-start(bf16[128,512]{1,0:T(8,128)(2,1)S(1)} %pad_maximum_fusion), channel_id=1, source_target_pairs={{0,1},{1,0},{2,3},{3,2},{4,5},{5,4},{6,7},{7,6},{8,9},{9,8},{10,11... | collective-permute-start | bytes 393224 | tf_op jit(solution)/shard_map/ppermute | solution.py:56
  113.5 3.4 %collective-permute-start.6 = (bf16[8,16,896]{2,1,0:T(8,128)(2,1)S(1)}, bf16[8,16,896]{2,1,0:T(8,128)(2,1)S(1)}, u32[]{:S(2)}, u32[]{:S(2)}) collective-permute-start(bf16[8,16,896]{2,1,0:T(8,128)(2,1)S(1)} %get-tuple-element.26), channel_id=1, source_target_pairs={{0,8},{8,0},{1,9},{9,1},{2,10},{10,2},{3,11},{11,3},{4,12},{12,4},... | collective-permute-start | bytes 688136 | tf_op jit(solution)/shard_map/ppermute | solution.py:56
  117.6 7.0 %collective-permute-start.7 = (bf16[64,512]{1,0:T(8,128)(2,1)S(1)}, bf16[64,512]{1,0:T(8,128)(2,1)S(1)}, u32[]{:S(2)}, u32[]{:S(2)}) collective-permute-start(bf16[64,512]{1,0:T(8,128)(2,1)S(1)} %get-tuple-element.28), channel_id=1, source_target_pairs={{0,1},{1,0},{2,3},{3,2},{4,5},{5,4},{6,7},{7,6},{8,9},{9,8},{10,11... | collective-permute-start | bytes 196616 | tf_op jit(solution)/shard_map/ppermute | solution.py:56
  121.1 14.1 %all-to-all-start.5 = ((bf16[8,16,896]{2,1,0:T(8,128)(2,1)}), bf16[8,16,896]{2,1,0:T(8,128)(2,1)S(1)}, u32[]{:S(2)}, u32[]{:S(2)}) async-start(bf16[8,16,896]{2,1,0:T(8,128)(2,1)} %add_convert_fusion), calls=%async_computation.5 | async-start | bytes 458752 | tf_op jit(solution)/shard_map/all_to_all | solution.py:37

commit v5 on v3

--- a/solution.py
+++ b/solution.py
@@ -29,8 +29,8 @@
     return jnp.concatenate([cosine, cosine], axis=-1), jnp.concatenate([-sine, sine], axis=-1)
 
 
-def shifted(value, axis, size, shift):
-    return lax.ppermute(value, axis, [(i, (i + shift) % size) for i in range(size)])
+def exchange(value, axis):
+    return lax.all_to_all(value, axis, split_axis=0, concat_axis=0, tiled=True)
 
 
 def swapped(value, axis, size):
@@ -43,57 +43,55 @@
     )
 
 
-def near_id(near_ref, at_ref, column, read):
-    return near_ref[lax.rem(at_ref[0] - column + NX, NX), read // NEIGH, read % NEIGH]
-
-
-def pick_kernel(near_ref, at_ref, mine_ref, theirs_ref, out_ref, sems):
-    core, reads = at_ref[1], out_ref.shape[1]
-    for column in range(NX):
-        for read in range(reads):
-            block = near_id(near_ref, at_ref, column, read)
-            row, same = lax.rem(block // NC, NY), lax.rem(block, NC) == core
-            sem = sems.at[column * reads + read]
-
-            @pl.when(same)
+def seat(block):
+    return lax.div(block, NC)
+
+
+def pick_kernel(ids_ref, from_ref, out_ref, sems):
+    copies = []
+    for read in range(out_ref.shape[0]):
+        block = ids_ref[1, read // NEIGH, read % NEIGH]
+        copies.append(
+            pltpu.make_async_copy(from_ref.at[seat(block)], out_ref.at[read], sems.at[read])
+        )
+        copies[-1].start()
+    for copy in copies:
+        copy.wait()
+
+
+def spread_kernel(ids_ref, core_ref, mine_ref, theirs_ref, out_ref, sems):
+    reads = theirs_ref.shape[0]
+    spans = reads // NEIGH
+    places = [(read, at) for read in range(reads) for at in range(read // NEIGH, NZ, spans)]
+    for count, (read, at) in enumerate(places):
+        block = ids_ref[0, read // NEIGH, read % NEIGH]
+        target, same = out_ref.at[at, read % NEIGH], lax.rem(block, NC) == core_ref[0]
+
+        @pl.when(same)
+        def _():
+            pltpu.make_async_copy(mine_ref.at[seat(block)], target, sems.at[count]).start()
+
+        @pl.when(jnp.logical_not(same))
+        def _():
+            pltpu.make_async_copy(theirs_ref.at[read], target, sems.at[count]).start()
+
+    for count, (read, at) in enumerate(places):
+        target = out_ref.at[at, read % NEIGH]
+        pltpu.make_async_copy(theirs_ref.at[read], target, sems.at[count]).wait()
+
+
+def owner_kernel(ids_ref, core_ref, mine_ref, theirs_ref, out_ref, total):
+    total[...] = jnp.zeros_like(total)
+    for side, reads_ref in enumerate((mine_ref, theirs_ref)):
+        for read in range(reads_ref.shape[0]):
+            block = ids_ref[side, read // NEIGH, read % NEIGH]
+
+            @pl.when(lax.rem(block, NC) == core_ref[0])
             def _():
-                pltpu.make_async_copy(mine_ref.at[row], out_ref.at[column, read], sem).start()
-
-            @pl.when(jnp.logical_not(same))
-            def _():
-                pltpu.make_async_copy(theirs_ref.at[row], out_ref.at[column, read], sem).start()
-
-    for column in range(NX):
-        for read in range(reads):
-            sem = sems.at[column * reads + read]
-            pltpu.make_async_copy(mine_ref.at[0], out_ref.at[column, read], sem).wait()
-
-
-def spread_kernel(near_ref, at_ref, from_ref, out_ref):
-    reads = from_ref.shape[1]
-    spans = reads // NEIGH
-    for read in range(reads):
-        owner = near_ref[0, read // NEIGH, read % NEIGH]
-        block = from_ref[owner // (NY * NC), read]
-        for at in range(read // NEIGH, NZ, spans):
-            out_ref[at, read % NEIGH] = block
-
-
-def owner_kernel(near_ref, at_ref, from_ref, mine_ref, theirs_ref, total):
-    total[...] = jnp.zeros_like(total)
-    here, core = at_ref[0], at_ref[1]
-    for column in range(NX):
-        for read in range(from_ref.shape[1]):
-            block = near_id(near_ref, at_ref, column, read)
-
-            @pl.when(block // (NY * NC) == here)
-            def _():
-                side = jnp.where(lax.rem(block, NC) == core, 0, NY)
-                at = side + lax.rem(block // NC, NY)
-                total[at] = total[at] + from_ref[column, read].astype(F32)
-
-    mine_ref[...] = total[:NY]
-    theirs_ref[...] = total[NY:].astype(BF16)
+                at = seat(block)
+                total[at] = total[at] + reads_ref[read].astype(F32)
+
+    out_ref[...] = total[...].astype(BF16)
 
 
 def attention_kernel(
@@ -182,7 +180,7 @@
 
 
 def local(queries, out_grad, encodings, kv_weight, neighbour_ids, rot_offset):
-    x_at, c_at, z_at = lax.axis_index("x"), lax.axis_index("c"), lax.axis_index("z")
+    c_at, z_at = lax.axis_index("c"), lax.axis_index("z")
     spans = neighbour_ids.shape[0]
     reads = spans * NEIGH
     span_at = z_at % 2
@@ -204,49 +202,41 @@
     key_cos, key_sin = rotary_tables(positions.reshape(NEIGH * NLEN))
     query_cos, query_sin = rotary_tables(jnp.arange(SPAN, dtype=jnp.int32))
 
-    at = jnp.stack([x_at, c_at])
-    near = [neighbour_ids] + [shifted(neighbour_ids, "x", NX, s) for s in range(1, NX)]
-    near = jnp.stack(near)
-    copies = jnp.broadcast_to(encodings, (NY, ROWS, DE))
-    over_y = lax.all_to_all(copies, "y", split_axis=0, concat_axis=0, tiled=True)
-    over_y, near, other = lax.optimization_barrier((over_y, near, other))
-    beside = swapped(over_y, "c", NC)
-    block = (reads, ROWS, DE)
+    core = c_at.reshape(1)
+    ids = jnp.stack([neighbour_ids, swapped(neighbour_ids, "c", NC)])
+    copies = jnp.broadcast_to(encodings, (NX * NY, ROWS, DE))
+    blocks = exchange(copies, ("x", "y"))
     asked = on_core(
-        pick_kernel, "pick", jax.ShapeDtypeStruct((NX, *block), BF16), (near, at),
-        over_y, beside, scratch=[pltpu.SemaphoreType.DMA((NX * reads,))], space=ANY,
-    )
-    found = lax.all_to_all(asked, "x", split_axis=0, concat_axis=0, tiled=True)
+        pick_kernel, "pick", jax.ShapeDtypeStruct((reads, ROWS, DE), BF16), (ids,),
+        blocks, scratch=[pltpu.SemaphoreType.DMA((reads,))], space=ANY,
+    )
+    arrived = swapped(asked, "c", NC)
 
     to_z = on_core(
-        spread_kernel, "spread", jax.ShapeDtypeStruct((NZ, NEIGH, ROWS, DE), BF16), (near, at),
-        found,
+        spread_kernel, "spread", jax.ShapeDtypeStruct((NZ, NEIGH, ROWS, DE), BF16), (ids, core),
+        blocks, arrived, scratch=[pltpu.SemaphoreType.DMA((NZ * NEIGH,))], space=ANY,
     )
     to_z, w_far = lax.optimization_barrier((to_z, w_far))
-    tok = lax.all_to_all(to_z, "z", split_axis=0, concat_axis=0, tiled=True)
+    tok = exchange(to_z, "z")
     from_pair = swapped(other, "z", NZ)
     part, dq_own, dq_pair = attention(
         tok, kv_weight, q_own, g_own, from_pair[:SPAN], from_pair[SPAN:],
         key_cos, key_sin, query_cos, query_sin, w_far,
     )
 
-    from_heads = lax.all_to_all(part, "z", split_axis=0, concat_axis=0, tiled=True)
+    from_heads = exchange(part, "z")
     from_heads = from_heads.reshape(NZ // spans, spans, NEIGH, ROWS, DE)
     read_sum = jnp.sum(from_heads.astype(F32), axis=0).astype(BF16).reshape(reads, ROWS, DE)
 
-    read_copies = jnp.broadcast_to(read_sum, (NX, *block))
-    read_x = lax.all_to_all(read_copies, "x", split_axis=0, concat_axis=0, tiled=True)
-    owners = (NY, ROWS, DE)
-    mine, theirs = on_core(
-        owner_kernel, "owner_sums",
-        (jax.ShapeDtypeStruct(owners, F32), jax.ShapeDtypeStruct(owners, BF16)),
-        (near, at), read_x, scratch=[pltpu.VMEM((NC * NY, ROWS, DE), F32)],
-    )
-    owner_part = (mine + swapped(theirs, "c", NC).astype(F32)).astype(BF16)
+    theirs = swapped(read_sum, "c", NC)
+    owners = (NX * NY, ROWS, DE)
+    owner_part = on_core(
+        owner_kernel, "owner_sums", jax.ShapeDtypeStruct(owners, BF16), (ids, core),
+        read_sum, theirs, scratch=[pltpu.VMEM(owners, F32)],
+    )
     owner_part, dq_pair = lax.optimization_barrier((owner_part, dq_pair))
     dq_back = swapped(dq_pair, "z", NZ)
-    from_y = lax.all_to_all(owner_part, "y", split_axis=0, concat_axis=0, tiled=True)
-    owned = jnp.sum(from_y.astype(F32), axis=0)
+    owned = jnp.sum(exchange(owner_part, ("x", "y")).astype(F32), axis=0)
 
     first = jnp.where(span_at == 0, dq_own, dq_back)
     second = jnp.where(span_at == 0, dq_back, dq_own)

time: 136 us -> 145 us (1.066)
  the two profiles are of different devices: /device:TPU:1 before, /device:TPU:8 now
where the time goes in v5:
time: 145 us; the launch traced here: 144 us
  waiting for transfers between devices  69.4 us (48%)
  starting transfers between devices  43.8 us (30%)
  blocking collectives  15.3 us (11%)
  Pallas kernels  10.5 us (7%)
  other arithmetic  2.55 us (2%)
  local copies, waits for them, and re-layouts  1.97 us (1%)
    all_to_all x3, waiting for transfers between devices, exchange(): return lax.all_to_all(value, axis, split_axis=0, concat_axis=0, tiled=True)  49.2 us
    all_to_all x3, starting transfers between devices, exchange(): return lax.all_to_all(value, axis, split_axis=0, concat_axis=0, tiled=True)  29.6 us
    ppermute x6, waiting for transfers between devices, swapped(): return lax.ppermute(value, axis, [(i, i ^ 1) for i in range(size)])  20.2 us
    all_to_all x1, blocking collectives, exchange(): return lax.all_to_all(value, axis, split_axis=0, concat_axis=0, tiled=True)  15.3 us
    ppermute x6, starting transfers between devices, swapped(): return lax.ppermute(value, axis, [(i, i ^ 1) for i in range(size)])  14.2 us
    pallas_call x1, Pallas kernels, attention(): pl.pallas_call(attention_kernel, out_shape=(jax.ShapeDtypeStruct((NZ, NEI...  6.41 us
    pallas_call x3, Pallas kernels, on_core(): pl.pallas_call(kernel, out_shape=shapes, in_specs=[SMEM] * len(scalars) +...  4.08 us
  transfers between devices with their start and end apart: 9, of which 7 were waited for; matrix products, arithmetic and copies ran while one was open for 1% of the time, Pallas kernels for 2%

profile of v5, /device:TPU:8, one launch (start us, length us, event | category | flops | bytes accessed | tf_op | source)
XLA Modules:
  0.0 144.4 jit_solution(17984947264661403628)
XLA Ops:
  0.7 1.9 %broadcast_in_dim.5 = bf16[32,16,896]{2,1,0:T(8,128)(2,1)} broadcast(bf16[16,896]{1,0:T(8,128)(2,1)} %bitcast.27), dimensions={1,2} | broadcast | bytes 946176 | tf_op jit(solution)/shard_map/broadcast_in_dim | solution.py:207
  2.6 10.2 %all-to-all-start = ((bf16[32,16,896]{2,1,0:T(8,128)(2,1)}), bf16[32,16,896]{2,1,0:T(8,128)(2,1)S(1)}, u32[]{:S(2)}, u32[]{:S(2)}) async-start(bf16[32,16,896]{2,1,0:T(8,128)(2,1)} %broadcast_in_dim.5), calls=%async_computation | async-start | bytes 1835008 | tf_op jit(solution)/shard_map/all_to_all | solution.py:33
  12.8 4.3 %collective-permute-start.2 = (bf16[2,896,512]{2,1,0:T(8,128)(2,1)S(1)}, bf16[2,896,512]{2,1,0:T(8,128)(2,1)}, u32[]{:S(2)}, u32[]{:S(2)}) collective-permute-start(bf16[2,896,512]{2,1,0:T(8,128)(2,1)S(1)} %copy-done.1), channel_id=1, source_target_pairs={{0,1},{1,0},{2,3},{3,2},{4,5},{5,4},{6,7},{7,6},{8,9},{9,8},{10,11... | collective-permute-start | bytes 5505032 | tf_op jit(solution)/shard_map/ppermute | solution.py:37
  17.1 1.9 %collective-permute-start = (s32[2,2]{1,0:T(2,128)S(1)}, s32[2,2]{1,0:T(2,128)S(1)}, u32[]{:S(2)}, u32[]{:S(2)}) collective-permute-start(s32[2,2]{1,0:T(2,128)S(1)} %copy-done.4), channel_id=1, source_target_pairs={{0,8},{8,0},{1,9},{9,1},{2,10},{10,2},{3,11},{11,3},{4,12},{12,4},... | collective-permute-start | bytes 56 | tf_op jit(solution)/shard_map/ppermute | solution.py:37
  19.1 1.9 %collective-permute-start.3 = (bf16[128,512]{1,0:T(8,128)(2,1)S(1)}, bf16[128,512]{1,0:T(8,128)(2,1)S(1)}, u32[]{:S(2)}, u32[]{:S(2)}) collective-permute-start(bf16[128,512]{1,0:T(8,128)(2,1)S(1)} %pad_maximum_fusion), channel_id=1, source_target_pairs={{0,1},{1,0},{2,3},{3,2},{4,5},{5,4},{6,7},{7,6},{8,9},{9,8},{10,11... | collective-permute-start | bytes 393224 | tf_op jit(solution)/shard_map/ppermute | solution.py:37
  21.1 17.5 %all-to-all-done.from_ref.mine_ref = bf16[32,16,896]{2,1,0:T(8,128)(2,1)S(1)} async-done(((bf16[32,16,896]{2,1,0:T(8,128)(2,1)}), bf16[32,16,896]{2,1,0:T(8,128)(2,1)S(1)}, u32[]{:S(2)}, u32[]{:S(2)}) %all-to-all-start) | async-done | bytes 917536 | tf_op jit(solution)/shard_map/all_to_all | solution.py:33
  38.6 0.8 pick.1
  39.4 1.9 %collective-permute-start.1 = (bf16[4,16,896]{2,1,0:T(8,128)(2,1)S(1)}, bf16[4,16,896]{2,1,0:T(8,128)(2,1)S(1)}, u32[]{:S(2)}, u32[]{:S(2)}) collective-permute-start(bf16[4,16,896]{2,1,0:T(8,128)(2,1)S(1)} %pick.1), channel_id=1, source_target_pairs={{0,8},{8,0},{1,9},{9,1},{2,10},{10,2},{3,11},{11,3},{4,12},{12,4},... | collective-permute-start | bytes 344072 | tf_op jit(solution)/shard_map/ppermute | solution.py:37
  41.6 1.1 collective-permute-done.1.theirs_ref
  42.6 1.5 %spread.1 = bf16[8,2,16,896]{3,2,1,0:T(8,128)(2,1)} custom-call(s32[2,2,2]{2,1,0:T(2,128)S(1)} %pad_add_fusion.ids_ref, s32[1]{0:T(128)} %bitcast.2.core_ref, bf16[32,16,896]{2,1,0:T(8,128)(2,1)S(1)} %all-to-all-done.from_ref.mine_ref, bf16[4,16,896]{2,1,0:T(8,128)(2,1)S(1)} %collective-permute-done.1.theirs_ref), custom_call_target="tpu_custom_call" | custom-call | tf_op jit(solution)/shard_map/spread/pallas_call | solution.py:146
  44.1 13.9 %collective-permute-done.2.w_far = bf16[2,896,512]{2,1,0:T(8,128)(2,1)} collective-permute-done((bf16[2,896,512]{2,1,0:T(8,128)(2,1)S(1)}, bf16[2,896,512]{2,1,0:T(8,128)(2,1)}, u32[]{:S(2)}, u32[]{:S(2)}) %collective-permute-start.2) | collective-permute-done | bytes 1835040 | tf_op jit(solution)/shard_map/ppermute | solution.py:37
  58.0 9.7 %all-to-all-start.1 = ((bf16[8,2,16,896]{3,2,1,0:T(8,128)(2,1)}), bf16[8,2,16,896]{3,2,1,0:T(8,128)(2,1)S(1)}, u32[]{:S(2)}, u32[]{:S(2)}) async-start(bf16[8,2,16,896]{3,2,1,0:T(8,128)(2,1)} %spread.1), calls=%async_computation.1 | async-start | bytes 917504 | tf_op jit(solution)/shard_map/all_to_all | solution.py:33
  68.6 12.3 %all-to-all-done.1.tok = bf16[8,2,16,896]{3,2,1,0:T(8,128)(2,1)S(1)} async-done(((bf16[8,2,16,896]{3,2,1,0:T(8,128)(2,1)}), bf16[8,2,16,896]{3,2,1,0:T(8,128)(2,1)S(1)}, u32[]{:S(2)}, u32[]{:S(2)}) %all-to-all-start.1) | async-done | bytes 458784 | tf_op jit(solution)/shard_map/all_to_all | solution.py:33
  80.9 6.4 %attention.1 = (bf16[8,2,16,896]{3,2,1,0:T(8,128)(2,1)S(1)}, bf16[64,512]{1,0:T(8,128)(2,1)S(1)}, bf16[64,512]{1,0:T(8,128)(2,1)S(1)}) custom-call(bf16[8,2,16,896]{3,2,1,0:T(8,128)(2,1)S(1)} %all-to-all-done.1.tok, bf16[2,896,512]{2,1,0:T(8,128)(2,1)S(1)} %copy-done.1, bf16[64,512]{1,0:T(8,128)(2,1)S(1)} %get-tuple-element.30.q_own, ...), custom_call_target="tpu_custom_call" | custom-call | flops 2100000000 | bytes 6000000 | tf_op jit(solution)/shard_map/attention/pallas_call | solution.py:159
  87.3 15.3 %all_to_all.20 = bf16[8,2,16,896]{3,2,1,0:T(8,128)(2,1)S(1)} all-to-all(bf16[8,2,16,896]{3,2,1,0:T(8,128)(2,1)S(1)} %get-tuple-element.12), channel_id=1, replica_groups=mesh['x'=4,'y'=8,'c'=2,'z'=8] {'z'}, dimensions={0} | all-to-all | bytes 917504 | tf_op jit(solution)/shard_map/all_to_all | solution.py:33
  102.6 1.9 %collective-permute-start.4 = (bf16[4,16,896]{2,1,0:T(8,128)(2,1)S(1)}, bf16[4,16,896]{2,1,0:T(8,128)(2,1)S(1)}, u32[]{:S(2)}, u32[]{:S(2)}) collective-permute-start(bf16[4,16,896]{2,1,0:T(8,128)(2,1)S(1)} %bitcast.21), channel_id=1, source_target_pairs={{0,8},{8,0},{1,9},{9,1},{2,10},{10,2},{3,11},{11,3},{4,12},{12,4},... | collective-permute-start | bytes 344072 | tf_op jit(solution)/shard_map/ppermute | solution.py:37
  104.6 1.3 collective-permute-done.4.theirs_ref
  105.8 1.8 %owner_sums.1 = bf16[32,16,896]{2,1,0:T(8,128)(2,1)} custom-call(s32[2,2,2]{2,1,0:T(2,128)S(1)} %pad_add_fusion.ids_ref, s32[1]{0:T(128)} %bitcast.2.core_ref, bf16[4,16,896]{2,1,0:T(8,128)(2,1)S(1)} %bitcast.22, bf16[4,16,896]{2,1,0:T(8,128)(2,1)S(1)} %collective-permute-done.4.theirs_ref), custom_call_target="tpu_custom_call" | custom-call | tf_op jit(solution)/shard_map/owner_sums/pallas_call | solution.py:146
  107.7 9.8 %all-to-all-start.3 = ((bf16[32,16,896]{2,1,0:T(8,128)(2,1)}), bf16[32,16,896]{2,1,0:T(8,128)(2,1)S(1)}, u32[]{:S(2)}, u32[]{:S(2)}) async-start(bf16[32,16,896]{2,1,0:T(8,128)(2,1)} %owner_sums.1), calls=%async_computation.3 | async-start | bytes 1835008 | tf_op jit(solution)/shard_map/all_to_all | solution.py:33
  117.4 2.2 %collective-permute-start.5 = (bf16[64,512]{1,0:T(8,128)(2,1)S(1)}, bf16[64,512]{1,0:T(8,128)(2,1)S(1)}, u32[]{:S(2)}, u32[]{:S(2)}) collective-permute-start(bf16[64,512]{1,0:T(8,128)(2,1)S(1)} %get-tuple-element.14), channel_id=1, source_target_pairs={{0,1},{1,0},{2,3},{3,2},{4,5},{5,4},{6,7},{7,6},{8,9},{9,8},{10,11... | collective-permute-start | bytes 196616 | tf_op jit(solution)/shard_map/ppermute | solution.py:37
  119.7 3.9 %collective-permute-done.5 = bf16[64,512]{1,0:T(8,128)(2,1)S(1)} collective-permute-done((bf16[64,512]{1,0:T(8,128)(2,1)S(1)}, bf16[64,512]{1,0:T(8,128)(2,1)S(1)}, u32[]{:S(2)}, u32[]{:S(2)}) %collective-permute-start.5) | collective-permute-done | bytes 65568 | tf_op jit(solution)/shard_map/ppermute | solution.py:37
  123.6 0.7 pad_maximum_fusion.3
  124.3 19.3 %all-to-all-done.3 = bf16[32,16,896]{2,1,0:T(8,128)(2,1)S(1)} async-done(((bf16[32,16,896]{2,1,0:T(8,128)(2,1)}), bf16[32,16,896]{2,1,0:T(8,128)(2,1)S(1)}, u32[]{:S(2)}, u32[]{:S(2)}) %all-to-all-start.3) | async-done | bytes 917536 | tf_op jit(solution)/shard_map/all_to_all | solution.py:33
  143.6 0.8 convert_reduce_fusion
  (26 shorter events, 1.2 us)
Async XLA Ops:
  0.6 40.9 %copy-start = (s32[2,2]{1,0:T(2,128)S(1)}, s32[2,2]{1,0:T(2,128)}, u32[]{:S(2)}) copy-start(s32[2,2]{1,0:T(2,128)} %param.11) | copy-start | bytes 52
  0.6 12.1 %copy-start.1 = (bf16[2,896,512]{2,1,0:T(8,128)(2,1)S(1)}, bf16[2,896,512]{2,1,0:T(8,128)(2,1)}, u32[]{:S(2)}) copy-start(bf16[2,896,512]{2,1,0:T(8,128)(2,1)} %w_own.1) | copy-start | bytes 5505028
  0.7 16.4 %copy-start.4 = (s32[2,2]{1,0:T(2,128)S(1)}, s32[2,2]{1,0:T(2,128)}, u32[]{:S(2)}) copy-start(s32[2,2]{1,0:T(2,128)} %param.10) | copy-start | bytes 52
  0.7 18.3 %copy-start.2 = (bf16[128,512]{1,0:T(8,128)(2,1)S(1)}, bf16[128,512]{1,0:T(8,128)(2,1)}, u32[]{:S(2)}) copy-start(bf16[128,512]{1,0:T(8,128)(2,1)} %param.7) | copy-start | bytes 393220
  0.7 18.3 %copy-start.3 = (bf16[128,512]{1,0:T(8,128)(2,1)S(1)}, bf16[128,512]{1,0:T(8,128)(2,1)}, u32[]{:S(2)}) copy-start(bf16[128,512]{1,0:T(8,128)(2,1)} %param.6) | copy-start | bytes 393220
  2.6 36.0 %all-to-all-start = ((bf16[32,16,896]{2,1,0:T(8,128)(2,1)}), bf16[32,16,896]{2,1,0:T(8,128)(2,1)S(1)}, u32[]{:S(2)}, u32[]{:S(2)}) async-start(bf16[32,16,896]{2,1,0:T(8,128)(2,1)} %broadcast_in_dim.5), calls=%async_computation | async-start | bytes 1835008 | tf_op jit(solution)/shard_map/all_to_all | solution.py:33
  12.8 45.2 %collective-permute-start.2 = (bf16[2,896,512]{2,1,0:T(8,128)(2,1)S(1)}, bf16[2,896,512]{2,1,0:T(8,128)(2,1)}, u32[]{:S(2)}, u32[]{:S(2)}) collective-permute-start(bf16[2,896,512]{2,1,0:T(8,128)(2,1)S(1)} %copy-done.1), channel_id=1, source_target_pairs={{0,1},{1,0},{2,3},{3,2},{4,5},{5,4},{6,7},{7,6},{8,9},{9,8},{10,11... | collective-permute-start | bytes 5505032 | tf_op jit(solution)/shard_map/ppermute | solution.py:37
  17.1 4.0 %collective-permute-start = (s32[2,2]{1,0:T(2,128)S(1)}, s32[2,2]{1,0:T(2,128)S(1)}, u32[]{:S(2)}, u32[]{:S(2)}) collective-permute-start(s32[2,2]{1,0:T(2,128)S(1)} %copy-done.4), channel_id=1, source_target_pairs={{0,8},{8,0},{1,9},{9,1},{2,10},{10,2},{3,11},{11,3},{4,12},{12,4},... | collective-permute-start | bytes 56 | tf_op jit(solution)/shard_map/ppermute | solution.py:37
  19.1 49.4 %collective-permute-start.3 = (bf16[128,512]{1,0:T(8,128)(2,1)S(1)}, bf16[128,512]{1,0:T(8,128)(2,1)S(1)}, u32[]{:S(2)}, u32[]{:S(2)}) collective-permute-start(bf16[128,512]{1,0:T(8,128)(2,1)S(1)} %pad_maximum_fusion), channel_id=1, source_target_pairs={{0,1},{1,0},{2,3},{3,2},{4,5},{5,4},{6,7},{7,6},{8,9},{9,8},{10,11... | collective-permute-start | bytes 393224 | tf_op jit(solution)/shard_map/ppermute | solution.py:37
  39.4 3.2 %collective-permute-start.1 = (bf16[4,16,896]{2,1,0:T(8,128)(2,1)S(1)}, bf16[4,16,896]{2,1,0:T(8,128)(2,1)S(1)}, u32[]{:S(2)}, u32[]{:S(2)}) collective-permute-start(bf16[4,16,896]{2,1,0:T(8,128)(2,1)S(1)} %pick.1), channel_id=1, source_target_pairs={{0,8},{8,0},{1,9},{9,1},{2,10},{10,2},{3,11},{11,3},{4,12},{12,4},... | collective-permute-start | bytes 344072 | tf_op jit(solution)/shard_map/ppermute | solution.py:37
  58.0 22.9 %all-to-all-start.1 = ((bf16[8,2,16,896]{3,2,1,0:T(8,128)(2,1)}), bf16[8,2,16,896]{3,2,1,0:T(8,128)(2,1)S(1)}, u32[]{:S(2)}, u32[]{:S(2)}) async-start(bf16[8,2,16,896]{3,2,1,0:T(8,128)(2,1)} %spread.1), calls=%async_computation.1 | async-start | bytes 917504 | tf_op jit(solution)/shard_map/all_to_all | solution.py:33
  102.6 3.2 %collective-permute-start.4 = (bf16[4,16,896]{2,1,0:T(8,128)(2,1)S(1)}, bf16[4,16,896]{2,1,0:T(8,128)(2,1)S(1)}, u32[]{:S(2)}, u32[]{:S(2)}) collective-permute-start(bf16[4,16,896]{2,1,0:T(8,128)(2,1)S(1)} %bitcast.21), channel_id=1, source_target_pairs={{0,8},{8,0},{1,9},{9,1},{2,10},{10,2},{3,11},{11,3},{4,12},{12,4},... | collective-permute-start | bytes 344072 | tf_op jit(solution)/shard_map/ppermute | solution.py:37
  107.7 36.0 %all-to-all-start.3 = ((bf16[32,16,896]{2,1,0:T(8,128)(2,1)}), bf16[32,16,896]{2,1,0:T(8,128)(2,1)S(1)}, u32[]{:S(2)}, u32[]{:S(2)}) async-start(bf16[32,16,896]{2,1,0:T(8,128)(2,1)} %owner_sums.1), calls=%async_computation.3 | async-start | bytes 1835008 | tf_op jit(solution)/shard_map/all_to_all | solution.py:33
  117.4 6.2 %collective-permute-start.5 = (bf16[64,512]{1,0:T(8,128)(2,1)S(1)}, bf16[64,512]{1,0:T(8,128)(2,1)S(1)}, u32[]{:S(2)}, u32[]{:S(2)}) collective-permute-start(bf16[64,512]{1,0:T(8,128)(2,1)S(1)} %get-tuple-element.14), channel_id=1, source_target_pairs={{0,1},{1,0},{2,3},{3,2},{4,5},{5,4},{6,7},{7,6},{8,9},{9,8},{10,11... | collective-permute-start | bytes 196616 | tf_op jit(solution)/shard_map/ppermute | solution.py:37

commit v6 on v5

--- a/solution.py
+++ b/solution.py
@@ -33,6 +33,10 @@
     return lax.all_to_all(value, axis, split_axis=0, concat_axis=0, tiled=True)
 
 
+def shifted(value, axis, size, shift):
+    return lax.ppermute(value, axis, [(i, (i + shift) % size) for i in range(size)])
+
+
 def swapped(value, axis, size):
     return lax.ppermute(value, axis, [(i, i ^ 1) for i in range(size)])
 
@@ -80,32 +84,45 @@
         pltpu.make_async_copy(theirs_ref.at[read], target, sems.at[count]).wait()
 
 
-def owner_kernel(ids_ref, core_ref, mine_ref, theirs_ref, out_ref, total):
+def near_id(near_ref, at_ref, column, read):
+    return near_ref[lax.rem(at_ref[0] - column + NX, NX), read // NEIGH, read % NEIGH]
+
+
+def owner_kernel(near_ref, at_ref, from_ref, mine_ref, theirs_ref, total):
     total[...] = jnp.zeros_like(total)
-    for side, reads_ref in enumerate((mine_ref, theirs_ref)):
-        for read in range(reads_ref.shape[0]):
-            block = ids_ref[side, read // NEIGH, read % NEIGH]
-
-            @pl.when(lax.rem(block, NC) == core_ref[0])
+    here, core = at_ref[0], at_ref[1]
+    for column in range(NX):
+        for read in range(from_ref.shape[1]):
+            block = near_id(near_ref, at_ref, column, read)
+
+            @pl.when(block // (NY * NC) == here)
             def _():
-                at = seat(block)
-                total[at] = total[at] + reads_ref[read].astype(F32)
-
-    out_ref[...] = total[...].astype(BF16)
+                side = jnp.where(lax.rem(block, NC) == core, 0, NY)
+                at = side + lax.rem(block // NC, NY)
+                total[at] = total[at] + from_ref[column, read].astype(F32)
+
+    mine_ref[...] = total[:NY]
+    theirs_ref[...] = total[NY:].astype(BF16)
 
 
 def attention_kernel(
-    tok, w_own, q_own, g_own, q_pair, g_pair, kc, ks, qc, qs, w_far,
-    part, dq_own, dq_pair, dk_all, dv_all, w_pair, sem,
+    core_ref, tok, w_own, q_own, g_own, q_pair, g_pair, kc, ks, qc, qs, w_near, w_far,
+    part, dq_own, dq_pair, dk_all, dv_all, w_pair, sems,
 ):
-    fetch = pltpu.make_async_copy(w_far, w_pair, sem)
-    fetch.start()
+    core = core_ref[0]
+    fetches = [
+        pltpu.make_async_copy(w_near, w_pair.at[core], sems.at[0]),
+        pltpu.make_async_copy(w_far, w_pair.at[1 - core], sems.at[1]),
+    ]
+    for fetch in fetches:
+        fetch.start()
     scale = 1.0 / math.sqrt(HEAD)
     half = HEAD // 2
     width = w_own.shape[2]
     rows = jnp.concatenate([tok[:, n].reshape(NLEN, DE) for n in range(NEIGH)], axis=0)
     projected = [(dot(rows, w_own[0]), dot(rows, w_own[1]).astype(BF16))]
-    fetch.wait()
+    for fetch in fetches:
+        fetch.wait()
     projected.append((dot(rows, w_pair[0]), dot(rows, w_pair[1]).astype(BF16)))
     key_cos, key_sin, query_cos, query_sin = kc[...], ks[...], qc[...], qs[...]
     for turn, (q, g, dq) in enumerate(((q_own, g_own, dq_own), (q_pair, g_pair, dq_pair))):
@@ -154,7 +171,7 @@
     )(*scalars, *operands)
 
 
-def attention(*operands):
+def attention(core, *operands):
     _, depth, width = operands[1].shape
     return pl.pallas_call(
         attention_kernel,
@@ -163,29 +180,30 @@
             jax.ShapeDtypeStruct((SPAN, width), BF16),
             jax.ShapeDtypeStruct((SPAN, width), BF16),
         ),
-        in_specs=[VMEM] * (len(operands) - 1) + [ANY],
+        in_specs=[SMEM] + [VMEM] * (len(operands) - 2) + [ANY] * 2,
         out_specs=(VMEM, VMEM, VMEM),
         scratch_shapes=[
             pltpu.VMEM((NEIGH * NLEN, 2 * width), BF16),
             pltpu.VMEM((NEIGH * NLEN, 2 * width), BF16),
             pltpu.VMEM((2, depth, width), BF16),
-            pltpu.SemaphoreType.DMA,
+            pltpu.SemaphoreType.DMA((2,)),
         ],
         compiler_params=pltpu.CompilerParams(vmem_limit_bytes=40 << 20),
         cost_estimate=pl.CostEstimate(
             flops=2_100_000_000, bytes_accessed=6_000_000, transcendentals=131072
         ),
         name="attention",
-    )(*operands)
+    )(core, *operands)
 
 
 def local(queries, out_grad, encodings, kv_weight, neighbour_ids, rot_offset):
-    c_at, z_at = lax.axis_index("c"), lax.axis_index("z")
+    x_at, c_at, z_at = lax.axis_index("x"), lax.axis_index("c"), lax.axis_index("z")
     spans = neighbour_ids.shape[0]
     reads = spans * NEIGH
     span_at = z_at % 2
 
-    w_far = swapped(kv_weight, "z", NZ)
+    w_near = swapped(lax.dynamic_index_in_dim(kv_weight, c_at, 0, keepdims=False), "z", NZ)
+    w_far = swapped(w_near, "c", NC)
     rows_q = queries.reshape(spans, SPAN, -1)
     rows_g = out_grad.reshape(spans, SPAN, -1)
     other = jnp.concatenate(
@@ -195,6 +213,7 @@
         ],
         axis=0,
     )
+    from_pair = swapped(other, "z", NZ)
     q_own = lax.dynamic_index_in_dim(rows_q, span_at, 0, keepdims=False)
     g_own = lax.dynamic_index_in_dim(rows_g, span_at, 0, keepdims=False)
     offsets = lax.dynamic_index_in_dim(rot_offset, span_at, 0, keepdims=False)
@@ -203,9 +222,14 @@
     query_cos, query_sin = rotary_tables(jnp.arange(SPAN, dtype=jnp.int32))
 
     core = c_at.reshape(1)
+    at = jnp.stack([x_at, c_at])
     ids = jnp.stack([neighbour_ids, swapped(neighbour_ids, "c", NC)])
     copies = jnp.broadcast_to(encodings, (NX * NY, ROWS, DE))
     blocks = exchange(copies, ("x", "y"))
+    near = [neighbour_ids] + [shifted(neighbour_ids, "x", NX, s) for s in range(1, NX)]
+    blocks, near, w_far, from_pair = lax.optimization_barrier(
+        (blocks, jnp.stack(near), w_far, from_pair)
+    )
     asked = on_core(
         pick_kernel, "pick", jax.ShapeDtypeStruct((reads, ROWS, DE), BF16), (ids,),
         blocks, scratch=[pltpu.SemaphoreType.DMA((reads,))], space=ANY,
@@ -216,27 +240,29 @@
         spread_kernel, "spread", jax.ShapeDtypeStruct((NZ, NEIGH, ROWS, DE), BF16), (ids, core),
         blocks, arrived, scratch=[pltpu.SemaphoreType.DMA((NZ * NEIGH,))], space=ANY,
     )
-    to_z, w_far = lax.optimization_barrier((to_z, w_far))
     tok = exchange(to_z, "z")
-    from_pair = swapped(other, "z", NZ)
     part, dq_own, dq_pair = attention(
-        tok, kv_weight, q_own, g_own, from_pair[:SPAN], from_pair[SPAN:],
-        key_cos, key_sin, query_cos, query_sin, w_far,
+        core, tok, kv_weight, q_own, g_own, from_pair[:SPAN], from_pair[SPAN:],
+        key_cos, key_sin, query_cos, query_sin, w_near, w_far,
     )
 
     from_heads = exchange(part, "z")
     from_heads = from_heads.reshape(NZ // spans, spans, NEIGH, ROWS, DE)
     read_sum = jnp.sum(from_heads.astype(F32), axis=0).astype(BF16).reshape(reads, ROWS, DE)
 
-    theirs = swapped(read_sum, "c", NC)
-    owners = (NX * NY, ROWS, DE)
-    owner_part = on_core(
-        owner_kernel, "owner_sums", jax.ShapeDtypeStruct(owners, BF16), (ids, core),
-        read_sum, theirs, scratch=[pltpu.VMEM(owners, F32)],
-    )
+    read_copies = jnp.broadcast_to(read_sum, (NX, reads, ROWS, DE))
+    read_x = exchange(read_copies, "x")
+    owners = (NY, ROWS, DE)
+    mine, theirs = on_core(
+        owner_kernel, "owner_sums",
+        (jax.ShapeDtypeStruct(owners, F32), jax.ShapeDtypeStruct(owners, BF16)),
+        (near, at), read_x, scratch=[pltpu.VMEM((NC * NY, ROWS, DE), F32)],
+    )
+    owner_part = (mine + swapped(theirs, "c", NC).astype(F32)).astype(BF16)
     owner_part, dq_pair = lax.optimization_barrier((owner_part, dq_pair))
     dq_back = swapped(dq_pair, "z", NZ)
-    owned = jnp.sum(exchange(owner_part, ("x", "y")).astype(F32), axis=0)
+    from_y = exchange(owner_part, "y")
+    owned = jnp.sum(from_y.astype(F32), axis=0)
 
     first = jnp.where(span_at == 0, dq_own, dq_back)
     second = jnp.where(span_at == 0, dq_back, dq_own)

time: 145 us -> 148 us (1.021)
  the two profiles are of different devices: /device:TPU:8 before, /device:TPU:1 now
where the time goes in v6:
time: 148 us; the launch traced here: 147 us
  starting transfers between devices  66.3 us (45%)
  waiting for transfers between devices  42.4 us (29%)
  blocking collectives  18.8 us (13%)
  Pallas kernels  9.41 us (6%)
  local copies, waits for them, and re-layouts  5.5 us (4%)
  other arithmetic  3.27 us (2%)
    all_to_all x4, waiting for transfers between devices, exchange(): return lax.all_to_all(value, axis, split_axis=0, concat_axis=0, tiled=True)  32.9 us
    all_to_all x4, starting transfers between devices, exchange(): return lax.all_to_all(value, axis, split_axis=0, concat_axis=0, tiled=True)  29.3 us
    ppermute x7, starting transfers between devices, swapped(): return lax.ppermute(value, axis, [(i, i ^ 1) for i in range(size)])  27.7 us
    all_to_all x1, blocking collectives, exchange(): return lax.all_to_all(value, axis, split_axis=0, concat_axis=0, tiled=True)  18.8 us
    ppermute x7, waiting for transfers between devices, swapped(): return lax.ppermute(value, axis, [(i, i ^ 1) for i in range(size)])  9.46 us
    ppermute x3, starting transfers between devices, shifted(): lax.ppermute(value, axis, [(i, (i + shift) % size) for i in range(size)])  9.33 us
    pallas_call x1, Pallas kernels, attention(): pl.pallas_call(attention_kernel, out_shape=(jax.ShapeDtypeStruct((NZ, NEI...  6.04 us
    pallas_call x3, Pallas kernels, on_core(): pl.pallas_call(kernel, out_shape=shapes, in_specs=[SMEM] * len(scalars) +...  3.38 us
  transfers between devices with their start and end apart: 14, of which 7 were waited for; matrix products, arithmetic and copies ran while one was open for 2% of the time, Pallas kernels for 0%

profile of v6, /device:TPU:1, one launch (start us, length us, event | category | flops | bytes accessed | tf_op | source)
XLA Modules:
  0.0 146.7 jit_solution(18014770462344541560)
XLA Ops:
  0.7 1.2 dynamic-slice_bitcast_fusion
  1.9 5.0 %collective-permute-start.4 = (bf16[896,512]{1,0:T(8,128)(2,1)S(1)}, bf16[896,512]{1,0:T(8,128)(2,1)S(1)}, u32[]{:S(2)}, u32[]{:S(2)}) collective-permute-start(bf16[896,512]{1,0:T(8,128)(2,1)S(1)} %dynamic-slice_bitcast_fusion), channel_id=1, source_target_pairs={{0,1},{1,0},{2,3},{3,2},{4,5},{5,4},{6,7},{7,6},{8,9},{9,8},{10,11... | collective-permute-start | bytes 2752520 | tf_op jit(solution)/shard_map/ppermute | solution.py:41
  7.9 9.7 %all-to-all-start = ((bf16[32,16,896]{2,1,0:T(8,128)(2,1)}), bf16[32,16,896]{2,1,0:T(8,128)(2,1)S(1)}, u32[]{:S(2)}, u32[]{:S(2)}) async-start(bf16[32,16,896]{2,1,0:T(8,128)(2,1)} %broadcast_in_dim.7), calls=%async_computation | async-start | bytes 1835008 | tf_op jit(solution)/shard_map/all_to_all | solution.py:33
  17.6 5.2 %collective-permute-done.4.w_near = bf16[896,512]{1,0:T(8,128)(2,1)S(1)} collective-permute-done((bf16[896,512]{1,0:T(8,128)(2,1)S(1)}, bf16[896,512]{1,0:T(8,128)(2,1)S(1)}, u32[]{:S(2)}, u32[]{:S(2)}) %collective-permute-start.4) | collective-permute-done | bytes 917536 | tf_op jit(solution)/shard_map/ppermute | solution.py:41
  22.8 7.3 %collective-permute-start.5 = (bf16[896,512]{1,0:T(8,128)(2,1)S(1)}, bf16[896,512]{1,0:T(8,128)(2,1)S(1)}, u32[]{:S(2)}, u32[]{:S(2)}) collective-permute-start(bf16[896,512]{1,0:T(8,128)(2,1)S(1)} %collective-permute-done.4.w_near), channel_id=1, source_target_pairs={{0,8},{8,0},{1,9},{9,1},{2,10},{10,2},{3,11},{11,3},{4,12},{12,4},... | collective-permute-start | bytes 2752520 | tf_op jit(solution)/shard_map/ppermute | solution.py:41
  30.1 1.9 %collective-permute-start = (s32[2,2]{1,0:T(2,128)S(1)}, s32[2,2]{1,0:T(2,128)S(1)}, u32[]{:S(2)}, u32[]{:S(2)}) collective-permute-start(s32[2,2]{1,0:T(2,128)S(1)} %copy-done.9), channel_id=1, source_target_pairs={{0,8},{8,0},{1,9},{9,1},{2,10},{10,2},{3,11},{11,3},{4,12},{12,4},... | collective-permute-start | bytes 56 | tf_op jit(solution)/shard_map/ppermute | solution.py:41
  32.0 4.4 %collective-permute-start.3 = (s32[2,2]{1,0:T(2,128)S(1)}, s32[2,2]{1,0:T(2,128)S(1)}, u32[]{:S(2)}, u32[]{:S(2)}) collective-permute-start(s32[2,2]{1,0:T(2,128)S(1)} %copy-done.9), channel_id=1, source_target_pairs={{0,384},{128,0},{256,128},{384,256},{1,385},{129,1},{257,129},{385... | collective-permute-start | bytes 56 | tf_op jit(solution)/shard_map/ppermute | solution.py:37
  36.4 2.4 %collective-permute-start.2 = (s32[2,2]{1,0:T(2,128)S(1)}, s32[2,2]{1,0:T(2,128)S(1)}, u32[]{:S(2)}, u32[]{:S(2)}) collective-permute-start(s32[2,2]{1,0:T(2,128)S(1)} %copy-done.9), channel_id=1, source_target_pairs={{0,256},{128,384},{256,0},{384,128},{1,257},{129,385},{257,1},{385... | collective-permute-start | bytes 56 | tf_op jit(solution)/shard_map/ppermute | solution.py:37
  38.9 2.5 %collective-permute-start.1 = (s32[2,2]{1,0:T(2,128)S(1)}, s32[2,2]{1,0:T(2,128)S(1)}, u32[]{:S(2)}, u32[]{:S(2)}) collective-permute-start(s32[2,2]{1,0:T(2,128)S(1)} %copy-done.9), channel_id=1, source_target_pairs={{0,128},{128,256},{256,384},{384,0},{1,129},{129,257},{257,385},{3... | collective-permute-start | bytes 56 | tf_op jit(solution)/shard_map/ppermute | solution.py:37
  41.7 3.4 %collective-permute-start.6 = (bf16[128,512]{1,0:T(8,128)(2,1)S(1)}, bf16[128,512]{1,0:T(8,128)(2,1)S(1)}, u32[]{:S(2)}, u32[]{:S(2)}) collective-permute-start(bf16[128,512]{1,0:T(8,128)(2,1)S(1)} %pad_maximum_fusion), channel_id=1, source_target_pairs={{0,1},{1,0},{2,3},{3,2},{4,5},{5,4},{6,7},{7,6},{8,9},{9,8},{10,11... | collective-permute-start | bytes 393224 | tf_op jit(solution)/shard_map/ppermute | solution.py:41
  45.2 2.3 %collective-permute-done.6 = bf16[128,512]{1,0:T(8,128)(2,1)S(1)} collective-permute-done((bf16[128,512]{1,0:T(8,128)(2,1)S(1)}, bf16[128,512]{1,0:T(8,128)(2,1)S(1)}, u32[]{:S(2)}, u32[]{:S(2)}) %collective-permute-start.6) | collective-permute-done | bytes 131104 | tf_op jit(solution)/shard_map/ppermute | solution.py:41
  48.2 4.4 %collective-permute-start.7 = (bf16[4,16,896]{2,1,0:T(8,128)(2,1)S(1)}, bf16[4,16,896]{2,1,0:T(8,128)(2,1)S(1)}, u32[]{:S(2)}, u32[]{:S(2)}) collective-permute-start(bf16[4,16,896]{2,1,0:T(8,128)(2,1)S(1)} %pick.1), channel_id=1, source_target_pairs={{0,8},{8,0},{1,9},{9,1},{2,10},{10,2},{3,11},{11,3},{4,12},{12,4},... | collective-permute-start | bytes 344072 | tf_op jit(solution)/shard_map/ppermute | solution.py:41
  53.6 1.5 %spread.1 = bf16[8,2,16,896]{3,2,1,0:T(8,128)(2,1)} custom-call(s32[2,2,2]{2,1,0:T(2,128)S(1)} %pad_add_fusion.1.ids_ref, s32[1]{0:T(128)} %bitcast.core_ref, bf16[32,16,896]{2,1,0:T(8,128)(2,1)S(1)} %all-to-all-done.from_ref.mine_ref, bf16[4,16,896]{2,1,0:T(8,128)(2,1)S(1)} %collective-permute-done.7.theirs_ref), custom_call_target="tpu_custom_call" | custom-call | tf_op jit(solution)/shard_map/spread/pallas_call | solution.py:163
  55.1 9.4 %all-to-all-start.1 = ((bf16[8,2,16,896]{3,2,1,0:T(8,128)(2,1)}), bf16[8,2,16,896]{3,2,1,0:T(8,128)(2,1)S(1)}, u32[]{:S(2)}, u32[]{:S(2)}) async-start(bf16[8,2,16,896]{3,2,1,0:T(8,128)(2,1)} %spread.1), calls=%async_computation.1 | async-start | bytes 917504 | tf_op jit(solution)/shard_map/all_to_all | solution.py:33
  65.3 15.8 %all-to-all-done.1.tok = bf16[8,2,16,896]{3,2,1,0:T(8,128)(2,1)S(1)} async-done(((bf16[8,2,16,896]{3,2,1,0:T(8,128)(2,1)}), bf16[8,2,16,896]{3,2,1,0:T(8,128)(2,1)S(1)}, u32[]{:S(2)}, u32[]{:S(2)}) %all-to-all-start.1) | async-done | bytes 458784 | tf_op jit(solution)/shard_map/all_to_all | solution.py:33
  81.1 1.2 copy-done.3
  83.4 6.0 %attention.1 = (bf16[8,2,16,896]{3,2,1,0:T(8,128)(2,1)S(1)}, bf16[64,512]{1,0:T(8,128)(2,1)S(1)}, bf16[64,512]{1,0:T(8,128)(2,1)S(1)}) custom-call(s32[1]{0:T(128)} %bitcast.core_ref, bf16[8,2,16,896]{3,2,1,0:T(8,128)(2,1)S(1)} %all-to-all-done.1.tok, bf16[2,896,512]{2,1,0:T(8,128)(2,1)S(1)} %copy-done.1, bf16[64,512]{1,0:T(8,128)(2,1)S(1)} %get-tuple-element.39.q_own, ...), custom_call_target="tpu_custom_call" | custom-call | flops 2100000000 | bytes 6000000 | tf_op jit(solution)/shard_map/attention/pallas_call | solution.py:176
  89.5 18.8 %all_to_all.25 = bf16[8,2,16,896]{3,2,1,0:T(8,128)(2,1)S(1)} all-to-all(bf16[8,2,16,896]{3,2,1,0:T(8,128)(2,1)S(1)} %get-tuple-element.18), channel_id=1, replica_groups=mesh['x'=4,'y'=8,'c'=2,'z'=8] {'z'}, dimensions={0} | all-to-all | bytes 917504 | tf_op jit(solution)/shard_map/all_to_all | solution.py:33
  109.2 3.5 %all-to-all-start.3 = ((bf16[4,4,16,896]{3,2,1,0:T(8,128)(2,1)}), bf16[4,4,16,896]{3,2,1,0:T(8,128)(2,1)S(1)}, u32[]{:S(2)}, u32[]{:S(2)}) async-start(bf16[4,4,16,896]{3,2,1,0:T(8,128)(2,1)} %broadcast_in_dim.8), calls=%async_computation.3 | async-start | bytes 917504 | tf_op jit(solution)/shard_map/all_to_all | solution.py:33
  112.8 7.7 %all-to-all-done.3.from_ref = bf16[4,4,16,896]{3,2,1,0:T(8,128)(2,1)S(1)} async-done(((bf16[4,4,16,896]{3,2,1,0:T(8,128)(2,1)}), bf16[4,4,16,896]{3,2,1,0:T(8,128)(2,1)S(1)}, u32[]{:S(2)}, u32[]{:S(2)}) %all-to-all-start.3) | async-done | bytes 458784 | tf_op jit(solution)/shard_map/all_to_all | solution.py:33
  121.5 3.9 %collective-permute-start.8 = (bf16[8,16,896]{2,1,0:T(8,128)(2,1)S(1)}, bf16[8,16,896]{2,1,0:T(8,128)(2,1)S(1)}, u32[]{:S(2)}, u32[]{:S(2)}) collective-permute-start(bf16[8,16,896]{2,1,0:T(8,128)(2,1)S(1)} %get-tuple-element.20), channel_id=1, source_target_pairs={{0,8},{8,0},{1,9},{9,1},{2,10},{10,2},{3,11},{11,3},{4,12},{12,4},... | collective-permute-start | bytes 688136 | tf_op jit(solution)/shard_map/ppermute | solution.py:41
  127.2 1.9 %collective-permute-start.9 = (bf16[64,512]{1,0:T(8,128)(2,1)S(1)}, bf16[64,512]{1,0:T(8,128)(2,1)S(1)}, u32[]{:S(2)}, u32[]{:S(2)}) collective-permute-start(bf16[64,512]{1,0:T(8,128)(2,1)S(1)} %get-tuple-element.22), channel_id=1, source_target_pairs={{0,1},{1,0},{2,3},{3,2},{4,5},{5,4},{6,7},{7,6},{8,9},{9,8},{10,11... | collective-permute-start | bytes 196616 | tf_op jit(solution)/shard_map/ppermute | solution.py:41
  129.2 6.8 %all-to-all-start.4 = ((bf16[8,16,896]{2,1,0:T(8,128)(2,1)}), bf16[8,16,896]{2,1,0:T(8,128)(2,1)S(1)}, u32[]{:S(2)}, u32[]{:S(2)}) async-start(bf16[8,16,896]{2,1,0:T(8,128)(2,1)} %add_convert_fusion), calls=%async_computation.4 | async-start | bytes 458752 | tf_op jit(solution)/shard_map/all_to_all | solution.py:33
  136.6 9.5 %all-to-all-done.4 = bf16[8,16,896]{2,1,0:T(8,128)(2,1)S(1)} async-done(((bf16[8,16,896]{2,1,0:T(8,128)(2,1)}), bf16[8,16,896]{2,1,0:T(8,128)(2,1)S(1)}, u32[]{:S(2)}, u32[]{:S(2)}) %all-to-all-start.4) | async-done | bytes 229408 | tf_op jit(solution)/shard_map/all_to_all | solution.py:33
  (51 shorter events, 10.2 us)
Async XLA Ops:
  0.6 52.0 %copy-start = (s32[2,2]{1,0:T(2,128)S(1)}, s32[2,2]{1,0:T(2,128)}, u32[]{:S(2)}) copy-start(s32[2,2]{1,0:T(2,128)} %param.11) | copy-start | bytes 52
  0.6 6.3 %copy-start.8 = (bf16[1,16,896]{2,1,0:T(8,128)(2,1)S(1)}, bf16[1,16,896]{2,1,0:T(8,128)(2,1)}, u32[]{:S(2)}) copy-start(bf16[1,16,896]{2,1,0:T(8,128)(2,1)} %param.8) | copy-start | bytes 86020
  1.9 28.2 %copy-start.9 = (s32[2,2]{1,0:T(2,128)S(1)}, s32[2,2]{1,0:T(2,128)}, u32[]{:S(2)}) copy-start(s32[2,2]{1,0:T(2,128)} %param.10) | copy-start | bytes 52
  1.9 39.5 %copy-start.6 = (bf16[128,512]{1,0:T(8,128)(2,1)S(1)}, bf16[128,512]{1,0:T(8,128)(2,1)}, u32[]{:S(2)}) copy-start(bf16[128,512]{1,0:T(8,128)(2,1)} %param.7) | copy-start | bytes 393220
  1.9 39.5 %copy-start.7 = (bf16[128,512]{1,0:T(8,128)(2,1)S(1)}, bf16[128,512]{1,0:T(8,128)(2,1)}, u32[]{:S(2)}) copy-start(bf16[128,512]{1,0:T(8,128)(2,1)} %param.6) | copy-start | bytes 393220
  1.9 20.9 %collective-permute-start.4 = (bf16[896,512]{1,0:T(8,128)(2,1)S(1)}, bf16[896,512]{1,0:T(8,128)(2,1)S(1)}, u32[]{:S(2)}, u32[]{:S(2)}) collective-permute-start(bf16[896,512]{1,0:T(8,128)(2,1)S(1)} %dynamic-slice_bitcast_fusion), channel_id=1, source_target_pairs={{0,1},{1,0},{2,3},{3,2},{4,5},{5,4},{6,7},{7,6},{8,9},{9,8},{10,11... | collective-permute-start | bytes 2752520 | tf_op jit(solution)/shard_map/ppermute | solution.py:41
  7.9 39.5 %all-to-all-start = ((bf16[32,16,896]{2,1,0:T(8,128)(2,1)}), bf16[32,16,896]{2,1,0:T(8,128)(2,1)S(1)}, u32[]{:S(2)}, u32[]{:S(2)}) async-start(bf16[32,16,896]{2,1,0:T(8,128)(2,1)} %broadcast_in_dim.7), calls=%async_computation | async-start | bytes 1835008 | tf_op jit(solution)/shard_map/all_to_all | solution.py:33
  22.8 30.8 %copy-start.2 = (bf16[896,512]{1,0:T(8,128)(2,1)}, bf16[896,512]{1,0:T(8,128)(2,1)S(1)}, u32[]{:S(2)}) copy-start(bf16[896,512]{1,0:T(8,128)(2,1)S(1)} %collective-permute-done.4.w_near) | copy-start | bytes 2752516
  22.8 24.6 %collective-permute-start.5 = (bf16[896,512]{1,0:T(8,128)(2,1)S(1)}, bf16[896,512]{1,0:T(8,128)(2,1)S(1)}, u32[]{:S(2)}, u32[]{:S(2)}) collective-permute-start(bf16[896,512]{1,0:T(8,128)(2,1)S(1)} %collective-permute-done.4.w_near), channel_id=1, source_target_pairs={{0,8},{8,0},{1,9},{9,1},{2,10},{10,2},{3,11},{11,3},{4,12},{12,4},... | collective-permute-start | bytes 2752520 | tf_op jit(solution)/shard_map/ppermute | solution.py:41
  30.1 11.6 %collective-permute-start = (s32[2,2]{1,0:T(2,128)S(1)}, s32[2,2]{1,0:T(2,128)S(1)}, u32[]{:S(2)}, u32[]{:S(2)}) collective-permute-start(s32[2,2]{1,0:T(2,128)S(1)} %copy-done.9), channel_id=1, source_target_pairs={{0,8},{8,0},{1,9},{9,1},{2,10},{10,2},{3,11},{11,3},{4,12},{12,4},... | collective-permute-start | bytes 56 | tf_op jit(solution)/shard_map/ppermute | solution.py:41
  32.0 13.1 %collective-permute-start.3 = (s32[2,2]{1,0:T(2,128)S(1)}, s32[2,2]{1,0:T(2,128)S(1)}, u32[]{:S(2)}, u32[]{:S(2)}) collective-permute-start(s32[2,2]{1,0:T(2,128)S(1)} %copy-done.9), channel_id=1, source_target_pairs={{0,384},{128,0},{256,128},{384,256},{1,385},{129,1},{257,129},{385... | collective-permute-start | bytes 56 | tf_op jit(solution)/shard_map/ppermute | solution.py:37
  36.4 8.7 %collective-permute-start.2 = (s32[2,2]{1,0:T(2,128)S(1)}, s32[2,2]{1,0:T(2,128)S(1)}, u32[]{:S(2)}, u32[]{:S(2)}) collective-permute-start(s32[2,2]{1,0:T(2,128)S(1)} %copy-done.9), channel_id=1, source_target_pairs={{0,256},{128,384},{256,0},{384,128},{1,257},{129,385},{257,1},{385... | collective-permute-start | bytes 56 | tf_op jit(solution)/shard_map/ppermute | solution.py:37
  38.9 6.3 %collective-permute-start.1 = (s32[2,2]{1,0:T(2,128)S(1)}, s32[2,2]{1,0:T(2,128)S(1)}, u32[]{:S(2)}, u32[]{:S(2)}) collective-permute-start(s32[2,2]{1,0:T(2,128)S(1)} %copy-done.9), channel_id=1, source_target_pairs={{0,128},{128,256},{256,384},{384,0},{1,129},{129,257},{257,385},{3... | collective-permute-start | bytes 56 | tf_op jit(solution)/shard_map/ppermute | solution.py:37
  41.7 5.7 %collective-permute-start.6 = (bf16[128,512]{1,0:T(8,128)(2,1)S(1)}, bf16[128,512]{1,0:T(8,128)(2,1)S(1)}, u32[]{:S(2)}, u32[]{:S(2)}) collective-permute-start(bf16[128,512]{1,0:T(8,128)(2,1)S(1)} %pad_maximum_fusion), channel_id=1, source_target_pairs={{0,1},{1,0},{2,3},{3,2},{4,5},{5,4},{6,7},{7,6},{8,9},{9,8},{10,11... | collective-permute-start | bytes 393224 | tf_op jit(solution)/shard_map/ppermute | solution.py:41
  47.5 6.1 %copy-start.4 = (bf16[896,512]{1,0:T(8,128)(2,1)}, bf16[896,512]{1,0:T(8,128)(2,1)S(1)}, u32[]{:S(2)}) copy-start(bf16[896,512]{1,0:T(8,128)(2,1)S(1)} %collective-permute-done.5.w_far) | copy-start | bytes 2752516
  48.2 5.3 %collective-permute-start.7 = (bf16[4,16,896]{2,1,0:T(8,128)(2,1)S(1)}, bf16[4,16,896]{2,1,0:T(8,128)(2,1)S(1)}, u32[]{:S(2)}, u32[]{:S(2)}) collective-permute-start(bf16[4,16,896]{2,1,0:T(8,128)(2,1)S(1)} %pick.1), channel_id=1, source_target_pairs={{0,8},{8,0},{1,9},{9,1},{2,10},{10,2},{3,11},{11,3},{4,12},{12,4},... | collective-permute-start | bytes 344072 | tf_op jit(solution)/shard_map/ppermute | solution.py:41
  53.6 27.5 %copy-start.1 = (bf16[2,896,512]{2,1,0:T(8,128)(2,1)S(1)}, bf16[2,896,512]{2,1,0:T(8,128)(2,1)}, u32[]{:S(2)}) copy-start(bf16[2,896,512]{2,1,0:T(8,128)(2,1)} %w_own.1) | copy-start | bytes 5505028
  55.1 26.0 %all-to-all-start.1 = ((bf16[8,2,16,896]{3,2,1,0:T(8,128)(2,1)}), bf16[8,2,16,896]{3,2,1,0:T(8,128)(2,1)S(1)}, u32[]{:S(2)}, u32[]{:S(2)}) async-start(bf16[8,2,16,896]{3,2,1,0:T(8,128)(2,1)} %spread.1), calls=%async_computation.1 | async-start | bytes 917504 | tf_op jit(solution)/shard_map/all_to_all | solution.py:33
  81.1 1.2 copy-start.3
  82.2 1.2 copy-start.5
  109.2 11.2 %all-to-all-start.3 = ((bf16[4,4,16,896]{3,2,1,0:T(8,128)(2,1)}), bf16[4,4,16,896]{3,2,1,0:T(8,128)(2,1)S(1)}, u32[]{:S(2)}, u32[]{:S(2)}) async-start(bf16[4,4,16,896]{3,2,1,0:T(8,128)(2,1)} %broadcast_in_dim.8), calls=%async_computation.3 | async-start | bytes 917504 | tf_op jit(solution)/shard_map/all_to_all | solution.py:33
  121.5 5.0 %collective-permute-start.8 = (bf16[8,16,896]{2,1,0:T(8,128)(2,1)S(1)}, bf16[8,16,896]{2,1,0:T(8,128)(2,1)S(1)}, u32[]{:S(2)}, u32[]{:S(2)}) collective-permute-start(bf16[8,16,896]{2,1,0:T(8,128)(2,1)S(1)} %get-tuple-element.20), channel_id=1, source_target_pairs={{0,8},{8,0},{1,9},{9,1},{2,10},{10,2},{3,11},{11,3},{4,12},{12,4},... | collective-permute-start | bytes 688136 | tf_op jit(solution)/shard_map/ppermute | solution.py:41
  127.2 8.7 %collective-permute-start.9 = (bf16[64,512]{1,0:T(8,128)(2,1)S(1)}, bf16[64,512]{1,0:T(8,128)(2,1)S(1)}, u32[]{:S(2)}, u32[]{:S(2)}) collective-permute-start(bf16[64,512]{1,0:T(8,128)(2,1)S(1)} %get-tuple-element.22), channel_id=1, source_target_pairs={{0,1},{1,0},{2,3},{3,2},{4,5},{5,4},{6,7},{7,6},{8,9},{9,8},{10,11... | collective-permute-start | bytes 196616 | tf_op jit(solution)/shard_map/ppermute | solution.py:41
  129.2 16.9 %all-to-all-start.4 = ((bf16[8,16,896]{2,1,0:T(8,128)(2,1)}), bf16[8,16,896]{2,1,0:T(8,128)(2,1)S(1)}, u32[]{:S(2)}, u32[]{:S(2)}) async-start(bf16[8,16,896]{2,1,0:T(8,128)(2,1)} %add_convert_fusion), calls=%async_computation.4 | async-start | bytes 458752 | tf_op jit(solution)/shard_map/all_to_all | solution.py:33

commit v7 on v3

--- a/solution.py
+++ b/solution.py
@@ -43,17 +43,19 @@
     )
 
 
-def near_id(near_ref, at_ref, column, read):
-    return near_ref[lax.rem(at_ref[0] - column + NX, NX), read // NEIGH, read % NEIGH]
-
-
-def pick_kernel(near_ref, at_ref, mine_ref, theirs_ref, out_ref, sems):
+def at_distance(at_ref, distance):
+    return lax.rem(at_ref[0] - distance + NX, NX)
+
+
+def pick_kernel(at_ref, *refs):
+    near, (mine_ref, theirs_ref, out_ref, sems) = refs[:NX], refs[NX:]
     core, reads = at_ref[1], out_ref.shape[1]
-    for column in range(NX):
+    for distance in range(NX):
+        column = at_distance(at_ref, distance)
         for read in range(reads):
-            block = near_id(near_ref, at_ref, column, read)
+            block = near[distance][read // NEIGH, read % NEIGH]
             row, same = lax.rem(block // NC, NY), lax.rem(block, NC) == core
-            sem = sems.at[column * reads + read]
+            sem = sems.at[distance * reads + read]
 
             @pl.when(same)
             def _():
@@ -63,28 +65,29 @@
             def _():
                 pltpu.make_async_copy(theirs_ref.at[row], out_ref.at[column, read], sem).start()
 
-    for column in range(NX):
-        for read in range(reads):
-            sem = sems.at[column * reads + read]
-            pltpu.make_async_copy(mine_ref.at[0], out_ref.at[column, read], sem).wait()
-
-
-def spread_kernel(near_ref, at_ref, from_ref, out_ref):
+    for count in range(NX * reads):
+        place = out_ref.at[count // reads, count % reads]
+        pltpu.make_async_copy(mine_ref.at[0], place, sems.at[count]).wait()
+
+
+def spread_kernel(ids_ref, from_ref, out_ref):
     reads = from_ref.shape[1]
     spans = reads // NEIGH
     for read in range(reads):
-        owner = near_ref[0, read // NEIGH, read % NEIGH]
+        owner = ids_ref[read // NEIGH, read % NEIGH]
         block = from_ref[owner // (NY * NC), read]
         for at in range(read // NEIGH, NZ, spans):
             out_ref[at, read % NEIGH] = block
 
 
-def owner_kernel(near_ref, at_ref, from_ref, mine_ref, theirs_ref, total):
+def owner_kernel(at_ref, *refs):
+    near, (from_ref, mine_ref, theirs_ref, total) = refs[:NX], refs[NX:]
     total[...] = jnp.zeros_like(total)
     here, core = at_ref[0], at_ref[1]
-    for column in range(NX):
+    for distance in range(NX):
+        column = at_distance(at_ref, distance)
         for read in range(from_ref.shape[1]):
-            block = near_id(near_ref, at_ref, column, read)
+            block = near[distance][read // NEIGH, read % NEIGH]
 
             @pl.when(block // (NY * NC) == here)
             def _():
@@ -206,25 +209,24 @@
 
     at = jnp.stack([x_at, c_at])
     near = [neighbour_ids] + [shifted(neighbour_ids, "x", NX, s) for s in range(1, NX)]
-    near = jnp.stack(near)
     copies = jnp.broadcast_to(encodings, (NY, ROWS, DE))
     over_y = lax.all_to_all(copies, "y", split_axis=0, concat_axis=0, tiled=True)
     over_y, near, other = lax.optimization_barrier((over_y, near, other))
     beside = swapped(over_y, "c", NC)
     block = (reads, ROWS, DE)
     asked = on_core(
-        pick_kernel, "pick", jax.ShapeDtypeStruct((NX, *block), BF16), (near, at),
+        pick_kernel, "pick", jax.ShapeDtypeStruct((NX, *block), BF16), (at, *near),
         over_y, beside, scratch=[pltpu.SemaphoreType.DMA((NX * reads,))], space=ANY,
     )
     found = lax.all_to_all(asked, "x", split_axis=0, concat_axis=0, tiled=True)
 
     to_z = on_core(
-        spread_kernel, "spread", jax.ShapeDtypeStruct((NZ, NEIGH, ROWS, DE), BF16), (near, at),
+        spread_kernel, "spread", jax.ShapeDtypeStruct((NZ, NEIGH, ROWS, DE), BF16), (neighbour_ids,),
         found,
     )
-    to_z, w_far = lax.optimization_barrier((to_z, w_far))
+    from_pair = swapped(other, "z", NZ)
+    to_z, w_far, from_pair = lax.optimization_barrier((to_z, w_far, from_pair))
     tok = lax.all_to_all(to_z, "z", split_axis=0, concat_axis=0, tiled=True)
-    from_pair = swapped(other, "z", NZ)
     part, dq_own, dq_pair = attention(
         tok, kv_weight, q_own, g_own, from_pair[:SPAN], from_pair[SPAN:],
         key_cos, key_sin, query_cos, query_sin, w_far,
@@ -240,7 +242,7 @@
     mine, theirs = on_core(
         owner_kernel, "owner_sums",
         (jax.ShapeDtypeStruct(owners, F32), jax.ShapeDtypeStruct(owners, BF16)),
-        (near, at), read_x, scratch=[pltpu.VMEM((NC * NY, ROWS, DE), F32)],
+        (at, *near), read_x, scratch=[pltpu.VMEM((NC * NY, ROWS, DE), F32)],
     )
     owner_part = (mine + swapped(theirs, "c", NC).astype(F32)).astype(BF16)
     owner_part, dq_pair = lax.optimization_barrier((owner_part, dq_pair))

time: 136 us -> 135 us (level)
  blocking collectives: 28.2 us -> 25.5 us
  waiting for transfers between devices: 31.7 us -> 33.3 us
    all_to_all x1, waiting for transfers between devices: 1.96 us -> 13.7 us  [local(): tok = lax.all_to_all(to_z, 'z', split_axis=0, concat_axis=0, tiled=True)]
    ppermute x5, waiting for transfers between devices: 10.8 us -> 2.09 us  [swapped(): return lax.ppermute(value, axis, [(i, i ^ 1) for i in range(size)])]
    all_to_all x1, blocking collectives: 19.3 us -> 15.1 us  [local(): lax.all_to_all(part, 'z', split_axis=0, concat_axis=0, tiled=True)]
    all_to_all x1, waiting for transfers between devices: 8.24 us -> 6.1 us  [local(): found = lax.all_to_all(asked, 'x', split_axis=0, concat_axis=0, tiled=True)]
    all_to_all x1, blocking collectives: 8.96 us -> 10.4 us  [local(): lax.all_to_all(read_copies, 'x', split_axis=0, concat_axis=0, tiled=True)]
  transfers between devices with their start and end apart: 12 -> 12, of which waited for: 7 -> 7; matrix products, arithmetic and copies ran while one was open for 4% -> 3% of each run, Pallas kernels for 2% -> 2%
where the time goes in v7:
time: 135 us; the launch traced here: 134 us
  starting transfers between devices  57.4 us (43%)
  waiting for transfers between devices  33.3 us (25%)
  blocking collectives  25.5 us (19%)
  Pallas kernels  10.3 us (8%)
  other arithmetic  3.25 us (2%)
  local copies, waits for them, and re-layouts  3.17 us (2%)
    ppermute x5, starting transfers between devices, swapped(): return lax.ppermute(value, axis, [(i, i ^ 1) for i in range(size)])  21.5 us
    all_to_all x1, blocking collectives, local(): lax.all_to_all(part, 'z', split_axis=0, concat_axis=0, tiled=True)  15.1 us
    all_to_all x1, waiting for transfers between devices, local(): tok = lax.all_to_all(to_z, 'z', split_axis=0, concat_axis=0, tiled=True)  13.7 us
    all_to_all x1, blocking collectives, local(): lax.all_to_all(read_copies, 'x', split_axis=0, concat_axis=0, tiled=True)  10.4 us
    all_to_all x1, starting transfers between devices, local(): tok = lax.all_to_all(to_z, 'z', split_axis=0, concat_axis=0, tiled=True)  9.47 us
    ppermute x3, starting transfers between devices, shifted(): lax.ppermute(value, axis, [(i, (i + shift) % size) for i in range(size)])  9.32 us
    all_to_all x1, waiting for transfers between devices, local(): lax.all_to_all(owner_part, 'y', split_axis=0, concat_axis=0, tiled=True)  9.08 us
    all_to_all x1, starting transfers between devices, local(): lax.all_to_all(owner_part, 'y', split_axis=0, concat_axis=0, tiled=True)  6.82 us
  transfers between devices with their start and end apart: 12, of which 7 were waited for; matrix products, arithmetic and copies ran while one was open for 3% of the time, Pallas kernels for 2%

profile of v7, /device:TPU:1, one launch (start us, length us, event | category | flops | bytes accessed | tf_op | source)
XLA Modules:
  0.0 133.8 jit_solution(15436665602635764625)
XLA Ops:
  0.6 4.8 %collective-permute-start.4 = (bf16[2,896,512]{2,1,0:T(8,128)(2,1)}, bf16[2,896,512]{2,1,0:T(8,128)(2,1)}, u32[]{:S(2)}, u32[]{:S(2)}) collective-permute-start(bf16[2,896,512]{2,1,0:T(8,128)(2,1)} %w_own.1), channel_id=1, source_target_pairs={{0,1},{1,0},{2,3},{3,2},{4,5},{5,4},{6,7},{7,6},{8,9},{9,8},{10,11... | collective-permute-start | bytes 5505032 | tf_op jit(solution)/shard_map/ppermute | solution.py:37
  5.5 1.5 %broadcast_in_dim.7 = bf16[8,16,896]{2,1,0:T(8,128)(2,1)} broadcast(bf16[16,896]{1,0:T(8,128)(2,1)} %bitcast.25), dimensions={1,2} | broadcast | bytes 258048 | tf_op jit(solution)/shard_map/broadcast_in_dim | solution.py:212
  7.0 6.8 %all-to-all-start = ((bf16[8,16,896]{2,1,0:T(8,128)(2,1)}), bf16[8,16,896]{2,1,0:T(8,128)(2,1)S(1)}, u32[]{:S(2)}, u32[]{:S(2)}) async-start(bf16[8,16,896]{2,1,0:T(8,128)(2,1)} %broadcast_in_dim.7), calls=%async_computation | async-start | bytes 458752 | tf_op jit(solution)/shard_map/all_to_all | solution.py:213
  13.8 4.4 %collective-permute-start.2 = (s32[2,2]{1,0:T(2,128)}, s32[2,2]{1,0:T(2,128)S(1)}, u32[]{:S(2)}, u32[]{:S(2)}) collective-permute-start(s32[2,2]{1,0:T(2,128)} %refs_0_.1), channel_id=1, source_target_pairs={{0,384},{128,0},{256,128},{384,256},{1,385},{129,1},{257,129},{385... | collective-permute-start | bytes 56 | tf_op jit(solution)/shard_map/ppermute | solution.py:33
  18.2 2.4 %collective-permute-start.1 = (s32[2,2]{1,0:T(2,128)}, s32[2,2]{1,0:T(2,128)S(1)}, u32[]{:S(2)}, u32[]{:S(2)}) collective-permute-start(s32[2,2]{1,0:T(2,128)} %refs_0_.1), channel_id=1, source_target_pairs={{0,256},{128,384},{256,0},{384,128},{1,257},{129,385},{257,1},{385... | collective-permute-start | bytes 56 | tf_op jit(solution)/shard_map/ppermute | solution.py:33
  20.6 2.5 %collective-permute-start = (s32[2,2]{1,0:T(2,128)}, s32[2,2]{1,0:T(2,128)S(1)}, u32[]{:S(2)}, u32[]{:S(2)}) collective-permute-start(s32[2,2]{1,0:T(2,128)} %refs_0_.1), channel_id=1, source_target_pairs={{0,128},{128,256},{256,384},{384,0},{1,129},{129,257},{257,385},{3... | collective-permute-start | bytes 56 | tf_op jit(solution)/shard_map/ppermute | solution.py:33
  24.2 2.3 %collective-permute-done.refs_1_ = s32[2,2]{1,0:T(2,128)S(1)} collective-permute-done((s32[2,2]{1,0:T(2,128)}, s32[2,2]{1,0:T(2,128)S(1)}, u32[]{:S(2)}, u32[]{:S(2)}) %collective-permute-start) | collective-permute-done | bytes 48 | tf_op jit(solution)/shard_map/ppermute | solution.py:33
  26.5 4.7 %collective-permute-start.3 = (bf16[8,16,896]{2,1,0:T(8,128)(2,1)S(1)}, bf16[8,16,896]{2,1,0:T(8,128)(2,1)S(1)}, u32[]{:S(2)}, u32[]{:S(2)}) collective-permute-start(bf16[8,16,896]{2,1,0:T(8,128)(2,1)S(1)} %all-to-all-done.refs_4_), channel_id=1, source_target_pairs={{0,8},{8,0},{1,9},{9,1},{2,10},{10,2},{3,11},{11,3},{4,12},{12,4},... | collective-permute-start | bytes 688136 | tf_op jit(solution)/shard_map/ppermute | solution.py:37
  33.0 1.5 %pick.1 = bf16[4,4,16,896]{3,2,1,0:T(8,128)(2,1)} custom-call(s32[2]{0:T(128)S(1)} %pad_add_fusion.at_ref, s32[2,2]{1,0:T(2,128)S(1)} %copy-done.1, s32[2,2]{1,0:T(2,128)S(1)} %collective-permute-done.refs_1_, s32[2,2]{1,0:T(2,128)S(1)} %collective-permute-done.1.refs_2_, s32[2,2]{1,0:T(2,128)S(1)} %collective-permute-done.2.refs_3_, ...), custom_call_target="tpu_custom_call" | custom-call | tf_op jit(solution)/shard_map/pick/pallas_call | solution.py:151
  34.5 3.5 %all-to-all-start.1 = ((bf16[4,4,16,896]{3,2,1,0:T(8,128)(2,1)}), bf16[4,4,16,896]{3,2,1,0:T(8,128)(2,1)S(1)}, u32[]{:S(2)}, u32[]{:S(2)}) async-start(bf16[4,4,16,896]{3,2,1,0:T(8,128)(2,1)} %pick.1), calls=%async_computation.1 | async-start | bytes 917504 | tf_op jit(solution)/shard_map/all_to_all | solution.py:221
  38.2 2.1 %collective-permute-start.5 = (bf16[128,512]{1,0:T(8,128)(2,1)S(1)}, bf16[128,512]{1,0:T(8,128)(2,1)S(1)}, u32[]{:S(2)}, u32[]{:S(2)}) collective-permute-start(bf16[128,512]{1,0:T(8,128)(2,1)S(1)} %pad_maximum_fusion), channel_id=1, source_target_pairs={{0,1},{1,0},{2,3},{3,2},{4,5},{5,4},{6,7},{7,6},{8,9},{9,8},{10,11... | collective-permute-start | bytes 393224 | tf_op jit(solution)/shard_map/ppermute | solution.py:37
  40.4 6.1 %all-to-all-done.1.from_ref = bf16[4,4,16,896]{3,2,1,0:T(8,128)(2,1)S(1)} async-done(((bf16[4,4,16,896]{3,2,1,0:T(8,128)(2,1)}), bf16[4,4,16,896]{3,2,1,0:T(8,128)(2,1)S(1)}, u32[]{:S(2)}, u32[]{:S(2)}) %all-to-all-start.1) | async-done | bytes 458784 | tf_op jit(solution)/shard_map/all_to_all | solution.py:221
  46.5 1.4 %spread.1 = bf16[8,2,16,896]{3,2,1,0:T(8,128)(2,1)} custom-call(s32[2,2]{1,0:T(2,128)S(1)} %copy-done.2, bf16[4,4,16,896]{3,2,1,0:T(8,128)(2,1)S(1)} %all-to-all-done.1.from_ref), custom_call_target="tpu_custom_call" | custom-call | tf_op jit(solution)/shard_map/spread/pallas_call | solution.py:151
  47.8 9.5 %all-to-all-start.2 = ((bf16[8,2,16,896]{3,2,1,0:T(8,128)(2,1)}), bf16[8,2,16,896]{3,2,1,0:T(8,128)(2,1)S(1)}, u32[]{:S(2)}, u32[]{:S(2)}) async-start(bf16[8,2,16,896]{3,2,1,0:T(8,128)(2,1)} %spread.1), calls=%async_computation.2 | async-start | bytes 917504 | tf_op jit(solution)/shard_map/all_to_all | solution.py:229
  58.1 13.7 %all-to-all-done.2.tok = bf16[8,2,16,896]{3,2,1,0:T(8,128)(2,1)S(1)} async-done(((bf16[8,2,16,896]{3,2,1,0:T(8,128)(2,1)}), bf16[8,2,16,896]{3,2,1,0:T(8,128)(2,1)S(1)}, u32[]{:S(2)}, u32[]{:S(2)}) %all-to-all-start.2) | async-done | bytes 458784 | tf_op jit(solution)/shard_map/all_to_all | solution.py:229
  71.8 6.4 %attention.1 = (bf16[8,2,16,896]{3,2,1,0:T(8,128)(2,1)S(1)}, bf16[64,512]{1,0:T(8,128)(2,1)S(1)}, bf16[64,512]{1,0:T(8,128)(2,1)S(1)}) custom-call(bf16[8,2,16,896]{3,2,1,0:T(8,128)(2,1)S(1)} %all-to-all-done.2.tok, bf16[2,896,512]{2,1,0:T(8,128)(2,1)S(1)} %copy-done.3, bf16[64,512]{1,0:T(8,128)(2,1)S(1)} %get-tuple-element.49.q_own, ...), custom_call_target="tpu_custom_call" | custom-call | flops 2100000000 | bytes 6000000 | tf_op jit(solution)/shard_map/attention/pallas_call | solution.py:164
  78.1 15.1 %all_to_all.30 = bf16[8,2,16,896]{3,2,1,0:T(8,128)(2,1)S(1)} all-to-all(bf16[8,2,16,896]{3,2,1,0:T(8,128)(2,1)S(1)} %get-tuple-element.28), channel_id=1, replica_groups=mesh['x'=4,'y'=8,'c'=2,'z'=8] {'z'}, dimensions={0} | all-to-all | bytes 917504 | tf_op jit(solution)/shard_map/all_to_all | solution.py:235
  93.3 10.4 %all_to_all.31.refs_4_ = bf16[4,4,16,896]{3,2,1,0:T(8,128)(2,1)S(1)} all-to-all(bf16[4,4,16,896]{3,2,1,0:T(8,128)(2,1)S(1)} %broadcast_in_dim.8), channel_id=1, replica_groups=mesh['x'=4,'y'=8,'c'=2,'z'=8] {'x'}, dimensions={0} | all-to-all | bytes 917504 | tf_op jit(solution)/shard_map/all_to_all | solution.py:240
  103.7 1.0 owner_sums.1
  104.8 7.7 %collective-permute-start.6 = (bf16[8,16,896]{2,1,0:T(8,128)(2,1)S(1)}, bf16[8,16,896]{2,1,0:T(8,128)(2,1)S(1)}, u32[]{:S(2)}, u32[]{:S(2)}) collective-permute-start(bf16[8,16,896]{2,1,0:T(8,128)(2,1)S(1)} %get-tuple-element.30), channel_id=1, source_target_pairs={{0,8},{8,0},{1,9},{9,1},{2,10},{10,2},{3,11},{11,3},{4,12},{12,4},... | collective-permute-start | bytes 688136 | tf_op jit(solution)/shard_map/ppermute | solution.py:37
  112.5 1.1 collective-permute-done.6
  114.3 2.2 %collective-permute-start.7 = (bf16[64,512]{1,0:T(8,128)(2,1)S(1)}, bf16[64,512]{1,0:T(8,128)(2,1)S(1)}, u32[]{:S(2)}, u32[]{:S(2)}) collective-permute-start(bf16[64,512]{1,0:T(8,128)(2,1)S(1)} %get-tuple-element.32), channel_id=1, source_target_pairs={{0,1},{1,0},{2,3},{3,2},{4,5},{5,4},{6,7},{7,6},{8,9},{9,8},{10,11... | collective-permute-start | bytes 196616 | tf_op jit(solution)/shard_map/ppermute | solution.py:37
  116.5 6.8 %all-to-all-start.5 = ((bf16[8,16,896]{2,1,0:T(8,128)(2,1)}), bf16[8,16,896]{2,1,0:T(8,128)(2,1)S(1)}, u32[]{:S(2)}, u32[]{:S(2)}) async-start(bf16[8,16,896]{2,1,0:T(8,128)(2,1)} %add_convert_fusion), calls=%async_computation.5 | async-start | bytes 458752 | tf_op jit(solution)/shard_map/all_to_all | solution.py:250
  124.0 9.1 %all-to-all-done.5 = bf16[8,16,896]{2,1,0:T(8,128)(2,1)S(1)} async-done(((bf16[8,16,896]{2,1,0:T(8,128)(2,1)}), bf16[8,16,896]{2,1,0:T(8,128)(2,1)S(1)}, u32[]{:S(2)}, u32[]{:S(2)}) %all-to-all-start.5) | async-done | bytes 229408 | tf_op jit(solution)/shard_map/all_to_all | solution.py:250
  (33 shorter events, 6.0 us)
Async XLA Ops:
  0.6 39.6 %copy-start = (s32[2,2]{1,0:T(2,128)S(1)}, s32[2,2]{1,0:T(2,128)}, u32[]{:S(2)}) copy-start(s32[2,2]{1,0:T(2,128)} %param.11) | copy-start | bytes 52
  0.6 47.2 %collective-permute-start.4 = (bf16[2,896,512]{2,1,0:T(8,128)(2,1)}, bf16[2,896,512]{2,1,0:T(8,128)(2,1)}, u32[]{:S(2)}, u32[]{:S(2)}) collective-permute-start(bf16[2,896,512]{2,1,0:T(8,128)(2,1)} %w_own.1), channel_id=1, source_target_pairs={{0,1},{1,0},{2,3},{3,2},{4,5},{5,4},{6,7},{7,6},{8,9},{9,8},{10,11... | collective-permute-start | bytes 5505032 | tf_op jit(solution)/shard_map/ppermute | solution.py:37
  5.5 41.0 %copy-start.2 = (s32[2,2]{1,0:T(2,128)S(1)}, s32[2,2]{1,0:T(2,128)}, u32[]{:S(2)}) copy-start(s32[2,2]{1,0:T(2,128)} %refs_0_.1) | copy-start | bytes 52
  7.0 19.5 %all-to-all-start = ((bf16[8,16,896]{2,1,0:T(8,128)(2,1)}), bf16[8,16,896]{2,1,0:T(8,128)(2,1)S(1)}, u32[]{:S(2)}, u32[]{:S(2)}) async-start(bf16[8,16,896]{2,1,0:T(8,128)(2,1)} %broadcast_in_dim.7), calls=%async_computation | async-start | bytes 458752 | tf_op jit(solution)/shard_map/all_to_all | solution.py:213
  13.8 10.4 %collective-permute-start.2 = (s32[2,2]{1,0:T(2,128)}, s32[2,2]{1,0:T(2,128)S(1)}, u32[]{:S(2)}, u32[]{:S(2)}) collective-permute-start(s32[2,2]{1,0:T(2,128)} %refs_0_.1), channel_id=1, source_target_pairs={{0,384},{128,0},{256,128},{384,256},{1,385},{129,1},{257,129},{385... | collective-permute-start | bytes 56 | tf_op jit(solution)/shard_map/ppermute | solution.py:33
  18.2 6.0 %collective-permute-start.1 = (s32[2,2]{1,0:T(2,128)}, s32[2,2]{1,0:T(2,128)S(1)}, u32[]{:S(2)}, u32[]{:S(2)}) collective-permute-start(s32[2,2]{1,0:T(2,128)} %refs_0_.1), channel_id=1, source_target_pairs={{0,256},{128,384},{256,0},{384,128},{1,257},{129,385},{257,1},{385... | collective-permute-start | bytes 56 | tf_op jit(solution)/shard_map/ppermute | solution.py:33
  20.6 5.9 %collective-permute-start = (s32[2,2]{1,0:T(2,128)}, s32[2,2]{1,0:T(2,128)S(1)}, u32[]{:S(2)}, u32[]{:S(2)}) collective-permute-start(s32[2,2]{1,0:T(2,128)} %refs_0_.1), channel_id=1, source_target_pairs={{0,128},{128,256},{256,384},{384,0},{1,129},{129,257},{257,385},{3... | collective-permute-start | bytes 56 | tf_op jit(solution)/shard_map/ppermute | solution.py:33
  26.5 5.8 %collective-permute-start.3 = (bf16[8,16,896]{2,1,0:T(8,128)(2,1)S(1)}, bf16[8,16,896]{2,1,0:T(8,128)(2,1)S(1)}, u32[]{:S(2)}, u32[]{:S(2)}) collective-permute-start(bf16[8,16,896]{2,1,0:T(8,128)(2,1)S(1)} %all-to-all-done.refs_4_), channel_id=1, source_target_pairs={{0,8},{8,0},{1,9},{9,1},{2,10},{10,2},{3,11},{11,3},{4,12},{12,4},... | collective-permute-start | bytes 688136 | tf_op jit(solution)/shard_map/ppermute | solution.py:37
  32.3 0.7 copy-start.1
  34.5 12.0 %all-to-all-start.1 = ((bf16[4,4,16,896]{3,2,1,0:T(8,128)(2,1)}), bf16[4,4,16,896]{3,2,1,0:T(8,128)(2,1)S(1)}, u32[]{:S(2)}, u32[]{:S(2)}) async-start(bf16[4,4,16,896]{3,2,1,0:T(8,128)(2,1)} %pick.1), calls=%async_computation.1 | async-start | bytes 917504 | tf_op jit(solution)/shard_map/all_to_all | solution.py:221
  38.0 33.8 %copy-start.3 = (bf16[2,896,512]{2,1,0:T(8,128)(2,1)S(1)}, bf16[2,896,512]{2,1,0:T(8,128)(2,1)}, u32[]{:S(2)}) copy-start(bf16[2,896,512]{2,1,0:T(8,128)(2,1)} %w_own.1) | copy-start | bytes 5505028
  38.2 9.6 %collective-permute-start.5 = (bf16[128,512]{1,0:T(8,128)(2,1)S(1)}, bf16[128,512]{1,0:T(8,128)(2,1)S(1)}, u32[]{:S(2)}, u32[]{:S(2)}) collective-permute-start(bf16[128,512]{1,0:T(8,128)(2,1)S(1)} %pad_maximum_fusion), channel_id=1, source_target_pairs={{0,1},{1,0},{2,3},{3,2},{4,5},{5,4},{6,7},{7,6},{8,9},{9,8},{10,11... | collective-permute-start | bytes 393224 | tf_op jit(solution)/shard_map/ppermute | solution.py:37
  47.8 23.9 %all-to-all-start.2 = ((bf16[8,2,16,896]{3,2,1,0:T(8,128)(2,1)}), bf16[8,2,16,896]{3,2,1,0:T(8,128)(2,1)S(1)}, u32[]{:S(2)}, u32[]{:S(2)}) async-start(bf16[8,2,16,896]{3,2,1,0:T(8,128)(2,1)} %spread.1), calls=%async_computation.2 | async-start | bytes 917504 | tf_op jit(solution)/shard_map/all_to_all | solution.py:229
  104.8 8.8 %collective-permute-start.6 = (bf16[8,16,896]{2,1,0:T(8,128)(2,1)S(1)}, bf16[8,16,896]{2,1,0:T(8,128)(2,1)S(1)}, u32[]{:S(2)}, u32[]{:S(2)}) collective-permute-start(bf16[8,16,896]{2,1,0:T(8,128)(2,1)S(1)} %get-tuple-element.30), channel_id=1, source_target_pairs={{0,8},{8,0},{1,9},{9,1},{2,10},{10,2},{3,11},{11,3},{4,12},{12,4},... | collective-permute-start | bytes 688136 | tf_op jit(solution)/shard_map/ppermute | solution.py:37
  114.3 9.0 %collective-permute-start.7 = (bf16[64,512]{1,0:T(8,128)(2,1)S(1)}, bf16[64,512]{1,0:T(8,128)(2,1)S(1)}, u32[]{:S(2)}, u32[]{:S(2)}) collective-permute-start(bf16[64,512]{1,0:T(8,128)(2,1)S(1)} %get-tuple-element.32), channel_id=1, source_target_pairs={{0,1},{1,0},{2,3},{3,2},{4,5},{5,4},{6,7},{7,6},{8,9},{9,8},{10,11... | collective-permute-start | bytes 196616 | tf_op jit(solution)/shard_map/ppermute | solution.py:37
  116.5 16.6 %all-to-all-start.5 = ((bf16[8,16,896]{2,1,0:T(8,128)(2,1)}), bf16[8,16,896]{2,1,0:T(8,128)(2,1)S(1)}, u32[]{:S(2)}, u32[]{:S(2)}) async-start(bf16[8,16,896]{2,1,0:T(8,128)(2,1)} %add_convert_fusion), calls=%async_computation.5 | async-start | bytes 458752 | tf_op jit(solution)/shard_map/all_to_all | solution.py:250

commit v8 on v7

--- a/solution.py
+++ b/solution.py
@@ -47,6 +47,17 @@
     return lax.rem(at_ref[0] - distance + NX, NX)
 
 
+def copies_kernel(from_ref, out_ref, sems):
+    copies = [
+        pltpu.make_async_copy(from_ref.at[0], out_ref.at[at], sems.at[at])
+        for at in range(out_ref.shape[0])
+    ]
+    for copy in copies:
+        copy.start()
+    for copy in copies:
+        copy.wait()
+
+
 def pick_kernel(at_ref, *refs):
     near, (mine_ref, theirs_ref, out_ref, sems) = refs[:NX], refs[NX:]
     core, reads = at_ref[1], out_ref.shape[1]
@@ -100,17 +111,14 @@
 
 
 def attention_kernel(
-    tok, w_own, q_own, g_own, q_pair, g_pair, kc, ks, qc, qs, w_far,
-    part, dq_own, dq_pair, dk_all, dv_all, w_pair, sem,
+    tok, w_own, q_own, g_own, q_pair, g_pair, kc, ks, qc, qs, w_pair,
+    part, dq_own, dq_pair, dk_all, dv_all,
 ):
-    fetch = pltpu.make_async_copy(w_far, w_pair, sem)
-    fetch.start()
     scale = 1.0 / math.sqrt(HEAD)
     half = HEAD // 2
     width = w_own.shape[2]
     rows = jnp.concatenate([tok[:, n].reshape(NLEN, DE) for n in range(NEIGH)], axis=0)
     projected = [(dot(rows, w_own[0]), dot(rows, w_own[1]).astype(BF16))]
-    fetch.wait()
     projected.append((dot(rows, w_pair[0]), dot(rows, w_pair[1]).astype(BF16)))
     key_cos, key_sin, query_cos, query_sin = kc[...], ks[...], qc[...], qs[...]
     for turn, (q, g, dq) in enumerate(((q_own, g_own, dq_own), (q_pair, g_pair, dq_pair))):
@@ -160,7 +168,7 @@
 
 
 def attention(*operands):
-    _, depth, width = operands[1].shape
+    width = operands[1].shape[2]
     return pl.pallas_call(
         attention_kernel,
         out_shape=(
@@ -168,13 +176,11 @@
             jax.ShapeDtypeStruct((SPAN, width), BF16),
             jax.ShapeDtypeStruct((SPAN, width), BF16),
         ),
-        in_specs=[VMEM] * (len(operands) - 1) + [ANY],
+        in_specs=[VMEM] * len(operands),
         out_specs=(VMEM, VMEM, VMEM),
         scratch_shapes=[
             pltpu.VMEM((NEIGH * NLEN, 2 * width), BF16),
             pltpu.VMEM((NEIGH * NLEN, 2 * width), BF16),
-            pltpu.VMEM((2, depth, width), BF16),
-            pltpu.SemaphoreType.DMA,
         ],
         compiler_params=pltpu.CompilerParams(vmem_limit_bytes=40 << 20),
         cost_estimate=pl.CostEstimate(
@@ -208,8 +214,12 @@
     query_cos, query_sin = rotary_tables(jnp.arange(SPAN, dtype=jnp.int32))
 
     at = jnp.stack([x_at, c_at])
-    near = [neighbour_ids] + [shifted(neighbour_ids, "x", NX, s) for s in range(1, NX)]
-    copies = jnp.broadcast_to(encodings, (NY, ROWS, DE))
+    ids = jnp.maximum(neighbour_ids, 0)
+    near = [ids] + [shifted(neighbour_ids, "x", NX, s) for s in range(1, NX)]
+    copies = on_core(
+        copies_kernel, "copies", jax.ShapeDtypeStruct((NY, ROWS, DE), BF16), (),
+        encodings, scratch=[pltpu.SemaphoreType.DMA((NY,))], space=ANY,
+    )
     over_y = lax.all_to_all(copies, "y", split_axis=0, concat_axis=0, tiled=True)
     over_y, near, other = lax.optimization_barrier((over_y, near, other))
     beside = swapped(over_y, "c", NC)
@@ -221,7 +231,7 @@
     found = lax.all_to_all(asked, "x", split_axis=0, concat_axis=0, tiled=True)
 
     to_z = on_core(
-        spread_kernel, "spread", jax.ShapeDtypeStruct((NZ, NEIGH, ROWS, DE), BF16), (neighbour_ids,),
+        spread_kernel, "spread", jax.ShapeDtypeStruct((NZ, NEIGH, ROWS, DE), BF16), (near[0],),
         found,
     )
     from_pair = swapped(other, "z", NZ)
@@ -237,7 +247,10 @@
     read_sum = jnp.sum(from_heads.astype(F32), axis=0).astype(BF16).reshape(reads, ROWS, DE)
 
     read_copies = jnp.broadcast_to(read_sum, (NX, *block))
+    read_copies, dq_pair = lax.optimization_barrier((read_copies, dq_pair))
     read_x = lax.all_to_all(read_copies, "x", split_axis=0, concat_axis=0, tiled=True)
+    dq_back = swapped(dq_pair, "z", NZ)
+    read_x, dq_back = lax.optimization_barrier((read_x, dq_back))
     owners = (NY, ROWS, DE)
     mine, theirs = on_core(
         owner_kernel, "owner_sums",
@@ -245,8 +258,6 @@
         (at, *near), read_x, scratch=[pltpu.VMEM((NC * NY, ROWS, DE), F32)],
     )
     owner_part = (mine + swapped(theirs, "c", NC).astype(F32)).astype(BF16)
-    owner_part, dq_pair = lax.optimization_barrier((owner_part, dq_pair))
-    dq_back = swapped(dq_pair, "z", NZ)
     from_y = lax.all_to_all(owner_part, "y", split_axis=0, concat_axis=0, tiled=True)
     owned = jnp.sum(from_y.astype(F32), axis=0)
 

time: 135 us -> 137 us (1.015)
  waiting for transfers between devices: 33.3 us -> 44.7 us
  blocking collectives: 25.5 us -> 15.2 us
    all_to_all x1 -> x0, blocking collectives: 10.4 us -> none  [local(): lax.all_to_all(read_copies, 'x', split_axis=0, concat_axis=0, tiled=True)]
    all_to_all x1, waiting for transfers between devices: 0.01 us -> 7.42 us  [local(): lax.all_to_all(copies, 'y', split_axis=0, concat_axis=0, tiled=True)]
    all_to_all x0 -> x1, starting transfers between devices: none -> 3.46 us  [local(): lax.all_to_all(read_copies, 'x', split_axis=0, concat_axis=0, tiled=True)]
    all_to_all x1, starting transfers between devices: 6.82 us -> 3.4 us  [local(): lax.all_to_all(owner_part, 'y', split_axis=0, concat_axis=0, tiled=True)]
    ppermute x5, waiting for transfers between devices: 2.09 us -> 5.16 us  [swapped(): return lax.ppermute(value, axis, [(i, i ^ 1) for i in range(size)])]
    ppermute x3, waiting for transfers between devices: 2.32 us -> 0.01 us  [shifted(): lax.ppermute(value, axis, [(i, (i + shift) % size) for i in range(size)])]
    all_to_all x1, waiting for transfers between devices: 9.08 us -> 10.8 us  [local(): lax.all_to_all(owner_part, 'y', split_axis=0, concat_axis=0, tiled=True)]
    all_to_all x0 -> x1, waiting for transfers between devices: none -> 1.54 us  [local(): lax.all_to_all(read_copies, 'x', split_axis=0, concat_axis=0, tiled=True)]
  transfers between devices with their start and end apart: 12 -> 13, of which waited for: 7 -> 8; matrix products, arithmetic and copies ran while one was open for 3% -> 3% of each run, Pallas kernels for 2% -> 3%
where the time goes in v8:
time: 137 us; the launch traced here: 136 us
  starting transfers between devices  57.6 us (42%)
  waiting for transfers between devices  44.7 us (33%)
  blocking collectives  15.2 us (11%)
  Pallas kernels  11.6 us (8%)
  other arithmetic  3.94 us (3%)
  local copies, waits for them, and re-layouts  2.54 us (2%)
    ppermute x5, starting transfers between devices, swapped(): return lax.ppermute(value, axis, [(i, i ^ 1) for i in range(size)])  21.3 us
    all_to_all x1, blocking collectives, local(): lax.all_to_all(part, 'z', split_axis=0, concat_axis=0, tiled=True)  15.2 us
    all_to_all x1, waiting for transfers between devices, local(): tok = lax.all_to_all(to_z, 'z', split_axis=0, concat_axis=0, tiled=True)  13.9 us
    all_to_all x1, waiting for transfers between devices, local(): lax.all_to_all(owner_part, 'y', split_axis=0, concat_axis=0, tiled=True)  10.8 us
    ppermute x3, starting transfers between devices, shifted(): lax.ppermute(value, axis, [(i, (i + shift) % size) for i in range(size)])  9.94 us
    all_to_all x1, starting transfers between devices, local(): tok = lax.all_to_all(to_z, 'z', split_axis=0, concat_axis=0, tiled=True)  9.13 us
    all_to_all x1, waiting for transfers between devices, local(): lax.all_to_all(copies, 'y', split_axis=0, concat_axis=0, tiled=True)  7.42 us
    pallas_call x1, Pallas kernels, attention(): pl.pallas_call(attention_kernel, out_shape=(jax.ShapeDtypeStruct((NZ, NEI...  6.9 us
  transfers between devices with their start and end apart: 13, of which 8 were waited for; matrix products, arithmetic and copies ran while one was open for 3% of the time, Pallas kernels for 3%

profile of v8, /device:TPU:1, one launch (start us, length us, event | category | flops | bytes accessed | tf_op | source)
XLA Modules:
  0.0 136.4 jit_solution(12986631763476638597)
XLA Ops:
  0.6 4.8 %collective-permute-start.4 = (bf16[2,896,512]{2,1,0:T(8,128)(2,1)}, bf16[2,896,512]{2,1,0:T(8,128)(2,1)}, u32[]{:S(2)}, u32[]{:S(2)}) collective-permute-start(bf16[2,896,512]{2,1,0:T(8,128)(2,1)} %w_own.1), channel_id=1, source_target_pairs={{0,1},{1,0},{2,3},{3,2},{4,5},{5,4},{6,7},{7,6},{8,9},{9,8},{10,11... | collective-permute-start | bytes 5505032 | tf_op jit(solution)/shard_map/ppermute | solution.py:37
  5.5 3.1 %collective-permute-start = (s32[2,2]{1,0:T(2,128)}, s32[2,2]{1,0:T(2,128)S(1)}, u32[]{:S(2)}, u32[]{:S(2)}) collective-permute-start(s32[2,2]{1,0:T(2,128)} %param.10), channel_id=1, source_target_pairs={{0,128},{128,256},{256,384},{384,0},{1,129},{129,257},{257,385},{3... | collective-permute-start | bytes 56 | tf_op jit(solution)/shard_map/ppermute | solution.py:33
  8.6 3.4 %collective-permute-start.2 = (s32[2,2]{1,0:T(2,128)}, s32[2,2]{1,0:T(2,128)S(1)}, u32[]{:S(2)}, u32[]{:S(2)}) collective-permute-start(s32[2,2]{1,0:T(2,128)} %param.10), channel_id=1, source_target_pairs={{0,384},{128,0},{256,128},{384,256},{1,385},{129,1},{257,129},{385... | collective-permute-start | bytes 56 | tf_op jit(solution)/shard_map/ppermute | solution.py:33
  12.0 3.4 %collective-permute-start.1 = (s32[2,2]{1,0:T(2,128)}, s32[2,2]{1,0:T(2,128)S(1)}, u32[]{:S(2)}, u32[]{:S(2)}) collective-permute-start(s32[2,2]{1,0:T(2,128)} %param.10), channel_id=1, source_target_pairs={{0,256},{128,384},{256,0},{384,128},{1,257},{129,385},{257,1},{385... | collective-permute-start | bytes 56 | tf_op jit(solution)/shard_map/ppermute | solution.py:33
  17.0 6.8 %all-to-all-start = ((bf16[8,16,896]{2,1,0:T(8,128)(2,1)}), bf16[8,16,896]{2,1,0:T(8,128)(2,1)S(1)}, u32[]{:S(2)}, u32[]{:S(2)}) async-start(bf16[8,16,896]{2,1,0:T(8,128)(2,1)} %copies.1), calls=%async_computation | async-start | bytes 458752 | tf_op jit(solution)/shard_map/all_to_all | solution.py:223
  25.5 7.4 %all-to-all-done.refs_4_ = bf16[8,16,896]{2,1,0:T(8,128)(2,1)S(1)} async-done(((bf16[8,16,896]{2,1,0:T(8,128)(2,1)}), bf16[8,16,896]{2,1,0:T(8,128)(2,1)S(1)}, u32[]{:S(2)}, u32[]{:S(2)}) %all-to-all-start) | async-done | bytes 229408 | tf_op jit(solution)/shard_map/all_to_all | solution.py:223
  32.9 5.0 %collective-permute-start.3 = (bf16[8,16,896]{2,1,0:T(8,128)(2,1)S(1)}, bf16[8,16,896]{2,1,0:T(8,128)(2,1)S(1)}, u32[]{:S(2)}, u32[]{:S(2)}) collective-permute-start(bf16[8,16,896]{2,1,0:T(8,128)(2,1)S(1)} %all-to-all-done.refs_4_), channel_id=1, source_target_pairs={{0,8},{8,0},{1,9},{9,1},{2,10},{10,2},{3,11},{11,3},{4,12},{12,4},... | collective-permute-start | bytes 688136 | tf_op jit(solution)/shard_map/ppermute | solution.py:37
  39.0 1.5 %pick.1 = bf16[4,4,16,896]{3,2,1,0:T(8,128)(2,1)} custom-call(s32[2]{0:T(128)S(1)} %pad_add_fusion.at_ref, s32[2,2]{1,0:T(2,128)S(1)} %broadcast_maximum_fusion.refs_0_.ids_ref, s32[2,2]{1,0:T(2,128)S(1)} %collective-permute-done.refs_1_, s32[2,2]{1,0:T(2,128)S(1)} %collective-permute-done.1.refs_2_, s32[2,2]{1,0:T(2,128)S(1)} %collective-permute-done.2.refs_3_, ...), custom_call_target="tpu_custom_call" | custom-call | tf_op jit(solution)/shard_map/pick/pallas_call | solution.py:159
  40.5 3.5 %all-to-all-start.1 = ((bf16[4,4,16,896]{3,2,1,0:T(8,128)(2,1)}), bf16[4,4,16,896]{3,2,1,0:T(8,128)(2,1)S(1)}, u32[]{:S(2)}, u32[]{:S(2)}) async-start(bf16[4,4,16,896]{3,2,1,0:T(8,128)(2,1)} %pick.1), calls=%async_computation.1 | async-start | bytes 917504 | tf_op jit(solution)/shard_map/all_to_all | solution.py:231
  44.2 2.3 %collective-permute-start.5 = (bf16[128,512]{1,0:T(8,128)(2,1)S(1)}, bf16[128,512]{1,0:T(8,128)(2,1)S(1)}, u32[]{:S(2)}, u32[]{:S(2)}) collective-permute-start(bf16[128,512]{1,0:T(8,128)(2,1)S(1)} %pad_maximum_fusion), channel_id=1, source_target_pairs={{0,1},{1,0},{2,3},{3,2},{4,5},{5,4},{6,7},{7,6},{8,9},{9,8},{10,11... | collective-permute-start | bytes 393224 | tf_op jit(solution)/shard_map/ppermute | solution.py:37
  46.6 5.9 %all-to-all-done.1.from_ref = bf16[4,4,16,896]{3,2,1,0:T(8,128)(2,1)S(1)} async-done(((bf16[4,4,16,896]{3,2,1,0:T(8,128)(2,1)}), bf16[4,4,16,896]{3,2,1,0:T(8,128)(2,1)S(1)}, u32[]{:S(2)}, u32[]{:S(2)}) %all-to-all-start.1) | async-done | bytes 458784 | tf_op jit(solution)/shard_map/all_to_all | solution.py:231
  52.5 1.4 spread.1
  53.9 9.1 %all-to-all-start.2 = ((bf16[8,2,16,896]{3,2,1,0:T(8,128)(2,1)}), bf16[8,2,16,896]{3,2,1,0:T(8,128)(2,1)S(1)}, u32[]{:S(2)}, u32[]{:S(2)}) async-start(bf16[8,2,16,896]{3,2,1,0:T(8,128)(2,1)} %spread.1), calls=%async_computation.2 | async-start | bytes 917504 | tf_op jit(solution)/shard_map/all_to_all | solution.py:239
  63.8 13.9 %all-to-all-done.2.tok = bf16[8,2,16,896]{3,2,1,0:T(8,128)(2,1)S(1)} async-done(((bf16[8,2,16,896]{3,2,1,0:T(8,128)(2,1)}), bf16[8,2,16,896]{3,2,1,0:T(8,128)(2,1)S(1)}, u32[]{:S(2)}, u32[]{:S(2)}) %all-to-all-start.2) | async-done | bytes 458784 | tf_op jit(solution)/shard_map/all_to_all | solution.py:239
  77.7 6.9 %attention.1 = (bf16[8,2,16,896]{3,2,1,0:T(8,128)(2,1)S(1)}, bf16[64,512]{1,0:T(8,128)(2,1)S(1)}, bf16[64,512]{1,0:T(8,128)(2,1)S(1)}) custom-call(bf16[8,2,16,896]{3,2,1,0:T(8,128)(2,1)S(1)} %all-to-all-done.2.tok, bf16[2,896,512]{2,1,0:T(8,128)(2,1)S(1)} %copy-done.2, bf16[64,512]{1,0:T(8,128)(2,1)S(1)} %get-tuple-element.53.q_own, ...), custom_call_target="tpu_custom_call" | custom-call | flops 2100000000 | bytes 6000000 | tf_op jit(solution)/shard_map/attention/pallas_call | solution.py:172
  84.6 15.2 %all_to_all.30 = bf16[8,2,16,896]{3,2,1,0:T(8,128)(2,1)S(1)} all-to-all(bf16[8,2,16,896]{3,2,1,0:T(8,128)(2,1)S(1)} %get-tuple-element.30), channel_id=1, replica_groups=mesh['x'=4,'y'=8,'c'=2,'z'=8] {'z'}, dimensions={0} | all-to-all | bytes 917504 | tf_op jit(solution)/shard_map/all_to_all | solution.py:245
  100.7 3.5 %all-to-all-start.4 = ((bf16[4,4,16,896]{3,2,1,0:T(8,128)(2,1)}), bf16[4,4,16,896]{3,2,1,0:T(8,128)(2,1)S(1)}, u32[]{:S(2)}, u32[]{:S(2)}) async-start(bf16[4,4,16,896]{3,2,1,0:T(8,128)(2,1)} %broadcast_in_dim.2), calls=%async_computation.4 | async-start | bytes 917504 | tf_op jit(solution)/shard_map/all_to_all | solution.py:251
  104.1 1.9 %collective-permute-start.6 = (bf16[64,512]{1,0:T(8,128)(2,1)S(1)}, bf16[64,512]{1,0:T(8,128)(2,1)S(1)}, u32[]{:S(2)}, u32[]{:S(2)}) collective-permute-start(bf16[64,512]{1,0:T(8,128)(2,1)S(1)} %get-tuple-element.33), channel_id=1, source_target_pairs={{0,1},{1,0},{2,3},{3,2},{4,5},{5,4},{6,7},{7,6},{8,9},{9,8},{10,11... | collective-permute-start | bytes 196616 | tf_op jit(solution)/shard_map/ppermute | solution.py:37
  106.1 3.1 %collective-permute-done.6 = bf16[64,512]{1,0:T(8,128)(2,1)S(1)} collective-permute-done((bf16[64,512]{1,0:T(8,128)(2,1)S(1)}, bf16[64,512]{1,0:T(8,128)(2,1)S(1)}, u32[]{:S(2)}, u32[]{:S(2)}) %collective-permute-start.6) | collective-permute-done | bytes 65568 | tf_op jit(solution)/shard_map/ppermute | solution.py:37
  109.1 1.5 %all-to-all-done.4.refs_4_ = bf16[4,4,16,896]{3,2,1,0:T(8,128)(2,1)S(1)} async-done(((bf16[4,4,16,896]{3,2,1,0:T(8,128)(2,1)}), bf16[4,4,16,896]{3,2,1,0:T(8,128)(2,1)S(1)}, u32[]{:S(2)}, u32[]{:S(2)}) %all-to-all-start.4) | async-done | bytes 458784 | tf_op jit(solution)/shard_map/all_to_all | solution.py:251
  111.7 7.3 %collective-permute-start.7 = (bf16[8,16,896]{2,1,0:T(8,128)(2,1)S(1)}, bf16[8,16,896]{2,1,0:T(8,128)(2,1)S(1)}, u32[]{:S(2)}, u32[]{:S(2)}) collective-permute-start(bf16[8,16,896]{2,1,0:T(8,128)(2,1)S(1)} %get-tuple-element.37), channel_id=1, source_target_pairs={{0,8},{8,0},{1,9},{9,1},{2,10},{10,2},{3,11},{11,3},{4,12},{12,4},... | collective-permute-start | bytes 688136 | tf_op jit(solution)/shard_map/ppermute | solution.py:37
  119.1 1.1 collective-permute-done.7
  120.9 3.4 %all-to-all-start.5 = ((bf16[8,16,896]{2,1,0:T(8,128)(2,1)}), bf16[8,16,896]{2,1,0:T(8,128)(2,1)S(1)}, u32[]{:S(2)}, u32[]{:S(2)}) async-start(bf16[8,16,896]{2,1,0:T(8,128)(2,1)} %add_convert_fusion), calls=%async_computation.5 | async-start | bytes 458752 | tf_op jit(solution)/shard_map/all_to_all | solution.py:261
  125.0 10.8 %all-to-all-done.5 = bf16[8,16,896]{2,1,0:T(8,128)(2,1)S(1)} async-done(((bf16[8,16,896]{2,1,0:T(8,128)(2,1)}), bf16[8,16,896]{2,1,0:T(8,128)(2,1)S(1)}, u32[]{:S(2)}, u32[]{:S(2)}) %all-to-all-start.5) | async-done | bytes 229408 | tf_op jit(solution)/shard_map/all_to_all | solution.py:261
  (33 shorter events, 9.3 us)
Async XLA Ops:
  0.6 45.9 %copy-start = (s32[2,2]{1,0:T(2,128)S(1)}, s32[2,2]{1,0:T(2,128)}, u32[]{:S(2)}) copy-start(s32[2,2]{1,0:T(2,128)} %param.11) | copy-start | bytes 52
  0.6 53.2 %collective-permute-start.4 = (bf16[2,896,512]{2,1,0:T(8,128)(2,1)}, bf16[2,896,512]{2,1,0:T(8,128)(2,1)}, u32[]{:S(2)}, u32[]{:S(2)}) collective-permute-start(bf16[2,896,512]{2,1,0:T(8,128)(2,1)} %w_own.1), channel_id=1, source_target_pairs={{0,1},{1,0},{2,3},{3,2},{4,5},{5,4},{6,7},{7,6},{8,9},{9,8},{10,11... | collective-permute-start | bytes 5505032 | tf_op jit(solution)/shard_map/ppermute | solution.py:37
  5.5 20.0 %collective-permute-start = (s32[2,2]{1,0:T(2,128)}, s32[2,2]{1,0:T(2,128)S(1)}, u32[]{:S(2)}, u32[]{:S(2)}) collective-permute-start(s32[2,2]{1,0:T(2,128)} %param.10), channel_id=1, source_target_pairs={{0,128},{128,256},{256,384},{384,0},{1,129},{129,257},{257,385},{3... | collective-permute-start | bytes 56 | tf_op jit(solution)/shard_map/ppermute | solution.py:33
  8.6 16.9 %collective-permute-start.2 = (s32[2,2]{1,0:T(2,128)}, s32[2,2]{1,0:T(2,128)S(1)}, u32[]{:S(2)}, u32[]{:S(2)}) collective-permute-start(s32[2,2]{1,0:T(2,128)} %param.10), channel_id=1, source_target_pairs={{0,384},{128,0},{256,128},{384,256},{1,385},{129,1},{257,129},{385... | collective-permute-start | bytes 56 | tf_op jit(solution)/shard_map/ppermute | solution.py:33
  12.0 13.5 %collective-permute-start.1 = (s32[2,2]{1,0:T(2,128)}, s32[2,2]{1,0:T(2,128)S(1)}, u32[]{:S(2)}, u32[]{:S(2)}) collective-permute-start(s32[2,2]{1,0:T(2,128)} %param.10), channel_id=1, source_target_pairs={{0,256},{128,384},{256,0},{384,128},{1,257},{129,385},{257,1},{385... | collective-permute-start | bytes 56 | tf_op jit(solution)/shard_map/ppermute | solution.py:33
  15.5 0.7 copy-start.1
  17.0 15.9 %all-to-all-start = ((bf16[8,16,896]{2,1,0:T(8,128)(2,1)}), bf16[8,16,896]{2,1,0:T(8,128)(2,1)S(1)}, u32[]{:S(2)}, u32[]{:S(2)}) async-start(bf16[8,16,896]{2,1,0:T(8,128)(2,1)} %copies.1), calls=%async_computation | async-start | bytes 458752 | tf_op jit(solution)/shard_map/all_to_all | solution.py:223
  32.9 6.1 %collective-permute-start.3 = (bf16[8,16,896]{2,1,0:T(8,128)(2,1)S(1)}, bf16[8,16,896]{2,1,0:T(8,128)(2,1)S(1)}, u32[]{:S(2)}, u32[]{:S(2)}) collective-permute-start(bf16[8,16,896]{2,1,0:T(8,128)(2,1)S(1)} %all-to-all-done.refs_4_), channel_id=1, source_target_pairs={{0,8},{8,0},{1,9},{9,1},{2,10},{10,2},{3,11},{11,3},{4,12},{12,4},... | collective-permute-start | bytes 688136 | tf_op jit(solution)/shard_map/ppermute | solution.py:37
  40.5 12.0 %all-to-all-start.1 = ((bf16[4,4,16,896]{3,2,1,0:T(8,128)(2,1)}), bf16[4,4,16,896]{3,2,1,0:T(8,128)(2,1)S(1)}, u32[]{:S(2)}, u32[]{:S(2)}) async-start(bf16[4,4,16,896]{3,2,1,0:T(8,128)(2,1)} %pick.1), calls=%async_computation.1 | async-start | bytes 917504 | tf_op jit(solution)/shard_map/all_to_all | solution.py:231
  44.0 33.7 %copy-start.2 = (bf16[2,896,512]{2,1,0:T(8,128)(2,1)S(1)}, bf16[2,896,512]{2,1,0:T(8,128)(2,1)}, u32[]{:S(2)}) copy-start(bf16[2,896,512]{2,1,0:T(8,128)(2,1)} %w_own.1) | copy-start | bytes 5505028
  44.2 9.6 %collective-permute-start.5 = (bf16[128,512]{1,0:T(8,128)(2,1)S(1)}, bf16[128,512]{1,0:T(8,128)(2,1)S(1)}, u32[]{:S(2)}, u32[]{:S(2)}) collective-permute-start(bf16[128,512]{1,0:T(8,128)(2,1)S(1)} %pad_maximum_fusion), channel_id=1, source_target_pairs={{0,1},{1,0},{2,3},{3,2},{4,5},{5,4},{6,7},{7,6},{8,9},{9,8},{10,11... | collective-permute-start | bytes 393224 | tf_op jit(solution)/shard_map/ppermute | solution.py:37
  53.9 23.8 %all-to-all-start.2 = ((bf16[8,2,16,896]{3,2,1,0:T(8,128)(2,1)}), bf16[8,2,16,896]{3,2,1,0:T(8,128)(2,1)S(1)}, u32[]{:S(2)}, u32[]{:S(2)}) async-start(bf16[8,2,16,896]{3,2,1,0:T(8,128)(2,1)} %spread.1), calls=%async_computation.2 | async-start | bytes 917504 | tf_op jit(solution)/shard_map/all_to_all | solution.py:239
  100.7 10.0 %all-to-all-start.4 = ((bf16[4,4,16,896]{3,2,1,0:T(8,128)(2,1)}), bf16[4,4,16,896]{3,2,1,0:T(8,128)(2,1)S(1)}, u32[]{:S(2)}, u32[]{:S(2)}) async-start(bf16[4,4,16,896]{3,2,1,0:T(8,128)(2,1)} %broadcast_in_dim.2), calls=%async_computation.4 | async-start | bytes 917504 | tf_op jit(solution)/shard_map/all_to_all | solution.py:251
  104.1 5.0 %collective-permute-start.6 = (bf16[64,512]{1,0:T(8,128)(2,1)S(1)}, bf16[64,512]{1,0:T(8,128)(2,1)S(1)}, u32[]{:S(2)}, u32[]{:S(2)}) collective-permute-start(bf16[64,512]{1,0:T(8,128)(2,1)S(1)} %get-tuple-element.33), channel_id=1, source_target_pairs={{0,1},{1,0},{2,3},{3,2},{4,5},{5,4},{6,7},{7,6},{8,9},{9,8},{10,11... | collective-permute-start | bytes 196616 | tf_op jit(solution)/shard_map/ppermute | solution.py:37
  111.7 8.4 %collective-permute-start.7 = (bf16[8,16,896]{2,1,0:T(8,128)(2,1)S(1)}, bf16[8,16,896]{2,1,0:T(8,128)(2,1)S(1)}, u32[]{:S(2)}, u32[]{:S(2)}) collective-permute-start(bf16[8,16,896]{2,1,0:T(8,128)(2,1)S(1)} %get-tuple-element.37), channel_id=1, source_target_pairs={{0,8},{8,0},{1,9},{9,1},{2,10},{10,2},{3,11},{11,3},{4,12},{12,4},... | collective-permute-start | bytes 688136 | tf_op jit(solution)/shard_map/ppermute | solution.py:37
  120.9 14.9 %all-to-all-start.5 = ((bf16[8,16,896]{2,1,0:T(8,128)(2,1)}), bf16[8,16,896]{2,1,0:T(8,128)(2,1)S(1)}, u32[]{:S(2)}, u32[]{:S(2)}) async-start(bf16[8,16,896]{2,1,0:T(8,128)(2,1)} %add_convert_fusion), calls=%async_computation.5 | async-start | bytes 458752 | tf_op jit(solution)/shard_map/all_to_all | solution.py:261

commit v9 on v7

--- a/solution.py
+++ b/solution.py
@@ -237,7 +237,10 @@
     read_sum = jnp.sum(from_heads.astype(F32), axis=0).astype(BF16).reshape(reads, ROWS, DE)
 
     read_copies = jnp.broadcast_to(read_sum, (NX, *block))
+    read_copies, dq_pair = lax.optimization_barrier((read_copies, dq_pair))
     read_x = lax.all_to_all(read_copies, "x", split_axis=0, concat_axis=0, tiled=True)
+    dq_back = swapped(dq_pair, "z", NZ)
+    read_x, dq_back = lax.optimization_barrier((read_x, dq_back))
     owners = (NY, ROWS, DE)
     mine, theirs = on_core(
         owner_kernel, "owner_sums",
@@ -245,8 +248,6 @@
         (at, *near), read_x, scratch=[pltpu.VMEM((NC * NY, ROWS, DE), F32)],
     )
     owner_part = (mine + swapped(theirs, "c", NC).astype(F32)).astype(BF16)
-    owner_part, dq_pair = lax.optimization_barrier((owner_part, dq_pair))
-    dq_back = swapped(dq_pair, "z", NZ)
     from_y = lax.all_to_all(owner_part, "y", split_axis=0, concat_axis=0, tiled=True)
     owned = jnp.sum(from_y.astype(F32), axis=0)
 

time: 135 us -> 134 us (level)
  blocking collectives: 25.5 us -> 15.1 us
  waiting for transfers between devices: 33.3 us -> 38.3 us
  starting transfers between devices: 57.4 us -> 61.2 us
    all_to_all x1 -> x0, blocking collectives: 10.4 us -> none  [local(): lax.all_to_all(read_copies, 'x', split_axis=0, concat_axis=0, tiled=True)]
    all_to_all x0 -> x1, starting transfers between devices: none -> 4.01 us  [local(): lax.all_to_all(read_copies, 'x', split_axis=0, concat_axis=0, tiled=True)]
    ppermute x5, waiting for transfers between devices: 2.09 us -> 5.16 us  [swapped(): return lax.ppermute(value, axis, [(i, i ^ 1) for i in range(size)])]
    all_to_all x0 -> x1, waiting for transfers between devices: none -> 1.58 us  [local(): lax.all_to_all(read_copies, 'x', split_axis=0, concat_axis=0, tiled=True)]
  transfers between devices with their start and end apart: 12 -> 13, of which waited for: 7 -> 9; matrix products, arithmetic and copies ran while one was open for 3% -> 3% of each run, Pallas kernels for 2% -> 2%
where the time goes in v9:
time: 134 us; the launch traced here: 133 us
  starting transfers between devices  61.2 us (46%)
  waiting for transfers between devices  38.3 us (29%)
  blocking collectives  15.1 us (11%)
  Pallas kernels  10.3 us (8%)
  local copies, waits for them, and re-layouts  3.94 us (3%)
  other arithmetic  3.25 us (2%)
    ppermute x5, starting transfers between devices, swapped(): return lax.ppermute(value, axis, [(i, i ^ 1) for i in range(size)])  21.2 us
    all_to_all x1, blocking collectives, local(): lax.all_to_all(part, 'z', split_axis=0, concat_axis=0, tiled=True)  15.1 us
    all_to_all x1, waiting for transfers between devices, local(): tok = lax.all_to_all(to_z, 'z', split_axis=0, concat_axis=0, tiled=True)  13.7 us
    all_to_all x1, waiting for transfers between devices, local(): lax.all_to_all(owner_part, 'y', split_axis=0, concat_axis=0, tiled=True)  9.48 us
    all_to_all x1, starting transfers between devices, local(): tok = lax.all_to_all(to_z, 'z', split_axis=0, concat_axis=0, tiled=True)  9.46 us
    ppermute x3, starting transfers between devices, shifted(): lax.ppermute(value, axis, [(i, (i + shift) % size) for i in range(size)])  9.32 us
    all_to_all x1, starting transfers between devices, local(): lax.all_to_all(owner_part, 'y', split_axis=0, concat_axis=0, tiled=True)  6.85 us
    all_to_all x1, starting transfers between devices, local(): lax.all_to_all(copies, 'y', split_axis=0, concat_axis=0, tiled=True)  6.82 us
  transfers between devices with their start and end apart: 13, of which 9 were waited for; matrix products, arithmetic and copies ran while one was open for 3% of the time, Pallas kernels for 2%

profile of v9, /device:TPU:1, one launch (start us, length us, event | category | flops | bytes accessed | tf_op | source)
XLA Modules:
  0.0 132.9 jit_solution(1330548667490319910)
XLA Ops:
  0.6 4.8 %collective-permute-start.4 = (bf16[2,896,512]{2,1,0:T(8,128)(2,1)}, bf16[2,896,512]{2,1,0:T(8,128)(2,1)}, u32[]{:S(2)}, u32[]{:S(2)}) collective-permute-start(bf16[2,896,512]{2,1,0:T(8,128)(2,1)} %w_own.1), channel_id=1, source_target_pairs={{0,1},{1,0},{2,3},{3,2},{4,5},{5,4},{6,7},{7,6},{8,9},{9,8},{10,11... | collective-permute-start | bytes 5505032 | tf_op jit(solution)/shard_map/ppermute | solution.py:37
  5.5 1.4 %broadcast_in_dim.7 = bf16[8,16,896]{2,1,0:T(8,128)(2,1)} broadcast(bf16[16,896]{1,0:T(8,128)(2,1)} %bitcast.25), dimensions={1,2} | broadcast | bytes 258048 | tf_op jit(solution)/shard_map/broadcast_in_dim | solution.py:212
  6.9 6.8 %all-to-all-start = ((bf16[8,16,896]{2,1,0:T(8,128)(2,1)}), bf16[8,16,896]{2,1,0:T(8,128)(2,1)S(1)}, u32[]{:S(2)}, u32[]{:S(2)}) async-start(bf16[8,16,896]{2,1,0:T(8,128)(2,1)} %broadcast_in_dim.7), calls=%async_computation | async-start | bytes 458752 | tf_op jit(solution)/shard_map/all_to_all | solution.py:213
  13.8 4.4 %collective-permute-start.2 = (s32[2,2]{1,0:T(2,128)}, s32[2,2]{1,0:T(2,128)S(1)}, u32[]{:S(2)}, u32[]{:S(2)}) collective-permute-start(s32[2,2]{1,0:T(2,128)} %refs_0_.1), channel_id=1, source_target_pairs={{0,384},{128,0},{256,128},{384,256},{1,385},{129,1},{257,129},{385... | collective-permute-start | bytes 56 | tf_op jit(solution)/shard_map/ppermute | solution.py:33
  18.2 2.4 %collective-permute-start.1 = (s32[2,2]{1,0:T(2,128)}, s32[2,2]{1,0:T(2,128)S(1)}, u32[]{:S(2)}, u32[]{:S(2)}) collective-permute-start(s32[2,2]{1,0:T(2,128)} %refs_0_.1), channel_id=1, source_target_pairs={{0,256},{128,384},{256,0},{384,128},{1,257},{129,385},{257,1},{385... | collective-permute-start | bytes 56 | tf_op jit(solution)/shard_map/ppermute | solution.py:33
  20.6 2.5 %collective-permute-start = (s32[2,2]{1,0:T(2,128)}, s32[2,2]{1,0:T(2,128)S(1)}, u32[]{:S(2)}, u32[]{:S(2)}) collective-permute-start(s32[2,2]{1,0:T(2,128)} %refs_0_.1), channel_id=1, source_target_pairs={{0,128},{128,256},{256,384},{384,0},{1,129},{129,257},{257,385},{3... | collective-permute-start | bytes 56 | tf_op jit(solution)/shard_map/ppermute | solution.py:33
  24.2 2.3 %collective-permute-done.refs_1_ = s32[2,2]{1,0:T(2,128)S(1)} collective-permute-done((s32[2,2]{1,0:T(2,128)}, s32[2,2]{1,0:T(2,128)S(1)}, u32[]{:S(2)}, u32[]{:S(2)}) %collective-permute-start) | collective-permute-done | bytes 48 | tf_op jit(solution)/shard_map/ppermute | solution.py:33
  26.5 4.7 %collective-permute-start.3 = (bf16[8,16,896]{2,1,0:T(8,128)(2,1)S(1)}, bf16[8,16,896]{2,1,0:T(8,128)(2,1)S(1)}, u32[]{:S(2)}, u32[]{:S(2)}) collective-permute-start(bf16[8,16,896]{2,1,0:T(8,128)(2,1)S(1)} %all-to-all-done.refs_4_), channel_id=1, source_target_pairs={{0,8},{8,0},{1,9},{9,1},{2,10},{10,2},{3,11},{11,3},{4,12},{12,4},... | collective-permute-start | bytes 688136 | tf_op jit(solution)/shard_map/ppermute | solution.py:37
  33.0 1.5 %pick.1 = bf16[4,4,16,896]{3,2,1,0:T(8,128)(2,1)} custom-call(s32[2]{0:T(128)S(1)} %pad_add_fusion.at_ref, s32[2,2]{1,0:T(2,128)S(1)} %copy-done.1, s32[2,2]{1,0:T(2,128)S(1)} %collective-permute-done.refs_1_, s32[2,2]{1,0:T(2,128)S(1)} %collective-permute-done.1.refs_2_, s32[2,2]{1,0:T(2,128)S(1)} %collective-permute-done.2.refs_3_, ...), custom_call_target="tpu_custom_call" | custom-call | tf_op jit(solution)/shard_map/pick/pallas_call | solution.py:151
  34.5 3.5 %all-to-all-start.1 = ((bf16[4,4,16,896]{3,2,1,0:T(8,128)(2,1)}), bf16[4,4,16,896]{3,2,1,0:T(8,128)(2,1)S(1)}, u32[]{:S(2)}, u32[]{:S(2)}) async-start(bf16[4,4,16,896]{3,2,1,0:T(8,128)(2,1)} %pick.1), calls=%async_computation.1 | async-start | bytes 917504 | tf_op jit(solution)/shard_map/all_to_all | solution.py:221
  38.2 2.1 %collective-permute-start.5 = (bf16[128,512]{1,0:T(8,128)(2,1)S(1)}, bf16[128,512]{1,0:T(8,128)(2,1)S(1)}, u32[]{:S(2)}, u32[]{:S(2)}) collective-permute-start(bf16[128,512]{1,0:T(8,128)(2,1)S(1)} %pad_maximum_fusion), channel_id=1, source_target_pairs={{0,1},{1,0},{2,3},{3,2},{4,5},{5,4},{6,7},{7,6},{8,9},{9,8},{10,11... | collective-permute-start | bytes 393224 | tf_op jit(solution)/shard_map/ppermute | solution.py:37
  40.4 6.1 %all-to-all-done.1.from_ref = bf16[4,4,16,896]{3,2,1,0:T(8,128)(2,1)S(1)} async-done(((bf16[4,4,16,896]{3,2,1,0:T(8,128)(2,1)}), bf16[4,4,16,896]{3,2,1,0:T(8,128)(2,1)S(1)}, u32[]{:S(2)}, u32[]{:S(2)}) %all-to-all-start.1) | async-done | bytes 458784 | tf_op jit(solution)/shard_map/all_to_all | solution.py:221
  46.5 1.4 %spread.1 = bf16[8,2,16,896]{3,2,1,0:T(8,128)(2,1)} custom-call(s32[2,2]{1,0:T(2,128)S(1)} %copy-done.2, bf16[4,4,16,896]{3,2,1,0:T(8,128)(2,1)S(1)} %all-to-all-done.1.from_ref), custom_call_target="tpu_custom_call" | custom-call | tf_op jit(solution)/shard_map/spread/pallas_call | solution.py:151
  47.8 9.5 %all-to-all-start.2 = ((bf16[8,2,16,896]{3,2,1,0:T(8,128)(2,1)}), bf16[8,2,16,896]{3,2,1,0:T(8,128)(2,1)S(1)}, u32[]{:S(2)}, u32[]{:S(2)}) async-start(bf16[8,2,16,896]{3,2,1,0:T(8,128)(2,1)} %spread.1), calls=%async_computation.2 | async-start | bytes 917504 | tf_op jit(solution)/shard_map/all_to_all | solution.py:229
  58.1 13.7 %all-to-all-done.2.tok = bf16[8,2,16,896]{3,2,1,0:T(8,128)(2,1)S(1)} async-done(((bf16[8,2,16,896]{3,2,1,0:T(8,128)(2,1)}), bf16[8,2,16,896]{3,2,1,0:T(8,128)(2,1)S(1)}, u32[]{:S(2)}, u32[]{:S(2)}) %all-to-all-start.2) | async-done | bytes 458784 | tf_op jit(solution)/shard_map/all_to_all | solution.py:229
  71.8 6.4 %attention.1 = (bf16[8,2,16,896]{3,2,1,0:T(8,128)(2,1)S(1)}, bf16[64,512]{1,0:T(8,128)(2,1)S(1)}, bf16[64,512]{1,0:T(8,128)(2,1)S(1)}) custom-call(bf16[8,2,16,896]{3,2,1,0:T(8,128)(2,1)S(1)} %all-to-all-done.2.tok, bf16[2,896,512]{2,1,0:T(8,128)(2,1)S(1)} %copy-done.3, bf16[64,512]{1,0:T(8,128)(2,1)S(1)} %get-tuple-element.53.q_own, ...), custom_call_target="tpu_custom_call" | custom-call | flops 2100000000 | bytes 6000000 | tf_op jit(solution)/shard_map/attention/pallas_call | solution.py:164
  78.1 15.1 %all_to_all.30 = bf16[8,2,16,896]{3,2,1,0:T(8,128)(2,1)S(1)} all-to-all(bf16[8,2,16,896]{3,2,1,0:T(8,128)(2,1)S(1)} %get-tuple-element.30), channel_id=1, replica_groups=mesh['x'=4,'y'=8,'c'=2,'z'=8] {'z'}, dimensions={0} | all-to-all | bytes 917504 | tf_op jit(solution)/shard_map/all_to_all | solution.py:235
  94.1 4.0 %all-to-all-start.4 = ((bf16[4,4,16,896]{3,2,1,0:T(8,128)(2,1)}), bf16[4,4,16,896]{3,2,1,0:T(8,128)(2,1)S(1)}, u32[]{:S(2)}, u32[]{:S(2)}) async-start(bf16[4,4,16,896]{3,2,1,0:T(8,128)(2,1)} %broadcast_in_dim.8), calls=%async_computation.4 | async-start | bytes 917504 | tf_op jit(solution)/shard_map/all_to_all | solution.py:241
  98.1 1.9 %collective-permute-start.6 = (bf16[64,512]{1,0:T(8,128)(2,1)S(1)}, bf16[64,512]{1,0:T(8,128)(2,1)S(1)}, u32[]{:S(2)}, u32[]{:S(2)}) collective-permute-start(bf16[64,512]{1,0:T(8,128)(2,1)S(1)} %get-tuple-element.33), channel_id=1, source_target_pairs={{0,1},{1,0},{2,3},{3,2},{4,5},{5,4},{6,7},{7,6},{8,9},{9,8},{10,11... | collective-permute-start | bytes 196616 | tf_op jit(solution)/shard_map/ppermute | solution.py:37
  100.0 3.1 %collective-permute-done.6 = bf16[64,512]{1,0:T(8,128)(2,1)S(1)} collective-permute-done((bf16[64,512]{1,0:T(8,128)(2,1)S(1)}, bf16[64,512]{1,0:T(8,128)(2,1)S(1)}, u32[]{:S(2)}, u32[]{:S(2)}) %collective-permute-start.6) | collective-permute-done | bytes 65568 | tf_op jit(solution)/shard_map/ppermute | solution.py:37
  103.1 1.6 %all-to-all-done.4.refs_4_ = bf16[4,4,16,896]{3,2,1,0:T(8,128)(2,1)S(1)} async-done(((bf16[4,4,16,896]{3,2,1,0:T(8,128)(2,1)}), bf16[4,4,16,896]{3,2,1,0:T(8,128)(2,1)S(1)}, u32[]{:S(2)}, u32[]{:S(2)}) %all-to-all-start.4) | async-done | bytes 458784 | tf_op jit(solution)/shard_map/all_to_all | solution.py:241
  105.7 7.7 %collective-permute-start.7 = (bf16[8,16,896]{2,1,0:T(8,128)(2,1)S(1)}, bf16[8,16,896]{2,1,0:T(8,128)(2,1)S(1)}, u32[]{:S(2)}, u32[]{:S(2)}) collective-permute-start(bf16[8,16,896]{2,1,0:T(8,128)(2,1)S(1)} %get-tuple-element.37), channel_id=1, source_target_pairs={{0,8},{8,0},{1,9},{9,1},{2,10},{10,2},{3,11},{11,3},{4,12},{12,4},... | collective-permute-start | bytes 688136 | tf_op jit(solution)/shard_map/ppermute | solution.py:37
  115.2 6.8 %all-to-all-start.5 = ((bf16[8,16,896]{2,1,0:T(8,128)(2,1)}), bf16[8,16,896]{2,1,0:T(8,128)(2,1)S(1)}, u32[]{:S(2)}, u32[]{:S(2)}) async-start(bf16[8,16,896]{2,1,0:T(8,128)(2,1)} %add_convert_fusion), calls=%async_computation.5 | async-start | bytes 458752 | tf_op jit(solution)/shard_map/all_to_all | solution.py:251
  122.7 9.5 %all-to-all-done.5 = bf16[8,16,896]{2,1,0:T(8,128)(2,1)S(1)} async-done(((bf16[8,16,896]{2,1,0:T(8,128)(2,1)}), bf16[8,16,896]{2,1,0:T(8,128)(2,1)S(1)}, u32[]{:S(2)}, u32[]{:S(2)}) %all-to-all-start.5) | async-done | bytes 229408 | tf_op jit(solution)/shard_map/all_to_all | solution.py:251
  (34 shorter events, 8.9 us)
Async XLA Ops:
  0.6 39.6 %copy-start = (s32[2,2]{1,0:T(2,128)S(1)}, s32[2,2]{1,0:T(2,128)}, u32[]{:S(2)}) copy-start(s32[2,2]{1,0:T(2,128)} %param.11) | copy-start | bytes 52
  0.6 47.2 %collective-permute-start.4 = (bf16[2,896,512]{2,1,0:T(8,128)(2,1)}, bf16[2,896,512]{2,1,0:T(8,128)(2,1)}, u32[]{:S(2)}, u32[]{:S(2)}) collective-permute-start(bf16[2,896,512]{2,1,0:T(8,128)(2,1)} %w_own.1), channel_id=1, source_target_pairs={{0,1},{1,0},{2,3},{3,2},{4,5},{5,4},{6,7},{7,6},{8,9},{9,8},{10,11... | collective-permute-start | bytes 5505032 | tf_op jit(solution)/shard_map/ppermute | solution.py:37
  5.5 41.0 %copy-start.2 = (s32[2,2]{1,0:T(2,128)S(1)}, s32[2,2]{1,0:T(2,128)}, u32[]{:S(2)}) copy-start(s32[2,2]{1,0:T(2,128)} %refs_0_.1) | copy-start | bytes 52
  6.9 19.5 %all-to-all-start = ((bf16[8,16,896]{2,1,0:T(8,128)(2,1)}), bf16[8,16,896]{2,1,0:T(8,128)(2,1)S(1)}, u32[]{:S(2)}, u32[]{:S(2)}) async-start(bf16[8,16,896]{2,1,0:T(8,128)(2,1)} %broadcast_in_dim.7), calls=%async_computation | async-start | bytes 458752 | tf_op jit(solution)/shard_map/all_to_all | solution.py:213
  13.8 10.4 %collective-permute-start.2 = (s32[2,2]{1,0:T(2,128)}, s32[2,2]{1,0:T(2,128)S(1)}, u32[]{:S(2)}, u32[]{:S(2)}) collective-permute-start(s32[2,2]{1,0:T(2,128)} %refs_0_.1), channel_id=1, source_target_pairs={{0,384},{128,0},{256,128},{384,256},{1,385},{129,1},{257,129},{385... | collective-permute-start | bytes 56 | tf_op jit(solution)/shard_map/ppermute | solution.py:33
  18.2 6.0 %collective-permute-start.1 = (s32[2,2]{1,0:T(2,128)}, s32[2,2]{1,0:T(2,128)S(1)}, u32[]{:S(2)}, u32[]{:S(2)}) collective-permute-start(s32[2,2]{1,0:T(2,128)} %refs_0_.1), channel_id=1, source_target_pairs={{0,256},{128,384},{256,0},{384,128},{1,257},{129,385},{257,1},{385... | collective-permute-start | bytes 56 | tf_op jit(solution)/shard_map/ppermute | solution.py:33
  20.6 5.9 %collective-permute-start = (s32[2,2]{1,0:T(2,128)}, s32[2,2]{1,0:T(2,128)S(1)}, u32[]{:S(2)}, u32[]{:S(2)}) collective-permute-start(s32[2,2]{1,0:T(2,128)} %refs_0_.1), channel_id=1, source_target_pairs={{0,128},{128,256},{256,384},{384,0},{1,129},{129,257},{257,385},{3... | collective-permute-start | bytes 56 | tf_op jit(solution)/shard_map/ppermute | solution.py:33
  26.5 5.8 %collective-permute-start.3 = (bf16[8,16,896]{2,1,0:T(8,128)(2,1)S(1)}, bf16[8,16,896]{2,1,0:T(8,128)(2,1)S(1)}, u32[]{:S(2)}, u32[]{:S(2)}) collective-permute-start(bf16[8,16,896]{2,1,0:T(8,128)(2,1)S(1)} %all-to-all-done.refs_4_), channel_id=1, source_target_pairs={{0,8},{8,0},{1,9},{9,1},{2,10},{10,2},{3,11},{11,3},{4,12},{12,4},... | collective-permute-start | bytes 688136 | tf_op jit(solution)/shard_map/ppermute | solution.py:37
  32.3 0.7 copy-start.1
  34.5 12.0 %all-to-all-start.1 = ((bf16[4,4,16,896]{3,2,1,0:T(8,128)(2,1)}), bf16[4,4,16,896]{3,2,1,0:T(8,128)(2,1)S(1)}, u32[]{:S(2)}, u32[]{:S(2)}) async-start(bf16[4,4,16,896]{3,2,1,0:T(8,128)(2,1)} %pick.1), calls=%async_computation.1 | async-start | bytes 917504 | tf_op jit(solution)/shard_map/all_to_all | solution.py:221
  38.0 33.8 %copy-start.3 = (bf16[2,896,512]{2,1,0:T(8,128)(2,1)S(1)}, bf16[2,896,512]{2,1,0:T(8,128)(2,1)}, u32[]{:S(2)}) copy-start(bf16[2,896,512]{2,1,0:T(8,128)(2,1)} %w_own.1) | copy-start | bytes 5505028
  38.2 9.7 %collective-permute-start.5 = (bf16[128,512]{1,0:T(8,128)(2,1)S(1)}, bf16[128,512]{1,0:T(8,128)(2,1)S(1)}, u32[]{:S(2)}, u32[]{:S(2)}) collective-permute-start(bf16[128,512]{1,0:T(8,128)(2,1)S(1)} %pad_maximum_fusion), channel_id=1, source_target_pairs={{0,1},{1,0},{2,3},{3,2},{4,5},{5,4},{6,7},{7,6},{8,9},{9,8},{10,11... | collective-permute-start | bytes 393224 | tf_op jit(solution)/shard_map/ppermute | solution.py:37
  47.8 23.9 %all-to-all-start.2 = ((bf16[8,2,16,896]{3,2,1,0:T(8,128)(2,1)}), bf16[8,2,16,896]{3,2,1,0:T(8,128)(2,1)S(1)}, u32[]{:S(2)}, u32[]{:S(2)}) async-start(bf16[8,2,16,896]{3,2,1,0:T(8,128)(2,1)} %spread.1), calls=%async_computation.2 | async-start | bytes 917504 | tf_op jit(solution)/shard_map/all_to_all | solution.py:229
  94.1 10.6 %all-to-all-start.4 = ((bf16[4,4,16,896]{3,2,1,0:T(8,128)(2,1)}), bf16[4,4,16,896]{3,2,1,0:T(8,128)(2,1)S(1)}, u32[]{:S(2)}, u32[]{:S(2)}) async-start(bf16[4,4,16,896]{3,2,1,0:T(8,128)(2,1)} %broadcast_in_dim.8), calls=%async_computation.4 | async-start | bytes 917504 | tf_op jit(solution)/shard_map/all_to_all | solution.py:241
  98.1 5.0 %collective-permute-start.6 = (bf16[64,512]{1,0:T(8,128)(2,1)S(1)}, bf16[64,512]{1,0:T(8,128)(2,1)S(1)}, u32[]{:S(2)}, u32[]{:S(2)}) collective-permute-start(bf16[64,512]{1,0:T(8,128)(2,1)S(1)} %get-tuple-element.33), channel_id=1, source_target_pairs={{0,1},{1,0},{2,3},{3,2},{4,5},{5,4},{6,7},{7,6},{8,9},{9,8},{10,11... | collective-permute-start | bytes 196616 | tf_op jit(solution)/shard_map/ppermute | solution.py:37
  105.7 8.8 %collective-permute-start.7 = (bf16[8,16,896]{2,1,0:T(8,128)(2,1)S(1)}, bf16[8,16,896]{2,1,0:T(8,128)(2,1)S(1)}, u32[]{:S(2)}, u32[]{:S(2)}) collective-permute-start(bf16[8,16,896]{2,1,0:T(8,128)(2,1)S(1)} %get-tuple-element.37), channel_id=1, source_target_pairs={{0,8},{8,0},{1,9},{9,1},{2,10},{10,2},{3,11},{11,3},{4,12},{12,4},... | collective-permute-start | bytes 688136 | tf_op jit(solution)/shard_map/ppermute | solution.py:37
  115.2 17.0 %all-to-all-start.5 = ((bf16[8,16,896]{2,1,0:T(8,128)(2,1)}), bf16[8,16,896]{2,1,0:T(8,128)(2,1)S(1)}, u32[]{:S(2)}, u32[]{:S(2)}) async-start(bf16[8,16,896]{2,1,0:T(8,128)(2,1)} %add_convert_fusion), calls=%async_computation.5 | async-start | bytes 458752 | tf_op jit(solution)/shard_map/all_to_all | solution.py:251

commit v10 on v9

--- a/solution.py
+++ b/solution.py
@@ -100,7 +100,7 @@
 
 
 def attention_kernel(
-    tok, w_own, q_own, g_own, q_pair, g_pair, kc, ks, qc, qs, w_far,
+    tok, w_own, q_own, g_own, from_pair, kc, ks, qc, qs, w_far,
     part, dq_own, dq_pair, dk_all, dv_all, w_pair, sem,
 ):
     fetch = pltpu.make_async_copy(w_far, w_pair, sem)
@@ -113,7 +113,10 @@
     fetch.wait()
     projected.append((dot(rows, w_pair[0]), dot(rows, w_pair[1]).astype(BF16)))
     key_cos, key_sin, query_cos, query_sin = kc[...], ks[...], qc[...], qs[...]
-    for turn, (q, g, dq) in enumerate(((q_own, g_own, dq_own), (q_pair, g_pair, dq_pair))):
+    for turn, (q, g, dq) in enumerate((
+        (q_own, g_own, dq_own),
+        (from_pair.at[:SPAN], from_pair.at[SPAN:], dq_pair),
+    )):
         key_raw, values = projected[turn]
         for head in range(width // HEAD):
             cols = slice(head * HEAD, (head + 1) * HEAD)
@@ -228,7 +231,7 @@
     to_z, w_far, from_pair = lax.optimization_barrier((to_z, w_far, from_pair))
     tok = lax.all_to_all(to_z, "z", split_axis=0, concat_axis=0, tiled=True)
     part, dq_own, dq_pair = attention(
-        tok, kv_weight, q_own, g_own, from_pair[:SPAN], from_pair[SPAN:],
+        tok, kv_weight, q_own, g_own, from_pair,
         key_cos, key_sin, query_cos, query_sin, w_far,
     )
 
@@ -240,7 +243,10 @@
     read_copies, dq_pair = lax.optimization_barrier((read_copies, dq_pair))
     read_x = lax.all_to_all(read_copies, "x", split_axis=0, concat_axis=0, tiled=True)
     dq_back = swapped(dq_pair, "z", NZ)
-    read_x, dq_back = lax.optimization_barrier((read_x, dq_back))
+    first = jnp.where(span_at == 0, dq_own, dq_back)
+    second = jnp.where(span_at == 0, dq_back, dq_own)
+    grad_query = jnp.concatenate([first, second], axis=0)
+    read_x, grad_query = lax.optimization_barrier((read_x, grad_query))
     owners = (NY, ROWS, DE)
     mine, theirs = on_core(
         owner_kernel, "owner_sums",
@@ -250,10 +256,6 @@
     owner_part = (mine + swapped(theirs, "c", NC).astype(F32)).astype(BF16)
     from_y = lax.all_to_all(owner_part, "y", split_axis=0, concat_axis=0, tiled=True)
     owned = jnp.sum(from_y.astype(F32), axis=0)
-
-    first = jnp.where(span_at == 0, dq_own, dq_back)
-    second = jnp.where(span_at == 0, dq_back, dq_own)
-    grad_query = jnp.concatenate([first, second], axis=0)
     return (grad_query, owned.reshape(1, ROWS, DE))
 
 

time: 134 us -> 135 us (level)
  blocking collectives: 15.1 us -> 31.8 us
  waiting for transfers between devices: 38.3 us -> 30.2 us
  starting transfers between devices: 61.2 us -> 54.8 us
    all_to_all x0 -> x1, blocking collectives: none -> 16.7 us  [local(): lax.all_to_all(owner_part, 'y', split_axis=0, concat_axis=0, tiled=True)]
    all_to_all x1 -> x0, waiting for transfers between devices: 9.48 us -> none  [local(): lax.all_to_all(owner_part, 'y', split_axis=0, concat_axis=0, tiled=True)]
    all_to_all x1 -> x0, starting transfers between devices: 6.85 us -> none  [local(): lax.all_to_all(owner_part, 'y', split_axis=0, concat_axis=0, tiled=True)]
    all_to_all x1, waiting for transfers between devices: 1.58 us -> 5.9 us  [local(): lax.all_to_all(read_copies, 'x', split_axis=0, concat_axis=0, tiled=True)]
    ppermute x5, waiting for transfers between devices: 5.16 us -> 2.11 us  [swapped(): return lax.ppermute(value, axis, [(i, i ^ 1) for i in range(size)])]
  transfers between devices with their start and end apart: 13 -> 12, of which waited for: 9 -> 7; matrix products, arithmetic and copies ran while one was open for 3% -> 3% of each run, Pallas kernels for 2% -> 2%
where the time goes in v10:
time: 135 us; the launch traced here: 134 us
  starting transfers between devices  54.8 us (41%)
  blocking collectives  31.8 us (24%)
  waiting for transfers between devices  30.2 us (22%)
  Pallas kernels  10.3 us (8%)
  local copies, waits for them, and re-layouts  3.93 us (3%)
  other arithmetic  2.56 us (2%)
    ppermute x5, starting transfers between devices, swapped(): return lax.ppermute(value, axis, [(i, i ^ 1) for i in range(size)])  21.6 us
    all_to_all x1, blocking collectives, local(): lax.all_to_all(owner_part, 'y', split_axis=0, concat_axis=0, tiled=True)  16.7 us
    all_to_all x1, blocking collectives, local(): lax.all_to_all(part, 'z', split_axis=0, concat_axis=0, tiled=True)  15.1 us
    all_to_all x1, waiting for transfers between devices, local(): tok = lax.all_to_all(to_z, 'z', split_axis=0, concat_axis=0, tiled=True)  13.6 us
    all_to_all x1, starting transfers between devices, local(): tok = lax.all_to_all(to_z, 'z', split_axis=0, concat_axis=0, tiled=True)  9.34 us
    ppermute x3, starting transfers between devices, shifted(): lax.ppermute(value, axis, [(i, (i + shift) % size) for i in range(size)])  9.32 us
    all_to_all x1, starting transfers between devices, local(): lax.all_to_all(copies, 'y', split_axis=0, concat_axis=0, tiled=True)  6.82 us
    pallas_call x1, Pallas kernels, attention(): pl.pallas_call(attention_kernel, out_shape=(jax.ShapeDtypeStruct((NZ, NEI...  6.37 us
  transfers between devices with their start and end apart: 12, of which 7 were waited for; matrix products, arithmetic and copies ran while one was open for 3% of the time, Pallas kernels for 2%

profile of v10, /device:TPU:1, one launch (start us, length us, event | category | flops | bytes accessed | tf_op | source)
XLA Modules:
  0.0 134.4 jit_solution(692288126411339700)
XLA Ops:
  0.7 4.8 %collective-permute-start.4 = (bf16[2,896,512]{2,1,0:T(8,128)(2,1)}, bf16[2,896,512]{2,1,0:T(8,128)(2,1)}, u32[]{:S(2)}, u32[]{:S(2)}) collective-permute-start(bf16[2,896,512]{2,1,0:T(8,128)(2,1)} %w_own.1), channel_id=1, source_target_pairs={{0,1},{1,0},{2,3},{3,2},{4,5},{5,4},{6,7},{7,6},{8,9},{9,8},{10,11... | collective-permute-start | bytes 5505032 | tf_op jit(solution)/shard_map/ppermute | solution.py:37
  5.5 1.4 %broadcast_in_dim.7 = bf16[8,16,896]{2,1,0:T(8,128)(2,1)} broadcast(bf16[16,896]{1,0:T(8,128)(2,1)} %bitcast.25), dimensions={1,2} | broadcast | bytes 258048 | tf_op jit(solution)/shard_map/broadcast_in_dim | solution.py:215
  6.9 6.8 %all-to-all-start = ((bf16[8,16,896]{2,1,0:T(8,128)(2,1)}), bf16[8,16,896]{2,1,0:T(8,128)(2,1)S(1)}, u32[]{:S(2)}, u32[]{:S(2)}) async-start(bf16[8,16,896]{2,1,0:T(8,128)(2,1)} %broadcast_in_dim.7), calls=%async_computation | async-start | bytes 458752 | tf_op jit(solution)/shard_map/all_to_all | solution.py:216
  13.8 4.4 %collective-permute-start.2 = (s32[2,2]{1,0:T(2,128)}, s32[2,2]{1,0:T(2,128)S(1)}, u32[]{:S(2)}, u32[]{:S(2)}) collective-permute-start(s32[2,2]{1,0:T(2,128)} %refs_0_.1), channel_id=1, source_target_pairs={{0,384},{128,0},{256,128},{384,256},{1,385},{129,1},{257,129},{385... | collective-permute-start | bytes 56 | tf_op jit(solution)/shard_map/ppermute | solution.py:33
  18.2 2.4 %collective-permute-start.1 = (s32[2,2]{1,0:T(2,128)}, s32[2,2]{1,0:T(2,128)S(1)}, u32[]{:S(2)}, u32[]{:S(2)}) collective-permute-start(s32[2,2]{1,0:T(2,128)} %refs_0_.1), channel_id=1, source_target_pairs={{0,256},{128,384},{256,0},{384,128},{1,257},{129,385},{257,1},{385... | collective-permute-start | bytes 56 | tf_op jit(solution)/shard_map/ppermute | solution.py:33
  20.6 2.5 %collective-permute-start = (s32[2,2]{1,0:T(2,128)}, s32[2,2]{1,0:T(2,128)S(1)}, u32[]{:S(2)}, u32[]{:S(2)}) collective-permute-start(s32[2,2]{1,0:T(2,128)} %refs_0_.1), channel_id=1, source_target_pairs={{0,128},{128,256},{256,384},{384,0},{1,129},{129,257},{257,385},{3... | collective-permute-start | bytes 56 | tf_op jit(solution)/shard_map/ppermute | solution.py:33
  24.2 2.3 %collective-permute-done.refs_1_ = s32[2,2]{1,0:T(2,128)S(1)} collective-permute-done((s32[2,2]{1,0:T(2,128)}, s32[2,2]{1,0:T(2,128)S(1)}, u32[]{:S(2)}, u32[]{:S(2)}) %collective-permute-start) | collective-permute-done | bytes 48 | tf_op jit(solution)/shard_map/ppermute | solution.py:33
  26.5 4.7 %collective-permute-start.3 = (bf16[8,16,896]{2,1,0:T(8,128)(2,1)S(1)}, bf16[8,16,896]{2,1,0:T(8,128)(2,1)S(1)}, u32[]{:S(2)}, u32[]{:S(2)}) collective-permute-start(bf16[8,16,896]{2,1,0:T(8,128)(2,1)S(1)} %all-to-all-done.refs_4_), channel_id=1, source_target_pairs={{0,8},{8,0},{1,9},{9,1},{2,10},{10,2},{3,11},{11,3},{4,12},{12,4},... | collective-permute-start | bytes 688136 | tf_op jit(solution)/shard_map/ppermute | solution.py:37
  31.3 1.0 collective-permute-done.3.refs_5_
  33.0 1.5 %pick.1 = bf16[4,4,16,896]{3,2,1,0:T(8,128)(2,1)} custom-call(s32[2]{0:T(128)S(1)} %pad_add_fusion.at_ref, s32[2,2]{1,0:T(2,128)S(1)} %copy-done.1, s32[2,2]{1,0:T(2,128)S(1)} %collective-permute-done.refs_1_, s32[2,2]{1,0:T(2,128)S(1)} %collective-permute-done.1.refs_2_, s32[2,2]{1,0:T(2,128)S(1)} %collective-permute-done.2.refs_3_, ...), custom_call_target="tpu_custom_call" | custom-call | tf_op jit(solution)/shard_map/pick/pallas_call | solution.py:154
  34.5 3.6 %all-to-all-start.1 = ((bf16[4,4,16,896]{3,2,1,0:T(8,128)(2,1)}), bf16[4,4,16,896]{3,2,1,0:T(8,128)(2,1)S(1)}, u32[]{:S(2)}, u32[]{:S(2)}) async-start(bf16[4,4,16,896]{3,2,1,0:T(8,128)(2,1)} %pick.1), calls=%async_computation.1 | async-start | bytes 917504 | tf_op jit(solution)/shard_map/all_to_all | solution.py:224
  38.1 1.9 %collective-permute-start.5 = (bf16[128,512]{1,0:T(8,128)(2,1)S(1)}, bf16[128,512]{1,0:T(8,128)(2,1)S(1)}, u32[]{:S(2)}, u32[]{:S(2)}) collective-permute-start(bf16[128,512]{1,0:T(8,128)(2,1)S(1)} %pad_maximum_fusion), channel_id=1, source_target_pairs={{0,1},{1,0},{2,3},{3,2},{4,5},{5,4},{6,7},{7,6},{8,9},{9,8},{10,11... | collective-permute-start | bytes 393224 | tf_op jit(solution)/shard_map/ppermute | solution.py:37
  40.3 6.3 %all-to-all-done.1.from_ref = bf16[4,4,16,896]{3,2,1,0:T(8,128)(2,1)S(1)} async-done(((bf16[4,4,16,896]{3,2,1,0:T(8,128)(2,1)}), bf16[4,4,16,896]{3,2,1,0:T(8,128)(2,1)S(1)}, u32[]{:S(2)}, u32[]{:S(2)}) %all-to-all-start.1) | async-done | bytes 458784 | tf_op jit(solution)/shard_map/all_to_all | solution.py:224
  46.6 1.4 %spread.1 = bf16[8,2,16,896]{3,2,1,0:T(8,128)(2,1)} custom-call(s32[2,2]{1,0:T(2,128)S(1)} %copy-done.2, bf16[4,4,16,896]{3,2,1,0:T(8,128)(2,1)S(1)} %all-to-all-done.1.from_ref), custom_call_target="tpu_custom_call" | custom-call | tf_op jit(solution)/shard_map/spread/pallas_call | solution.py:154
  48.0 9.3 %all-to-all-start.2 = ((bf16[8,2,16,896]{3,2,1,0:T(8,128)(2,1)}), bf16[8,2,16,896]{3,2,1,0:T(8,128)(2,1)S(1)}, u32[]{:S(2)}, u32[]{:S(2)}) async-start(bf16[8,2,16,896]{3,2,1,0:T(8,128)(2,1)} %spread.1), calls=%async_computation.2 | async-start | bytes 917504 | tf_op jit(solution)/shard_map/all_to_all | solution.py:232
  58.2 13.6 %all-to-all-done.2.tok = bf16[8,2,16,896]{3,2,1,0:T(8,128)(2,1)S(1)} async-done(((bf16[8,2,16,896]{3,2,1,0:T(8,128)(2,1)}), bf16[8,2,16,896]{3,2,1,0:T(8,128)(2,1)S(1)}, u32[]{:S(2)}, u32[]{:S(2)}) %all-to-all-start.2) | async-done | bytes 458784 | tf_op jit(solution)/shard_map/all_to_all | solution.py:232
  71.8 6.4 %attention.1 = (bf16[8,2,16,896]{3,2,1,0:T(8,128)(2,1)S(1)}, bf16[64,512]{1,0:T(8,128)(2,1)S(1)}, bf16[64,512]{1,0:T(8,128)(2,1)S(1)}) custom-call(bf16[8,2,16,896]{3,2,1,0:T(8,128)(2,1)S(1)} %all-to-all-done.2.tok, bf16[2,896,512]{2,1,0:T(8,128)(2,1)S(1)} %copy-done.3, bf16[64,512]{1,0:T(8,128)(2,1)S(1)} %get-tuple-element.51.q_own, ...), custom_call_target="tpu_custom_call" | custom-call | flops 2100000000 | bytes 6000000 | tf_op jit(solution)/shard_map/attention/pallas_call | solution.py:167
  78.2 15.1 %all_to_all.30 = bf16[8,2,16,896]{3,2,1,0:T(8,128)(2,1)S(1)} all-to-all(bf16[8,2,16,896]{3,2,1,0:T(8,128)(2,1)S(1)} %get-tuple-element.29), channel_id=1, replica_groups=mesh['x'=4,'y'=8,'c'=2,'z'=8] {'z'}, dimensions={0} | all-to-all | bytes 917504 | tf_op jit(solution)/shard_map/all_to_all | solution.py:238
  94.1 1.9 %collective-permute-start.6 = (bf16[64,512]{1,0:T(8,128)(2,1)S(1)}, bf16[64,512]{1,0:T(8,128)(2,1)S(1)}, u32[]{:S(2)}, u32[]{:S(2)}) collective-permute-start(bf16[64,512]{1,0:T(8,128)(2,1)S(1)} %get-tuple-element.33), channel_id=1, source_target_pairs={{0,1},{1,0},{2,3},{3,2},{4,5},{5,4},{6,7},{7,6},{8,9},{9,8},{10,11... | collective-permute-start | bytes 196616 | tf_op jit(solution)/shard_map/ppermute | solution.py:37
  96.0 4.0 %all-to-all-start.4 = ((bf16[4,4,16,896]{3,2,1,0:T(8,128)(2,1)}), bf16[4,4,16,896]{3,2,1,0:T(8,128)(2,1)S(1)}, u32[]{:S(2)}, u32[]{:S(2)}) async-start(bf16[4,4,16,896]{3,2,1,0:T(8,128)(2,1)} %broadcast_in_dim.8), calls=%async_computation.4 | async-start | bytes 917504 | tf_op jit(solution)/shard_map/all_to_all | solution.py:244
  100.7 5.9 %all-to-all-done.4.refs_4_ = bf16[4,4,16,896]{3,2,1,0:T(8,128)(2,1)S(1)} async-done(((bf16[4,4,16,896]{3,2,1,0:T(8,128)(2,1)}), bf16[4,4,16,896]{3,2,1,0:T(8,128)(2,1)S(1)}, u32[]{:S(2)}, u32[]{:S(2)}) %all-to-all-start.4) | async-done | bytes 458784 | tf_op jit(solution)/shard_map/all_to_all | solution.py:244
  107.6 8.3 %collective-permute-start.7 = (bf16[8,16,896]{2,1,0:T(8,128)(2,1)S(1)}, bf16[8,16,896]{2,1,0:T(8,128)(2,1)S(1)}, u32[]{:S(2)}, u32[]{:S(2)}) collective-permute-start(bf16[8,16,896]{2,1,0:T(8,128)(2,1)S(1)} %get-tuple-element.37), channel_id=1, source_target_pairs={{0,8},{8,0},{1,9},{9,1},{2,10},{10,2},{3,11},{11,3},{4,12},{12,4},... | collective-permute-start | bytes 688136 | tf_op jit(solution)/shard_map/ppermute | solution.py:37
  115.9 1.1 collective-permute-done.7
  117.0 16.7 %all_to_all.31 = bf16[8,16,896]{2,1,0:T(8,128)(2,1)S(1)} all-to-all(bf16[8,16,896]{2,1,0:T(8,128)(2,1)S(1)} %add_convert_fusion), channel_id=1, replica_groups=mesh['x'=4,'y'=8,'c'=2,'z'=8] {'y'}, dimensions={0} | all-to-all | bytes 458752 | tf_op jit(solution)/shard_map/all_to_all | solution.py:257
  (32 shorter events, 6.1 us)
Async XLA Ops:
  0.6 56.7 %copy-start = (s32[2,2]{1,0:T(2,128)S(1)}, s32[2,2]{1,0:T(2,128)}, u32[]{:S(2)}) copy-start(s32[2,2]{1,0:T(2,128)} %param.11) | copy-start | bytes 52
  0.6 46.0 %copy-start.2 = (s32[2,2]{1,0:T(2,128)S(1)}, s32[2,2]{1,0:T(2,128)}, u32[]{:S(2)}) copy-start(s32[2,2]{1,0:T(2,128)} %refs_0_.1) | copy-start | bytes 52
  0.7 47.3 %collective-permute-start.4 = (bf16[2,896,512]{2,1,0:T(8,128)(2,1)}, bf16[2,896,512]{2,1,0:T(8,128)(2,1)}, u32[]{:S(2)}, u32[]{:S(2)}) collective-permute-start(bf16[2,896,512]{2,1,0:T(8,128)(2,1)} %w_own.1), channel_id=1, source_target_pairs={{0,1},{1,0},{2,3},{3,2},{4,5},{5,4},{6,7},{7,6},{8,9},{9,8},{10,11... | collective-permute-start | bytes 5505032 | tf_op jit(solution)/shard_map/ppermute | solution.py:37
  6.9 19.5 %all-to-all-start = ((bf16[8,16,896]{2,1,0:T(8,128)(2,1)}), bf16[8,16,896]{2,1,0:T(8,128)(2,1)S(1)}, u32[]{:S(2)}, u32[]{:S(2)}) async-start(bf16[8,16,896]{2,1,0:T(8,128)(2,1)} %broadcast_in_dim.7), calls=%async_computation | async-start | bytes 458752 | tf_op jit(solution)/shard_map/all_to_all | solution.py:216
  13.8 10.4 %collective-permute-start.2 = (s32[2,2]{1,0:T(2,128)}, s32[2,2]{1,0:T(2,128)S(1)}, u32[]{:S(2)}, u32[]{:S(2)}) collective-permute-start(s32[2,2]{1,0:T(2,128)} %refs_0_.1), channel_id=1, source_target_pairs={{0,384},{128,0},{256,128},{384,256},{1,385},{129,1},{257,129},{385... | collective-permute-start | bytes 56 | tf_op jit(solution)/shard_map/ppermute | solution.py:33
  18.2 6.0 %collective-permute-start.1 = (s32[2,2]{1,0:T(2,128)}, s32[2,2]{1,0:T(2,128)S(1)}, u32[]{:S(2)}, u32[]{:S(2)}) collective-permute-start(s32[2,2]{1,0:T(2,128)} %refs_0_.1), channel_id=1, source_target_pairs={{0,256},{128,384},{256,0},{384,128},{1,257},{129,385},{257,1},{385... | collective-permute-start | bytes 56 | tf_op jit(solution)/shard_map/ppermute | solution.py:33
  20.6 5.9 %collective-permute-start = (s32[2,2]{1,0:T(2,128)}, s32[2,2]{1,0:T(2,128)S(1)}, u32[]{:S(2)}, u32[]{:S(2)}) collective-permute-start(s32[2,2]{1,0:T(2,128)} %refs_0_.1), channel_id=1, source_target_pairs={{0,128},{128,256},{256,384},{384,0},{1,129},{129,257},{257,385},{3... | collective-permute-start | bytes 56 | tf_op jit(solution)/shard_map/ppermute | solution.py:33
  26.5 5.8 %collective-permute-start.3 = (bf16[8,16,896]{2,1,0:T(8,128)(2,1)S(1)}, bf16[8,16,896]{2,1,0:T(8,128)(2,1)S(1)}, u32[]{:S(2)}, u32[]{:S(2)}) collective-permute-start(bf16[8,16,896]{2,1,0:T(8,128)(2,1)S(1)} %all-to-all-done.refs_4_), channel_id=1, source_target_pairs={{0,8},{8,0},{1,9},{9,1},{2,10},{10,2},{3,11},{11,3},{4,12},{12,4},... | collective-permute-start | bytes 688136 | tf_op jit(solution)/shard_map/ppermute | solution.py:37
  32.3 0.7 copy-start.1
  34.5 37.3 %copy-start.3 = (bf16[2,896,512]{2,1,0:T(8,128)(2,1)S(1)}, bf16[2,896,512]{2,1,0:T(8,128)(2,1)}, u32[]{:S(2)}) copy-start(bf16[2,896,512]{2,1,0:T(8,128)(2,1)} %w_own.1) | copy-start | bytes 5505028
  34.5 12.1 %all-to-all-start.1 = ((bf16[4,4,16,896]{3,2,1,0:T(8,128)(2,1)}), bf16[4,4,16,896]{3,2,1,0:T(8,128)(2,1)S(1)}, u32[]{:S(2)}, u32[]{:S(2)}) async-start(bf16[4,4,16,896]{3,2,1,0:T(8,128)(2,1)} %pick.1), calls=%async_computation.1 | async-start | bytes 917504 | tf_op jit(solution)/shard_map/all_to_all | solution.py:224
  38.1 9.8 %collective-permute-start.5 = (bf16[128,512]{1,0:T(8,128)(2,1)S(1)}, bf16[128,512]{1,0:T(8,128)(2,1)S(1)}, u32[]{:S(2)}, u32[]{:S(2)}) collective-permute-start(bf16[128,512]{1,0:T(8,128)(2,1)S(1)} %pad_maximum_fusion), channel_id=1, source_target_pairs={{0,1},{1,0},{2,3},{3,2},{4,5},{5,4},{6,7},{7,6},{8,9},{9,8},{10,11... | collective-permute-start | bytes 393224 | tf_op jit(solution)/shard_map/ppermute | solution.py:37
  48.0 23.8 %all-to-all-start.2 = ((bf16[8,2,16,896]{3,2,1,0:T(8,128)(2,1)}), bf16[8,2,16,896]{3,2,1,0:T(8,128)(2,1)S(1)}, u32[]{:S(2)}, u32[]{:S(2)}) async-start(bf16[8,2,16,896]{3,2,1,0:T(8,128)(2,1)} %spread.1), calls=%async_computation.2 | async-start | bytes 917504 | tf_op jit(solution)/shard_map/all_to_all | solution.py:232
  94.1 5.9 %collective-permute-start.6 = (bf16[64,512]{1,0:T(8,128)(2,1)S(1)}, bf16[64,512]{1,0:T(8,128)(2,1)S(1)}, u32[]{:S(2)}, u32[]{:S(2)}) collective-permute-start(bf16[64,512]{1,0:T(8,128)(2,1)S(1)} %get-tuple-element.33), channel_id=1, source_target_pairs={{0,1},{1,0},{2,3},{3,2},{4,5},{5,4},{6,7},{7,6},{8,9},{9,8},{10,11... | collective-permute-start | bytes 196616 | tf_op jit(solution)/shard_map/ppermute | solution.py:37
  96.0 10.6 %all-to-all-start.4 = ((bf16[4,4,16,896]{3,2,1,0:T(8,128)(2,1)}), bf16[4,4,16,896]{3,2,1,0:T(8,128)(2,1)S(1)}, u32[]{:S(2)}, u32[]{:S(2)}) async-start(bf16[4,4,16,896]{3,2,1,0:T(8,128)(2,1)} %broadcast_in_dim.8), calls=%async_computation.4 | async-start | bytes 917504 | tf_op jit(solution)/shard_map/all_to_all | solution.py:244
  107.6 9.4 %collective-permute-start.7 = (bf16[8,16,896]{2,1,0:T(8,128)(2,1)S(1)}, bf16[8,16,896]{2,1,0:T(8,128)(2,1)S(1)}, u32[]{:S(2)}, u32[]{:S(2)}) collective-permute-start(bf16[8,16,896]{2,1,0:T(8,128)(2,1)S(1)} %get-tuple-element.37), channel_id=1, source_target_pairs={{0,8},{8,0},{1,9},{9,1},{2,10},{10,2},{3,11},{11,3},{4,12},{12,4},... | collective-permute-start | bytes 688136 | tf_op jit(solution)/shard_map/ppermute | solution.py:37

commit v11 on v10

--- a/solution.py
+++ b/solution.py
@@ -214,7 +214,7 @@
     near = [neighbour_ids] + [shifted(neighbour_ids, "x", NX, s) for s in range(1, NX)]
     copies = jnp.broadcast_to(encodings, (NY, ROWS, DE))
     over_y = lax.all_to_all(copies, "y", split_axis=0, concat_axis=0, tiled=True)
-    over_y, near, other = lax.optimization_barrier((over_y, near, other))
+    over_y, near[:-1], other = lax.optimization_barrier((over_y, near[:-1], other))
     beside = swapped(over_y, "c", NC)
     block = (reads, ROWS, DE)
     asked = on_core(
@@ -243,10 +243,10 @@
     read_copies, dq_pair = lax.optimization_barrier((read_copies, dq_pair))
     read_x = lax.all_to_all(read_copies, "x", split_axis=0, concat_axis=0, tiled=True)
     dq_back = swapped(dq_pair, "z", NZ)
+    read_x, dq_back = lax.optimization_barrier((read_x, dq_back))
     first = jnp.where(span_at == 0, dq_own, dq_back)
     second = jnp.where(span_at == 0, dq_back, dq_own)
     grad_query = jnp.concatenate([first, second], axis=0)
-    read_x, grad_query = lax.optimization_barrier((read_x, grad_query))
     owners = (NY, ROWS, DE)
     mine, theirs = on_core(
         owner_kernel, "owner_sums",
@@ -254,6 +254,7 @@
         (at, *near), read_x, scratch=[pltpu.VMEM((NC * NY, ROWS, DE), F32)],
     )
     owner_part = (mine + swapped(theirs, "c", NC).astype(F32)).astype(BF16)
+    owner_part, grad_query = lax.optimization_barrier((owner_part, grad_query))
     from_y = lax.all_to_all(owner_part, "y", split_axis=0, concat_axis=0, tiled=True)
     owned = jnp.sum(from_y.astype(F32), axis=0)
     return (grad_query, owned.reshape(1, ROWS, DE))

time: 135 us -> 133 us (0.985)
  waiting for transfers between devices: 30.2 us -> 26.1 us
  starting transfers between devices: 54.8 us -> 57.4 us
    all_to_all x1, waiting for transfers between devices: 5.9 us -> 1.58 us  [local(): lax.all_to_all(read_copies, 'x', split_axis=0, concat_axis=0, tiled=True)]
    all_to_all x1, starting transfers between devices: 4.03 us -> 6.64 us  [local(): lax.all_to_all(read_copies, 'x', split_axis=0, concat_axis=0, tiled=True)]
    ppermute x3, waiting for transfers between devices: 2.33 us -> 4.16 us  [shifted(): lax.ppermute(value, axis, [(i, (i + shift) % size) for i in range(size)])]
    all_to_all x1, waiting for transfers between devices: 13.6 us -> 12 us  [local(): tok = lax.all_to_all(to_z, 'z', split_axis=0, concat_axis=0, tiled=True)]
    all_to_all x1, waiting for transfers between devices: 6.33 us -> 4.92 us  [local(): found = lax.all_to_all(asked, 'x', split_axis=0, concat_axis=0, tiled=True)]
    ppermute x5, waiting for transfers between devices: 2.11 us -> 3.49 us  [swapped(): return lax.ppermute(value, axis, [(i, i ^ 1) for i in range(size)])]
where the time goes in v11:
time: 133 us; the launch traced here: 132 us
  starting transfers between devices  57.4 us (43%)
  blocking collectives  30.8 us (23%)
  waiting for transfers between devices  26.1 us (20%)
  Pallas kernels  10.2 us (8%)
  local copies, waits for them, and re-layouts  3.93 us (3%)
  other arithmetic  2.57 us (2%)
    ppermute x5, starting transfers between devices, swapped(): return lax.ppermute(value, axis, [(i, i ^ 1) for i in range(size)])  20.7 us
    all_to_all x1, blocking collectives, local(): lax.all_to_all(owner_part, 'y', split_axis=0, concat_axis=0, tiled=True)  16.8 us
    all_to_all x1, blocking collectives, local(): lax.all_to_all(part, 'z', split_axis=0, concat_axis=0, tiled=True)  14 us
    all_to_all x1, waiting for transfers between devices, local(): tok = lax.all_to_all(to_z, 'z', split_axis=0, concat_axis=0, tiled=True)  12 us
    ppermute x3, starting transfers between devices, shifted(): lax.ppermute(value, axis, [(i, (i + shift) % size) for i in range(size)])  10.3 us
    all_to_all x1, starting transfers between devices, local(): tok = lax.all_to_all(to_z, 'z', split_axis=0, concat_axis=0, tiled=True)  9.21 us
    all_to_all x1, starting transfers between devices, local(): lax.all_to_all(copies, 'y', split_axis=0, concat_axis=0, tiled=True)  6.82 us
    all_to_all x1, starting transfers between devices, local(): lax.all_to_all(read_copies, 'x', split_axis=0, concat_axis=0, tiled=True)  6.64 us
  transfers between devices with their start and end apart: 12, of which 7 were waited for; matrix products, arithmetic and copies ran while one was open for 3% of the time, Pallas kernels for 2%

profile of v11, /device:TPU:1, one launch (start us, length us, event | category | flops | bytes accessed | tf_op | source)
XLA Modules:
  0.0 132.0 jit_solution(637304291227382703)
XLA Ops:
  0.7 4.8 %collective-permute-start.4 = (bf16[2,896,512]{2,1,0:T(8,128)(2,1)}, bf16[2,896,512]{2,1,0:T(8,128)(2,1)}, u32[]{:S(2)}, u32[]{:S(2)}) collective-permute-start(bf16[2,896,512]{2,1,0:T(8,128)(2,1)} %w_own.1), channel_id=1, source_target_pairs={{0,1},{1,0},{2,3},{3,2},{4,5},{5,4},{6,7},{7,6},{8,9},{9,8},{10,11... | collective-permute-start | bytes 5505032 | tf_op jit(solution)/shard_map/ppermute | solution.py:37
  5.5 1.4 %broadcast_in_dim.7 = bf16[8,16,896]{2,1,0:T(8,128)(2,1)} broadcast(bf16[16,896]{1,0:T(8,128)(2,1)} %bitcast.25), dimensions={1,2} | broadcast | bytes 258048 | tf_op jit(solution)/shard_map/broadcast_in_dim | solution.py:215
  6.9 6.8 %all-to-all-start = ((bf16[8,16,896]{2,1,0:T(8,128)(2,1)}), bf16[8,16,896]{2,1,0:T(8,128)(2,1)S(1)}, u32[]{:S(2)}, u32[]{:S(2)}) async-start(bf16[8,16,896]{2,1,0:T(8,128)(2,1)} %broadcast_in_dim.7), calls=%async_computation | async-start | bytes 458752 | tf_op jit(solution)/shard_map/all_to_all | solution.py:216
  13.8 4.6 %collective-permute-start.1 = (s32[2,2]{1,0:T(2,128)}, s32[2,2]{1,0:T(2,128)S(1)}, u32[]{:S(2)}, u32[]{:S(2)}) collective-permute-start(s32[2,2]{1,0:T(2,128)} %refs_0_.1), channel_id=1, source_target_pairs={{0,256},{128,384},{256,0},{384,128},{1,257},{129,385},{257,1},{385... | collective-permute-start | bytes 56 | tf_op jit(solution)/shard_map/ppermute | solution.py:33
  18.4 2.2 %collective-permute-start = (s32[2,2]{1,0:T(2,128)}, s32[2,2]{1,0:T(2,128)S(1)}, u32[]{:S(2)}, u32[]{:S(2)}) collective-permute-start(s32[2,2]{1,0:T(2,128)} %refs_0_.1), channel_id=1, source_target_pairs={{0,128},{128,256},{256,384},{384,0},{1,129},{129,257},{257,385},{3... | collective-permute-start | bytes 56 | tf_op jit(solution)/shard_map/ppermute | solution.py:33
  21.7 2.8 %collective-permute-done.refs_1_ = s32[2,2]{1,0:T(2,128)S(1)} collective-permute-done((s32[2,2]{1,0:T(2,128)}, s32[2,2]{1,0:T(2,128)S(1)}, u32[]{:S(2)}, u32[]{:S(2)}) %collective-permute-start) | collective-permute-done | bytes 48 | tf_op jit(solution)/shard_map/ppermute | solution.py:33
  24.5 4.3 %collective-permute-start.3 = (bf16[8,16,896]{2,1,0:T(8,128)(2,1)S(1)}, bf16[8,16,896]{2,1,0:T(8,128)(2,1)S(1)}, u32[]{:S(2)}, u32[]{:S(2)}) collective-permute-start(bf16[8,16,896]{2,1,0:T(8,128)(2,1)S(1)} %all-to-all-done.refs_4_), channel_id=1, source_target_pairs={{0,8},{8,0},{1,9},{9,1},{2,10},{10,2},{3,11},{11,3},{4,12},{12,4},... | collective-permute-start | bytes 688136 | tf_op jit(solution)/shard_map/ppermute | solution.py:37
  28.7 3.5 %collective-permute-start.2 = (s32[2,2]{1,0:T(2,128)}, s32[2,2]{1,0:T(2,128)S(1)}, u32[]{:S(2)}, u32[]{:S(2)}) collective-permute-start(s32[2,2]{1,0:T(2,128)} %refs_0_.1), channel_id=1, source_target_pairs={{0,384},{128,0},{256,128},{384,256},{1,385},{129,1},{257,129},{385... | collective-permute-start | bytes 56 | tf_op jit(solution)/shard_map/ppermute | solution.py:33
  32.3 1.4 %collective-permute-done.2.refs_3_ = s32[2,2]{1,0:T(2,128)S(1)} collective-permute-done((s32[2,2]{1,0:T(2,128)}, s32[2,2]{1,0:T(2,128)S(1)}, u32[]{:S(2)}, u32[]{:S(2)}) %collective-permute-start.2) | collective-permute-done | bytes 48 | tf_op jit(solution)/shard_map/ppermute | solution.py:33
  34.3 1.5 %pick.1 = bf16[4,4,16,896]{3,2,1,0:T(8,128)(2,1)} custom-call(s32[2]{0:T(128)S(1)} %pad_add_fusion.at_ref, s32[2,2]{1,0:T(2,128)S(1)} %copy-done.1, s32[2,2]{1,0:T(2,128)S(1)} %collective-permute-done.refs_1_, s32[2,2]{1,0:T(2,128)S(1)} %collective-permute-done.1.refs_2_, s32[2,2]{1,0:T(2,128)S(1)} %collective-permute-done.2.refs_3_, ...), custom_call_target="tpu_custom_call" | custom-call | tf_op jit(solution)/shard_map/pick/pallas_call | solution.py:154
  35.9 3.8 %all-to-all-start.1 = ((bf16[4,4,16,896]{3,2,1,0:T(8,128)(2,1)}), bf16[4,4,16,896]{3,2,1,0:T(8,128)(2,1)S(1)}, u32[]{:S(2)}, u32[]{:S(2)}) async-start(bf16[4,4,16,896]{3,2,1,0:T(8,128)(2,1)} %pick.1), calls=%async_computation.1 | async-start | bytes 917504 | tf_op jit(solution)/shard_map/all_to_all | solution.py:224
  39.7 1.9 %collective-permute-start.5 = (bf16[128,512]{1,0:T(8,128)(2,1)S(1)}, bf16[128,512]{1,0:T(8,128)(2,1)S(1)}, u32[]{:S(2)}, u32[]{:S(2)}) collective-permute-start(bf16[128,512]{1,0:T(8,128)(2,1)S(1)} %pad_maximum_fusion), channel_id=1, source_target_pairs={{0,1},{1,0},{2,3},{3,2},{4,5},{5,4},{6,7},{7,6},{8,9},{9,8},{10,11... | collective-permute-start | bytes 393224 | tf_op jit(solution)/shard_map/ppermute | solution.py:37
  41.8 4.9 %all-to-all-done.1.from_ref = bf16[4,4,16,896]{3,2,1,0:T(8,128)(2,1)S(1)} async-done(((bf16[4,4,16,896]{3,2,1,0:T(8,128)(2,1)}), bf16[4,4,16,896]{3,2,1,0:T(8,128)(2,1)S(1)}, u32[]{:S(2)}, u32[]{:S(2)}) %all-to-all-start.1) | async-done | bytes 458784 | tf_op jit(solution)/shard_map/all_to_all | solution.py:224
  46.7 1.4 %spread.1 = bf16[8,2,16,896]{3,2,1,0:T(8,128)(2,1)} custom-call(s32[2,2]{1,0:T(2,128)S(1)} %copy-done.2, bf16[4,4,16,896]{3,2,1,0:T(8,128)(2,1)S(1)} %all-to-all-done.1.from_ref), custom_call_target="tpu_custom_call" | custom-call | tf_op jit(solution)/shard_map/spread/pallas_call | solution.py:154
  48.1 9.2 %all-to-all-start.2 = ((bf16[8,2,16,896]{3,2,1,0:T(8,128)(2,1)}), bf16[8,2,16,896]{3,2,1,0:T(8,128)(2,1)S(1)}, u32[]{:S(2)}, u32[]{:S(2)}) async-start(bf16[8,2,16,896]{3,2,1,0:T(8,128)(2,1)} %spread.1), calls=%async_computation.2 | async-start | bytes 917504 | tf_op jit(solution)/shard_map/all_to_all | solution.py:232
  58.2 12.0 %all-to-all-done.2.tok = bf16[8,2,16,896]{3,2,1,0:T(8,128)(2,1)S(1)} async-done(((bf16[8,2,16,896]{3,2,1,0:T(8,128)(2,1)}), bf16[8,2,16,896]{3,2,1,0:T(8,128)(2,1)S(1)}, u32[]{:S(2)}, u32[]{:S(2)}) %all-to-all-start.2) | async-done | bytes 458784 | tf_op jit(solution)/shard_map/all_to_all | solution.py:232
  70.2 6.4 %attention.1 = (bf16[8,2,16,896]{3,2,1,0:T(8,128)(2,1)S(1)}, bf16[64,512]{1,0:T(8,128)(2,1)S(1)}, bf16[64,512]{1,0:T(8,128)(2,1)S(1)}) custom-call(bf16[8,2,16,896]{3,2,1,0:T(8,128)(2,1)S(1)} %all-to-all-done.2.tok, bf16[2,896,512]{2,1,0:T(8,128)(2,1)S(1)} %copy-done.3, bf16[64,512]{1,0:T(8,128)(2,1)S(1)} %get-tuple-element.53.q_own, ...), custom_call_target="tpu_custom_call" | custom-call | flops 2100000000 | bytes 6000000 | tf_op jit(solution)/shard_map/attention/pallas_call | solution.py:167
  76.5 14.0 %all_to_all.30 = bf16[8,2,16,896]{3,2,1,0:T(8,128)(2,1)S(1)} all-to-all(bf16[8,2,16,896]{3,2,1,0:T(8,128)(2,1)S(1)} %get-tuple-element.29), channel_id=1, replica_groups=mesh['x'=4,'y'=8,'c'=2,'z'=8] {'z'}, dimensions={0} | all-to-all | bytes 917504 | tf_op jit(solution)/shard_map/all_to_all | solution.py:238
  91.5 6.6 %all-to-all-start.4 = ((bf16[4,4,16,896]{3,2,1,0:T(8,128)(2,1)}), bf16[4,4,16,896]{3,2,1,0:T(8,128)(2,1)S(1)}, u32[]{:S(2)}, u32[]{:S(2)}) async-start(bf16[4,4,16,896]{3,2,1,0:T(8,128)(2,1)} %broadcast_in_dim.8), calls=%async_computation.4 | async-start | bytes 917504 | tf_op jit(solution)/shard_map/all_to_all | solution.py:244
  98.1 1.9 %collective-permute-start.6 = (bf16[64,512]{1,0:T(8,128)(2,1)S(1)}, bf16[64,512]{1,0:T(8,128)(2,1)S(1)}, u32[]{:S(2)}, u32[]{:S(2)}) collective-permute-start(bf16[64,512]{1,0:T(8,128)(2,1)S(1)} %get-tuple-element.32), channel_id=1, source_target_pairs={{0,1},{1,0},{2,3},{3,2},{4,5},{5,4},{6,7},{7,6},{8,9},{9,8},{10,11... | collective-permute-start | bytes 196616 | tf_op jit(solution)/shard_map/ppermute | solution.py:37
  100.0 3.1 %collective-permute-done.6 = bf16[64,512]{1,0:T(8,128)(2,1)S(1)} collective-permute-done((bf16[64,512]{1,0:T(8,128)(2,1)S(1)}, bf16[64,512]{1,0:T(8,128)(2,1)S(1)}, u32[]{:S(2)}, u32[]{:S(2)}) %collective-permute-start.6) | collective-permute-done | bytes 65568 | tf_op jit(solution)/shard_map/ppermute | solution.py:37
  103.1 1.6 %all-to-all-done.4.refs_4_ = bf16[4,4,16,896]{3,2,1,0:T(8,128)(2,1)S(1)} async-done(((bf16[4,4,16,896]{3,2,1,0:T(8,128)(2,1)}), bf16[4,4,16,896]{3,2,1,0:T(8,128)(2,1)S(1)}, u32[]{:S(2)}, u32[]{:S(2)}) %all-to-all-start.4) | async-done | bytes 458784 | tf_op jit(solution)/shard_map/all_to_all | solution.py:244
  105.6 7.7 %collective-permute-start.7 = (bf16[8,16,896]{2,1,0:T(8,128)(2,1)S(1)}, bf16[8,16,896]{2,1,0:T(8,128)(2,1)S(1)}, u32[]{:S(2)}, u32[]{:S(2)}) collective-permute-start(bf16[8,16,896]{2,1,0:T(8,128)(2,1)S(1)} %get-tuple-element.35), channel_id=1, source_target_pairs={{0,8},{8,0},{1,9},{9,1},{2,10},{10,2},{3,11},{11,3},{4,12},{12,4},... | collective-permute-start | bytes 688136 | tf_op jit(solution)/shard_map/ppermute | solution.py:37
  114.5 16.8 %all_to_all.31 = bf16[8,16,896]{2,1,0:T(8,128)(2,1)S(1)} all-to-all(bf16[8,16,896]{2,1,0:T(8,128)(2,1)S(1)} %add_convert_fusion), channel_id=1, replica_groups=mesh['x'=4,'y'=8,'c'=2,'z'=8] {'y'}, dimensions={0} | all-to-all | bytes 458752 | tf_op jit(solution)/shard_map/all_to_all | solution.py:258
  (32 shorter events, 6.4 us)
Async XLA Ops:
  0.6 56.7 %copy-start = (s32[2,2]{1,0:T(2,128)S(1)}, s32[2,2]{1,0:T(2,128)}, u32[]{:S(2)}) copy-start(s32[2,2]{1,0:T(2,128)} %param.11) | copy-start | bytes 52
  0.6 46.1 %copy-start.2 = (s32[2,2]{1,0:T(2,128)S(1)}, s32[2,2]{1,0:T(2,128)}, u32[]{:S(2)}) copy-start(s32[2,2]{1,0:T(2,128)} %refs_0_.1) | copy-start | bytes 52
  0.7 47.5 %collective-permute-start.4 = (bf16[2,896,512]{2,1,0:T(8,128)(2,1)}, bf16[2,896,512]{2,1,0:T(8,128)(2,1)}, u32[]{:S(2)}, u32[]{:S(2)}) collective-permute-start(bf16[2,896,512]{2,1,0:T(8,128)(2,1)} %w_own.1), channel_id=1, source_target_pairs={{0,1},{1,0},{2,3},{3,2},{4,5},{5,4},{6,7},{7,6},{8,9},{9,8},{10,11... | collective-permute-start | bytes 5505032 | tf_op jit(solution)/shard_map/ppermute | solution.py:37
  6.9 17.5 %all-to-all-start = ((bf16[8,16,896]{2,1,0:T(8,128)(2,1)}), bf16[8,16,896]{2,1,0:T(8,128)(2,1)S(1)}, u32[]{:S(2)}, u32[]{:S(2)}) async-start(bf16[8,16,896]{2,1,0:T(8,128)(2,1)} %broadcast_in_dim.7), calls=%async_computation | async-start | bytes 458752 | tf_op jit(solution)/shard_map/all_to_all | solution.py:216
  13.8 7.9 %collective-permute-start.1 = (s32[2,2]{1,0:T(2,128)}, s32[2,2]{1,0:T(2,128)S(1)}, u32[]{:S(2)}, u32[]{:S(2)}) collective-permute-start(s32[2,2]{1,0:T(2,128)} %refs_0_.1), channel_id=1, source_target_pairs={{0,256},{128,384},{256,0},{384,128},{1,257},{129,385},{257,1},{385... | collective-permute-start | bytes 56 | tf_op jit(solution)/shard_map/ppermute | solution.py:33
  18.4 6.0 %collective-permute-start = (s32[2,2]{1,0:T(2,128)}, s32[2,2]{1,0:T(2,128)S(1)}, u32[]{:S(2)}, u32[]{:S(2)}) collective-permute-start(s32[2,2]{1,0:T(2,128)} %refs_0_.1), channel_id=1, source_target_pairs={{0,128},{128,256},{256,384},{384,0},{1,129},{129,257},{257,385},{3... | collective-permute-start | bytes 56 | tf_op jit(solution)/shard_map/ppermute | solution.py:33
  24.5 9.2 %collective-permute-start.3 = (bf16[8,16,896]{2,1,0:T(8,128)(2,1)S(1)}, bf16[8,16,896]{2,1,0:T(8,128)(2,1)S(1)}, u32[]{:S(2)}, u32[]{:S(2)}) collective-permute-start(bf16[8,16,896]{2,1,0:T(8,128)(2,1)S(1)} %all-to-all-done.refs_4_), channel_id=1, source_target_pairs={{0,8},{8,0},{1,9},{9,1},{2,10},{10,2},{3,11},{11,3},{4,12},{12,4},... | collective-permute-start | bytes 688136 | tf_op jit(solution)/shard_map/ppermute | solution.py:37
  28.7 4.9 %collective-permute-start.2 = (s32[2,2]{1,0:T(2,128)}, s32[2,2]{1,0:T(2,128)S(1)}, u32[]{:S(2)}, u32[]{:S(2)}) collective-permute-start(s32[2,2]{1,0:T(2,128)} %refs_0_.1), channel_id=1, source_target_pairs={{0,384},{128,0},{256,128},{384,256},{1,385},{129,1},{257,129},{385... | collective-permute-start | bytes 56 | tf_op jit(solution)/shard_map/ppermute | solution.py:33
  33.7 0.7 copy-start.1
  35.9 34.3 %copy-start.3 = (bf16[2,896,512]{2,1,0:T(8,128)(2,1)S(1)}, bf16[2,896,512]{2,1,0:T(8,128)(2,1)}, u32[]{:S(2)}) copy-start(bf16[2,896,512]{2,1,0:T(8,128)(2,1)} %w_own.1) | copy-start | bytes 5505028
  35.9 10.8 %all-to-all-start.1 = ((bf16[4,4,16,896]{3,2,1,0:T(8,128)(2,1)}), bf16[4,4,16,896]{3,2,1,0:T(8,128)(2,1)S(1)}, u32[]{:S(2)}, u32[]{:S(2)}) async-start(bf16[4,4,16,896]{3,2,1,0:T(8,128)(2,1)} %pick.1), calls=%async_computation.1 | async-start | bytes 917504 | tf_op jit(solution)/shard_map/all_to_all | solution.py:224
  39.7 8.4 %collective-permute-start.5 = (bf16[128,512]{1,0:T(8,128)(2,1)S(1)}, bf16[128,512]{1,0:T(8,128)(2,1)S(1)}, u32[]{:S(2)}, u32[]{:S(2)}) collective-permute-start(bf16[128,512]{1,0:T(8,128)(2,1)S(1)} %pad_maximum_fusion), channel_id=1, source_target_pairs={{0,1},{1,0},{2,3},{3,2},{4,5},{5,4},{6,7},{7,6},{8,9},{9,8},{10,11... | collective-permute-start | bytes 393224 | tf_op jit(solution)/shard_map/ppermute | solution.py:37
  48.1 22.1 %all-to-all-start.2 = ((bf16[8,2,16,896]{3,2,1,0:T(8,128)(2,1)}), bf16[8,2,16,896]{3,2,1,0:T(8,128)(2,1)S(1)}, u32[]{:S(2)}, u32[]{:S(2)}) async-start(bf16[8,2,16,896]{3,2,1,0:T(8,128)(2,1)} %spread.1), calls=%async_computation.2 | async-start | bytes 917504 | tf_op jit(solution)/shard_map/all_to_all | solution.py:232
  91.5 13.2 %all-to-all-start.4 = ((bf16[4,4,16,896]{3,2,1,0:T(8,128)(2,1)}), bf16[4,4,16,896]{3,2,1,0:T(8,128)(2,1)S(1)}, u32[]{:S(2)}, u32[]{:S(2)}) async-start(bf16[4,4,16,896]{3,2,1,0:T(8,128)(2,1)} %broadcast_in_dim.8), calls=%async_computation.4 | async-start | bytes 917504 | tf_op jit(solution)/shard_map/all_to_all | solution.py:244
  98.1 5.0 %collective-permute-start.6 = (bf16[64,512]{1,0:T(8,128)(2,1)S(1)}, bf16[64,512]{1,0:T(8,128)(2,1)S(1)}, u32[]{:S(2)}, u32[]{:S(2)}) collective-permute-start(bf16[64,512]{1,0:T(8,128)(2,1)S(1)} %get-tuple-element.32), channel_id=1, source_target_pairs={{0,1},{1,0},{2,3},{3,2},{4,5},{5,4},{6,7},{7,6},{8,9},{9,8},{10,11... | collective-permute-start | bytes 196616 | tf_op jit(solution)/shard_map/ppermute | solution.py:37
  105.6 8.8 %collective-permute-start.7 = (bf16[8,16,896]{2,1,0:T(8,128)(2,1)S(1)}, bf16[8,16,896]{2,1,0:T(8,128)(2,1)S(1)}, u32[]{:S(2)}, u32[]{:S(2)}) collective-permute-start(bf16[8,16,896]{2,1,0:T(8,128)(2,1)S(1)} %get-tuple-element.35), channel_id=1, source_target_pairs={{0,8},{8,0},{1,9},{9,1},{2,10},{10,2},{3,11},{11,3},{4,12},{12,4},... | collective-permute-start | bytes 688136 | tf_op jit(solution)/shard_map/ppermute | solution.py:37

commit v12 on v11

--- a/solution.py
+++ b/solution.py
@@ -13,6 +13,7 @@
 NEIGH = 2
 NLEN = 128
 NX, NY, NC, NZ = 4, 8, 2, 8
+FETCHES = 4
 ROWS = NLEN // NZ
 F32, BF16 = jnp.float32, jnp.bfloat16
 VMEM = pl.BlockSpec(memory_space=pltpu.VMEM)
@@ -43,17 +44,23 @@
     )
 
 
+def read_id(at_ref, near, distance, read):
+    if distance == 0:
+        return at_ref[2 + read]
+    return near[distance - 1][read // NEIGH, read % NEIGH]
+
+
 def at_distance(at_ref, distance):
     return lax.rem(at_ref[0] - distance + NX, NX)
 
 
 def pick_kernel(at_ref, *refs):
-    near, (mine_ref, theirs_ref, out_ref, sems) = refs[:NX], refs[NX:]
+    near, (mine_ref, theirs_ref, out_ref, sems) = refs[:NX - 1], refs[NX - 1:]
     core, reads = at_ref[1], out_ref.shape[1]
     for distance in range(NX):
         column = at_distance(at_ref, distance)
         for read in range(reads):
-            block = near[distance][read // NEIGH, read % NEIGH]
+            block = read_id(at_ref, near, distance, read)
             row, same = lax.rem(block // NC, NY), lax.rem(block, NC) == core
             sem = sems.at[distance * reads + read]
 
@@ -70,24 +77,24 @@
         pltpu.make_async_copy(mine_ref.at[0], place, sems.at[count]).wait()
 
 
-def spread_kernel(ids_ref, from_ref, out_ref):
+def spread_kernel(at_ref, from_ref, out_ref):
     reads = from_ref.shape[1]
     spans = reads // NEIGH
     for read in range(reads):
-        owner = ids_ref[read // NEIGH, read % NEIGH]
+        owner = at_ref[2 + read]
         block = from_ref[owner // (NY * NC), read]
         for at in range(read // NEIGH, NZ, spans):
             out_ref[at, read % NEIGH] = block
 
 
 def owner_kernel(at_ref, *refs):
-    near, (from_ref, mine_ref, theirs_ref, total) = refs[:NX], refs[NX:]
+    near, (from_ref, mine_ref, theirs_ref, total) = refs[:NX - 1], refs[NX - 1:]
     total[...] = jnp.zeros_like(total)
     here, core = at_ref[0], at_ref[1]
     for distance in range(NX):
         column = at_distance(at_ref, distance)
         for read in range(from_ref.shape[1]):
-            block = near[distance][read // NEIGH, read % NEIGH]
+            block = read_id(at_ref, near, distance, read)
 
             @pl.when(block // (NY * NC) == here)
             def _():
@@ -101,23 +108,29 @@
 
 def attention_kernel(
     tok, w_own, q_own, g_own, from_pair, kc, ks, qc, qs, w_far,
-    part, dq_own, dq_pair, dk_all, dv_all, w_pair, sem,
+    part, dq_own, dq_pair, dk_all, dv_all, w_pair, sems,
 ):
-    fetch = pltpu.make_async_copy(w_far, w_pair, sem)
-    fetch.start()
+    step = w_own.shape[1] // FETCHES
+    fetches = [
+        [
+            pltpu.make_async_copy(
+                w_far.at[part_at, pl.ds(i * step, step)],
+                w_pair.at[part_at, pl.ds(i * step, step)],
+                sems.at[part_at, i],
+            )
+            for i in range(FETCHES)
+        ]
+        for part_at in range(2)
+    ]
+    for fetch in fetches[0] + fetches[1]:
+        fetch.start()
     scale = 1.0 / math.sqrt(HEAD)
     half = HEAD // 2
     width = w_own.shape[2]
     rows = jnp.concatenate([tok[:, n].reshape(NLEN, DE) for n in range(NEIGH)], axis=0)
-    projected = [(dot(rows, w_own[0]), dot(rows, w_own[1]).astype(BF16))]
-    fetch.wait()
-    projected.append((dot(rows, w_pair[0]), dot(rows, w_pair[1]).astype(BF16)))
     key_cos, key_sin, query_cos, query_sin = kc[...], ks[...], qc[...], qs[...]
-    for turn, (q, g, dq) in enumerate((
-        (q_own, g_own, dq_own),
-        (from_pair.at[:SPAN], from_pair.at[SPAN:], dq_pair),
-    )):
-        key_raw, values = projected[turn]
+
+    def heads(turn, key_raw, values, q, g, dq):
         for head in range(width // HEAD):
             cols = slice(head * HEAD, (head + 1) * HEAD)
             place = slice(turn * width + head * HEAD, turn * width + (head + 1) * HEAD)
@@ -142,6 +155,16 @@
             dk_all[:, place] = (
                 grad_key * key_cos - pltpu.roll(grad_key, half, 1) * key_sin
             ).astype(BF16)
+
+    key_own, values_own = dot(rows, w_own[0]), dot(rows, w_own[1]).astype(BF16)
+    for fetch in fetches[0]:
+        fetch.wait()
+    key_pair = dot(rows, w_pair[0])
+    heads(0, key_own, values_own, q_own, g_own, dq_own)
+    for fetch in fetches[1]:
+        fetch.wait()
+    values_pair = dot(rows, w_pair[1]).astype(BF16)
+    heads(1, key_pair, values_pair, from_pair.at[:SPAN], from_pair.at[SPAN:], dq_pair)
     product = dot(dk_all[:, :width], w_own[0], (1, 1)) + dot(dv_all[:, :width], w_own[1], (1, 1))
     product = product + dot(dk_all[:, width:], w_pair[0], (1, 1))
     product = product + dot(dv_all[:, width:], w_pair[1], (1, 1))
@@ -177,7 +200,7 @@
             pltpu.VMEM((NEIGH * NLEN, 2 * width), BF16),
             pltpu.VMEM((NEIGH * NLEN, 2 * width), BF16),
             pltpu.VMEM((2, depth, width), BF16),
-            pltpu.SemaphoreType.DMA,
+            pltpu.SemaphoreType.DMA((2, FETCHES)),
         ],
         compiler_params=pltpu.CompilerParams(vmem_limit_bytes=40 << 20),
         cost_estimate=pl.CostEstimate(
@@ -210,8 +233,8 @@
     key_cos, key_sin = rotary_tables(positions.reshape(NEIGH * NLEN))
     query_cos, query_sin = rotary_tables(jnp.arange(SPAN, dtype=jnp.int32))
 
-    at = jnp.stack([x_at, c_at])
-    near = [neighbour_ids] + [shifted(neighbour_ids, "x", NX, s) for s in range(1, NX)]
+    at = jnp.concatenate([x_at.reshape(1), c_at.reshape(1), neighbour_ids.reshape(reads)])
+    near = [shifted(neighbour_ids, "x", NX, s) for s in range(1, NX)]
     copies = jnp.broadcast_to(encodings, (NY, ROWS, DE))
     over_y = lax.all_to_all(copies, "y", split_axis=0, concat_axis=0, tiled=True)
     over_y, near[:-1], other = lax.optimization_barrier((over_y, near[:-1], other))
@@ -224,7 +247,7 @@
     found = lax.all_to_all(asked, "x", split_axis=0, concat_axis=0, tiled=True)
 
     to_z = on_core(
-        spread_kernel, "spread", jax.ShapeDtypeStruct((NZ, NEIGH, ROWS, DE), BF16), (neighbour_ids,),
+        spread_kernel, "spread", jax.ShapeDtypeStruct((NZ, NEIGH, ROWS, DE), BF16), (at,),
         found,
     )
     from_pair = swapped(other, "z", NZ)

time: 133 us -> 133 us (level)
  waiting for transfers between devices: 26.1 us -> 23.7 us
  blocking collectives: 30.8 us -> 32.7 us
    ppermute x3, waiting for transfers between devices: 4.16 us -> 0.72 us  [shifted(): lax.ppermute(value, axis, [(i, (i + shift) % size) for i in range(size)])]
    all_to_all x1, starting transfers between devices: 6.64 us -> 3.99 us  [local(): lax.all_to_all(read_copies, 'x', split_axis=0, concat_axis=0, tiled=True)]
    all_to_all x1, blocking collectives: 14 us -> 15.9 us  [local(): lax.all_to_all(part, 'z', split_axis=0, concat_axis=0, tiled=True)]
    ppermute x3, starting transfers between devices: 10.3 us -> 11.9 us  [shifted(): lax.ppermute(value, axis, [(i, (i + shift) % size) for i in range(size)])]
  transfers between devices with their start and end apart: 12 -> 12, of which waited for: 7 -> 8; matrix products, arithmetic and copies ran while one was open for 3% -> 4% of each run, Pallas kernels for 2% -> 2%
where the time goes in v12:
time: 133 us; the launch traced here: 132 us
  starting transfers between devices  57.9 us (44%)
  blocking collectives  32.7 us (25%)
  waiting for transfers between devices  23.7 us (18%)
  Pallas kernels  10.3 us (8%)
  local copies, waits for them, and re-layouts  4.02 us (3%)
  other arithmetic  2.58 us (2%)
    ppermute x5, starting transfers between devices, swapped(): return lax.ppermute(value, axis, [(i, i ^ 1) for i in range(size)])  21 us
    all_to_all x1, blocking collectives, local(): lax.all_to_all(owner_part, 'y', split_axis=0, concat_axis=0, tiled=True)  16.7 us
    all_to_all x1, blocking collectives, local(): lax.all_to_all(part, 'z', split_axis=0, concat_axis=0, tiled=True)  15.9 us
    all_to_all x1, waiting for transfers between devices, local(): tok = lax.all_to_all(to_z, 'z', split_axis=0, concat_axis=0, tiled=True)  12.7 us
    ppermute x3, starting transfers between devices, shifted(): lax.ppermute(value, axis, [(i, (i + shift) % size) for i in range(size)])  11.9 us
    all_to_all x1, starting transfers between devices, local(): tok = lax.all_to_all(to_z, 'z', split_axis=0, concat_axis=0, tiled=True)  9.91 us
    all_to_all x1, starting transfers between devices, local(): lax.all_to_all(copies, 'y', split_axis=0, concat_axis=0, tiled=True)  6.82 us
    pallas_call x1, Pallas kernels, attention(): pl.pallas_call(attention_kernel, out_shape=(jax.ShapeDtypeStruct((NZ, NEI...  6.5 us
  transfers between devices with their start and end apart: 12, of which 8 were waited for; matrix products, arithmetic and copies ran while one was open for 4% of the time, Pallas kernels for 2%

profile of v12, /device:TPU:1, one launch (start us, length us, event | category | flops | bytes accessed | tf_op | source)
XLA Modules:
  0.0 132.1 jit_solution(4872223497082147067)
XLA Ops:
  0.6 4.8 %collective-permute-start.4 = (bf16[2,896,512]{2,1,0:T(8,128)(2,1)}, bf16[2,896,512]{2,1,0:T(8,128)(2,1)}, u32[]{:S(2)}, u32[]{:S(2)}) collective-permute-start(bf16[2,896,512]{2,1,0:T(8,128)(2,1)} %w_own.1), channel_id=1, source_target_pairs={{0,1},{1,0},{2,3},{3,2},{4,5},{5,4},{6,7},{7,6},{8,9},{9,8},{10,11... | collective-permute-start | bytes 5505032 | tf_op jit(solution)/shard_map/ppermute | solution.py:38
  5.5 1.5 %broadcast_in_dim.7 = bf16[8,16,896]{2,1,0:T(8,128)(2,1)} broadcast(bf16[16,896]{1,0:T(8,128)(2,1)} %bitcast.25), dimensions={1,2} | broadcast | bytes 258048 | tf_op jit(solution)/shard_map/broadcast_in_dim | solution.py:238
  6.9 6.8 %all-to-all-start = ((bf16[8,16,896]{2,1,0:T(8,128)(2,1)}), bf16[8,16,896]{2,1,0:T(8,128)(2,1)S(1)}, u32[]{:S(2)}, u32[]{:S(2)}) async-start(bf16[8,16,896]{2,1,0:T(8,128)(2,1)} %broadcast_in_dim.7), calls=%async_computation | async-start | bytes 458752 | tf_op jit(solution)/shard_map/all_to_all | solution.py:239
  13.8 3.1 %collective-permute-start = (s32[2,2]{1,0:T(2,128)}, s32[2,2]{1,0:T(2,128)S(1)}, u32[]{:S(2)}, u32[]{:S(2)}) collective-permute-start(s32[2,2]{1,0:T(2,128)} %param.10), channel_id=1, source_target_pairs={{0,128},{128,256},{256,384},{384,0},{1,129},{129,257},{257,385},{3... | collective-permute-start | bytes 56 | tf_op jit(solution)/shard_map/ppermute | solution.py:34
  16.9 4.4 %collective-permute-start.1 = (s32[2,2]{1,0:T(2,128)}, s32[2,2]{1,0:T(2,128)S(1)}, u32[]{:S(2)}, u32[]{:S(2)}) collective-permute-start(s32[2,2]{1,0:T(2,128)} %param.10), channel_id=1, source_target_pairs={{0,256},{128,384},{256,0},{384,128},{1,257},{129,385},{257,1},{385... | collective-permute-start | bytes 56 | tf_op jit(solution)/shard_map/ppermute | solution.py:34
  21.3 1.0 dynamic-slice_bitcast_fusion
  23.2 4.6 %collective-permute-start.3 = (bf16[8,16,896]{2,1,0:T(8,128)(2,1)S(1)}, bf16[8,16,896]{2,1,0:T(8,128)(2,1)S(1)}, u32[]{:S(2)}, u32[]{:S(2)}) collective-permute-start(bf16[8,16,896]{2,1,0:T(8,128)(2,1)S(1)} %all-to-all-done.refs_3_), channel_id=1, source_target_pairs={{0,8},{8,0},{1,9},{9,1},{2,10},{10,2},{3,11},{11,3},{4,12},{12,4},... | collective-permute-start | bytes 688136 | tf_op jit(solution)/shard_map/ppermute | solution.py:38
  27.8 4.4 %collective-permute-start.2 = (s32[2,2]{1,0:T(2,128)}, s32[2,2]{1,0:T(2,128)S(1)}, u32[]{:S(2)}, u32[]{:S(2)}) collective-permute-start(s32[2,2]{1,0:T(2,128)} %param.10), channel_id=1, source_target_pairs={{0,384},{128,0},{256,128},{384,256},{1,385},{129,1},{257,129},{385... | collective-permute-start | bytes 56 | tf_op jit(solution)/shard_map/ppermute | solution.py:34
  33.1 1.5 %pick.1 = bf16[4,4,16,896]{3,2,1,0:T(8,128)(2,1)} custom-call(s32[6]{0:T(128)S(1)} %pad_add_fusion.at_ref, s32[2,2]{1,0:T(2,128)S(1)} %collective-permute-done.refs_0_, s32[2,2]{1,0:T(2,128)S(1)} %collective-permute-done.1.refs_1_, s32[2,2]{1,0:T(2,128)S(1)} %collective-permute-done.2.refs_2_, bf16[8,16,896]{2,1,0:T(8,128)(2,1)S(1)} %all-to-all-done.refs_3_, ...), custom_call_target="tpu_custom_call" | custom-call | tf_op jit(solution)/shard_map/pick/pallas_call | solution.py:177
  34.7 4.3 %all-to-all-start.1 = ((bf16[4,4,16,896]{3,2,1,0:T(8,128)(2,1)}), bf16[4,4,16,896]{3,2,1,0:T(8,128)(2,1)S(1)}, u32[]{:S(2)}, u32[]{:S(2)}) async-start(bf16[4,4,16,896]{3,2,1,0:T(8,128)(2,1)} %pick.1), calls=%async_computation.1 | async-start | bytes 917504 | tf_op jit(solution)/shard_map/all_to_all | solution.py:247
  39.0 1.9 %collective-permute-start.5 = (bf16[128,512]{1,0:T(8,128)(2,1)S(1)}, bf16[128,512]{1,0:T(8,128)(2,1)S(1)}, u32[]{:S(2)}, u32[]{:S(2)}) collective-permute-start(bf16[128,512]{1,0:T(8,128)(2,1)S(1)} %pad_maximum_fusion), channel_id=1, source_target_pairs={{0,1},{1,0},{2,3},{3,2},{4,5},{5,4},{6,7},{7,6},{8,9},{9,8},{10,11... | collective-permute-start | bytes 393224 | tf_op jit(solution)/shard_map/ppermute | solution.py:38
  41.1 4.9 %all-to-all-done.1.from_ref = bf16[4,4,16,896]{3,2,1,0:T(8,128)(2,1)S(1)} async-done(((bf16[4,4,16,896]{3,2,1,0:T(8,128)(2,1)}), bf16[4,4,16,896]{3,2,1,0:T(8,128)(2,1)S(1)}, u32[]{:S(2)}, u32[]{:S(2)}) %all-to-all-start.1) | async-done | bytes 458784 | tf_op jit(solution)/shard_map/all_to_all | solution.py:247
  46.0 1.4 %spread.1 = bf16[8,2,16,896]{3,2,1,0:T(8,128)(2,1)} custom-call(s32[6]{0:T(128)S(1)} %pad_add_fusion.at_ref, bf16[4,4,16,896]{3,2,1,0:T(8,128)(2,1)S(1)} %all-to-all-done.1.from_ref), custom_call_target="tpu_custom_call" | custom-call | tf_op jit(solution)/shard_map/spread/pallas_call | solution.py:177
  47.4 9.9 %all-to-all-start.2 = ((bf16[8,2,16,896]{3,2,1,0:T(8,128)(2,1)}), bf16[8,2,16,896]{3,2,1,0:T(8,128)(2,1)S(1)}, u32[]{:S(2)}, u32[]{:S(2)}) async-start(bf16[8,2,16,896]{3,2,1,0:T(8,128)(2,1)} %spread.1), calls=%async_computation.2 | async-start | bytes 917504 | tf_op jit(solution)/shard_map/all_to_all | solution.py:255
  58.2 12.7 %all-to-all-done.2.tok = bf16[8,2,16,896]{3,2,1,0:T(8,128)(2,1)S(1)} async-done(((bf16[8,2,16,896]{3,2,1,0:T(8,128)(2,1)}), bf16[8,2,16,896]{3,2,1,0:T(8,128)(2,1)S(1)}, u32[]{:S(2)}, u32[]{:S(2)}) %all-to-all-start.2) | async-done | bytes 458784 | tf_op jit(solution)/shard_map/all_to_all | solution.py:255
  70.9 6.5 %attention.1 = (bf16[8,2,16,896]{3,2,1,0:T(8,128)(2,1)S(1)}, bf16[64,512]{1,0:T(8,128)(2,1)S(1)}, bf16[64,512]{1,0:T(8,128)(2,1)S(1)}) custom-call(bf16[8,2,16,896]{3,2,1,0:T(8,128)(2,1)S(1)} %all-to-all-done.2.tok, bf16[2,896,512]{2,1,0:T(8,128)(2,1)S(1)} %copy-done.1, bf16[64,512]{1,0:T(8,128)(2,1)S(1)} %get-tuple-element.51.q_own, ...), custom_call_target="tpu_custom_call" | custom-call | flops 2100000000 | bytes 6000000 | tf_op jit(solution)/shard_map/attention/pallas_call | solution.py:190
  77.4 15.9 %all_to_all.30 = bf16[8,2,16,896]{3,2,1,0:T(8,128)(2,1)S(1)} all-to-all(bf16[8,2,16,896]{3,2,1,0:T(8,128)(2,1)S(1)} %get-tuple-element.27), channel_id=1, replica_groups=mesh['x'=4,'y'=8,'c'=2,'z'=8] {'z'}, dimensions={0} | all-to-all | bytes 917504 | tf_op jit(solution)/shard_map/all_to_all | solution.py:261
  94.2 4.0 %all-to-all-start.4 = ((bf16[4,4,16,896]{3,2,1,0:T(8,128)(2,1)}), bf16[4,4,16,896]{3,2,1,0:T(8,128)(2,1)S(1)}, u32[]{:S(2)}, u32[]{:S(2)}) async-start(bf16[4,4,16,896]{3,2,1,0:T(8,128)(2,1)} %broadcast_in_dim.8), calls=%async_computation.4 | async-start | bytes 917504 | tf_op jit(solution)/shard_map/all_to_all | solution.py:267
  98.2 1.9 %collective-permute-start.6 = (bf16[64,512]{1,0:T(8,128)(2,1)S(1)}, bf16[64,512]{1,0:T(8,128)(2,1)S(1)}, u32[]{:S(2)}, u32[]{:S(2)}) collective-permute-start(bf16[64,512]{1,0:T(8,128)(2,1)S(1)} %get-tuple-element.30), channel_id=1, source_target_pairs={{0,1},{1,0},{2,3},{3,2},{4,5},{5,4},{6,7},{7,6},{8,9},{9,8},{10,11... | collective-permute-start | bytes 196616 | tf_op jit(solution)/shard_map/ppermute | solution.py:38
  100.1 3.1 %collective-permute-done.6 = bf16[64,512]{1,0:T(8,128)(2,1)S(1)} collective-permute-done((bf16[64,512]{1,0:T(8,128)(2,1)S(1)}, bf16[64,512]{1,0:T(8,128)(2,1)S(1)}, u32[]{:S(2)}, u32[]{:S(2)}) %collective-permute-start.6) | collective-permute-done | bytes 65568 | tf_op jit(solution)/shard_map/ppermute | solution.py:38
  103.2 1.6 %all-to-all-done.4.refs_3_ = bf16[4,4,16,896]{3,2,1,0:T(8,128)(2,1)S(1)} async-done(((bf16[4,4,16,896]{3,2,1,0:T(8,128)(2,1)}), bf16[4,4,16,896]{3,2,1,0:T(8,128)(2,1)S(1)}, u32[]{:S(2)}, u32[]{:S(2)}) %all-to-all-start.4) | async-done | bytes 458784 | tf_op jit(solution)/shard_map/all_to_all | solution.py:267
  104.8 1.0 owner_sums.1
  105.8 7.7 %collective-permute-start.7 = (bf16[8,16,896]{2,1,0:T(8,128)(2,1)S(1)}, bf16[8,16,896]{2,1,0:T(8,128)(2,1)S(1)}, u32[]{:S(2)}, u32[]{:S(2)}) collective-permute-start(bf16[8,16,896]{2,1,0:T(8,128)(2,1)S(1)} %get-tuple-element.33), channel_id=1, source_target_pairs={{0,8},{8,0},{1,9},{9,1},{2,10},{10,2},{3,11},{11,3},{4,12},{12,4},... | collective-permute-start | bytes 688136 | tf_op jit(solution)/shard_map/ppermute | solution.py:38
  114.7 16.7 %all_to_all.31 = bf16[8,16,896]{2,1,0:T(8,128)(2,1)S(1)} all-to-all(bf16[8,16,896]{2,1,0:T(8,128)(2,1)S(1)} %add_convert_fusion), channel_id=1, replica_groups=mesh['x'=4,'y'=8,'c'=2,'z'=8] {'y'}, dimensions={0} | all-to-all | bytes 458752 | tf_op jit(solution)/shard_map/all_to_all | solution.py:281
  (29 shorter events, 5.6 us)
Async XLA Ops:
  0.6 56.7 %copy-start = (s32[2,2]{1,0:T(2,128)S(1)}, s32[2,2]{1,0:T(2,128)}, u32[]{:S(2)}) copy-start(s32[2,2]{1,0:T(2,128)} %param.11) | copy-start | bytes 52
  0.6 46.8 %collective-permute-start.4 = (bf16[2,896,512]{2,1,0:T(8,128)(2,1)}, bf16[2,896,512]{2,1,0:T(8,128)(2,1)}, u32[]{:S(2)}, u32[]{:S(2)}) collective-permute-start(bf16[2,896,512]{2,1,0:T(8,128)(2,1)} %w_own.1), channel_id=1, source_target_pairs={{0,1},{1,0},{2,3},{3,2},{4,5},{5,4},{6,7},{7,6},{8,9},{9,8},{10,11... | collective-permute-start | bytes 5505032 | tf_op jit(solution)/shard_map/ppermute | solution.py:38
  6.9 16.2 %all-to-all-start = ((bf16[8,16,896]{2,1,0:T(8,128)(2,1)}), bf16[8,16,896]{2,1,0:T(8,128)(2,1)S(1)}, u32[]{:S(2)}, u32[]{:S(2)}) async-start(bf16[8,16,896]{2,1,0:T(8,128)(2,1)} %broadcast_in_dim.7), calls=%async_computation | async-start | bytes 458752 | tf_op jit(solution)/shard_map/all_to_all | solution.py:239
  13.8 8.5 %collective-permute-start = (s32[2,2]{1,0:T(2,128)}, s32[2,2]{1,0:T(2,128)S(1)}, u32[]{:S(2)}, u32[]{:S(2)}) collective-permute-start(s32[2,2]{1,0:T(2,128)} %param.10), channel_id=1, source_target_pairs={{0,128},{128,256},{256,384},{384,0},{1,129},{129,257},{257,385},{3... | collective-permute-start | bytes 56 | tf_op jit(solution)/shard_map/ppermute | solution.py:34
  16.9 6.0 %collective-permute-start.1 = (s32[2,2]{1,0:T(2,128)}, s32[2,2]{1,0:T(2,128)S(1)}, u32[]{:S(2)}, u32[]{:S(2)}) collective-permute-start(s32[2,2]{1,0:T(2,128)} %param.10), channel_id=1, source_target_pairs={{0,256},{128,384},{256,0},{384,128},{1,257},{129,385},{257,1},{385... | collective-permute-start | bytes 56 | tf_op jit(solution)/shard_map/ppermute | solution.py:34
  23.2 10.0 %collective-permute-start.3 = (bf16[8,16,896]{2,1,0:T(8,128)(2,1)S(1)}, bf16[8,16,896]{2,1,0:T(8,128)(2,1)S(1)}, u32[]{:S(2)}, u32[]{:S(2)}) collective-permute-start(bf16[8,16,896]{2,1,0:T(8,128)(2,1)S(1)} %all-to-all-done.refs_3_), channel_id=1, source_target_pairs={{0,8},{8,0},{1,9},{9,1},{2,10},{10,2},{3,11},{11,3},{4,12},{12,4},... | collective-permute-start | bytes 688136 | tf_op jit(solution)/shard_map/ppermute | solution.py:38
  27.8 5.3 %collective-permute-start.2 = (s32[2,2]{1,0:T(2,128)}, s32[2,2]{1,0:T(2,128)S(1)}, u32[]{:S(2)}, u32[]{:S(2)}) collective-permute-start(s32[2,2]{1,0:T(2,128)} %param.10), channel_id=1, source_target_pairs={{0,384},{128,0},{256,128},{384,256},{1,385},{129,1},{257,129},{385... | collective-permute-start | bytes 56 | tf_op jit(solution)/shard_map/ppermute | solution.py:34
  34.6 36.3 %copy-start.1 = (bf16[2,896,512]{2,1,0:T(8,128)(2,1)S(1)}, bf16[2,896,512]{2,1,0:T(8,128)(2,1)}, u32[]{:S(2)}) copy-start(bf16[2,896,512]{2,1,0:T(8,128)(2,1)} %w_own.1) | copy-start | bytes 5505028
  34.7 11.4 %all-to-all-start.1 = ((bf16[4,4,16,896]{3,2,1,0:T(8,128)(2,1)}), bf16[4,4,16,896]{3,2,1,0:T(8,128)(2,1)S(1)}, u32[]{:S(2)}, u32[]{:S(2)}) async-start(bf16[4,4,16,896]{3,2,1,0:T(8,128)(2,1)} %pick.1), calls=%async_computation.1 | async-start | bytes 917504 | tf_op jit(solution)/shard_map/all_to_all | solution.py:247
  39.0 8.4 %collective-permute-start.5 = (bf16[128,512]{1,0:T(8,128)(2,1)S(1)}, bf16[128,512]{1,0:T(8,128)(2,1)S(1)}, u32[]{:S(2)}, u32[]{:S(2)}) collective-permute-start(bf16[128,512]{1,0:T(8,128)(2,1)S(1)} %pad_maximum_fusion), channel_id=1, source_target_pairs={{0,1},{1,0},{2,3},{3,2},{4,5},{5,4},{6,7},{7,6},{8,9},{9,8},{10,11... | collective-permute-start | bytes 393224 | tf_op jit(solution)/shard_map/ppermute | solution.py:38
  47.4 23.5 %all-to-all-start.2 = ((bf16[8,2,16,896]{3,2,1,0:T(8,128)(2,1)}), bf16[8,2,16,896]{3,2,1,0:T(8,128)(2,1)S(1)}, u32[]{:S(2)}, u32[]{:S(2)}) async-start(bf16[8,2,16,896]{3,2,1,0:T(8,128)(2,1)} %spread.1), calls=%async_computation.2 | async-start | bytes 917504 | tf_op jit(solution)/shard_map/all_to_all | solution.py:255
  94.2 10.6 %all-to-all-start.4 = ((bf16[4,4,16,896]{3,2,1,0:T(8,128)(2,1)}), bf16[4,4,16,896]{3,2,1,0:T(8,128)(2,1)S(1)}, u32[]{:S(2)}, u32[]{:S(2)}) async-start(bf16[4,4,16,896]{3,2,1,0:T(8,128)(2,1)} %broadcast_in_dim.8), calls=%async_computation.4 | async-start | bytes 917504 | tf_op jit(solution)/shard_map/all_to_all | solution.py:267
  98.2 5.0 %collective-permute-start.6 = (bf16[64,512]{1,0:T(8,128)(2,1)S(1)}, bf16[64,512]{1,0:T(8,128)(2,1)S(1)}, u32[]{:S(2)}, u32[]{:S(2)}) collective-permute-start(bf16[64,512]{1,0:T(8,128)(2,1)S(1)} %get-tuple-element.30), channel_id=1, source_target_pairs={{0,1},{1,0},{2,3},{3,2},{4,5},{5,4},{6,7},{7,6},{8,9},{9,8},{10,11... | collective-permute-start | bytes 196616 | tf_op jit(solution)/shard_map/ppermute | solution.py:38
  105.8 8.8 %collective-permute-start.7 = (bf16[8,16,896]{2,1,0:T(8,128)(2,1)S(1)}, bf16[8,16,896]{2,1,0:T(8,128)(2,1)S(1)}, u32[]{:S(2)}, u32[]{:S(2)}) collective-permute-start(bf16[8,16,896]{2,1,0:T(8,128)(2,1)S(1)} %get-tuple-element.33), channel_id=1, source_target_pairs={{0,8},{8,0},{1,9},{9,1},{2,10},{10,2},{3,11},{11,3},{4,12},{12,4},... | collective-permute-start | bytes 688136 | tf_op jit(solution)/shard_map/ppermute | solution.py:38

commit v13 on v12

--- a/solution.py
+++ b/solution.py
@@ -157,13 +157,10 @@
             ).astype(BF16)
 
     key_own, values_own = dot(rows, w_own[0]), dot(rows, w_own[1]).astype(BF16)
-    for fetch in fetches[0]:
+    for fetch in fetches[0] + fetches[1]:
         fetch.wait()
-    key_pair = dot(rows, w_pair[0])
+    key_pair, values_pair = dot(rows, w_pair[0]), dot(rows, w_pair[1]).astype(BF16)
     heads(0, key_own, values_own, q_own, g_own, dq_own)
-    for fetch in fetches[1]:
-        fetch.wait()
-    values_pair = dot(rows, w_pair[1]).astype(BF16)
     heads(1, key_pair, values_pair, from_pair.at[:SPAN], from_pair.at[SPAN:], dq_pair)
     product = dot(dk_all[:, :width], w_own[0], (1, 1)) + dot(dv_all[:, :width], w_own[1], (1, 1))
     product = product + dot(dk_all[:, width:], w_pair[0], (1, 1))
@@ -237,7 +234,7 @@
     near = [shifted(neighbour_ids, "x", NX, s) for s in range(1, NX)]
     copies = jnp.broadcast_to(encodings, (NY, ROWS, DE))
     over_y = lax.all_to_all(copies, "y", split_axis=0, concat_axis=0, tiled=True)
-    over_y, near[:-1], other = lax.optimization_barrier((over_y, near[:-1], other))
+    over_y, near[:-1], other, at = lax.optimization_barrier((over_y, near[:-1], other, at))
     beside = swapped(over_y, "c", NC)
     block = (reads, ROWS, DE)
     asked = on_core(

time: 133 us -> 133 us (level)
  waiting for transfers between devices: 23.7 us -> 26.1 us
  starting transfers between devices: 57.9 us -> 55.5 us
    ppermute x3, waiting for transfers between devices: 0.72 us -> 3.38 us  [shifted(): lax.ppermute(value, axis, [(i, (i + shift) % size) for i in range(size)])]
    ppermute x3, starting transfers between devices: 11.9 us -> 10.3 us  [shifted(): lax.ppermute(value, axis, [(i, (i + shift) % size) for i in range(size)])]
  transfers between devices with their start and end apart: 12 -> 12, of which waited for: 8 -> 7; matrix products, arithmetic and copies ran while one was open for 4% -> 4% of each run, Pallas kernels for 2% -> 2%
where the time goes in v13:
time: 133 us; the launch traced here: 132 us
  starting transfers between devices  55.5 us (42%)
  blocking collectives  32.6 us (25%)
  waiting for transfers between devices  26.1 us (20%)
  Pallas kernels  10.5 us (8%)
  local copies, waits for them, and re-layouts  4.03 us (3%)
  other arithmetic  2.58 us (2%)
    ppermute x5, starting transfers between devices, swapped(): return lax.ppermute(value, axis, [(i, i ^ 1) for i in range(size)])  20.7 us
    all_to_all x1, blocking collectives, local(): lax.all_to_all(owner_part, 'y', split_axis=0, concat_axis=0, tiled=True)  16.7 us
    all_to_all x1, blocking collectives, local(): lax.all_to_all(part, 'z', split_axis=0, concat_axis=0, tiled=True)  15.9 us
    all_to_all x1, waiting for transfers between devices, local(): tok = lax.all_to_all(to_z, 'z', split_axis=0, concat_axis=0, tiled=True)  12.7 us
    ppermute x3, starting transfers between devices, shifted(): lax.ppermute(value, axis, [(i, (i + shift) % size) for i in range(size)])  10.3 us
    all_to_all x1, starting transfers between devices, local(): tok = lax.all_to_all(to_z, 'z', split_axis=0, concat_axis=0, tiled=True)  9.91 us
    all_to_all x1, starting transfers between devices, local(): lax.all_to_all(copies, 'y', split_axis=0, concat_axis=0, tiled=True)  6.82 us
    pallas_call x1, Pallas kernels, attention(): pl.pallas_call(attention_kernel, out_shape=(jax.ShapeDtypeStruct((NZ, NEI...  6.63 us
  transfers between devices with their start and end apart: 12, of which 7 were waited for; matrix products, arithmetic and copies ran while one was open for 4% of the time, Pallas kernels for 2%

profile of v13, /device:TPU:1, one launch (start us, length us, event | category | flops | bytes accessed | tf_op | source)
XLA Modules:
  0.0 132.2 jit_solution(7979279956169388056)
XLA Ops:
  0.6 4.8 %collective-permute-start.4 = (bf16[2,896,512]{2,1,0:T(8,128)(2,1)}, bf16[2,896,512]{2,1,0:T(8,128)(2,1)}, u32[]{:S(2)}, u32[]{:S(2)}) collective-permute-start(bf16[2,896,512]{2,1,0:T(8,128)(2,1)} %w_own.1), channel_id=1, source_target_pairs={{0,1},{1,0},{2,3},{3,2},{4,5},{5,4},{6,7},{7,6},{8,9},{9,8},{10,11... | collective-permute-start | bytes 5505032 | tf_op jit(solution)/shard_map/ppermute | solution.py:38
  5.5 1.5 %broadcast_in_dim.7 = bf16[8,16,896]{2,1,0:T(8,128)(2,1)} broadcast(bf16[16,896]{1,0:T(8,128)(2,1)} %bitcast.25), dimensions={1,2} | broadcast | bytes 258048 | tf_op jit(solution)/shard_map/broadcast_in_dim | solution.py:235
  6.9 6.8 %all-to-all-start = ((bf16[8,16,896]{2,1,0:T(8,128)(2,1)}), bf16[8,16,896]{2,1,0:T(8,128)(2,1)S(1)}, u32[]{:S(2)}, u32[]{:S(2)}) async-start(bf16[8,16,896]{2,1,0:T(8,128)(2,1)} %broadcast_in_dim.7), calls=%async_computation | async-start | bytes 458752 | tf_op jit(solution)/shard_map/all_to_all | solution.py:236
  13.8 4.6 %collective-permute-start.1 = (s32[2,2]{1,0:T(2,128)}, s32[2,2]{1,0:T(2,128)S(1)}, u32[]{:S(2)}, u32[]{:S(2)}) collective-permute-start(s32[2,2]{1,0:T(2,128)} %param.10), channel_id=1, source_target_pairs={{0,256},{128,384},{256,0},{384,128},{1,257},{129,385},{257,1},{385... | collective-permute-start | bytes 56 | tf_op jit(solution)/shard_map/ppermute | solution.py:34
  18.4 2.2 %collective-permute-start = (s32[2,2]{1,0:T(2,128)}, s32[2,2]{1,0:T(2,128)S(1)}, u32[]{:S(2)}, u32[]{:S(2)}) collective-permute-start(s32[2,2]{1,0:T(2,128)} %param.10), channel_id=1, source_target_pairs={{0,128},{128,256},{256,384},{384,0},{1,129},{129,257},{257,385},{3... | collective-permute-start | bytes 56 | tf_op jit(solution)/shard_map/ppermute | solution.py:34
  22.5 1.9 %collective-permute-done.refs_0_ = s32[2,2]{1,0:T(2,128)S(1)} collective-permute-done((s32[2,2]{1,0:T(2,128)}, s32[2,2]{1,0:T(2,128)S(1)}, u32[]{:S(2)}, u32[]{:S(2)}) %collective-permute-start) | collective-permute-done | bytes 48 | tf_op jit(solution)/shard_map/ppermute | solution.py:34
  24.4 4.3 %collective-permute-start.3 = (bf16[8,16,896]{2,1,0:T(8,128)(2,1)S(1)}, bf16[8,16,896]{2,1,0:T(8,128)(2,1)S(1)}, u32[]{:S(2)}, u32[]{:S(2)}) collective-permute-start(bf16[8,16,896]{2,1,0:T(8,128)(2,1)S(1)} %all-to-all-done.refs_3_), channel_id=1, source_target_pairs={{0,8},{8,0},{1,9},{9,1},{2,10},{10,2},{3,11},{11,3},{4,12},{12,4},... | collective-permute-start | bytes 688136 | tf_op jit(solution)/shard_map/ppermute | solution.py:38
  28.7 3.5 %collective-permute-start.2 = (s32[2,2]{1,0:T(2,128)}, s32[2,2]{1,0:T(2,128)S(1)}, u32[]{:S(2)}, u32[]{:S(2)}) collective-permute-start(s32[2,2]{1,0:T(2,128)} %param.10), channel_id=1, source_target_pairs={{0,384},{128,0},{256,128},{384,256},{1,385},{129,1},{257,129},{385... | collective-permute-start | bytes 56 | tf_op jit(solution)/shard_map/ppermute | solution.py:34
  32.2 1.5 %collective-permute-done.2.refs_2_ = s32[2,2]{1,0:T(2,128)S(1)} collective-permute-done((s32[2,2]{1,0:T(2,128)}, s32[2,2]{1,0:T(2,128)S(1)}, u32[]{:S(2)}, u32[]{:S(2)}) %collective-permute-start.2) | collective-permute-done | bytes 48 | tf_op jit(solution)/shard_map/ppermute | solution.py:34
  33.7 1.5 %pick.1 = bf16[4,4,16,896]{3,2,1,0:T(8,128)(2,1)} custom-call(s32[6]{0:T(128)S(1)} %pad_add_fusion.at_ref, s32[2,2]{1,0:T(2,128)S(1)} %collective-permute-done.refs_0_, s32[2,2]{1,0:T(2,128)S(1)} %collective-permute-done.1.refs_1_, s32[2,2]{1,0:T(2,128)S(1)} %collective-permute-done.2.refs_2_, bf16[8,16,896]{2,1,0:T(8,128)(2,1)S(1)} %all-to-all-done.refs_3_, ...), custom_call_target="tpu_custom_call" | custom-call | tf_op jit(solution)/shard_map/pick/pallas_call | solution.py:174
  35.2 3.8 %all-to-all-start.1 = ((bf16[4,4,16,896]{3,2,1,0:T(8,128)(2,1)}), bf16[4,4,16,896]{3,2,1,0:T(8,128)(2,1)S(1)}, u32[]{:S(2)}, u32[]{:S(2)}) async-start(bf16[4,4,16,896]{3,2,1,0:T(8,128)(2,1)} %pick.1), calls=%async_computation.1 | async-start | bytes 917504 | tf_op jit(solution)/shard_map/all_to_all | solution.py:244
  39.0 1.9 %collective-permute-start.5 = (bf16[128,512]{1,0:T(8,128)(2,1)S(1)}, bf16[128,512]{1,0:T(8,128)(2,1)S(1)}, u32[]{:S(2)}, u32[]{:S(2)}) collective-permute-start(bf16[128,512]{1,0:T(8,128)(2,1)S(1)} %pad_maximum_fusion), channel_id=1, source_target_pairs={{0,1},{1,0},{2,3},{3,2},{4,5},{5,4},{6,7},{7,6},{8,9},{9,8},{10,11... | collective-permute-start | bytes 393224 | tf_op jit(solution)/shard_map/ppermute | solution.py:38
  41.1 4.9 %all-to-all-done.1.from_ref = bf16[4,4,16,896]{3,2,1,0:T(8,128)(2,1)S(1)} async-done(((bf16[4,4,16,896]{3,2,1,0:T(8,128)(2,1)}), bf16[4,4,16,896]{3,2,1,0:T(8,128)(2,1)S(1)}, u32[]{:S(2)}, u32[]{:S(2)}) %all-to-all-start.1) | async-done | bytes 458784 | tf_op jit(solution)/shard_map/all_to_all | solution.py:244
  46.0 1.4 %spread.1 = bf16[8,2,16,896]{3,2,1,0:T(8,128)(2,1)} custom-call(s32[6]{0:T(128)S(1)} %pad_add_fusion.at_ref, bf16[4,4,16,896]{3,2,1,0:T(8,128)(2,1)S(1)} %all-to-all-done.1.from_ref), custom_call_target="tpu_custom_call" | custom-call | tf_op jit(solution)/shard_map/spread/pallas_call | solution.py:174
  47.4 9.9 %all-to-all-start.2 = ((bf16[8,2,16,896]{3,2,1,0:T(8,128)(2,1)}), bf16[8,2,16,896]{3,2,1,0:T(8,128)(2,1)S(1)}, u32[]{:S(2)}, u32[]{:S(2)}) async-start(bf16[8,2,16,896]{3,2,1,0:T(8,128)(2,1)} %spread.1), calls=%async_computation.2 | async-start | bytes 917504 | tf_op jit(solution)/shard_map/all_to_all | solution.py:252
  58.2 12.7 %all-to-all-done.2.tok = bf16[8,2,16,896]{3,2,1,0:T(8,128)(2,1)S(1)} async-done(((bf16[8,2,16,896]{3,2,1,0:T(8,128)(2,1)}), bf16[8,2,16,896]{3,2,1,0:T(8,128)(2,1)S(1)}, u32[]{:S(2)}, u32[]{:S(2)}) %all-to-all-start.2) | async-done | bytes 458784 | tf_op jit(solution)/shard_map/all_to_all | solution.py:252
  70.9 6.6 %attention.1 = (bf16[8,2,16,896]{3,2,1,0:T(8,128)(2,1)S(1)}, bf16[64,512]{1,0:T(8,128)(2,1)S(1)}, bf16[64,512]{1,0:T(8,128)(2,1)S(1)}) custom-call(bf16[8,2,16,896]{3,2,1,0:T(8,128)(2,1)S(1)} %all-to-all-done.2.tok, bf16[2,896,512]{2,1,0:T(8,128)(2,1)S(1)} %copy-done.1, bf16[64,512]{1,0:T(8,128)(2,1)S(1)} %get-tuple-element.53.q_own, ...), custom_call_target="tpu_custom_call" | custom-call | flops 2100000000 | bytes 6000000 | tf_op jit(solution)/shard_map/attention/pallas_call | solution.py:187
  77.6 15.9 %all_to_all.30 = bf16[8,2,16,896]{3,2,1,0:T(8,128)(2,1)S(1)} all-to-all(bf16[8,2,16,896]{3,2,1,0:T(8,128)(2,1)S(1)} %get-tuple-element.29), channel_id=1, replica_groups=mesh['x'=4,'y'=8,'c'=2,'z'=8] {'z'}, dimensions={0} | all-to-all | bytes 917504 | tf_op jit(solution)/shard_map/all_to_all | solution.py:258
  94.3 4.0 %all-to-all-start.4 = ((bf16[4,4,16,896]{3,2,1,0:T(8,128)(2,1)}), bf16[4,4,16,896]{3,2,1,0:T(8,128)(2,1)S(1)}, u32[]{:S(2)}, u32[]{:S(2)}) async-start(bf16[4,4,16,896]{3,2,1,0:T(8,128)(2,1)} %broadcast_in_dim.8), calls=%async_computation.4 | async-start | bytes 917504 | tf_op jit(solution)/shard_map/all_to_all | solution.py:264
  98.4 1.9 %collective-permute-start.6 = (bf16[64,512]{1,0:T(8,128)(2,1)S(1)}, bf16[64,512]{1,0:T(8,128)(2,1)S(1)}, u32[]{:S(2)}, u32[]{:S(2)}) collective-permute-start(bf16[64,512]{1,0:T(8,128)(2,1)S(1)} %get-tuple-element.32), channel_id=1, source_target_pairs={{0,1},{1,0},{2,3},{3,2},{4,5},{5,4},{6,7},{7,6},{8,9},{9,8},{10,11... | collective-permute-start | bytes 196616 | tf_op jit(solution)/shard_map/ppermute | solution.py:38
  100.3 3.1 %collective-permute-done.6 = bf16[64,512]{1,0:T(8,128)(2,1)S(1)} collective-permute-done((bf16[64,512]{1,0:T(8,128)(2,1)S(1)}, bf16[64,512]{1,0:T(8,128)(2,1)S(1)}, u32[]{:S(2)}, u32[]{:S(2)}) %collective-permute-start.6) | collective-permute-done | bytes 65568 | tf_op jit(solution)/shard_map/ppermute | solution.py:38
  103.4 1.6 %all-to-all-done.4.refs_3_ = bf16[4,4,16,896]{3,2,1,0:T(8,128)(2,1)S(1)} async-done(((bf16[4,4,16,896]{3,2,1,0:T(8,128)(2,1)}), bf16[4,4,16,896]{3,2,1,0:T(8,128)(2,1)S(1)}, u32[]{:S(2)}, u32[]{:S(2)}) %all-to-all-start.4) | async-done | bytes 458784 | tf_op jit(solution)/shard_map/all_to_all | solution.py:264
  105.9 7.7 %collective-permute-start.7 = (bf16[8,16,896]{2,1,0:T(8,128)(2,1)S(1)}, bf16[8,16,896]{2,1,0:T(8,128)(2,1)S(1)}, u32[]{:S(2)}, u32[]{:S(2)}) collective-permute-start(bf16[8,16,896]{2,1,0:T(8,128)(2,1)S(1)} %get-tuple-element.35), channel_id=1, source_target_pairs={{0,8},{8,0},{1,9},{9,1},{2,10},{10,2},{3,11},{11,3},{4,12},{12,4},... | collective-permute-start | bytes 688136 | tf_op jit(solution)/shard_map/ppermute | solution.py:38
  114.8 16.7 %all_to_all.31 = bf16[8,16,896]{2,1,0:T(8,128)(2,1)S(1)} all-to-all(bf16[8,16,896]{2,1,0:T(8,128)(2,1)S(1)} %add_convert_fusion), channel_id=1, replica_groups=mesh['x'=4,'y'=8,'c'=2,'z'=8] {'y'}, dimensions={0} | all-to-all | bytes 458752 | tf_op jit(solution)/shard_map/all_to_all | solution.py:278
  (29 shorter events, 6.6 us)
Async XLA Ops:
  0.6 56.7 %copy-start = (s32[2,2]{1,0:T(2,128)S(1)}, s32[2,2]{1,0:T(2,128)}, u32[]{:S(2)}) copy-start(s32[2,2]{1,0:T(2,128)} %param.11) | copy-start | bytes 52
  0.6 46.8 %collective-permute-start.4 = (bf16[2,896,512]{2,1,0:T(8,128)(2,1)}, bf16[2,896,512]{2,1,0:T(8,128)(2,1)}, u32[]{:S(2)}, u32[]{:S(2)}) collective-permute-start(bf16[2,896,512]{2,1,0:T(8,128)(2,1)} %w_own.1), channel_id=1, source_target_pairs={{0,1},{1,0},{2,3},{3,2},{4,5},{5,4},{6,7},{7,6},{8,9},{9,8},{10,11... | collective-permute-start | bytes 5505032 | tf_op jit(solution)/shard_map/ppermute | solution.py:38
  6.9 17.5 %all-to-all-start = ((bf16[8,16,896]{2,1,0:T(8,128)(2,1)}), bf16[8,16,896]{2,1,0:T(8,128)(2,1)S(1)}, u32[]{:S(2)}, u32[]{:S(2)}) async-start(bf16[8,16,896]{2,1,0:T(8,128)(2,1)} %broadcast_in_dim.7), calls=%async_computation | async-start | bytes 458752 | tf_op jit(solution)/shard_map/all_to_all | solution.py:236
  13.8 8.7 %collective-permute-start.1 = (s32[2,2]{1,0:T(2,128)}, s32[2,2]{1,0:T(2,128)S(1)}, u32[]{:S(2)}, u32[]{:S(2)}) collective-permute-start(s32[2,2]{1,0:T(2,128)} %param.10), channel_id=1, source_target_pairs={{0,256},{128,384},{256,0},{384,128},{1,257},{129,385},{257,1},{385... | collective-permute-start | bytes 56 | tf_op jit(solution)/shard_map/ppermute | solution.py:34
  18.4 6.0 %collective-permute-start = (s32[2,2]{1,0:T(2,128)}, s32[2,2]{1,0:T(2,128)S(1)}, u32[]{:S(2)}, u32[]{:S(2)}) collective-permute-start(s32[2,2]{1,0:T(2,128)} %param.10), channel_id=1, source_target_pairs={{0,128},{128,256},{256,384},{384,0},{1,129},{129,257},{257,385},{3... | collective-permute-start | bytes 56 | tf_op jit(solution)/shard_map/ppermute | solution.py:34
  24.4 9.2 %collective-permute-start.3 = (bf16[8,16,896]{2,1,0:T(8,128)(2,1)S(1)}, bf16[8,16,896]{2,1,0:T(8,128)(2,1)S(1)}, u32[]{:S(2)}, u32[]{:S(2)}) collective-permute-start(bf16[8,16,896]{2,1,0:T(8,128)(2,1)S(1)} %all-to-all-done.refs_3_), channel_id=1, source_target_pairs={{0,8},{8,0},{1,9},{9,1},{2,10},{10,2},{3,11},{11,3},{4,12},{12,4},... | collective-permute-start | bytes 688136 | tf_op jit(solution)/shard_map/ppermute | solution.py:38
  28.7 4.9 %collective-permute-start.2 = (s32[2,2]{1,0:T(2,128)}, s32[2,2]{1,0:T(2,128)S(1)}, u32[]{:S(2)}, u32[]{:S(2)}) collective-permute-start(s32[2,2]{1,0:T(2,128)} %param.10), channel_id=1, source_target_pairs={{0,384},{128,0},{256,128},{384,256},{1,385},{129,1},{257,129},{385... | collective-permute-start | bytes 56 | tf_op jit(solution)/shard_map/ppermute | solution.py:34
  35.2 35.7 %copy-start.1 = (bf16[2,896,512]{2,1,0:T(8,128)(2,1)S(1)}, bf16[2,896,512]{2,1,0:T(8,128)(2,1)}, u32[]{:S(2)}) copy-start(bf16[2,896,512]{2,1,0:T(8,128)(2,1)} %w_own.1) | copy-start | bytes 5505028
  35.2 10.8 %all-to-all-start.1 = ((bf16[4,4,16,896]{3,2,1,0:T(8,128)(2,1)}), bf16[4,4,16,896]{3,2,1,0:T(8,128)(2,1)S(1)}, u32[]{:S(2)}, u32[]{:S(2)}) async-start(bf16[4,4,16,896]{3,2,1,0:T(8,128)(2,1)} %pick.1), calls=%async_computation.1 | async-start | bytes 917504 | tf_op jit(solution)/shard_map/all_to_all | solution.py:244
  39.0 8.4 %collective-permute-start.5 = (bf16[128,512]{1,0:T(8,128)(2,1)S(1)}, bf16[128,512]{1,0:T(8,128)(2,1)S(1)}, u32[]{:S(2)}, u32[]{:S(2)}) collective-permute-start(bf16[128,512]{1,0:T(8,128)(2,1)S(1)} %pad_maximum_fusion), channel_id=1, source_target_pairs={{0,1},{1,0},{2,3},{3,2},{4,5},{5,4},{6,7},{7,6},{8,9},{9,8},{10,11... | collective-permute-start | bytes 393224 | tf_op jit(solution)/shard_map/ppermute | solution.py:38
  47.4 23.5 %all-to-all-start.2 = ((bf16[8,2,16,896]{3,2,1,0:T(8,128)(2,1)}), bf16[8,2,16,896]{3,2,1,0:T(8,128)(2,1)S(1)}, u32[]{:S(2)}, u32[]{:S(2)}) async-start(bf16[8,2,16,896]{3,2,1,0:T(8,128)(2,1)} %spread.1), calls=%async_computation.2 | async-start | bytes 917504 | tf_op jit(solution)/shard_map/all_to_all | solution.py:252
  94.3 10.6 %all-to-all-start.4 = ((bf16[4,4,16,896]{3,2,1,0:T(8,128)(2,1)}), bf16[4,4,16,896]{3,2,1,0:T(8,128)(2,1)S(1)}, u32[]{:S(2)}, u32[]{:S(2)}) async-start(bf16[4,4,16,896]{3,2,1,0:T(8,128)(2,1)} %broadcast_in_dim.8), calls=%async_computation.4 | async-start | bytes 917504 | tf_op jit(solution)/shard_map/all_to_all | solution.py:264
  98.4 5.0 %collective-permute-start.6 = (bf16[64,512]{1,0:T(8,128)(2,1)S(1)}, bf16[64,512]{1,0:T(8,128)(2,1)S(1)}, u32[]{:S(2)}, u32[]{:S(2)}) collective-permute-start(bf16[64,512]{1,0:T(8,128)(2,1)S(1)} %get-tuple-element.32), channel_id=1, source_target_pairs={{0,1},{1,0},{2,3},{3,2},{4,5},{5,4},{6,7},{7,6},{8,9},{9,8},{10,11... | collective-permute-start | bytes 196616 | tf_op jit(solution)/shard_map/ppermute | solution.py:38
  105.9 8.8 %collective-permute-start.7 = (bf16[8,16,896]{2,1,0:T(8,128)(2,1)S(1)}, bf16[8,16,896]{2,1,0:T(8,128)(2,1)S(1)}, u32[]{:S(2)}, u32[]{:S(2)}) collective-permute-start(bf16[8,16,896]{2,1,0:T(8,128)(2,1)S(1)} %get-tuple-element.35), channel_id=1, source_target_pairs={{0,8},{8,0},{1,9},{9,1},{2,10},{10,2},{3,11},{11,3},{4,12},{12,4},... | collective-permute-start | bytes 688136 | tf_op jit(solution)/shard_map/ppermute | solution.py:38

commit v14 on v11

--- a/solution.py
+++ b/solution.py
@@ -78,6 +78,16 @@
         block = from_ref[owner // (NY * NC), read]
         for at in range(read // NEIGH, NZ, spans):
             out_ref[at, read % NEIGH] = block
+
+
+def sum_kernel(from_ref, out_ref):
+    spans = out_ref.shape[1] // NEIGH
+    for read in range(out_ref.shape[1]):
+        total = from_ref[read // NEIGH, read % NEIGH].astype(F32)
+        for at in range(read // NEIGH + spans, NZ, spans):
+            total = total + from_ref[at, read % NEIGH].astype(F32)
+        for column in range(NX):
+            out_ref[column, read] = total.astype(BF16)
 
 
 def owner_kernel(at_ref, *refs):
@@ -228,7 +238,7 @@
         found,
     )
     from_pair = swapped(other, "z", NZ)
-    to_z, w_far, from_pair = lax.optimization_barrier((to_z, w_far, from_pair))
+    to_z, w_far = lax.optimization_barrier((to_z, w_far))
     tok = lax.all_to_all(to_z, "z", split_axis=0, concat_axis=0, tiled=True)
     part, dq_own, dq_pair = attention(
         tok, kv_weight, q_own, g_own, from_pair,
@@ -236,10 +246,9 @@
     )
 
     from_heads = lax.all_to_all(part, "z", split_axis=0, concat_axis=0, tiled=True)
-    from_heads = from_heads.reshape(NZ // spans, spans, NEIGH, ROWS, DE)
-    read_sum = jnp.sum(from_heads.astype(F32), axis=0).astype(BF16).reshape(reads, ROWS, DE)
-
-    read_copies = jnp.broadcast_to(read_sum, (NX, *block))
+    read_copies = on_core(
+        sum_kernel, "sums", jax.ShapeDtypeStruct((NX, *block), BF16), (), from_heads
+    )
     read_copies, dq_pair = lax.optimization_barrier((read_copies, dq_pair))
     read_x = lax.all_to_all(read_copies, "x", split_axis=0, concat_axis=0, tiled=True)
     dq_back = swapped(dq_pair, "z", NZ)

time: 133 us -> 135 us (1.015)
  blocking collectives: 30.8 us -> 36.2 us
  waiting for transfers between devices: 26.1 us -> 24.1 us
  starting transfers between devices: 57.4 us -> 55.8 us
    all_to_all x1, waiting for transfers between devices: 12 us -> 0.25 us  [local(): tok = lax.all_to_all(to_z, 'z', split_axis=0, concat_axis=0, tiled=True)]
    ppermute x5, waiting for transfers between devices: 3.49 us -> 11.2 us  [swapped(): return lax.ppermute(value, axis, [(i, i ^ 1) for i in range(size)])]
    all_to_all x1, blocking collectives: 14 us -> 18.5 us  [local(): lax.all_to_all(part, 'z', split_axis=0, concat_axis=0, tiled=True)]
    all_to_all x1, starting transfers between devices: 6.64 us -> 3.46 us  [local(): lax.all_to_all(read_copies, 'x', split_axis=0, concat_axis=0, tiled=True)]
    all_to_all x1, waiting for transfers between devices: 4.92 us -> 6.96 us  [local(): found = lax.all_to_all(asked, 'x', split_axis=0, concat_axis=0, tiled=True)]
    ppermute x5, starting transfers between devices: 20.7 us -> 22.3 us  [swapped(): return lax.ppermute(value, axis, [(i, i ^ 1) for i in range(size)])]
    pallas_call x3 -> x4, Pallas kernels: 3.84 us -> 4.76 us  [on_core(): pl.pallas_call(kernel, out_shape=shapes, in_specs=[SMEM] * len(scalars) +...]
  transfers between devices with their start and end apart: 12 -> 12, of which waited for: 7 -> 8; matrix products, arithmetic and copies ran while one was open for 3% -> 3% of each run, Pallas kernels for 2% -> 2%
where the time goes in v14:
time: 135 us; the launch traced here: 134 us
  starting transfers between devices  55.8 us (41%)
  blocking collectives  36.2 us (27%)
  waiting for transfers between devices  24.1 us (18%)
  Pallas kernels  11.1 us (8%)
  local copies, waits for them, and re-layouts  3.12 us (2%)
  other arithmetic  2.5 us (2%)
    ppermute x5, starting transfers between devices, swapped(): return lax.ppermute(value, axis, [(i, i ^ 1) for i in range(size)])  22.3 us
    all_to_all x1, blocking collectives, local(): lax.all_to_all(part, 'z', split_axis=0, concat_axis=0, tiled=True)  18.5 us
    all_to_all x1, blocking collectives, local(): lax.all_to_all(owner_part, 'y', split_axis=0, concat_axis=0, tiled=True)  17.7 us
    ppermute x5, waiting for transfers between devices, swapped(): return lax.ppermute(value, axis, [(i, i ^ 1) for i in range(size)])  11.2 us
    ppermute x3, starting transfers between devices, shifted(): lax.ppermute(value, axis, [(i, (i + shift) % size) for i in range(size)])  10.3 us
    all_to_all x1, starting transfers between devices, local(): tok = lax.all_to_all(to_z, 'z', split_axis=0, concat_axis=0, tiled=True)  9.13 us
    all_to_all x1, waiting for transfers between devices, local(): found = lax.all_to_all(asked, 'x', split_axis=0, concat_axis=0, tiled=True)  6.96 us
    all_to_all x1, starting transfers between devices, local(): lax.all_to_all(copies, 'y', split_axis=0, concat_axis=0, tiled=True)  6.82 us
  transfers between devices with their start and end apart: 12, of which 8 were waited for; matrix products, arithmetic and copies ran while one was open for 3% of the time, Pallas kernels for 2%

profile of v14, /device:TPU:1, one launch (start us, length us, event | category | flops | bytes accessed | tf_op | source)
XLA Modules:
  0.0 133.7 jit_solution(697225136350251280)
XLA Ops:
  0.7 4.8 %collective-permute-start.4 = (bf16[2,896,512]{2,1,0:T(8,128)(2,1)}, bf16[2,896,512]{2,1,0:T(8,128)(2,1)}, u32[]{:S(2)}, u32[]{:S(2)}) collective-permute-start(bf16[2,896,512]{2,1,0:T(8,128)(2,1)} %w_own.1), channel_id=1, source_target_pairs={{0,1},{1,0},{2,3},{3,2},{4,5},{5,4},{6,7},{7,6},{8,9},{9,8},{10,11... | collective-permute-start | bytes 5505032 | tf_op jit(solution)/shard_map/ppermute | solution.py:37
  5.5 1.4 %broadcast_in_dim.5 = bf16[8,16,896]{2,1,0:T(8,128)(2,1)} broadcast(bf16[16,896]{1,0:T(8,128)(2,1)} %bitcast.21), dimensions={1,2} | broadcast | bytes 258048 | tf_op jit(solution)/shard_map/broadcast_in_dim | solution.py:225
  6.9 6.8 %all-to-all-start = ((bf16[8,16,896]{2,1,0:T(8,128)(2,1)}), bf16[8,16,896]{2,1,0:T(8,128)(2,1)S(1)}, u32[]{:S(2)}, u32[]{:S(2)}) async-start(bf16[8,16,896]{2,1,0:T(8,128)(2,1)} %broadcast_in_dim.5), calls=%async_computation | async-start | bytes 458752 | tf_op jit(solution)/shard_map/all_to_all | solution.py:226
  13.8 4.6 %collective-permute-start.1 = (s32[2,2]{1,0:T(2,128)}, s32[2,2]{1,0:T(2,128)S(1)}, u32[]{:S(2)}, u32[]{:S(2)}) collective-permute-start(s32[2,2]{1,0:T(2,128)} %refs_0_.1), channel_id=1, source_target_pairs={{0,256},{128,384},{256,0},{384,128},{1,257},{129,385},{257,1},{385... | collective-permute-start | bytes 56 | tf_op jit(solution)/shard_map/ppermute | solution.py:33
  18.4 2.2 %collective-permute-start = (s32[2,2]{1,0:T(2,128)}, s32[2,2]{1,0:T(2,128)S(1)}, u32[]{:S(2)}, u32[]{:S(2)}) collective-permute-start(s32[2,2]{1,0:T(2,128)} %refs_0_.1), channel_id=1, source_target_pairs={{0,128},{128,256},{256,384},{384,0},{1,129},{129,257},{257,385},{3... | collective-permute-start | bytes 56 | tf_op jit(solution)/shard_map/ppermute | solution.py:33
  21.7 2.8 %collective-permute-done.refs_1_ = s32[2,2]{1,0:T(2,128)S(1)} collective-permute-done((s32[2,2]{1,0:T(2,128)}, s32[2,2]{1,0:T(2,128)S(1)}, u32[]{:S(2)}, u32[]{:S(2)}) %collective-permute-start) | collective-permute-done | bytes 48 | tf_op jit(solution)/shard_map/ppermute | solution.py:33
  24.4 4.3 %collective-permute-start.3 = (bf16[8,16,896]{2,1,0:T(8,128)(2,1)S(1)}, bf16[8,16,896]{2,1,0:T(8,128)(2,1)S(1)}, u32[]{:S(2)}, u32[]{:S(2)}) collective-permute-start(bf16[8,16,896]{2,1,0:T(8,128)(2,1)S(1)} %all-to-all-done.refs_4_), channel_id=1, source_target_pairs={{0,8},{8,0},{1,9},{9,1},{2,10},{10,2},{3,11},{11,3},{4,12},{12,4},... | collective-permute-start | bytes 688136 | tf_op jit(solution)/shard_map/ppermute | solution.py:37
  28.7 3.5 %collective-permute-start.2 = (s32[2,2]{1,0:T(2,128)}, s32[2,2]{1,0:T(2,128)S(1)}, u32[]{:S(2)}, u32[]{:S(2)}) collective-permute-start(s32[2,2]{1,0:T(2,128)} %refs_0_.1), channel_id=1, source_target_pairs={{0,384},{128,0},{256,128},{384,256},{1,385},{129,1},{257,129},{385... | collective-permute-start | bytes 56 | tf_op jit(solution)/shard_map/ppermute | solution.py:33
  32.3 1.4 %collective-permute-done.2.refs_3_ = s32[2,2]{1,0:T(2,128)S(1)} collective-permute-done((s32[2,2]{1,0:T(2,128)}, s32[2,2]{1,0:T(2,128)S(1)}, u32[]{:S(2)}, u32[]{:S(2)}) %collective-permute-start.2) | collective-permute-done | bytes 48 | tf_op jit(solution)/shard_map/ppermute | solution.py:33
  34.3 1.5 %pick.1 = bf16[4,4,16,896]{3,2,1,0:T(8,128)(2,1)} custom-call(s32[2]{0:T(128)S(1)} %pad_add_fusion.at_ref, s32[2,2]{1,0:T(2,128)S(1)} %copy-done.1, s32[2,2]{1,0:T(2,128)S(1)} %collective-permute-done.refs_1_, s32[2,2]{1,0:T(2,128)S(1)} %collective-permute-done.1.refs_2_, s32[2,2]{1,0:T(2,128)S(1)} %collective-permute-done.2.refs_3_, ...), custom_call_target="tpu_custom_call" | custom-call | tf_op jit(solution)/shard_map/pick/pallas_call | solution.py:164
  35.9 3.8 %all-to-all-start.1 = ((bf16[4,4,16,896]{3,2,1,0:T(8,128)(2,1)}), bf16[4,4,16,896]{3,2,1,0:T(8,128)(2,1)S(1)}, u32[]{:S(2)}, u32[]{:S(2)}) async-start(bf16[4,4,16,896]{3,2,1,0:T(8,128)(2,1)} %pick.1), calls=%async_computation.1 | async-start | bytes 917504 | tf_op jit(solution)/shard_map/all_to_all | solution.py:234
  39.8 7.0 %all-to-all-done.1.from_ref = bf16[4,4,16,896]{3,2,1,0:T(8,128)(2,1)S(1)} async-done(((bf16[4,4,16,896]{3,2,1,0:T(8,128)(2,1)}), bf16[4,4,16,896]{3,2,1,0:T(8,128)(2,1)S(1)}, u32[]{:S(2)}, u32[]{:S(2)}) %all-to-all-start.1) | async-done | bytes 458784 | tf_op jit(solution)/shard_map/all_to_all | solution.py:234
  46.7 1.4 %spread.1 = bf16[8,2,16,896]{3,2,1,0:T(8,128)(2,1)} custom-call(s32[2,2]{1,0:T(2,128)S(1)} %copy-done.2, bf16[4,4,16,896]{3,2,1,0:T(8,128)(2,1)S(1)} %all-to-all-done.1.from_ref), custom_call_target="tpu_custom_call" | custom-call | tf_op jit(solution)/shard_map/spread/pallas_call | solution.py:164
  48.1 9.1 %all-to-all-start.2 = ((bf16[8,2,16,896]{3,2,1,0:T(8,128)(2,1)}), bf16[8,2,16,896]{3,2,1,0:T(8,128)(2,1)S(1)}, u32[]{:S(2)}, u32[]{:S(2)}) async-start(bf16[8,2,16,896]{3,2,1,0:T(8,128)(2,1)} %spread.1), calls=%async_computation.2 | async-start | bytes 917504 | tf_op jit(solution)/shard_map/all_to_all | solution.py:242
  58.0 3.4 %collective-permute-start.5 = (bf16[128,512]{1,0:T(8,128)(2,1)S(1)}, bf16[128,512]{1,0:T(8,128)(2,1)S(1)}, u32[]{:S(2)}, u32[]{:S(2)}) collective-permute-start(bf16[128,512]{1,0:T(8,128)(2,1)S(1)} %pad_maximum_fusion), channel_id=1, source_target_pairs={{0,1},{1,0},{2,3},{3,2},{4,5},{5,4},{6,7},{7,6},{8,9},{9,8},{10,11... | collective-permute-start | bytes 393224 | tf_op jit(solution)/shard_map/ppermute | solution.py:37
  61.6 7.7 %collective-permute-done.5.from_pair = bf16[128,512]{1,0:T(8,128)(2,1)S(1)} collective-permute-done((bf16[128,512]{1,0:T(8,128)(2,1)S(1)}, bf16[128,512]{1,0:T(8,128)(2,1)S(1)}, u32[]{:S(2)}, u32[]{:S(2)}) %collective-permute-start.5) | collective-permute-done | bytes 131104 | tf_op jit(solution)/shard_map/ppermute | solution.py:37
  69.5 6.4 %attention.1 = (bf16[8,2,16,896]{3,2,1,0:T(8,128)(2,1)S(1)}, bf16[64,512]{1,0:T(8,128)(2,1)S(1)}, bf16[64,512]{1,0:T(8,128)(2,1)S(1)}) custom-call(bf16[8,2,16,896]{3,2,1,0:T(8,128)(2,1)S(1)} %all-to-all-done.2.tok, bf16[2,896,512]{2,1,0:T(8,128)(2,1)S(1)} %copy-done.3, bf16[64,512]{1,0:T(8,128)(2,1)S(1)} %get-tuple-element.51.q_own, ...), custom_call_target="tpu_custom_call" | custom-call | flops 2100000000 | bytes 6000000 | tf_op jit(solution)/shard_map/attention/pallas_call | solution.py:177
  75.9 18.5 %all_to_all.30.from_ref = bf16[8,2,16,896]{3,2,1,0:T(8,128)(2,1)S(1)} all-to-all(bf16[8,2,16,896]{3,2,1,0:T(8,128)(2,1)S(1)} %get-tuple-element.27), channel_id=1, replica_groups=mesh['x'=4,'y'=8,'c'=2,'z'=8] {'z'}, dimensions={0} | all-to-all | bytes 917504 | tf_op jit(solution)/shard_map/all_to_all | solution.py:248
  95.2 3.5 %all-to-all-start.4 = ((bf16[4,4,16,896]{3,2,1,0:T(8,128)(2,1)}), bf16[4,4,16,896]{3,2,1,0:T(8,128)(2,1)S(1)}, u32[]{:S(2)}, u32[]{:S(2)}) async-start(bf16[4,4,16,896]{3,2,1,0:T(8,128)(2,1)} %sums.1), calls=%async_computation.4 | async-start | bytes 917504 | tf_op jit(solution)/shard_map/all_to_all | solution.py:253
  98.7 1.9 %collective-permute-start.6 = (bf16[64,512]{1,0:T(8,128)(2,1)S(1)}, bf16[64,512]{1,0:T(8,128)(2,1)S(1)}, u32[]{:S(2)}, u32[]{:S(2)}) collective-permute-start(bf16[64,512]{1,0:T(8,128)(2,1)S(1)} %get-tuple-element.30), channel_id=1, source_target_pairs={{0,1},{1,0},{2,3},{3,2},{4,5},{5,4},{6,7},{7,6},{8,9},{9,8},{10,11... | collective-permute-start | bytes 196616 | tf_op jit(solution)/shard_map/ppermute | solution.py:37
  100.6 3.1 %collective-permute-done.6 = bf16[64,512]{1,0:T(8,128)(2,1)S(1)} collective-permute-done((bf16[64,512]{1,0:T(8,128)(2,1)S(1)}, bf16[64,512]{1,0:T(8,128)(2,1)S(1)}, u32[]{:S(2)}, u32[]{:S(2)}) %collective-permute-start.6) | collective-permute-done | bytes 65568 | tf_op jit(solution)/shard_map/ppermute | solution.py:37
  103.7 1.5 %all-to-all-done.4.refs_4_ = bf16[4,4,16,896]{3,2,1,0:T(8,128)(2,1)S(1)} async-done(((bf16[4,4,16,896]{3,2,1,0:T(8,128)(2,1)}), bf16[4,4,16,896]{3,2,1,0:T(8,128)(2,1)S(1)}, u32[]{:S(2)}, u32[]{:S(2)}) %all-to-all-start.4) | async-done | bytes 458784 | tf_op jit(solution)/shard_map/all_to_all | solution.py:253
  106.3 7.9 %collective-permute-start.7 = (bf16[8,16,896]{2,1,0:T(8,128)(2,1)S(1)}, bf16[8,16,896]{2,1,0:T(8,128)(2,1)S(1)}, u32[]{:S(2)}, u32[]{:S(2)}) collective-permute-start(bf16[8,16,896]{2,1,0:T(8,128)(2,1)S(1)} %get-tuple-element.33), channel_id=1, source_target_pairs={{0,8},{8,0},{1,9},{9,1},{2,10},{10,2},{3,11},{11,3},{4,12},{12,4},... | collective-permute-start | bytes 688136 | tf_op jit(solution)/shard_map/ppermute | solution.py:37
  115.3 17.7 %all_to_all.31 = bf16[8,16,896]{2,1,0:T(8,128)(2,1)S(1)} all-to-all(bf16[8,16,896]{2,1,0:T(8,128)(2,1)S(1)} %add_convert_fusion), channel_id=1, replica_groups=mesh['x'=4,'y'=8,'c'=2,'z'=8] {'y'}, dimensions={0} | all-to-all | bytes 458752 | tf_op jit(solution)/shard_map/all_to_all | solution.py:267
  (31 shorter events, 6.7 us)
Async XLA Ops:
  0.6 39.0 %copy-start = (s32[2,2]{1,0:T(2,128)S(1)}, s32[2,2]{1,0:T(2,128)}, u32[]{:S(2)}) copy-start(s32[2,2]{1,0:T(2,128)} %param.11) | copy-start | bytes 52
  0.6 46.1 %copy-start.2 = (s32[2,2]{1,0:T(2,128)S(1)}, s32[2,2]{1,0:T(2,128)}, u32[]{:S(2)}) copy-start(s32[2,2]{1,0:T(2,128)} %refs_0_.1) | copy-start | bytes 52
  0.7 47.5 %collective-permute-start.4 = (bf16[2,896,512]{2,1,0:T(8,128)(2,1)}, bf16[2,896,512]{2,1,0:T(8,128)(2,1)}, u32[]{:S(2)}, u32[]{:S(2)}) collective-permute-start(bf16[2,896,512]{2,1,0:T(8,128)(2,1)} %w_own.1), channel_id=1, source_target_pairs={{0,1},{1,0},{2,3},{3,2},{4,5},{5,4},{6,7},{7,6},{8,9},{9,8},{10,11... | collective-permute-start | bytes 5505032 | tf_op jit(solution)/shard_map/ppermute | solution.py:37
  6.9 17.5 %all-to-all-start = ((bf16[8,16,896]{2,1,0:T(8,128)(2,1)}), bf16[8,16,896]{2,1,0:T(8,128)(2,1)S(1)}, u32[]{:S(2)}, u32[]{:S(2)}) async-start(bf16[8,16,896]{2,1,0:T(8,128)(2,1)} %broadcast_in_dim.5), calls=%async_computation | async-start | bytes 458752 | tf_op jit(solution)/shard_map/all_to_all | solution.py:226
  13.8 7.9 %collective-permute-start.1 = (s32[2,2]{1,0:T(2,128)}, s32[2,2]{1,0:T(2,128)S(1)}, u32[]{:S(2)}, u32[]{:S(2)}) collective-permute-start(s32[2,2]{1,0:T(2,128)} %refs_0_.1), channel_id=1, source_target_pairs={{0,256},{128,384},{256,0},{384,128},{1,257},{129,385},{257,1},{385... | collective-permute-start | bytes 56 | tf_op jit(solution)/shard_map/ppermute | solution.py:33
  18.4 6.0 %collective-permute-start = (s32[2,2]{1,0:T(2,128)}, s32[2,2]{1,0:T(2,128)S(1)}, u32[]{:S(2)}, u32[]{:S(2)}) collective-permute-start(s32[2,2]{1,0:T(2,128)} %refs_0_.1), channel_id=1, source_target_pairs={{0,128},{128,256},{256,384},{384,0},{1,129},{129,257},{257,385},{3... | collective-permute-start | bytes 56 | tf_op jit(solution)/shard_map/ppermute | solution.py:33
  24.4 9.2 %collective-permute-start.3 = (bf16[8,16,896]{2,1,0:T(8,128)(2,1)S(1)}, bf16[8,16,896]{2,1,0:T(8,128)(2,1)S(1)}, u32[]{:S(2)}, u32[]{:S(2)}) collective-permute-start(bf16[8,16,896]{2,1,0:T(8,128)(2,1)S(1)} %all-to-all-done.refs_4_), channel_id=1, source_target_pairs={{0,8},{8,0},{1,9},{9,1},{2,10},{10,2},{3,11},{11,3},{4,12},{12,4},... | collective-permute-start | bytes 688136 | tf_op jit(solution)/shard_map/ppermute | solution.py:37
  28.7 4.9 %collective-permute-start.2 = (s32[2,2]{1,0:T(2,128)}, s32[2,2]{1,0:T(2,128)S(1)}, u32[]{:S(2)}, u32[]{:S(2)}) collective-permute-start(s32[2,2]{1,0:T(2,128)} %refs_0_.1), channel_id=1, source_target_pairs={{0,384},{128,0},{256,128},{384,256},{1,385},{129,1},{257,129},{385... | collective-permute-start | bytes 56 | tf_op jit(solution)/shard_map/ppermute | solution.py:33
  33.7 0.7 copy-start.1
  35.9 33.6 %copy-start.3 = (bf16[2,896,512]{2,1,0:T(8,128)(2,1)S(1)}, bf16[2,896,512]{2,1,0:T(8,128)(2,1)}, u32[]{:S(2)}) copy-start(bf16[2,896,512]{2,1,0:T(8,128)(2,1)} %w_own.1) | copy-start | bytes 5505028
  35.9 10.9 %all-to-all-start.1 = ((bf16[4,4,16,896]{3,2,1,0:T(8,128)(2,1)}), bf16[4,4,16,896]{3,2,1,0:T(8,128)(2,1)S(1)}, u32[]{:S(2)}, u32[]{:S(2)}) async-start(bf16[4,4,16,896]{3,2,1,0:T(8,128)(2,1)} %pick.1), calls=%async_computation.1 | async-start | bytes 917504 | tf_op jit(solution)/shard_map/all_to_all | solution.py:234
  48.1 21.4 %all-to-all-start.2 = ((bf16[8,2,16,896]{3,2,1,0:T(8,128)(2,1)}), bf16[8,2,16,896]{3,2,1,0:T(8,128)(2,1)S(1)}, u32[]{:S(2)}, u32[]{:S(2)}) async-start(bf16[8,2,16,896]{3,2,1,0:T(8,128)(2,1)} %spread.1), calls=%async_computation.2 | async-start | bytes 917504 | tf_op jit(solution)/shard_map/all_to_all | solution.py:242
  58.0 11.3 %collective-permute-start.5 = (bf16[128,512]{1,0:T(8,128)(2,1)S(1)}, bf16[128,512]{1,0:T(8,128)(2,1)S(1)}, u32[]{:S(2)}, u32[]{:S(2)}) collective-permute-start(bf16[128,512]{1,0:T(8,128)(2,1)S(1)} %pad_maximum_fusion), channel_id=1, source_target_pairs={{0,1},{1,0},{2,3},{3,2},{4,5},{5,4},{6,7},{7,6},{8,9},{9,8},{10,11... | collective-permute-start | bytes 393224 | tf_op jit(solution)/shard_map/ppermute | solution.py:37
  95.2 10.0 %all-to-all-start.4 = ((bf16[4,4,16,896]{3,2,1,0:T(8,128)(2,1)}), bf16[4,4,16,896]{3,2,1,0:T(8,128)(2,1)S(1)}, u32[]{:S(2)}, u32[]{:S(2)}) async-start(bf16[4,4,16,896]{3,2,1,0:T(8,128)(2,1)} %sums.1), calls=%async_computation.4 | async-start | bytes 917504 | tf_op jit(solution)/shard_map/all_to_all | solution.py:253
  98.7 5.0 %collective-permute-start.6 = (bf16[64,512]{1,0:T(8,128)(2,1)S(1)}, bf16[64,512]{1,0:T(8,128)(2,1)S(1)}, u32[]{:S(2)}, u32[]{:S(2)}) collective-permute-start(bf16[64,512]{1,0:T(8,128)(2,1)S(1)} %get-tuple-element.30), channel_id=1, source_target_pairs={{0,1},{1,0},{2,3},{3,2},{4,5},{5,4},{6,7},{7,6},{8,9},{9,8},{10,11... | collective-permute-start | bytes 196616 | tf_op jit(solution)/shard_map/ppermute | solution.py:37
  106.3 9.0 %collective-permute-start.7 = (bf16[8,16,896]{2,1,0:T(8,128)(2,1)S(1)}, bf16[8,16,896]{2,1,0:T(8,128)(2,1)S(1)}, u32[]{:S(2)}, u32[]{:S(2)}) collective-permute-start(bf16[8,16,896]{2,1,0:T(8,128)(2,1)S(1)} %get-tuple-element.33), channel_id=1, source_target_pairs={{0,8},{8,0},{1,9},{9,1},{2,10},{10,2},{3,11},{11,3},{4,12},{12,4},... | collective-permute-start | bytes 688136 | tf_op jit(solution)/shard_map/ppermute | solution.py:37
